TPU v7x, 512 devices: a whole 4x4x16 slice. The times are simulated.
512 devices in a mesh: dp: 8 (over x, y_hi), seq: 64 (over z, y_lo, core).
Axes of the slice: x: 4, y: 4 (y_hi: 2, y_lo: 2; y = y_hi * 2 + y_lo), z: 16, core: 2. Of those that a mesh axis runs over, the one named last changes fastest.
Arguments:
- tokens: bfloat16 [8, 64, 256, 1024], P('dp', 'seq'), may hold values from -24 to 24
- cotangent: bfloat16 [8, 64, 256, 1024], P('dp', 'seq'), may hold values from -16 to 16
- row_mask: int32 [4, 64, 2, 2], P(None, 'seq'), may hold values from 0 to 1, as said below
- column_mask: int32 [4, 256, 8, 8], P(None, 'seq'), may hold values from 0 to 1, as said below
- w_query: bfloat16 [1024, 512], P('dp'), may hold values from -0.25 to 0.25
- w_key: bfloat16 [1024, 512], P('dp'), may hold values from -0.25 to 0.25
- w_value: bfloat16 [1024, 512], P('dp'), may hold values from -0.1875 to 0.1875
- w_out: bfloat16 [512, 1024], P('dp'), may hold values from -0.25 to 0.25
Outputs:
- mixed: bfloat16 [8, 64, 256, 1024], P('dp', 'seq')
- grad_tokens: bfloat16 [8, 64, 256, 1024], P('dp', 'seq')
- grad_value: float32 [1024, 512], P(('dp', 'seq'))
- grad_output: float32 [512, 1024], P(None, ('dp', 'seq'))
Inputs may be any that keep to these rules, and one draw needn't show every extreme that they name: `row_mask`: each block mask is lower triangular with ones on its diagonal. `column_mask`: each block mask is lower triangular with ones on its diagonal.
All inputs are finite; a program needn't handle non-finite values.
Results may differ from a plain program's by a relative error of at most 0.015.
Values may be sent and summed in bfloat16 or wider, within the bound.
No kernel may reach another device: no remote copies, remote signals or barrier semaphores. Data moves between devices by JAX's collectives and lax.ppermute only.
A program may use at most 64 MiB of HBM per device.

v0:
```python
import math

import jax
import jax.numpy as jnp
from jax import lax
from jax.sharding import PartitionSpec as P

HEAD_DIM = 64
ROWBLK = 128
COLBLK = 8


row_forms = ("blhe,bmhe->bhlm", "bhlm,bmhe->blhe")
column_forms = ("lbhe,mbhe->bhlm", "bhlm,mbhe->lbhe")
contract_last = (((1,), (1,)), ((), ()))
contract_first = (((0,), (0,)), ((), ()))


def allowed_cells(mask_blocks, block_size):
    expanded = jnp.repeat(jnp.repeat(mask_blocks, block_size, axis=-2), block_size, axis=-1)
    length = expanded.shape[-1]
    causal = jnp.arange(length)[:, None] >= jnp.arange(length)[None, :]
    return (expanded == 1) & causal


def attend(queries, key_part, value_part, allowed, forms):
    scale_factor = 1.0 / math.sqrt(queries.shape[-1])
    scores = (
        jnp.einsum(forms[0], queries.astype(jnp.float32), key_part.astype(jnp.float32))
        * scale_factor
    )
    scores = jnp.where(allowed, scores, -1e30)
    highest = lax.stop_gradient(jnp.max(scores, axis=-1, keepdims=True))
    weights = jnp.exp(scores - highest)
    weights = weights / jnp.sum(weights, axis=-1, keepdims=True)
    rounded = lax.optimization_barrier(weights.astype(jnp.bfloat16)).astype(jnp.float32)
    result = jnp.einsum(forms[1], rounded, value_part.astype(jnp.float32))
    return result.astype(jnp.bfloat16)


def body(tokens, cotangent, row_mask, column_mask, w_query, w_key, w_value, w_out):
    rows_here = tokens.shape[1]
    grid_cols = tokens.shape[2]
    width = tokens.shape[3]
    heads_width = w_query.shape[1]
    half = heads_width // HEAD_DIM // 2
    split = half * HEAD_DIM
    flat = tokens.reshape(-1, width)
    cot_flat = cotangent.reshape(-1, width)
    token_count = flat.shape[0]
    seq_count = lax.axis_size("seq")
    grid_rows = rows_here * seq_count
    cols_here = grid_cols // seq_count
    full_query, full_key, full_value, full_out = (
        lax.all_gather(w_query, "dp", axis=0, tiled=True),
        lax.all_gather(w_key, "dp", axis=0, tiled=True),
        lax.all_gather(w_value, "dp", axis=0, tiled=True),
        lax.all_gather(w_out, "dp", axis=0, tiled=True),
    )
    proj_query = jnp.dot(flat, full_query, preferred_element_type=jnp.float32)
    proj_key = jnp.dot(flat, full_key, preferred_element_type=jnp.float32)
    proj_value = jnp.dot(flat, full_value, preferred_element_type=jnp.float32)
    query_flat = proj_query.astype(jnp.bfloat16)
    key_flat = proj_key.astype(jnp.bfloat16)
    value_flat = proj_value.astype(jnp.bfloat16)
    row_allowed = allowed_cells(jnp.transpose(row_mask, (1, 0, 2, 3)), ROWBLK)
    column_allowed = allowed_cells(jnp.transpose(column_mask, (1, 0, 2, 3)), COLBLK)

    def row_core(first, second, third):
        return attend(first, second, third, row_allowed, row_forms)

    def column_core(first, second, third):
        return attend(first, second, third, column_allowed, column_forms)

    def row_heads(matrix):
        return matrix[:, :split].reshape(rows_here, grid_cols, half, HEAD_DIM)

    def column_heads(matrix):
        return matrix[:, split:].reshape(rows_here, grid_cols, split)

    def as_columns(block):
        return block.reshape(grid_rows, cols_here, half, HEAD_DIM)

    def joined(row_part, col_part):
        return jnp.concatenate(
            [row_part.reshape(token_count, split), col_part.reshape(token_count, split)], axis=1
        )

    col_query, col_key, col_value = (
        lax.all_to_all(column_heads(query_flat), "seq", split_axis=1, concat_axis=0, tiled=True),
        lax.all_to_all(column_heads(key_flat), "seq", split_axis=1, concat_axis=0, tiled=True),
        lax.all_to_all(column_heads(value_flat), "seq", split_axis=1, concat_axis=0, tiled=True),
    )
    row_out, row_back = jax.vjp(
        row_core, row_heads(query_flat), row_heads(key_flat), row_heads(value_flat)
    )
    column_out, column_back = jax.vjp(
        column_core, as_columns(col_query), as_columns(col_key), as_columns(col_value)
    )
    returned = lax.all_to_all(
        column_out.reshape(grid_rows, cols_here, split),
        "seq",
        split_axis=0,
        concat_axis=1,
        tiled=True,
    )
    attended = joined(row_out, returned)
    mixed = jnp.dot(attended, full_out, preferred_element_type=jnp.float32)
    grad_heads = lax.dot_general(
        cot_flat, full_out, contract_last, preferred_element_type=jnp.float32
    )
    mixed = mixed.astype(jnp.bfloat16).reshape(tokens.shape)
    grad_heads = grad_heads.astype(jnp.bfloat16)
    row_grads = row_back(grad_heads[:, :split].reshape(rows_here, grid_cols, half, HEAD_DIM))
    grad_columns = lax.all_to_all(
        grad_heads[:, split:].reshape(rows_here, grid_cols, split),
        "seq",
        split_axis=1,
        concat_axis=0,
        tiled=True,
    )
    col_grads = column_back(as_columns(grad_columns))
    back_grads = (
        lax.all_to_all(
            col_grads[0].reshape(grid_rows, cols_here, split),
            "seq",
            split_axis=0,
            concat_axis=1,
            tiled=True,
        ),
        lax.all_to_all(
            col_grads[1].reshape(grid_rows, cols_here, split),
            "seq",
            split_axis=0,
            concat_axis=1,
            tiled=True,
        ),
        lax.all_to_all(
            col_grads[2].reshape(grid_rows, cols_here, split),
            "seq",
            split_axis=0,
            concat_axis=1,
            tiled=True,
        ),
    )
    grad_query = joined(row_grads[0], back_grads[0])
    grad_key = joined(row_grads[1], back_grads[1])
    grad_val = joined(row_grads[2], back_grads[2])
    grad_tokens = (
        lax.dot_general(grad_query, full_query, contract_last, preferred_element_type=jnp.float32)
        + lax.dot_general(grad_key, full_key, contract_last, preferred_element_type=jnp.float32)
        + lax.dot_general(grad_val, full_value, contract_last, preferred_element_type=jnp.float32)
    )
    grad_tokens = grad_tokens.astype(jnp.bfloat16).reshape(tokens.shape)
    summed = lax.psum_scatter(
        jnp.concatenate(
            [
                lax.dot_general(flat, grad_val, contract_first, preferred_element_type=jnp.float32),
                lax.dot_general(
                    cot_flat, attended, contract_first, preferred_element_type=jnp.float32
                ),
            ],
            axis=1,
        ),
        ("dp", "seq"),
        scatter_dimension=0,
        tiled=True,
    )
    grad_value = summed[:, :heads_width]
    grad_output = jnp.transpose(summed[:, heads_width:])
    return (mixed, grad_tokens, grad_value, grad_output)


def solution(mesh):
    return jax.shard_map(
        body,
        mesh=mesh,
        in_specs=(
            P("dp", "seq", None, None),
            P("dp", "seq", None, None),
            P(None, "seq", None, None),
            P(None, "seq", None, None),
            P("dp", None),
            P("dp", None),
            P("dp", None),
            P("dp", None),
        ),
        out_specs=(
            P("dp", "seq", None, None),
            P("dp", "seq", None, None),
            P(("dp", "seq"), None),
            P(None, ("dp", "seq")),
        ),
        check_vma=False,
    )
```

profile of v0, /device:TPU:6, one launch (start us, length us, event | category | flops | bytes accessed | tf_op | source)
XLA Modules:
  0.0 911.2 jit_solution(8901984965203188989)
XLA Ops:
  10.0 0.9 compare_bitcast_fusion
  12.5 65.7 %all-gather.9.cloned.1.call-done = bf16[1024,512]{1,0:T(8,128)(2,1)} async-done(((bf16[128,512]{1,0:T(8,128)(2,1)}), bf16[1024,512]{1,0:T(8,128)(2,1)}) %all-gather.9.cloned.1.call-update) | async-done | bytes 1048592 | tf_op jit(solution)/shard_map/all_gather | solution.py:56
  78.2 1.7 convolution_convert_fusion.8
  80.6 1.4 reduce.13
  82.0 0.7 reshape.317
  82.8 13.2 %all-to-all-start.2 = ((bf16[64,2,512]{2,1,0:T(2,128)(2,1)}), bf16[64,2,512]{2,1,0:T(2,128)(2,1)S(1)}, u32[]{:S(2)}, u32[]{:S(2)}) async-start(bf16[64,2,512]{2,1,0:T(2,128)(2,1)} %reshape.317), calls=%async_computation.2 | async-start | bytes 262144 | tf_op jit(solution)/shard_map/all_to_all | solution.py:91
  96.0 47.4 %all-gather.7.cloned.1.call-done = bf16[1024,512]{1,0:T(8,128)(2,1)} async-done(((bf16[128,512]{1,0:T(8,128)(2,1)}), bf16[1024,512]{1,0:T(8,128)(2,1)}) %all-gather.7.cloned.1.call-update) | async-done | bytes 1048592 | tf_op jit(solution)/shard_map/all_gather | solution.py:55
  143.4 1.7 convolution_convert_fusion.9
  145.1 63.3 %all-gather.5.cloned.1.call-done = bf16[1024,512]{1,0:T(8,128)(2,1)} async-done(((bf16[128,512]{1,0:T(8,128)(2,1)}), bf16[1024,512]{1,0:T(8,128)(2,1)}) %all-gather.5.cloned.1.call-update) | async-done | bytes 1048592 | tf_op jit(solution)/shard_map/all_gather | solution.py:57
  208.3 1.7 convolution_convert_fusion.10
  210.2 1.4 reduce.14
  211.6 0.7 reshape.319
  212.6 1.4 reduce.15
  214.0 0.8 reshape.321
  214.8 58.4 %all-gather.11.cloned.1.call-done = bf16[512,1024]{1,0:T(8,128)(2,1)} async-done(((bf16[64,1024]{1,0:T(8,128)(2,1)}), bf16[512,1024]{1,0:T(8,128)(2,1)}) %all-gather.11.cloned.1.call-update) | async-done | bytes 1048592 | tf_op jit(solution)/shard_map/all_gather | solution.py:58
  273.1 1.7 convolution_convert_fusion.6
  275.1 1.4 reduce.16
  277.6 13.2 %all-to-all-start.1 = ((bf16[64,2,512]{2,1,0:T(2,128)(2,1)}), bf16[64,2,512]{2,1,0:T(2,128)(2,1)S(1)}, u32[]{:S(2)}, u32[]{:S(2)}) async-start(bf16[64,2,512]{2,1,0:T(2,128)(2,1)} %reshape.319), calls=%async_computation.1 | async-start | bytes 262144 | tf_op jit(solution)/shard_map/all_to_all | solution.py:90
  291.6 16.3 %all-to-all-done.1 = bf16[64,2,512]{2,1,0:T(2,128)(2,1)S(1)} async-done(((bf16[64,2,512]{2,1,0:T(2,128)(2,1)}), bf16[64,2,512]{2,1,0:T(2,128)(2,1)S(1)}, u32[]{:S(2)}, u32[]{:S(2)}) %all-to-all-start.1) | async-done | bytes 131104 | tf_op jit(solution)/shard_map/all_to_all | solution.py:90
  307.9 4.8 all-to-all-start
  312.7 0.9 convolution_convert_fusion.12
  315.2 14.3 %all-to-all-done = bf16[64,2,512]{2,1,0:T(2,128)(2,1)S(1)} async-done(((bf16[64,2,512]{2,1,0:T(2,128)(2,1)}), bf16[64,2,512]{2,1,0:T(2,128)(2,1)S(1)}, u32[]{:S(2)}, u32[]{:S(2)}) %all-to-all-start) | async-done | bytes 131104 | tf_op jit(solution)/shard_map/all_to_all | solution.py:92
  329.5 4.6 all-to-all-start.4
  335.0 0.9 reshape.289
  335.9 0.9 reshape.287
  336.9 1.3 fusion.11
  338.2 0.8 copy-done.8
  339.0 0.9 fusion.68
  339.9 11.2 %all-to-all-done.4 = bf16[64,2,512]{2,1,0:T(2,128)(2,1)S(1)} async-done(((bf16[64,2,512]{2,1,0:T(2,128)(2,1)}), bf16[64,2,512]{2,1,0:T(2,128)(2,1)S(1)}, u32[]{:S(2)}, u32[]{:S(2)}) %all-to-all-start.4) | async-done | bytes 131104 | tf_op jit(solution)/shard_map/all_to_all | solution.py:115
  352.5 1.3 fusion.26
  354.0 0.8 copy.130
  354.8 5.4 all-to-all-start.3
  360.6 1.0 copy.131
  361.6 0.9 convolution_convert_fusion.11
  362.6 1.1 copy.153
  363.7 1.0 convolution_convert_fusion.2
  364.7 1.8 copy.152
  366.4 10.7 %all-to-all-done.3 = bf16[64,4,256]{2,1,0:T(4,128)(2,1)} async-done(((bf16[64,4,256]{2,1,0:T(4,128)(2,1)}), bf16[64,4,256]{2,1,0:T(4,128)(2,1)}, u32[]{:S(2)}, u32[]{:S(2)}) %all-to-all-start.3) | async-done | bytes 131104 | tf_op jit(solution)/shard_map/all_to_all | solution.py:100
  377.1 4.6 all-to-all-start.7
  381.8 2.6 fusion.12
  384.3 1.2 copy.168
  385.5 0.9 reshape.309
  386.4 0.9 reshape.291
  387.3 1.8 convolution_bitcast_fusion
  389.1 9.7 %all-to-all-done.7 = bf16[64,4,256]{2,1,0:T(4,128)(2,1)S(1)} async-done(((bf16[64,4,256]{2,1,0:T(4,128)(2,1)}), bf16[64,4,256]{2,1,0:T(4,128)(2,1)S(1)}, u32[]{:S(2)}, u32[]{:S(2)}) %all-to-all-start.7) | async-done | bytes 131104 | tf_op jit(solution)/shard_map/all_to_all | solution.py:138
  398.8 4.6 all-to-all-start.5
  404.2 1.1 copy-done.1
  405.3 2.5 pad_maximum_fusion
  407.8 0.9 copy-done.7
  408.8 2.3 fusion.13
  411.1 1.2 copy.169
  412.3 0.9 reshape.310
  413.2 7.3 all-to-all-done.5
  420.4 6.6 all-to-all-start.6
  427.5 1.2 fusion.71
  428.8 1.2 fusion.70
  430.1 1.0 reshape.301
  431.2 13.3 %all-to-all-done.6 = bf16[64,4,256]{2,1,0:T(4,128)(2,1)} async-done(((bf16[64,4,256]{2,1,0:T(4,128)(2,1)}), bf16[64,4,256]{2,1,0:T(4,128)(2,1)}, u32[]{:S(2)}, u32[]{:S(2)}) %all-to-all-start.6) | async-done | bytes 131104 | tf_op jit(solution)/shard_map/all_to_all | solution.py:131
  444.5 1.6 reshape.304
  446.1 2.5 fusion.10
  448.6 1.7 fusion.36
  450.8 1.3 fusion.9
  452.1 449.9 %all-reduce.3.cloned.1.call-done = f32[1024,1024]{0,1:T(8,128)} async-done(((f32[1024,1024]{0,1:T(8,128)}), f32[1024,1024]{0,1:T(8,128)}) %all-reduce.3.cloned.1.call-update) | async-done | bytes 4194320
  902.0 1.2 dynamic-slice_bitcast_fusion
  (89 shorter events, 15.6 us)
Async XLA Ops:
  7.2 71.0 %copy-start = (bf16[1,1,256,1024]{3,2,1,0:T(8,128)(2,1)S(1)}, bf16[1,1,256,1024]{3,2,1,0:T(8,128)(2,1)}, u32[]{:S(2)}) copy-start(bf16[1,1,256,1024]{3,2,1,0:T(8,128)(2,1)} %param.8) | copy-start | bytes 1572868
  7.2 71.0 %all-gather.9.cloned.1.call-start = ((), (), s32[]{:S(2)}) async-start(), calls=%async_computation.10 | async-start | bytes 1179648 | tf_op jit(solution)/shard_map/all_gather | solution.py:56
  7.9 135.5 %all-gather.7.cloned.1.call-start = ((), (), s32[]{:S(2)}) async-start(), calls=%async_computation.9 | async-start | bytes 1179648 | tf_op jit(solution)/shard_map/all_gather | solution.py:55
  8.7 199.7 %all-gather.5.cloned.1.call-start = ((), (), s32[]{:S(2)}) async-start(), calls=%async_computation.8 | async-start | bytes 1179648 | tf_op jit(solution)/shard_map/all_gather | solution.py:57
  9.4 263.7 %all-gather.11.cloned.1.call-start = ((), (), s32[]{:S(2)}) async-start(), calls=%async_computation.11 | async-start | bytes 1179648 | tf_op jit(solution)/shard_map/all_gather | solution.py:58
  79.9 193.3 %copy-start.4 = (bf16[1,1,256,1024]{3,2,1,0:T(8,128)(2,1)S(1)}, bf16[1,1,256,1024]{3,2,1,0:T(8,128)(2,1)}, u32[]{:S(2)}) copy-start(bf16[1,1,256,1024]{3,2,1,0:T(8,128)(2,1)} %param.9) | copy-start | bytes 1572868
  82.8 194.8 %all-to-all-start.2 = ((bf16[64,2,512]{2,1,0:T(2,128)(2,1)}), bf16[64,2,512]{2,1,0:T(2,128)(2,1)S(1)}, u32[]{:S(2)}, u32[]{:S(2)}) async-start(bf16[64,2,512]{2,1,0:T(2,128)(2,1)} %reshape.317), calls=%async_computation.2 | async-start | bytes 262144 | tf_op jit(solution)/shard_map/all_to_all | solution.py:91
  277.4 14.0 %copy-start.10 = (bf16[256,256]{0,1:T(8,128)(2,1)}, bf16[256,256]{0,1:T(8,128)(2,1)S(1)}, u32[]{:S(2)}) copy-start(bf16[256,256]{0,1:T(8,128)(2,1)S(1)} %copy.119) | copy-start | bytes 393220
  277.6 35.1 %copy-start.11 = (bf16[256,256]{0,1:T(8,128)(2,1)}, bf16[256,256]{0,1:T(8,128)(2,1)S(1)}, u32[]{:S(2)}) copy-start(bf16[256,256]{0,1:T(8,128)(2,1)S(1)} %copy.120) | copy-start | bytes 393220
  277.6 30.3 %all-to-all-start.1 = ((bf16[64,2,512]{2,1,0:T(2,128)(2,1)}), bf16[64,2,512]{2,1,0:T(2,128)(2,1)S(1)}, u32[]{:S(2)}, u32[]{:S(2)}) async-start(bf16[64,2,512]{2,1,0:T(2,128)(2,1)} %reshape.319), calls=%async_computation.1 | async-start | bytes 262144 | tf_op jit(solution)/shard_map/all_to_all | solution.py:90
  307.9 21.7 %all-to-all-start = ((bf16[64,2,512]{2,1,0:T(2,128)(2,1)}), bf16[64,2,512]{2,1,0:T(2,128)(2,1)S(1)}, u32[]{:S(2)}, u32[]{:S(2)}) async-start(bf16[64,2,512]{2,1,0:T(2,128)(2,1)} %reshape.321), calls=%async_computation | async-start | bytes 262144 | tf_op jit(solution)/shard_map/all_to_all | solution.py:92
  329.5 21.6 %all-to-all-start.4 = ((bf16[64,2,512]{2,1,0:T(2,128)(2,1)}), bf16[64,2,512]{2,1,0:T(2,128)(2,1)S(1)}, u32[]{:S(2)}, u32[]{:S(2)}) async-start(bf16[64,2,512]{2,1,0:T(2,128)(2,1)} %reshape.323), calls=%async_computation.4 | async-start | bytes 262144 | tf_op jit(solution)/shard_map/all_to_all | solution.py:115
  338.2 0.8 copy-start.8
  352.4 1.3 copy-start.6
  354.8 22.3 %all-to-all-start.3 = ((bf16[64,4,256]{2,1,0:T(4,128)(2,1)}), bf16[64,4,256]{2,1,0:T(4,128)(2,1)}, u32[]{:S(2)}, u32[]{:S(2)}) async-start(bf16[64,4,256]{2,1,0:T(4,128)(2,1)} %copy.130), calls=%async_computation.3 | async-start | bytes 262144 | tf_op jit(solution)/shard_map/all_to_all | solution.py:100
  362.6 24.7 %copy-start.5 = (bf16[1,1,256,1024]{3,2,1,0:T(8,128)(2,1)S(1)}, bf16[1,1,256,1024]{3,2,1,0:T(8,128)(2,1)}, u32[]{:S(2)}) copy-start(bf16[1,1,256,1024]{3,2,1,0:T(8,128)(2,1)} %param.9) | copy-start | bytes 1572868
  377.1 21.6 %all-to-all-start.7 = ((bf16[64,4,256]{2,1,0:T(4,128)(2,1)}), bf16[64,4,256]{2,1,0:T(4,128)(2,1)S(1)}, u32[]{:S(2)}, u32[]{:S(2)}) async-start(bf16[64,4,256]{2,1,0:T(4,128)(2,1)} %copy.152), calls=%async_computation.7 | async-start | bytes 262144 | tf_op jit(solution)/shard_map/all_to_all | solution.py:138
  398.8 21.7 %all-to-all-start.5 = ((bf16[64,4,256]{2,1,0:T(4,128)(2,1)}), bf16[64,4,256]{2,1,0:T(4,128)(2,1)S(1)}, u32[]{:S(2)}, u32[]{:S(2)}) async-start(bf16[64,4,256]{2,1,0:T(4,128)(2,1)} %reshape.309), calls=%async_computation.5 | async-start | bytes 262144 | tf_op jit(solution)/shard_map/all_to_all | solution.py:124
  403.4 498.6 %all-reduce.3.cloned.1.call-start = ((), (), s32[]{:S(2)}) async-start(), calls=%async_computation.12 | async-start | bytes 8388608
  403.7 1.6 copy-start.1
  407.8 0.9 copy-start.7
  407.8 1.0 copy-start.13
  420.4 6.8 copy-start.9
  420.4 24.0 %all-to-all-start.6 = ((bf16[64,4,256]{2,1,0:T(4,128)(2,1)}), bf16[64,4,256]{2,1,0:T(4,128)(2,1)}, u32[]{:S(2)}, u32[]{:S(2)}) async-start(bf16[64,4,256]{2,1,0:T(4,128)(2,1)} %reshape.310), calls=%async_computation.6 | async-start | bytes 262144 | tf_op jit(solution)/shard_map/all_to_all | solution.py:131
  427.5 22.8 %copy-start.2 = (bf16[1024,512]{1,0:T(8,128)(2,1)S(1)}, bf16[1024,512]{1,0:T(8,128)(2,1)}, u32[]{:S(2)}) copy-start(bf16[1024,512]{1,0:T(8,128)(2,1)} %all-gather.9.cloned.1.call-done) | copy-start | bytes 3145732
  430.0 20.7 %copy-start.3 = (bf16[1024,512]{1,0:T(8,128)(2,1)S(1)}, bf16[1024,512]{1,0:T(8,128)(2,1)}, u32[]{:S(2)}) copy-start(bf16[1024,512]{1,0:T(8,128)(2,1)} %all-gather.5.cloned.1.call-done) | copy-start | bytes 3145732
  446.1 4.2 copy-start.12
Sparse Core Ops, SparseCore 0:
  11.2 66.9 all-gather.8
  81.4 61.9 all-gather.6
  146.6 61.6 all-gather.4
  211.4 61.6 all-gather.10
  409.4 492.5 all-reduce.2
where the time goes:
time: 913 us; the launch traced here: 911 us
  waiting for transfers between devices  770 us (84%)
  starting transfers between devices  57.5 us (6%)
  local copies, waits for them, and re-layouts  29 us (3%)
  matrix products  27.7 us (3%)
  between operations  14.4 us (2%)
  other arithmetic  12.6 us (1%)
    unnamed x6, waiting for transfers between devices  453 us
    all_gather x1, waiting for transfers between devices, body(): lax.all_gather(w_key, 'dp', axis=0, tiled=True)  65.7 us
    all_gather x1, waiting for transfers between devices, body(): lax.all_gather(w_value, 'dp', axis=0, tiled=True)  63.3 us
    all_gather x1, waiting for transfers between devices, body(): lax.all_gather(w_out, 'dp', axis=0, tiled=True)  58.4 us
    all_gather x1, waiting for transfers between devices, body(): lax.all_gather(w_query, 'dp', axis=0, tiled=True)  47.4 us
  transfers between devices with their start and end apart: 13, of which 12 were waited for; matrix products, arithmetic and copies ran while one was open for 7% of the time, Pallas kernels for 0%

commit v1 on v0

v1 whole, which is shorter than its diff:
```python
import functools

import jax
import jax.numpy as jnp
from jax import lax
from jax.experimental import pallas as pl
from jax.experimental.pallas import tpu as pltpu
from jax.sharding import Mesh, PartitionSpec as P

HEAD_DIM = 64
ROWBLK = 128
COLBLK = 8
BF = jnp.bfloat16
F32 = jnp.float32
LAST = (((1,), (1,)), ((), ()))
FIRST = (((0,), (0,)), ((), ()))
MASKED = -1e30


def weight_copies(core, own, other, slots, wo_ref, sems, kinds):
    copies = []
    for k, kind in enumerate(kinds):
        for half, src in ((core, own), (1 - core, other)):
            for b in range(2):
                copies.append(
                    pltpu.make_async_copy(
                        src.at[pl.ds(kind * 4, 4), pl.ds(b * 64, 64), pl.ds(768, 256)],
                        wo_ref.at[k, half * 2 + b],
                        sems.at[len(copies)],
                    )
                )
    return copies


def head_kernel(
    kind,
    core_ref,
    x_ref,
    ct_ref,
    bias_ref,
    own_ref,
    other_ref,
    parts_ref,
    keep_ref,
    send_ref,
    wqkv,
    wo,
    sems,
):
    core = core_ref[0]
    copies = weight_copies(core, own_ref, other_ref, None, wo, sems, (kind,))
    projections = pl.ds(0, 768)

    @pl.when(core == kind)
    def _():
        pltpu.make_async_copy(own_ref.at[:, :, projections], wqkv, sems.at[4]).start()

    @pl.when(core != kind)
    def _():
        pltpu.make_async_copy(other_ref.at[:, :, projections], wqkv, sems.at[4]).start()

    for copy in copies:
        copy.start()
    pltpu.make_async_copy(own_ref.at[:, :, projections], wqkv, sems.at[4]).wait()
    for copy in copies:
        copy.wait()

    x = x_ref[...]
    ct = ct_ref[...]
    width = x.shape[1]
    qkv = jnp.dot(x, wqkv[...].reshape(width, 768), preferred_element_type=F32).astype(BF)
    q, k, v = qkv[:, :256], qkv[:, 256:512], qkv[:, 512:]
    do = jnp.zeros((x.shape[0], 256), F32)
    for block in range(4):
        do += lax.dot_general(
            ct[:, block * 256 : (block + 1) * 256],
            wo[0, block].reshape(256, 256),
            LAST,
            preferred_element_type=F32,
        )
    do = do.astype(BF)
    lane = lax.broadcasted_iota(jnp.int32, (x.shape[0], 256), 1) // HEAD_DIM
    zero = jnp.zeros_like(q)
    out = jnp.zeros((x.shape[0], 256), F32)
    dq, dk, dv = out, out, out
    for h in range(4):
        mine = lane == h
        kh, vh = jnp.where(mine, k, zero), jnp.where(mine, v, zero)
        qh, doh = jnp.where(mine, q, zero), jnp.where(mine, do, zero)
        s = lax.dot_general(q, kh, LAST, preferred_element_type=F32) * 0.125
        s = s + bias_ref[h].astype(F32)
        e = jnp.exp(s - jnp.max(s, axis=-1, keepdims=True))
        w = e * (1.0 / jnp.sum(e, axis=-1, keepdims=True))
        p = w.astype(BF)
        out += jnp.dot(p, vh, preferred_element_type=F32)
        dp = lax.dot_general(do, vh, LAST, preferred_element_type=F32).astype(BF).astype(F32)
        ds = w * (dp - jnp.sum(dp * w, axis=-1, keepdims=True)) * 0.125
        ds = ds.astype(BF)
        dq += jnp.dot(ds, kh, preferred_element_type=F32)
        dk += lax.dot_general(ds, qh, FIRST, preferred_element_type=F32)
        dv += lax.dot_general(p, doh, FIRST, preferred_element_type=F32)
    out, dv = out.astype(BF), dv.astype(BF)
    parts_ref[:, 0:256] = out
    parts_ref[:, 256:512] = dq.astype(BF)
    parts_ref[:, 512:768] = dk.astype(BF)
    parts_ref[:, 768:1024] = dv
    grad_value = lax.dot_general(x, dv, FIRST, preferred_element_type=F32).astype(BF)
    grad_out = lax.dot_general(ct, out, FIRST, preferred_element_type=F32).astype(BF)

    @pl.when(core == 0)
    def _():
        keep_ref[...] = grad_value
        send_ref[...] = grad_out

    @pl.when(core != 0)
    def _():
        keep_ref[...] = grad_out
        send_ref[...] = grad_value


def heads_call(kind, core, x, ct, bias, own, other):
    rows, width = x.shape
    vmem = pl.BlockSpec(memory_space=pltpu.VMEM)
    return pl.pallas_call(
        functools.partial(head_kernel, kind),
        out_shape=(
            jax.ShapeDtypeStruct((rows, 1024), BF),
            jax.ShapeDtypeStruct((width, 256), BF),
            jax.ShapeDtypeStruct((width, 256), BF),
        ),
        in_specs=[
            pl.BlockSpec(memory_space=pltpu.SMEM),
            vmem,
            vmem,
            vmem,
            pl.BlockSpec(memory_space=pl.ANY),
            pl.BlockSpec(memory_space=pl.ANY),
        ],
        out_specs=(vmem, vmem, vmem),
        scratch_shapes=[
            pltpu.VMEM((8, 128, 768), BF),
            pltpu.VMEM((1, 4, 4, 64, 256), BF),
            pltpu.SemaphoreType.DMA((5,)),
        ],
        compiler_params=pltpu.CompilerParams(vmem_limit_bytes=40 * 1024 * 1024),
        cost_estimate=pl.CostEstimate(flops=1400000000, bytes_accessed=6000000, transcendentals=262144),
        name="row_heads" if kind == 0 else "column_heads",
    )(core, x, ct, bias, own, other)


def final_kernel(core_ref, row_ref, col_ref, own_ref, other_ref, mixed_ref, gt_ref, wqkv, wo, sems):
    core = core_ref[0]
    copies = weight_copies(core, own_ref, other_ref, None, wo, sems, (0, 1))
    for half, src in ((core, own_ref), (1 - core, other_ref)):
        copies.append(
            pltpu.make_async_copy(src.at[:, :, pl.ds(0, 768)], wqkv.at[half], sems.at[len(copies)])
        )
    for copy in copies:
        copy.start()
    for copy in copies:
        copy.wait()
    sides = (row_ref[...], col_ref[...])
    for block in range(4):
        total = jnp.zeros((row_ref.shape[0], 256), F32)
        for kind in range(2):
            total += jnp.dot(
                sides[kind][:, :256], wo[kind, block].reshape(256, 256), preferred_element_type=F32
            )
        mixed_ref[:, block * 256 : (block + 1) * 256] = total.astype(BF)
    total = jnp.zeros(gt_ref.shape, F32)
    for kind in range(2):
        total += lax.dot_general(
            sides[kind][:, 256:],
            wqkv[kind].reshape(1024, 768),
            LAST,
            preferred_element_type=F32,
        )
    gt_ref[...] = total.astype(BF)


def final_call(core, row_parts, col_parts, own, other):
    rows = row_parts.shape[0]
    vmem = pl.BlockSpec(memory_space=pltpu.VMEM)
    anywhere = pl.BlockSpec(memory_space=pl.ANY)
    return pl.pallas_call(
        final_kernel,
        out_shape=(
            jax.ShapeDtypeStruct((rows, 1024), BF),
            jax.ShapeDtypeStruct((rows, 1024), BF),
        ),
        in_specs=[pl.BlockSpec(memory_space=pltpu.SMEM), vmem, vmem, anywhere, anywhere],
        out_specs=(vmem, vmem),
        scratch_shapes=[
            pltpu.VMEM((2, 8, 128, 768), BF),
            pltpu.VMEM((2, 4, 4, 64, 256), BF),
            pltpu.SemaphoreType.DMA((10,)),
        ],
        compiler_params=pltpu.CompilerParams(vmem_limit_bytes=40 * 1024 * 1024),
        cost_estimate=pl.CostEstimate(flops=1100000000, bytes_accessed=6000000, transcendentals=0),
        name="output_products",
    )(core, row_parts, col_parts, own, other)


def one_hot(index, size):
    return (index[:, None] == jnp.arange(size)[None, :]).astype(BF)


def biases(row_mask, column_mask):
    position = jnp.arange(256)
    seen = position[:, None] >= position[None, :]
    row_in = one_hot(position // ROWBLK, 2)
    row_blocks = jnp.einsum(
        "ia,hab,jb->hij", row_in, row_mask[:, 0].astype(BF), row_in, preferred_element_type=BF
    )
    same = (position[:, None] % 4) == (position[None, :] % 4)
    col_left = one_hot((position % 4) * 8 + position // (4 * COLBLK), 32)
    col_right = one_hot(position // (4 * COLBLK), 8)
    col_blocks = jnp.einsum(
        "ia,hab,jb->hij",
        col_left,
        column_mask.reshape(4, 32, 8).astype(BF),
        col_right,
        preferred_element_type=BF,
    )
    row_bias = jnp.where((row_blocks > 0.5) & seen, 0.0, MASKED).astype(BF)
    col_bias = jnp.where((col_blocks > 0.5) & seen & same, 0.0, MASKED).astype(BF)
    return row_bias, col_bias


def body(tokens, cotangent, row_mask, column_mask, w_query, w_key, w_value, w_out):
    core = lax.axis_index("c")
    core_arg = core.astype(jnp.int32).reshape(1)
    flat = tokens.reshape(256, 1024)
    cot_flat = cotangent.reshape(256, 1024)
    seq = ("z", "yl", "c")

    def to_columns(matrix):
        moved = lax.all_to_all(
            matrix.reshape(64, 4, 1024), seq, split_axis=0, concat_axis=0, tiled=True
        )
        return moved.reshape(256, 1024)

    with jax.named_scope("weights"):
        def half_of(weight):
            return lax.dynamic_slice_in_dim(weight, core * 256, 256, axis=1)

        out_half = lax.dynamic_slice_in_dim(w_out, core * 512, 512, axis=1)
        packed = jnp.concatenate(
            [
                half_of(w_query),
                half_of(w_key),
                half_of(w_value),
                jnp.concatenate([out_half[:, :256], out_half[:, 256:]], axis=0),
            ],
            axis=1,
        )
        own = lax.all_to_all(
            jnp.broadcast_to(packed[None], (8, 128, 1024)),
            ("x", "yh"),
            split_axis=0,
            concat_axis=0,
            tiled=True,
        )
        other = lax.ppermute(own, "c", [(0, 1), (1, 0)])
    with jax.named_scope("to_columns"):
        col_tokens = to_columns(flat)
        col_cot = to_columns(cot_flat)
    with jax.named_scope("masks"):
        row_bias, col_bias = biases(row_mask, column_mask)
    row_parts, row_keep, row_send = heads_call(0, core_arg, flat, cot_flat, row_bias, own, other)
    col_parts, col_keep, col_send = heads_call(
        1, core_arg, col_tokens, col_cot, col_bias, own, other
    )
    with jax.named_scope("from_columns"):
        returned = lax.all_to_all(
            col_parts.reshape(64, 4, 1024), seq, split_axis=0, concat_axis=0, tiled=True
        ).reshape(256, 1024)
    with jax.named_scope("gradient_sums"):
        def core_sum(keep, send):
            got = lax.ppermute(send, "c", [(0, 1), (1, 0)])
            return (keep.astype(F32) + got.astype(F32)).astype(BF).reshape(8, 1, 128, 256)

        pair = jnp.concatenate([core_sum(row_keep, row_send), core_sum(col_keep, col_send)], axis=1)
        plane = lax.all_to_all(
            pair.reshape(16, 128, 256), ("x", "yh", "yl"), split_axis=0, concat_axis=0, tiled=True
        )
        plane = jnp.sum(plane.astype(F32), axis=0)
        line = lax.all_to_all(
            plane.reshape(16, 8, 256), "z", split_axis=0, concat_axis=0, tiled=True
        )
        line = jnp.sum(line, axis=0)
        last = lax.all_to_all(
            line.reshape(4, 2, 256), ("yl", "c"), split_axis=0, concat_axis=0, tiled=True
        ).reshape(2, 2, 2, 256)
        grad_value = jnp.transpose(last[:, 0], (1, 0, 2)).reshape(2, 512)
        grad_output = jnp.transpose(last[:, 1], (0, 2, 1)).reshape(512, 2)
    mixed, grad_tokens = final_call(core_arg, row_parts, returned, own, other)
    return (
        mixed.reshape(tokens.shape),
        grad_tokens.reshape(tokens.shape),
        grad_value,
        grad_output,
    )


def solution(mesh):
    fine = Mesh(mesh.devices.reshape(4, 2, 16, 2, 2), ("x", "yh", "z", "yl", "c"))
    dp, seq = ("x", "yh"), ("z", "yl", "c")
    return jax.shard_map(
        body,
        mesh=fine,
        in_specs=(
            P(dp, seq, None, None),
            P(dp, seq, None, None),
            P(None, seq, None, None),
            P(None, seq, None, None),
            P(dp, None),
            P(dp, None),
            P(dp, None),
            P(dp, None),
        ),
        out_specs=(
            P(dp, seq, None, None),
            P(dp, seq, None, None),
            P(dp + seq, None),
            P(None, dp + seq),
        ),
        check_vma=False,
    )
```

time: 913 us -> 248 us (0.27)
  waiting for transfers between devices: 770 us -> 120 us
  blocking collectives: 0 us -> 39.2 us
  matrix products: 27.7 us -> 2.76 us
  between operations: 14.4 us -> 0.9 us
  Pallas kernels: 0 us -> 13.4 us
  other arithmetic: 12.6 us -> 1.71 us
  local copies, waits for them, and re-layouts: 29 us -> 18.7 us
    unnamed x6 -> x0, waiting for transfers between devices: 453 us -> none
    all_gather x4 -> x0, waiting for transfers between devices: 235 us -> none  [the longest x1 65.7 us: body(): lax.all_gather(w_key, 'dp', axis=0, tiled=True)]
    all_to_all x0 -> x2, blocking collectives: none -> 39.2 us  [the longest x1 22.5 us: body(): lax.all_to_all(pair.reshape(16, 128, 256), ('x', 'yh', 'yl'), split_axis=...]
    all_to_all x8 -> x5, waiting for transfers between devices: 82.7 us -> 119 us  [the longest x2 60.4 us: to_columns(): lax.all_to_all(matrix.reshape(64, 4, 1024), seq, split_axis=0, concat_axi...]
    dot_general x21 -> x2, matrix products: 27.1 us -> 2.76 us  [the longest x1 1.41 us: biases(): jnp.einsum('ia,hab,jb->hij', col_left, column_mask.reshape(4, 32, 8).asty...]
    all_to_all x8 -> x5, starting transfers between devices: 57.1 us -> 42 us  [the longest x2 23.7 us: to_columns(): lax.all_to_all(matrix.reshape(64, 4, 1024), seq, split_axis=0, concat_axi...]
    pallas_call x0 -> x3, Pallas kernels: none -> 13.4 us  [the longest x2 9.54 us: heads_call(): pl.pallas_call(functools.partial(head_kernel, kind), out_shape=(jax.Shape...]
  transfers between devices with their start and end apart: 13 -> 8, of which waited for: 12 -> 6; matrix products, arithmetic and copies ran while one was open for 7% -> 5% of each run, Pallas kernels for 0% -> 2%
where the time goes in v1:
time: 248 us; the launch traced here: 245 us
  waiting for transfers between devices  120 us (48%)
  starting transfers between devices  48.5 us (20%)
  blocking collectives  39.2 us (16%)
  local copies, waits for them, and re-layouts  18.7 us (8%)
  Pallas kernels  13.4 us (5%)
  matrix products  2.76 us (1%)
    all_to_all x2, waiting for transfers between devices, to_columns(): lax.all_to_all(matrix.reshape(64, 4, 1024), seq, split_axis=0, concat_axi...  60.4 us
    all_to_all x1, waiting for transfers between devices, body(): lax.all_to_all(col_parts.reshape(64, 4, 1024), seq, split_axis=0, concat_...  32.9 us
    all_to_all x2, starting transfers between devices, to_columns(): lax.all_to_all(matrix.reshape(64, 4, 1024), seq, split_axis=0, concat_axi...  23.7 us
    all_to_all x1, waiting for transfers between devices, body(): lax.all_to_all(jnp.broadcast_to(packed[None], (8, 128, 1024)), ('x', 'yh'...  23.1 us
    all_to_all x1, blocking collectives, body(): lax.all_to_all(pair.reshape(16, 128, 256), ('x', 'yh', 'yl'), split_axis=...  22.5 us
    all_to_all x1, blocking collectives, body(): lax.all_to_all(plane.reshape(16, 8, 256), 'z', split_axis=0, concat_axis=...  16.7 us
    pallas_call x2, Pallas kernels, heads_call(): pl.pallas_call(functools.partial(head_kernel, kind), out_shape=(jax.Shape...  9.54 us
    all_to_all x1, starting transfers between devices, body(): lax.all_to_all(jnp.broadcast_to(packed[None], (8, 128, 1024)), ('x', 'yh'...  9.52 us
  transfers between devices with their start and end apart: 8, of which 6 were waited for; matrix products, arithmetic and copies ran while one was open for 5% of the time, Pallas kernels for 2%

profile of v1, /device:TPU:6, one launch (start us, length us, event | category | flops | bytes accessed | tf_op | source)
XLA Modules:
  0.0 244.6 jit_solution(9862289391621224596)
XLA Ops:
  0.6 0.0 copy-start
  0.7 0.8 constant_dynamic-slice_fusion
  1.5 0.1 copy-done
  1.6 0.9 constant_dynamic-slice_fusion.2
  2.5 1.6 broadcast_in_dim.12
  4.1 0.0 copy-start.1
  4.1 9.5 %all-to-all-start = ((bf16[8,128,1024]{2,1,0:T(8,128)(2,1)}), bf16[8,128,1024]{2,1,0:T(8,128)(2,1)S(1)}, u32[]{:S(2)}, u32[]{:S(2)}) async-start(bf16[8,128,1024]{2,1,0:T(8,128)(2,1)} %broadcast_in_dim.12), calls=%async_computation | async-start | bytes 4194304 | tf_op jit(solution)/shard_map/weights/all_to_all | solution.py:257
  13.6 0.0 copy-done.1
  13.6 0.0 copy-start.2
  13.6 0.0 copy-start.13
  13.7 1.0 reshape_reshape.6
  14.6 23.1 %all-to-all-done.own_ref = bf16[8,128,1024]{2,1,0:T(8,128)(2,1)S(1)} async-done(((bf16[8,128,1024]{2,1,0:T(8,128)(2,1)}), bf16[8,128,1024]{2,1,0:T(8,128)(2,1)S(1)}, u32[]{:S(2)}, u32[]{:S(2)}) %all-to-all-start) | async-done | bytes 2097184 | tf_op jit(solution)/shard_map/weights/all_to_all | solution.py:257
  37.7 18.2 %all-to-all-start.1 = ((bf16[64,4,1024]{2,1,0:T(4,128)(2,1)}), bf16[64,4,1024]{2,1,0:T(4,128)(2,1)}, u32[]{:S(2)}, u32[]{:S(2)}) async-start(bf16[64,4,1024]{2,1,0:T(4,128)(2,1)} %reshape_reshape.6), calls=%async_computation.1 | async-start | bytes 1048576 | tf_op jit(solution)/shard_map/to_columns/all_to_all | solution.py:238
  55.9 1.9 collective-permute-start
  57.9 0.0 copy-done.2
  57.9 1.0 reshape_reshape.7
  58.9 30.6 %all-to-all-done.1 = bf16[64,4,1024]{2,1,0:T(4,128)(2,1)} async-done(((bf16[64,4,1024]{2,1,0:T(4,128)(2,1)}), bf16[64,4,1024]{2,1,0:T(4,128)(2,1)}, u32[]{:S(2)}, u32[]{:S(2)}) %all-to-all-start.1) | async-done | bytes 524320 | tf_op jit(solution)/shard_map/to_columns/all_to_all | solution.py:238
  89.5 5.5 %all-to-all-start.2 = ((bf16[64,4,1024]{2,1,0:T(4,128)(2,1)}), bf16[64,4,1024]{2,1,0:T(4,128)(2,1)}, u32[]{:S(2)}, u32[]{:S(2)}) async-start(bf16[64,4,1024]{2,1,0:T(4,128)(2,1)} %reshape_reshape.7), calls=%async_computation.2 | async-start | bytes 1048576 | tf_op jit(solution)/shard_map/to_columns/all_to_all | solution.py:238
  95.0 0.0 copy-done.14
  95.0 0.1 copy.14
  95.1 0.0 copy-done.13
  95.1 0.1 copy.15
  95.2 0.1 iota_compare_fusion
  95.3 1.4 fusion.3.bias_ref
  96.8 2.0 reshape.164.x_ref
  98.7 29.8 %all-to-all-done.2 = bf16[64,4,1024]{2,1,0:T(4,128)(2,1)} async-done(((bf16[64,4,1024]{2,1,0:T(4,128)(2,1)}), bf16[64,4,1024]{2,1,0:T(4,128)(2,1)}, u32[]{:S(2)}, u32[]{:S(2)}) %all-to-all-start.2) | async-done | bytes 524320 | tf_op jit(solution)/shard_map/to_columns/all_to_all | solution.py:238
  128.5 2.0 reshape.165.ct_ref
  130.5 0.0 collective-permute-done.other_ref
  130.5 1.0 copy-done.3
  131.5 1.0 copy-done.4
  132.6 1.0 copy-done.7
  133.6 5.3 %column_heads.1 = (bf16[256,1024]{1,0:T(8,128)(2,1)S(1)}, bf16[1024,256]{1,0:T(8,128)(2,1)S(1)}, bf16[1024,256]{1,0:T(8,128)(2,1)}) custom-call(s32[1]{0:T(128)} %bitcast.core_ref, bf16[256,1024]{1,0:T(8,128)(2,1)S(1)} %copy-done.3, bf16[256,1024]{1,0:T(8,128)(2,1)S(1)} %copy-done.4, bf16[4,256,256]{2,1,0:T(8,128)(2,1)S(1)} %copy-done.7, ...), custom_call_target="tpu_custom_call" | custom-call | flops 1400000000 | bytes 6000000 | tf_op jit(solution)/shard_map/column_heads/pallas_call | solution.py:124
  138.9 0.0 copy-start.5
  138.9 0.8 copy-done.5
  139.7 0.8 copy-done.9
  140.5 1.9 collective-permute-start.2
  142.4 1.3 fusion.6.bias_ref
  143.8 1.0 copy-done.8
  144.8 4.3 %row_heads.1 = (bf16[256,1024]{1,0:T(8,128)(2,1)S(1)}, bf16[1024,256]{1,0:T(8,128)(2,1)S(1)}, bf16[1024,256]{1,0:T(8,128)(2,1)S(1)}) custom-call(s32[1]{0:T(128)} %bitcast.core_ref, bf16[256,1024]{1,0:T(8,128)(2,1)S(1)} %bitcast.56, bf16[256,1024]{1,0:T(8,128)(2,1)S(1)} %bitcast.57, bf16[4,256,256]{2,1,0:T(8,128)(2,1)S(1)} %copy-done.8, ...), custom_call_target="tpu_custom_call" | custom-call | flops 1400000000 | bytes 6000000 | tf_op jit(solution)/shard_map/row_heads/pallas_call | solution.py:124
  149.1 0.0 copy-start.11
  149.1 2.7 %collective-permute-start.1 = (bf16[1024,256]{1,0:T(8,128)(2,1)S(1)}, bf16[1024,256]{1,0:T(8,128)(2,1)S(1)}, u32[]{:S(2)}, u32[]{:S(2)}) collective-permute-start(bf16[1024,256]{1,0:T(8,128)(2,1)S(1)} %get-tuple-element.17), channel_id=1, source_target_pairs={{0,1},{1,0},{2,3},{3,2},{4,5},{5,4},{6,7},{7,6},{8,9},{9,8},{10,11... | collective-permute-start | bytes 1572872 | tf_op jit(solution)/shard_map/gradient_sums/ppermute | solution.py:280
  151.8 0.0 collective-permute-done.2
  151.8 0.0 copy-done.6
  151.8 1.2 add_convert_fusion
  153.0 0.3 collective-permute-done.1
  153.3 0.1 add_convert_fusion.1
  153.4 0.1 pad_maximum_fusion
  153.5 0.0 copy-done.11
  153.5 0.0 copy-start.10
  153.5 22.5 %all_to_all.35 = bf16[16,128,256]{2,1,0:T(8,128)(2,1)S(1)} all-to-all(bf16[16,128,256]{2,1,0:T(8,128)(2,1)S(1)} %bitcast.58), channel_id=1, replica_groups=mesh['x'=4,'yh'=2,'z'=16,'yl'=2,'c'=2] {'x','yh','yl'}, dimensions={0} | all-to-all | bytes 2097152 | tf_op jit(solution)/shard_map/gradient_sums/all_to_all | solution.py:284
  176.0 0.1 convert_reduce_fusion
  176.2 0.0 copy-start.12
  176.2 16.7 %all_to_all.36 = f32[16,8,256]{2,1,0:T(8,128)S(1)} all-to-all(f32[16,8,256]{2,1,0:T(8,128)S(1)} %bitcast.61), channel_id=1, replica_groups=mesh['x'=4,'yh'=2,'z'=16,'yl'=2,'c'=2] {'z'}, dimensions={0} | all-to-all | bytes 262144 | tf_op jit(solution)/shard_map/gradient_sums/all_to_all | solution.py:288
  192.9 0.6 reshape.174
  193.5 3.2 %all-to-all-start.6 = ((f32[4,2,256]{2,1,0:T(2,128)}), f32[4,2,256]{2,1,0:T(2,128)S(1)}, u32[]{:S(2)}, u32[]{:S(2)}) async-start(f32[4,2,256]{2,1,0:T(2,128)} %reshape.174), calls=%async_computation.6 | async-start | bytes 16384 | tf_op jit(solution)/shard_map/gradient_sums/all_to_all | solution.py:292
  196.7 0.0 copy-done.10
  196.7 1.0 reshape.166
  197.7 2.8 %all-to-all-done.6 = f32[4,2,256]{2,1,0:T(2,128)S(1)} async-done(((f32[4,2,256]{2,1,0:T(2,128)}), f32[4,2,256]{2,1,0:T(2,128)S(1)}, u32[]{:S(2)}, u32[]{:S(2)}) %all-to-all-start.6) | async-done | bytes 8224 | tf_op jit(solution)/shard_map/gradient_sums/all_to_all | solution.py:292
  200.5 5.5 %all-to-all-start.3 = ((bf16[64,4,1024]{2,1,0:T(4,128)(2,1)}), bf16[64,4,1024]{2,1,0:T(4,128)(2,1)}, u32[]{:S(2)}, u32[]{:S(2)}) async-start(bf16[64,4,1024]{2,1,0:T(4,128)(2,1)} %reshape.166), calls=%async_computation.3 | async-start | bytes 1048576 | tf_op jit(solution)/shard_map/from_columns/all_to_all | solution.py:275
  206.0 0.6 fusion.23
  206.6 32.9 %all-to-all-done.3 = bf16[64,4,1024]{2,1,0:T(4,128)(2,1)} async-done(((bf16[64,4,1024]{2,1,0:T(4,128)(2,1)}), bf16[64,4,1024]{2,1,0:T(4,128)(2,1)}, u32[]{:S(2)}, u32[]{:S(2)}) %all-to-all-start.3) | async-done | bytes 524320 | tf_op jit(solution)/shard_map/from_columns/all_to_all | solution.py:275
  239.6 1.2 reshape.167.col_ref
  240.7 0.0 copy-done.12
  240.7 3.9 %output_products.1 = (bf16[256,1024]{1,0:T(8,128)(2,1)}, bf16[256,1024]{1,0:T(8,128)(2,1)}) custom-call(s32[1]{0:T(128)} %bitcast.core_ref, bf16[256,1024]{1,0:T(8,128)(2,1)S(1)} %copy-done.12, bf16[256,1024]{1,0:T(8,128)(2,1)S(1)} %reshape.167.col_ref, bf16[8,128,1024]{2,1,0:T(8,128)(2,1)S(1)} %all-to-all-done.own_ref, ...), custom_call_target="tpu_custom_call" | custom-call | flops 1100000000 | bytes 6000000 | tf_op jit(solution)/shard_map/output_products/pallas_call | solution.py:185
  (15 shorter events, 0.1 us)
Async XLA Ops:
  0.6 0.9 copy-start
  4.1 9.5 %copy-start.1 = (bf16[1,1,256,1024]{3,2,1,0:T(8,128)(2,1)S(1)}, bf16[1,1,256,1024]{3,2,1,0:T(8,128)(2,1)}, u32[]{:S(2)}) copy-start(bf16[1,1,256,1024]{3,2,1,0:T(8,128)(2,1)} %param.8) | copy-start | bytes 1572868
  4.1 33.6 %all-to-all-start = ((bf16[8,128,1024]{2,1,0:T(8,128)(2,1)}), bf16[8,128,1024]{2,1,0:T(8,128)(2,1)S(1)}, u32[]{:S(2)}, u32[]{:S(2)}) async-start(bf16[8,128,1024]{2,1,0:T(8,128)(2,1)} %broadcast_in_dim.12), calls=%async_computation | async-start | bytes 4194304 | tf_op jit(solution)/shard_map/weights/all_to_all | solution.py:257
  13.6 44.2 %copy-start.2 = (bf16[1,1,256,1024]{3,2,1,0:T(8,128)(2,1)S(1)}, bf16[1,1,256,1024]{3,2,1,0:T(8,128)(2,1)}, u32[]{:S(2)}) copy-start(bf16[1,1,256,1024]{3,2,1,0:T(8,128)(2,1)} %param.9) | copy-start | bytes 1572868
  13.6 81.3 %copy-start.14 = (s32[4,1,2,2]{0,3,2,1:T(2,128)S(1)}, s32[4,1,2,2]{0,3,2,1:T(2,128)}, u32[]{:S(2)}) copy-start(s32[4,1,2,2]{0,3,2,1:T(2,128)} %param.10) | copy-start | bytes 196
  13.6 81.5 %copy-start.13 = (s32[4,4,8,8]{3,2,1,0:T(8,128)S(1)}, s32[4,4,8,8]{3,2,1,0:T(8,128)}, u32[]{:S(2)}) copy-start(s32[4,4,8,8]{3,2,1,0:T(8,128)} %param.11) | copy-start | bytes 12292
  37.7 51.8 %all-to-all-start.1 = ((bf16[64,4,1024]{2,1,0:T(4,128)(2,1)}), bf16[64,4,1024]{2,1,0:T(4,128)(2,1)}, u32[]{:S(2)}, u32[]{:S(2)}) async-start(bf16[64,4,1024]{2,1,0:T(4,128)(2,1)} %reshape_reshape.6), calls=%async_computation.1 | async-start | bytes 1048576 | tf_op jit(solution)/shard_map/to_columns/all_to_all | solution.py:238
  55.9 74.5 %collective-permute-start = (bf16[8,128,1024]{2,1,0:T(8,128)(2,1)S(1)}, bf16[8,128,1024]{2,1,0:T(8,128)(2,1)}, u32[]{:S(2)}, u32[]{:S(2)}) collective-permute-start(bf16[8,128,1024]{2,1,0:T(8,128)(2,1)S(1)} %all-to-all-done.own_ref), channel_id=1, source_target_pairs={{0,1},{1,0},{2,3},{3,2},{4,5},{5,4},{6,7},{7,6},{8,9},{9,8},{10,11... | collective-permute-start | bytes 6291464 | tf_op jit(solution)/shard_map/weights/ppermute | solution.py:264
  89.5 39.0 %all-to-all-start.2 = ((bf16[64,4,1024]{2,1,0:T(4,128)(2,1)}), bf16[64,4,1024]{2,1,0:T(4,128)(2,1)}, u32[]{:S(2)}, u32[]{:S(2)}) async-start(bf16[64,4,1024]{2,1,0:T(4,128)(2,1)} %reshape_reshape.7), calls=%async_computation.2 | async-start | bytes 1048576 | tf_op jit(solution)/shard_map/to_columns/all_to_all | solution.py:238
  130.5 1.0 copy-start.3
  131.5 1.0 copy-start.4
  132.6 1.0 copy-start.7
  138.9 0.8 copy-start.5
  139.7 0.8 copy-start.9
  140.5 11.3 %collective-permute-start.2 = (bf16[1024,256]{1,0:T(8,128)(2,1)}, bf16[1024,256]{1,0:T(8,128)(2,1)}, u32[]{:S(2)}, u32[]{:S(2)}) collective-permute-start(bf16[1024,256]{1,0:T(8,128)(2,1)} %get-tuple-element.19), channel_id=1, source_target_pairs={{0,1},{1,0},{2,3},{3,2},{4,5},{5,4},{6,7},{7,6},{8,9},{9,8},{10,11... | collective-permute-start | bytes 1572872 | tf_op jit(solution)/shard_map/gradient_sums/ppermute | solution.py:280
  143.8 1.0 copy-start.8
  144.8 7.0 %copy-start.6 = (bf16[1024,256]{1,0:T(8,128)(2,1)S(1)}, bf16[1024,256]{1,0:T(8,128)(2,1)}, u32[]{:S(2)}) copy-start(bf16[1024,256]{1,0:T(8,128)(2,1)} %copy-done.5) | copy-start | bytes 1572868
  149.1 4.4 %copy-start.11 = (bf16[256,1024]{1,0:T(8,128)(2,1)}, bf16[256,1024]{1,0:T(8,128)(2,1)S(1)}, u32[]{:S(2)}) copy-start(bf16[256,1024]{1,0:T(8,128)(2,1)S(1)} %get-tuple-element.12.row_ref) | copy-start | bytes 1572868
  149.1 4.2 %collective-permute-start.1 = (bf16[1024,256]{1,0:T(8,128)(2,1)S(1)}, bf16[1024,256]{1,0:T(8,128)(2,1)S(1)}, u32[]{:S(2)}, u32[]{:S(2)}) collective-permute-start(bf16[1024,256]{1,0:T(8,128)(2,1)S(1)} %get-tuple-element.17), channel_id=1, source_target_pairs={{0,1},{1,0},{2,3},{3,2},{4,5},{5,4},{6,7},{7,6},{8,9},{9,8},{10,11... | collective-permute-start | bytes 1572872 | tf_op jit(solution)/shard_map/gradient_sums/ppermute | solution.py:280
  153.5 43.2 %copy-start.10 = (bf16[256,1024]{1,0:T(8,128)(2,1)S(1)}, bf16[256,1024]{1,0:T(8,128)(2,1)}, u32[]{:S(2)}) copy-start(bf16[256,1024]{1,0:T(8,128)(2,1)} %copy-done.9) | copy-start | bytes 1572868
  176.2 64.6 %copy-start.12 = (bf16[256,1024]{1,0:T(8,128)(2,1)S(1)}, bf16[256,1024]{1,0:T(8,128)(2,1)}, u32[]{:S(2)}) copy-start(bf16[256,1024]{1,0:T(8,128)(2,1)} %copy-done.11) | copy-start | bytes 1572868
  193.5 7.0 %all-to-all-start.6 = ((f32[4,2,256]{2,1,0:T(2,128)}), f32[4,2,256]{2,1,0:T(2,128)S(1)}, u32[]{:S(2)}, u32[]{:S(2)}) async-start(f32[4,2,256]{2,1,0:T(2,128)} %reshape.174), calls=%async_computation.6 | async-start | bytes 16384 | tf_op jit(solution)/shard_map/gradient_sums/all_to_all | solution.py:292
  200.5 39.0 %all-to-all-start.3 = ((bf16[64,4,1024]{2,1,0:T(4,128)(2,1)}), bf16[64,4,1024]{2,1,0:T(4,128)(2,1)}, u32[]{:S(2)}, u32[]{:S(2)}) async-start(bf16[64,4,1024]{2,1,0:T(4,128)(2,1)} %reshape.166), calls=%async_computation.3 | async-start | bytes 1048576 | tf_op jit(solution)/shard_map/from_columns/all_to_all | solution.py:275

commit v2 on v1

v2 whole, which is shorter than its diff:
```python
import functools

import jax
import jax.numpy as jnp
from jax import lax
from jax.experimental import pallas as pl
from jax.experimental.pallas import tpu as pltpu
from jax.sharding import Mesh, PartitionSpec as P

HEAD_DIM = 64
ROWBLK = 128
COLBLK = 8
BF = jnp.bfloat16
F32 = jnp.float32
LAST = (((1,), (1,)), ((), ()))
FIRST = (((0,), (0,)), ((), ()))
MASKED = -1e30
VMEM = pl.BlockSpec(memory_space=pltpu.VMEM)
SMEM = pl.BlockSpec(memory_space=pltpu.SMEM)
ANYWHERE = pl.BlockSpec(memory_space=pl.ANY)
PARAMS = pltpu.CompilerParams(vmem_limit_bytes=24 * 1024 * 1024)
OFFSETS = [(dx, dy) for dx in range(4) for dy in range(2)]
SWAP = [(0, 1), (1, 0)]


def product(a, b, dims=(((1,), (0,)), ((), ()))):
    return lax.dot_general(a, b, dims, preferred_element_type=F32)


def eights(first):
    row = lax.broadcasted_iota(jnp.int32, (512, 256), 0)
    col = lax.broadcasted_iota(jnp.int32, (512, 256), 1)
    inside = (row & 4) == (0 if first else 4)
    return ((col == (row >> 3) * 4 + (row & 3)) & inside).astype(F32).astype(BF)


def interleave(first, second):
    return (product(eights(True), first) + product(eights(False), second)).astype(BF)


def separate(both):
    return tuple(product(eights(t), both, FIRST).astype(BF) for t in (True, False))


def start_copies(pairs, sems, first=0):
    copies = [
        pltpu.make_async_copy(source, target, sems.at[first + i])
        for i, (source, target) in enumerate(pairs)
    ]
    for copy in copies:
        copy.start()
    return copies


def wait_for(copies):
    for copy in copies:
        copy.wait()


def prepare_kernel(
    place, x_ref, ct_ref, wq_ref, wk_ref, wv_ref, wo_ref, packed_ref, sent_ref, x, ct, sems
):
    core = place[0]
    here = pl.ds(pl.multiple_of(core * 256, 256), 256)
    pairs = [(x_ref, x), (ct_ref, ct)]
    for i, ref in enumerate((wq_ref, wk_ref, wv_ref)):
        pairs.append((ref.at[:, here], packed_ref.at[:, pl.ds(i * 256, 256)]))
    for b in range(2):
        there = pl.ds(pl.multiple_of(core * 512 + b * 256, 256), 256)
        pairs.append((wo_ref.at[:, there], packed_ref.at[pl.ds(b * 64, 64), pl.ds(768, 256)]))
    copies = start_copies(pairs, sems)
    wait_for(copies[:2])
    sent_ref[...] = interleave(x[...], ct[...])
    wait_for(copies[2:])


def attention(x, ct, weights, kind, bias_ref):
    qkv = product(x, weights[kind, :, :, 0:768].reshape(1024, 768)).astype(BF)
    q, k, v = qkv[:, :256], qkv[:, 256:512], qkv[:, 512:]
    do = jnp.zeros((256, 256), F32)
    for half in range(2):
        for b in range(2):
            block = weights[half, kind * 4 : kind * 4 + 4, b * 64 : (b + 1) * 64, 768:1024]
            start = half * 512 + b * 256
            do += product(ct[:, start : start + 256], block.reshape(256, 256), LAST)
    do = do.astype(BF)
    lane = lax.broadcasted_iota(jnp.int32, (256, 256), 1) // HEAD_DIM
    zero = jnp.zeros_like(q)
    out = jnp.zeros((256, 256), F32)
    dq, dk, dv = out, out, out
    for h in range(4):
        mine = lane == h
        kh, vh = jnp.where(mine, k, zero), jnp.where(mine, v, zero)
        qh, doh = jnp.where(mine, q, zero), jnp.where(mine, do, zero)
        s = product(q, kh, LAST) * 0.125 + bias_ref[h].astype(F32)
        e = jnp.exp(s - jnp.max(s, axis=-1, keepdims=True))
        w = e * (1.0 / jnp.sum(e, axis=-1, keepdims=True))
        p = w.astype(BF)
        out += product(p, vh)
        dp = product(do, vh, LAST).astype(BF).astype(F32)
        ds = (w * (dp - jnp.sum(dp * w, axis=-1, keepdims=True)) * 0.125).astype(BF)
        dq += product(ds, kh)
        dk += product(ds, qh, FIRST)
        dv += product(p, doh, FIRST)
    return tuple(a.astype(BF) for a in (out, dq, dk, dv))


def store_gradients(core, x, ct, out, dv, keep_ref, send_ref):
    grad_value = product(x, dv, FIRST).astype(BF)
    grad_out = product(ct, out, FIRST).astype(BF)

    @pl.when(core == 0)
    def _():
        keep_ref[...] = grad_value
        send_ref[...] = grad_out

    @pl.when(core != 0)
    def _():
        keep_ref[...] = grad_out
        send_ref[...] = grad_value


def row_kernel(
    place,
    x_ref,
    ct_ref,
    bias_ref,
    own_ref,
    other_ref,
    parts_ref,
    keep_ref,
    send_ref,
    w_ref,
    x_here,
    ct_here,
    bias,
    sems,
):
    core = place[0]
    pairs = []
    for index, (dx, dy) in enumerate(OFFSETS):
        source = ((place[1] + 4 - dx) & 3) * 2 + ((place[2] + dy) & 1)
        for half, ref in ((core, own_ref), (1 - core, other_ref)):
            pairs.append((ref.at[index], w_ref.at[half, source]))
    pairs += [(x_ref, x_here), (ct_ref, ct_here), (bias_ref, bias)]
    wait_for(start_copies(pairs, sems))
    x, ct = x_here[...], ct_here[...]
    out, dq, dk, dv = attention(x, ct, w_ref, 0, bias)
    for i, part in enumerate((out, dq, dk, dv)):
        parts_ref[:, i * 256 : (i + 1) * 256] = part
    store_gradients(core, x, ct, out, dv, keep_ref, send_ref)


def column_kernel(
    place, both_ref, bias_ref, w_ref, parts_ref, keep_ref, send_ref, both, bias, weights, sems
):
    copies = start_copies(((both_ref, both), (w_ref, weights), (bias_ref, bias)), sems)
    wait_for(copies[:1])
    x, ct = separate(both[...])
    wait_for(copies[1:])
    out, dq, dk, dv = attention(x, ct, weights, 1, bias)
    parts_ref[...] = interleave(
        jnp.concatenate([out, dq], axis=1), jnp.concatenate([dk, dv], axis=1)
    )
    store_gradients(place[0], x, ct, out, dv, keep_ref, send_ref)


def final_kernel(row_ref, col_ref, weights, mixed_ref, gt_ref, row, col, w_ref, sems):
    copies = start_copies(((col_ref, col), (row_ref, row), (weights, w_ref)), sems)
    wait_for(copies[:2])
    first, second = separate(col[...])
    wait_for(copies[2:])
    sides = (
        (row[:, 0:256], row[:, 256:1024]),
        (first[:, 0:256], jnp.concatenate([first[:, 256:512], second], axis=1)),
    )
    for half in range(2):
        for b in range(2):
            total = jnp.zeros((256, 256), F32)
            for kind in range(2):
                block = w_ref[half, kind * 4 : kind * 4 + 4, b * 64 : (b + 1) * 64, 768:1024]
                total += product(sides[kind][0], block.reshape(256, 256))
            start = half * 512 + b * 256
            mixed_ref[:, start : start + 256] = total.astype(BF)
    total = jnp.zeros(gt_ref.shape, F32)
    for kind in range(2):
        total += product(sides[kind][1], w_ref[kind, :, :, 0:768].reshape(1024, 768), LAST)
    gt_ref[...] = total.astype(BF)


def shape(*dims):
    return jax.ShapeDtypeStruct(dims, BF)


def buffer(*dims):
    return pltpu.VMEM(dims, BF)


def cost(flops, moved):
    return pl.CostEstimate(flops=flops, bytes_accessed=moved, transcendentals=0)


def one_hot(index, size):
    return (index[:, None] == jnp.arange(size)[None, :]).astype(BF)


def biases(row_mask, column_mask):
    position = jnp.arange(256)
    seen = position[:, None] >= position[None, :]
    row_in = one_hot(position // ROWBLK, 2)
    row_blocks = jnp.einsum(
        "ia,hab,jb->hij", row_in, row_mask[:, 0].astype(BF), row_in, preferred_element_type=BF
    )
    same = (position[:, None] % 4) == (position[None, :] % 4)
    col_left = one_hot((position % 4) * 8 + position // (4 * COLBLK), 32)
    col_right = one_hot(position // (4 * COLBLK), 8)
    col_blocks = jnp.einsum(
        "ia,hab,jb->hij",
        col_left,
        column_mask.reshape(4, 32, 8).astype(BF),
        col_right,
        preferred_element_type=BF,
    )
    row_bias = jnp.where((row_blocks > 0.5) & seen, 0.0, MASKED).astype(BF)
    col_bias = jnp.where((col_blocks > 0.5) & seen & same, 0.0, MASKED).astype(BF)
    return row_bias, col_bias


def shifted(dx, dy):
    return [
        (x * 2 + y, (x + dx) % 4 * 2 + (y + dy) % 2) for x in range(4) for y in range(2)
    ]


def body(tokens, cotangent, row_mask, column_mask, w_query, w_key, w_value, w_out):
    core, across, high, low = (lax.axis_index(name) for name in ("c", "x", "yh", "yl"))
    place = jnp.stack([core, across, high]).astype(jnp.int32)
    flat = tokens.reshape(256, 1024)
    cot_flat = cotangent.reshape(256, 1024)
    seq = ("z", "yl", "c")

    packed, sent = pl.pallas_call(
        prepare_kernel,
        out_shape=(shape(128, 1024), shape(512, 1024)),
        in_specs=[SMEM] + [ANYWHERE] * 6,
        out_specs=(VMEM, VMEM),
        scratch_shapes=[buffer(256, 1024), buffer(256, 1024), pltpu.SemaphoreType.DMA((7,))],
        compiler_params=PARAMS,
        cost_estimate=cost(540000000, 4000000),
        name="prepare",
    )(place, flat, cot_flat, w_query, w_key, w_value, w_out)
    with jax.named_scope("to_columns"):
        both = lax.all_to_all(
            sent.reshape(64, 8, 1024), seq, split_axis=0, concat_axis=0, tiled=True
        ).reshape(512, 1024)
    with jax.named_scope("weights"):
        own = jnp.stack(
            [packed]
            + [lax.ppermute(packed, ("x", "yh"), shifted(dx, dy)) for dx, dy in OFFSETS[1:]]
        )
        other = lax.ppermute(own, "c", SWAP)
    with jax.named_scope("masks"):
        row_bias, col_bias = biases(row_mask, column_mask)
    row_parts, row_keep, row_send, weights = pl.pallas_call(
        row_kernel,
        out_shape=(shape(256, 1024), shape(1024, 256), shape(1024, 256), shape(2, 8, 128, 1024)),
        in_specs=[SMEM] + [ANYWHERE] * 5,
        out_specs=(VMEM,) * 4,
        scratch_shapes=[
            buffer(256, 1024),
            buffer(256, 1024),
            buffer(4, 256, 256),
            pltpu.SemaphoreType.DMA((19,)),
        ],
        compiler_params=PARAMS,
        cost_estimate=cost(1400000000, 12000000),
        name="row_heads",
    )(place, flat, cot_flat, row_bias, own, other)
    col_parts, col_keep, col_send = pl.pallas_call(
        column_kernel,
        out_shape=(shape(512, 512), shape(1024, 256), shape(1024, 256)),
        in_specs=[SMEM] + [ANYWHERE] * 3,
        out_specs=(VMEM,) * 3,
        scratch_shapes=[
            buffer(512, 1024),
            buffer(4, 256, 256),
            buffer(2, 8, 128, 1024),
            pltpu.SemaphoreType.DMA((3,)),
        ],
        compiler_params=PARAMS,
        cost_estimate=cost(1900000000, 8000000),
        name="column_heads",
    )(place, both, col_bias, weights)
    with jax.named_scope("from_columns"):
        returned = lax.all_to_all(
            col_parts.reshape(64, 8, 512), seq, split_axis=0, concat_axis=0, tiled=True
        ).reshape(512, 512)

    def plane_sum(keep, send):
        got = lax.ppermute(send, "c", SWAP)
        held = (keep.astype(F32) + got.astype(F32)).astype(BF)

        def rows_of(step):
            return lax.dynamic_slice_in_dim(held, ((across + step) & 3) * 256, 256, axis=0)

        terms = [rows_of(0)]
        for step in (1, 3, 2):
            pairs = [(x, (x + step) % 4) for x in range(4)]
            terms.append(lax.ppermute(rows_of(step), "x", pairs))
        held_rows = sum(term.astype(F32) for term in terms).astype(BF)

        def block_of(dh, dl):
            return lax.dynamic_slice(held_rows, ((high ^ dh) * 128, (low ^ dl) * 128), (128, 128))

        terms = [block_of(0, 0)]
        for dh, dl in ((0, 1), (1, 0), (1, 1)):
            pairs = [(h * 2 + l, (h ^ dh) * 2 + (l ^ dl)) for h in range(2) for l in range(2)]
            terms.append(lax.ppermute(block_of(dh, dl), ("yh", "yl"), pairs))
        return sum(term.astype(F32) for term in terms)

    with jax.named_scope("gradient_sums"):
        plane = jnp.concatenate([plane_sum(row_keep, row_send), plane_sum(col_keep, col_send)], axis=1)
        plane, returned = lax.optimization_barrier((plane, returned))
        line = lax.all_to_all(
            plane.reshape(64, 2, 256), seq, split_axis=0, concat_axis=0, tiled=True
        )
        line = jnp.sum(line.reshape(16, 2, 2, 2, 2, 128), axis=0)
        grad_value = jnp.transpose(line[:, 0], (1, 2, 0, 3)).reshape(2, 512)
        grad_output = jnp.transpose(line[:, 1], (2, 0, 3, 1)).reshape(512, 2)
    mixed, grad_tokens = pl.pallas_call(
        final_kernel,
        out_shape=(shape(256, 1024), shape(256, 1024)),
        in_specs=[ANYWHERE] * 3,
        out_specs=(VMEM, VMEM),
        scratch_shapes=[
            buffer(256, 1024),
            buffer(512, 512),
            buffer(2, 8, 128, 1024),
            pltpu.SemaphoreType.DMA((3,)),
        ],
        compiler_params=PARAMS,
        cost_estimate=cost(1200000000, 8000000),
        name="output_products",
    )(row_parts, returned, weights)
    return (
        mixed.reshape(tokens.shape),
        grad_tokens.reshape(tokens.shape),
        grad_value,
        grad_output,
    )


def solution(mesh):
    fine = Mesh(mesh.devices.reshape(4, 2, 16, 2, 2), ("x", "yh", "z", "yl", "c"))
    dp, seq = ("x", "yh"), ("z", "yl", "c")
    return jax.shard_map(
        body,
        mesh=fine,
        in_specs=(
            P(dp, seq, None, None),
            P(dp, seq, None, None),
            P(None, seq, None, None),
            P(None, seq, None, None),
            P(dp, None),
            P(dp, None),
            P(dp, None),
            P(dp, None),
        ),
        out_specs=(
            P(dp, seq, None, None),
            P(dp, seq, None, None),
            P(dp + seq, None),
            P(None, dp + seq),
        ),
        check_vma=False,
    )
```

time: 248 us -> 199 us (0.80)
  waiting for transfers between devices: 120 us -> 40.2 us
  starting transfers between devices: 48.5 us -> 108 us
  blocking collectives: 39.2 us -> 0 us
  local copies, waits for them, and re-layouts: 18.7 us -> 24.1 us
  Pallas kernels: 13.4 us -> 17.5 us
    all_to_all x5 -> x3, waiting for transfers between devices: 119 us -> 27 us  [the longest x1 15.1 us: body(): lax.all_to_all(sent.reshape(64, 8, 1024), seq, split_axis=0, concat_axis=...]
    ppermute x3 -> x22, starting transfers between devices: 6.5 us -> 75.6 us  [the longest x7 29.1 us: body(): lax.ppermute(packed, ('x', 'yh'), shifted(dx, dy))]
    all_to_all x2 -> x0, blocking collectives: 39.2 us -> none  [the longest x1 22.5 us: body(): lax.all_to_all(pair.reshape(16, 128, 256), ('x', 'yh', 'yl'), split_axis=...]
    unnamed x30 -> x43, local copies, waits for them, and re-layouts: 5.91 us -> 21.6 us
    ppermute x3 -> x22, waiting for transfers between devices: 0.32 us -> 13.2 us  [the longest x7 7.22 us: body(): lax.ppermute(packed, ('x', 'yh'), shifted(dx, dy))]
    all_to_all x5 -> x3, starting transfers between devices: 42 us -> 32.5 us  [the longest x1 15 us: body(): lax.all_to_all(sent.reshape(64, 8, 1024), seq, split_axis=0, concat_axis=...]
    reshape x5 -> x3, local copies, waits for them, and re-layouts: 6.66 us -> 1.48 us  [the longest x1 0.72 us: body(): plane.reshape(64, 2, 256)]
    pallas_call x3 -> x4, Pallas kernels: 13.4 us -> 17.5 us  [the longest x1 6.11 us: body(): pl.pallas_call(row_kernel, out_shape=(shape(256, 1024), shape(1024, 256),...]
  transfers between devices with their start and end apart: 8 -> 25, of which waited for: 6 -> 6; matrix products, arithmetic and copies ran while one was open for 5% -> 5% of each run, Pallas kernels for 2% -> 8%
where the time goes in v2:
time: 199 us; the launch traced here: 195 us
  starting transfers between devices  108 us (54%)
  waiting for transfers between devices  40.2 us (20%)
  local copies, waits for them, and re-layouts  24.1 us (12%)
  Pallas kernels  17.5 us (9%)
    ppermute x7, starting transfers between devices, body(): lax.ppermute(packed, ('x', 'yh'), shifted(dx, dy))  29.1 us
    unnamed x43, local copies, waits for them, and re-layouts  21.6 us
    ppermute x6, starting transfers between devices, plane_sum(): terms.append(lax.ppermute(block_of(dh, dl), ('yh', 'yl'), pairs))  20.8 us
    ppermute x6, starting transfers between devices, plane_sum(): terms.append(lax.ppermute(rows_of(step), 'x', pairs))  19.8 us
    all_to_all x1, waiting for transfers between devices, body(): lax.all_to_all(sent.reshape(64, 8, 1024), seq, split_axis=0, concat_axis=...  15.1 us
    all_to_all x1, starting transfers between devices, body(): lax.all_to_all(sent.reshape(64, 8, 1024), seq, split_axis=0, concat_axis=...  15 us
    all_to_all x1, starting transfers between devices, body(): lax.all_to_all(plane.reshape(64, 2, 256), seq, split_axis=0, concat_axis=...  12.7 us
    all_to_all x1, waiting for transfers between devices, body(): lax.all_to_all(plane.reshape(64, 2, 256), seq, split_axis=0, concat_axis=...  11.9 us
  transfers between devices with their start and end apart: 25, of which 6 were waited for; matrix products, arithmetic and copies ran while one was open for 5% of the time, Pallas kernels for 8%

profile of v2, /device:TPU:6, one launch (start us, length us, event | category | flops | bytes accessed | tf_op | source)
XLA Modules:
  0.0 194.9 jit_solution(4285809754651703115)
XLA Ops:
  0.7 1.0 copy-done.3
  1.8 1.0 copy-done.5
  2.8 0.9 copy-done.12
  3.7 0.9 copy-done.13
  4.6 0.9 copy-done.14
  5.5 0.9 copy-done.15
  6.4 2.4 %prepare.1 = (bf16[128,1024]{1,0:T(8,128)(2,1)S(1)}, bf16[512,1024]{1,0:T(8,128)(2,1)}) custom-call(s32[3]{0:T(128)S(1)} %pad_add_fusion.place, bf16[256,1024]{1,0:T(8,128)(2,1)S(1)} %bitcast.66, bf16[256,1024]{1,0:T(8,128)(2,1)S(1)} %bitcast.68, bf16[128,512]{1,0:T(8,128)(2,1)S(1)} %copy-done.12, bf16[128,512]{1,0:T(8,128)(2,1)S(1)} %copy-done.13, ...), custom_call_target="tpu_custom_call" | custom-call | flops 540000000 | bytes 4000000 | tf_op jit(solution)/shard_map/prepare/pallas_call | solution.py:242
  8.9 5.1 %collective-permute-start = (bf16[128,1024]{1,0:T(8,128)(2,1)S(1)}, bf16[128,1024]{1,0:T(8,128)(2,1)}, u32[]{:S(2)}, u32[]{:S(2)}) collective-permute-start(bf16[128,1024]{1,0:T(8,128)(2,1)S(1)} %get-tuple-element.17), channel_id=1, source_target_pairs={{0,64},{64,0},{128,192},{192,128},{256,320},{320,256},{384,448},{4... | collective-permute-start | bytes 786440 | tf_op jit(solution)/shard_map/weights/ppermute | solution.py:259
  14.0 4.6 %collective-permute-start.1 = (bf16[128,1024]{1,0:T(8,128)(2,1)S(1)}, bf16[128,1024]{1,0:T(8,128)(2,1)}, u32[]{:S(2)}, u32[]{:S(2)}) collective-permute-start(bf16[128,1024]{1,0:T(8,128)(2,1)S(1)} %get-tuple-element.17), channel_id=1, source_target_pairs={{0,128},{64,192},{128,256},{192,320},{256,384},{320,448},{384,0},{... | collective-permute-start | bytes 786440 | tf_op jit(solution)/shard_map/weights/ppermute | solution.py:259
  18.6 4.9 %collective-permute-start.2 = (bf16[128,1024]{1,0:T(8,128)(2,1)S(1)}, bf16[128,1024]{1,0:T(8,128)(2,1)}, u32[]{:S(2)}, u32[]{:S(2)}) collective-permute-start(bf16[128,1024]{1,0:T(8,128)(2,1)S(1)} %get-tuple-element.17), channel_id=1, source_target_pairs={{0,192},{64,128},{128,320},{192,256},{256,448},{320,384},{384,64},... | collective-permute-start | bytes 786440 | tf_op jit(solution)/shard_map/weights/ppermute | solution.py:259
  23.5 1.9 collective-permute-start.3
  25.4 5.4 %collective-permute-start.4 = (bf16[128,1024]{1,0:T(8,128)(2,1)S(1)}, bf16[128,1024]{1,0:T(8,128)(2,1)}, u32[]{:S(2)}, u32[]{:S(2)}) collective-permute-start(bf16[128,1024]{1,0:T(8,128)(2,1)S(1)} %get-tuple-element.17), channel_id=1, source_target_pairs={{0,320},{64,256},{128,448},{192,384},{256,64},{320,0},{384,192},{4... | collective-permute-start | bytes 786440 | tf_op jit(solution)/shard_map/weights/ppermute | solution.py:259
  30.8 15.0 %all-to-all-start = ((bf16[64,8,1024]{2,1,0:T(8,128)(2,1)}), bf16[64,8,1024]{2,1,0:T(8,128)(2,1)S(1)}, u32[]{:S(2)}, u32[]{:S(2)}) async-start(bf16[64,8,1024]{2,1,0:T(8,128)(2,1)} %bitcast.16), calls=%async_computation | async-start | bytes 2097152 | tf_op jit(solution)/shard_map/to_columns/all_to_all | solution.py:253
  45.9 2.4 %collective-permute-start.5 = (bf16[128,1024]{1,0:T(8,128)(2,1)S(1)}, bf16[128,1024]{1,0:T(8,128)(2,1)S(1)}, u32[]{:S(2)}, u32[]{:S(2)}) collective-permute-start(bf16[128,1024]{1,0:T(8,128)(2,1)S(1)} %get-tuple-element.17), channel_id=1, source_target_pairs={{0,384},{64,448},{128,0},{192,64},{256,128},{320,192},{384,256},{4... | collective-permute-start | bytes 786440 | tf_op jit(solution)/shard_map/weights/ppermute | solution.py:259
  48.3 1.0 bitcast_dynamic-update-slice_fusion.6
  49.3 4.7 %collective-permute-start.6 = (bf16[128,1024]{1,0:T(8,128)(2,1)S(1)}, bf16[128,1024]{1,0:T(8,128)(2,1)S(1)}, u32[]{:S(2)}, u32[]{:S(2)}) collective-permute-start(bf16[128,1024]{1,0:T(8,128)(2,1)S(1)} %get-tuple-element.17), channel_id=1, source_target_pairs={{0,448},{64,384},{128,64},{192,0},{256,192},{320,128},{384,320},{4... | collective-permute-start | bytes 786440 | tf_op jit(solution)/shard_map/weights/ppermute | solution.py:259
  54.0 1.0 bitcast_dynamic-update-slice_fusion.5
  55.0 1.0 bitcast_dynamic-update-slice_fusion.4
  56.0 1.0 bitcast_dynamic-update-slice_fusion.3
  57.0 1.0 bitcast_dynamic-update-slice_fusion.2
  57.9 0.2 collective-permute-done.5
  58.1 7.0 %collective-permute-done.6 = bf16[128,1024]{1,0:T(8,128)(2,1)S(1)} collective-permute-done((bf16[128,1024]{1,0:T(8,128)(2,1)S(1)}, bf16[128,1024]{1,0:T(8,128)(2,1)S(1)}, u32[]{:S(2)}, u32[]{:S(2)}) %collective-permute-start.6) | collective-permute-done | bytes 262176 | tf_op jit(solution)/shard_map/weights/ppermute | solution.py:259
  65.2 1.9 collective-permute-start.7
  67.1 0.1 copy.12
  67.4 0.1 broadcast_compare_fusion
  67.5 1.3 fusion.6.bias_ref
  68.9 2.5 %collective-permute-done.7.other_ref = bf16[8,128,1024]{2,1,0:T(8,128)(2,1)} collective-permute-done((bf16[8,128,1024]{2,1,0:T(8,128)(2,1)S(1)}, bf16[8,128,1024]{2,1,0:T(8,128)(2,1)}, u32[]{:S(2)}, u32[]{:S(2)}) %collective-permute-start.7) | collective-permute-done | bytes 2097184 | tf_op jit(solution)/shard_map/weights/ppermute | solution.py:261
  71.4 1.0 copy-done.4
  72.4 1.0 copy-done.6
  73.5 1.0 copy-done.11
  74.5 6.1 %row_heads.1 = (bf16[256,1024]{1,0:T(8,128)(2,1)S(1)}, bf16[1024,256]{1,0:T(8,128)(2,1)S(1)}, bf16[1024,256]{1,0:T(8,128)(2,1)}, bf16[2,8,128,1024]{3,2,1,0:T(8,128)(2,1)S(1)}) custom-call(s32[3]{0:T(128)S(1)} %pad_add_fusion.place, bf16[256,1024]{1,0:T(8,128)(2,1)S(1)} %bitcast.67, bf16[256,1024]{1,0:T(8,128)(2,1)S(1)} %bitcast.69, ...), custom_call_target="tpu_custom_call" | custom-call | flops 1400000000 | bytes 12000000 | tf_op jit(solution)/shard_map/row_heads/pallas_call | solution.py:264
  80.6 2.0 %copy-done = bf16[2,8,128,1024]{3,2,1,0:T(8,128)(2,1)} copy-done((bf16[2,8,128,1024]{3,2,1,0:T(8,128)(2,1)}, bf16[2,8,128,1024]{3,2,1,0:T(8,128)(2,1)S(1)}, u32[]{:S(2)}) %copy-start) | copy-done | bytes 4194328
  82.6 0.8 copy-done.7
  83.4 0.8 copy-done.9
  84.2 2.0 %collective-permute-start.8 = (bf16[1024,256]{1,0:T(8,128)(2,1)}, bf16[1024,256]{1,0:T(8,128)(2,1)}, u32[]{:S(2)}, u32[]{:S(2)}) collective-permute-start(bf16[1024,256]{1,0:T(8,128)(2,1)} %get-tuple-element.20), channel_id=1, source_target_pairs={{0,1},{1,0},{2,3},{3,2},{4,5},{5,4},{6,7},{7,6},{8,9},{9,8},{10,11... | collective-permute-start | bytes 1572872 | tf_op jit(solution)/shard_map/gradient_sums/ppermute | solution.py:300
  86.2 0.6 fusion.3.bias_ref
  86.8 15.1 %all-to-all-done = bf16[64,8,1024]{2,1,0:T(8,128)(2,1)S(1)} async-done(((bf16[64,8,1024]{2,1,0:T(8,128)(2,1)}), bf16[64,8,1024]{2,1,0:T(8,128)(2,1)S(1)}, u32[]{:S(2)}, u32[]{:S(2)}) %all-to-all-start) | async-done | bytes 1048608 | tf_op jit(solution)/shard_map/to_columns/all_to_all | solution.py:253
  101.9 2.2 %copy-done.1 = bf16[2,8,128,1024]{3,2,1,0:T(8,128)(2,1)S(1)} copy-done((bf16[2,8,128,1024]{3,2,1,0:T(8,128)(2,1)S(1)}, bf16[2,8,128,1024]{3,2,1,0:T(8,128)(2,1)}, u32[]{:S(2)}) %copy-start.1) | copy-done | bytes 4194328
  104.1 6.0 %column_heads.1 = (bf16[512,512]{1,0:T(8,128)(2,1)}, bf16[1024,256]{1,0:T(8,128)(2,1)S(1)}, bf16[1024,256]{1,0:T(8,128)(2,1)S(1)}) custom-call(s32[3]{0:T(128)S(1)} %pad_add_fusion.place, bf16[512,1024]{1,0:T(8,128)(2,1)S(1)} %bitcast.65, bf16[4,256,256]{2,1,0:T(8,128)(2,1)S(1)} %fusion.3.bias_ref, bf16[2,8,128,1024]{3,2,1,0:T(8,128)(2,1)S(1)} %copy-done.1), custom_call_target="tpu_custom_call" | custom-call | flops 1900000000 | bytes 8000000 | tf_op jit(solution)/shard_map/column_heads/pallas_call | solution.py:279
  110.1 1.9 collective-permute-start.15
  112.1 4.8 %all-to-all-start.1 = ((bf16[64,8,512]{2,1,0:T(8,128)(2,1)}), bf16[64,8,512]{2,1,0:T(8,128)(2,1)S(1)}, u32[]{:S(2)}, u32[]{:S(2)}) async-start(bf16[64,8,512]{2,1,0:T(8,128)(2,1)} %bitcast.24), calls=%async_computation.1 | async-start | bytes 1048576 | tf_op jit(solution)/shard_map/from_columns/all_to_all | solution.py:295
  116.9 1.2 add_convert_fusion.1
  118.2 2.4 %collective-permute-start.10 = (bf16[256,256]{1,0:T(8,128)(2,1)S(1)}, bf16[256,256]{1,0:T(8,128)(2,1)S(1)}, u32[]{:S(2)}, u32[]{:S(2)}) collective-permute-start(bf16[256,256]{1,0:T(8,128)(2,1)S(1)} %get-tuple-element.32), channel_id=1, source_target_pairs={{0,384},{128,0},{256,128},{384,256},{1,385},{129,1},{257,129},{385... | collective-permute-start | bytes 393224 | tf_op jit(solution)/shard_map/gradient_sums/ppermute | solution.py:309
  120.6 4.3 %collective-permute-start.11 = (bf16[256,256]{1,0:T(8,128)(2,1)S(1)}, bf16[256,256]{1,0:T(8,128)(2,1)S(1)}, u32[]{:S(2)}, u32[]{:S(2)}) collective-permute-start(bf16[256,256]{1,0:T(8,128)(2,1)S(1)} %get-tuple-element.31), channel_id=1, source_target_pairs={{0,256},{128,384},{256,0},{384,128},{1,257},{129,385},{257,1},{385... | collective-permute-start | bytes 393224 | tf_op jit(solution)/shard_map/gradient_sums/ppermute | solution.py:309
  124.9 3.7 %collective-permute-start.9 = (bf16[256,256]{1,0:T(8,128)(2,1)S(1)}, bf16[256,256]{1,0:T(8,128)(2,1)S(1)}, u32[]{:S(2)}, u32[]{:S(2)}) collective-permute-start(bf16[256,256]{1,0:T(8,128)(2,1)S(1)} %get-tuple-element.30), channel_id=1, source_target_pairs={{0,128},{128,256},{256,384},{384,0},{1,129},{129,257},{257,385},{3... | collective-permute-start | bytes 393224 | tf_op jit(solution)/shard_map/gradient_sums/ppermute | solution.py:309
  128.7 0.1 add_convert_fusion
  128.9 2.1 %collective-permute-start.16 = (bf16[256,256]{1,0:T(8,128)(2,1)S(1)}, bf16[256,256]{1,0:T(8,128)(2,1)S(1)}, u32[]{:S(2)}, u32[]{:S(2)}) collective-permute-start(bf16[256,256]{1,0:T(8,128)(2,1)S(1)} %get-tuple-element.33), channel_id=1, source_target_pairs={{0,128},{128,256},{256,384},{384,0},{1,129},{129,257},{257,385},{3... | collective-permute-start | bytes 393224 | tf_op jit(solution)/shard_map/gradient_sums/ppermute | solution.py:309
  130.9 3.9 %collective-permute-start.17 = (bf16[256,256]{1,0:T(8,128)(2,1)S(1)}, bf16[256,256]{1,0:T(8,128)(2,1)S(1)}, u32[]{:S(2)}, u32[]{:S(2)}) collective-permute-start(bf16[256,256]{1,0:T(8,128)(2,1)S(1)} %get-tuple-element.35), channel_id=1, source_target_pairs={{0,384},{128,0},{256,128},{384,256},{1,385},{129,1},{257,129},{385... | collective-permute-start | bytes 393224 | tf_op jit(solution)/shard_map/gradient_sums/ppermute | solution.py:309
  134.9 3.3 %collective-permute-start.18 = (bf16[256,256]{1,0:T(8,128)(2,1)S(1)}, bf16[256,256]{1,0:T(8,128)(2,1)S(1)}, u32[]{:S(2)}, u32[]{:S(2)}) collective-permute-start(bf16[256,256]{1,0:T(8,128)(2,1)S(1)} %get-tuple-element.34), channel_id=1, source_target_pairs={{0,256},{128,384},{256,0},{384,128},{1,257},{129,385},{257,1},{385... | collective-permute-start | bytes 393224 | tf_op jit(solution)/shard_map/gradient_sums/ppermute | solution.py:309
  138.3 3.2 %collective-permute-start.12 = (bf16[128,128]{1,0:T(8,128)(2,1)S(1)}, bf16[128,128]{1,0:T(8,128)(2,1)S(1)}, u32[]{:S(2)}, u32[]{:S(2)}) collective-permute-start(bf16[128,128]{1,0:T(8,128)(2,1)S(1)} %get-tuple-element.36), channel_id=1, source_target_pairs={{0,2},{2,0},{64,66},{66,64},{1,3},{3,1},{65,67},{67,65},{4,6},{6,4... | collective-permute-start | bytes 98312 | tf_op jit(solution)/shard_map/gradient_sums/ppermute | solution.py:318
  141.6 3.7 %collective-permute-start.13 = (bf16[128,128]{1,0:T(8,128)(2,1)S(1)}, bf16[128,128]{1,0:T(8,128)(2,1)S(1)}, u32[]{:S(2)}, u32[]{:S(2)}) collective-permute-start(bf16[128,128]{1,0:T(8,128)(2,1)S(1)} %get-tuple-element.38), channel_id=1, source_target_pairs={{0,64},{2,66},{64,0},{66,2},{1,65},{3,67},{65,1},{67,3},{4,68},{6,... | collective-permute-start | bytes 98312 | tf_op jit(solution)/shard_map/gradient_sums/ppermute | solution.py:318
  145.3 3.5 %collective-permute-start.14 = (bf16[128,128]{1,0:T(8,128)(2,1)S(1)}, bf16[128,128]{1,0:T(8,128)(2,1)S(1)}, u32[]{:S(2)}, u32[]{:S(2)}) collective-permute-start(bf16[128,128]{1,0:T(8,128)(2,1)S(1)} %get-tuple-element.37), channel_id=1, source_target_pairs={{0,66},{2,64},{64,2},{66,0},{1,67},{3,65},{65,3},{67,1},{4,70},{6,... | collective-permute-start | bytes 98312 | tf_op jit(solution)/shard_map/gradient_sums/ppermute | solution.py:318
  148.9 2.0 %collective-permute-start.19 = (bf16[128,128]{1,0:T(8,128)(2,1)S(1)}, bf16[128,128]{1,0:T(8,128)(2,1)S(1)}, u32[]{:S(2)}, u32[]{:S(2)}) collective-permute-start(bf16[128,128]{1,0:T(8,128)(2,1)S(1)} %get-tuple-element.39), channel_id=1, source_target_pairs={{0,2},{2,0},{64,66},{66,64},{1,3},{3,1},{65,67},{67,65},{4,6},{6,4... | collective-permute-start | bytes 98312 | tf_op jit(solution)/shard_map/gradient_sums/ppermute | solution.py:318
  150.9 5.0 %collective-permute-start.20 = (bf16[128,128]{1,0:T(8,128)(2,1)S(1)}, bf16[128,128]{1,0:T(8,128)(2,1)S(1)}, u32[]{:S(2)}, u32[]{:S(2)}) collective-permute-start(bf16[128,128]{1,0:T(8,128)(2,1)S(1)} %get-tuple-element.41), channel_id=1, source_target_pairs={{0,64},{2,66},{64,0},{66,2},{1,65},{3,67},{65,1},{67,3},{4,68},{6,... | collective-permute-start | bytes 98312 | tf_op jit(solution)/shard_map/gradient_sums/ppermute | solution.py:318
  155.9 3.5 %collective-permute-start.21 = (bf16[128,128]{1,0:T(8,128)(2,1)S(1)}, bf16[128,128]{1,0:T(8,128)(2,1)S(1)}, u32[]{:S(2)}, u32[]{:S(2)}) collective-permute-start(bf16[128,128]{1,0:T(8,128)(2,1)S(1)} %get-tuple-element.40), channel_id=1, source_target_pairs={{0,66},{2,64},{64,2},{66,0},{1,67},{3,65},{65,3},{67,1},{4,70},{6,... | collective-permute-start | bytes 98312 | tf_op jit(solution)/shard_map/gradient_sums/ppermute | solution.py:318
  159.5 3.5 %collective-permute-done.21 = bf16[128,128]{1,0:T(8,128)(2,1)S(1)} collective-permute-done((bf16[128,128]{1,0:T(8,128)(2,1)S(1)}, bf16[128,128]{1,0:T(8,128)(2,1)S(1)}, u32[]{:S(2)}, u32[]{:S(2)}) %collective-permute-start.21) | collective-permute-done | bytes 32800 | tf_op jit(solution)/shard_map/gradient_sums/ppermute | solution.py:318
  163.0 0.7 reshape.153
  163.7 12.7 %all-to-all-start.2 = ((f32[64,2,256]{2,1,0:T(2,128)}), f32[64,2,256]{2,1,0:T(2,128)S(1)}, u32[]{:S(2)}, u32[]{:S(2)}) async-start(f32[64,2,256]{2,1,0:T(2,128)} %reshape.153), calls=%async_computation.2 | async-start | bytes 262144 | tf_op jit(solution)/shard_map/gradient_sums/all_to_all | solution.py:324
  176.4 2.2 %copy-done.2 = bf16[2,8,128,1024]{3,2,1,0:T(8,128)(2,1)S(1)} copy-done((bf16[2,8,128,1024]{3,2,1,0:T(8,128)(2,1)S(1)}, bf16[2,8,128,1024]{3,2,1,0:T(8,128)(2,1)}, u32[]{:S(2)}) %copy-start.2) | copy-done | bytes 4194328
  178.6 3.0 %output_products.1 = (bf16[256,1024]{1,0:T(8,128)(2,1)}, bf16[256,1024]{1,0:T(8,128)(2,1)}) custom-call(bf16[256,1024]{1,0:T(8,128)(2,1)S(1)} %copy-done.8, bf16[512,512]{1,0:T(8,128)(2,1)S(1)} %bitcast.64, bf16[2,8,128,1024]{3,2,1,0:T(8,128)(2,1)S(1)} %copy-done.2), custom_call_target="tpu_custom_call" | custom-call | flops 1200000000 | bytes 8000000 | tf_op jit(solution)/shard_map/output_products/pallas_call | solution.py:330
  181.6 11.9 %all-to-all-done.2 = f32[64,2,256]{2,1,0:T(2,128)S(1)} async-done(((f32[64,2,256]{2,1,0:T(2,128)}), f32[64,2,256]{2,1,0:T(2,128)S(1)}, u32[]{:S(2)}, u32[]{:S(2)}) %all-to-all-start.2) | async-done | bytes 131104 | tf_op jit(solution)/shard_map/gradient_sums/all_to_all | solution.py:324
  193.4 0.2 reshape.154
  193.7 0.6 reshape.155
  194.3 0.6 copy.15
  (64 shorter events, 0.8 us)
Async XLA Ops:
  0.7 1.0 copy-start.3
  1.8 1.0 copy-start.5
  2.8 0.9 copy-start.12
  3.7 0.9 copy-start.13
  4.6 0.9 copy-start.14
  5.5 0.9 copy-start.15
  8.9 37.0 %collective-permute-start = (bf16[128,1024]{1,0:T(8,128)(2,1)S(1)}, bf16[128,1024]{1,0:T(8,128)(2,1)}, u32[]{:S(2)}, u32[]{:S(2)}) collective-permute-start(bf16[128,1024]{1,0:T(8,128)(2,1)S(1)} %get-tuple-element.17), channel_id=1, source_target_pairs={{0,64},{64,0},{128,192},{192,128},{256,320},{320,256},{384,448},{4... | collective-permute-start | bytes 786440 | tf_op jit(solution)/shard_map/weights/ppermute | solution.py:259
  14.0 35.3 %collective-permute-start.1 = (bf16[128,1024]{1,0:T(8,128)(2,1)S(1)}, bf16[128,1024]{1,0:T(8,128)(2,1)}, u32[]{:S(2)}, u32[]{:S(2)}) collective-permute-start(bf16[128,1024]{1,0:T(8,128)(2,1)S(1)} %get-tuple-element.17), channel_id=1, source_target_pairs={{0,128},{64,192},{128,256},{192,320},{256,384},{320,448},{384,0},{... | collective-permute-start | bytes 786440 | tf_op jit(solution)/shard_map/weights/ppermute | solution.py:259
  18.6 36.4 %collective-permute-start.2 = (bf16[128,1024]{1,0:T(8,128)(2,1)S(1)}, bf16[128,1024]{1,0:T(8,128)(2,1)}, u32[]{:S(2)}, u32[]{:S(2)}) collective-permute-start(bf16[128,1024]{1,0:T(8,128)(2,1)S(1)} %get-tuple-element.17), channel_id=1, source_target_pairs={{0,192},{64,128},{128,320},{192,256},{256,448},{320,384},{384,64},... | collective-permute-start | bytes 786440 | tf_op jit(solution)/shard_map/weights/ppermute | solution.py:259
  23.5 32.5 %collective-permute-start.3 = (bf16[128,1024]{1,0:T(8,128)(2,1)S(1)}, bf16[128,1024]{1,0:T(8,128)(2,1)}, u32[]{:S(2)}, u32[]{:S(2)}) collective-permute-start(bf16[128,1024]{1,0:T(8,128)(2,1)S(1)} %get-tuple-element.17), channel_id=1, source_target_pairs={{0,256},{64,320},{128,384},{192,448},{256,0},{320,64},{384,128},{4... | collective-permute-start | bytes 786440 | tf_op jit(solution)/shard_map/weights/ppermute | solution.py:259
  25.4 31.6 %collective-permute-start.4 = (bf16[128,1024]{1,0:T(8,128)(2,1)S(1)}, bf16[128,1024]{1,0:T(8,128)(2,1)}, u32[]{:S(2)}, u32[]{:S(2)}) collective-permute-start(bf16[128,1024]{1,0:T(8,128)(2,1)S(1)} %get-tuple-element.17), channel_id=1, source_target_pairs={{0,320},{64,256},{128,448},{192,384},{256,64},{320,0},{384,192},{4... | collective-permute-start | bytes 786440 | tf_op jit(solution)/shard_map/weights/ppermute | solution.py:259
  30.8 71.1 %all-to-all-start = ((bf16[64,8,1024]{2,1,0:T(8,128)(2,1)}), bf16[64,8,1024]{2,1,0:T(8,128)(2,1)S(1)}, u32[]{:S(2)}, u32[]{:S(2)}) async-start(bf16[64,8,1024]{2,1,0:T(8,128)(2,1)} %bitcast.16), calls=%async_computation | async-start | bytes 2097152 | tf_op jit(solution)/shard_map/to_columns/all_to_all | solution.py:253
  45.8 21.3 %copy-start.17 = (s32[4,1,2,2]{0,3,2,1:T(2,128)S(1)}, s32[4,1,2,2]{0,3,2,1:T(2,128)}, u32[]{:S(2)}) copy-start(s32[4,1,2,2]{0,3,2,1:T(2,128)} %param.10) | copy-start | bytes 196
  45.8 21.5 %copy-start.16 = (s32[4,4,8,8]{3,2,1,0:T(8,128)S(1)}, s32[4,4,8,8]{3,2,1,0:T(8,128)}, u32[]{:S(2)}) copy-start(s32[4,4,8,8]{3,2,1,0:T(8,128)} %param.11) | copy-start | bytes 12292
  45.9 12.3 %collective-permute-start.5 = (bf16[128,1024]{1,0:T(8,128)(2,1)S(1)}, bf16[128,1024]{1,0:T(8,128)(2,1)S(1)}, u32[]{:S(2)}, u32[]{:S(2)}) collective-permute-start(bf16[128,1024]{1,0:T(8,128)(2,1)S(1)} %get-tuple-element.17), channel_id=1, source_target_pairs={{0,384},{64,448},{128,0},{192,64},{256,128},{320,192},{384,256},{4... | collective-permute-start | bytes 786440 | tf_op jit(solution)/shard_map/weights/ppermute | solution.py:259
  49.3 15.9 %collective-permute-start.6 = (bf16[128,1024]{1,0:T(8,128)(2,1)S(1)}, bf16[128,1024]{1,0:T(8,128)(2,1)S(1)}, u32[]{:S(2)}, u32[]{:S(2)}) collective-permute-start(bf16[128,1024]{1,0:T(8,128)(2,1)S(1)} %get-tuple-element.17), channel_id=1, source_target_pairs={{0,448},{64,384},{128,64},{192,0},{256,192},{320,128},{384,320},{4... | collective-permute-start | bytes 786440 | tf_op jit(solution)/shard_map/weights/ppermute | solution.py:259
  65.2 6.2 %collective-permute-start.7 = (bf16[8,128,1024]{2,1,0:T(8,128)(2,1)S(1)}, bf16[8,128,1024]{2,1,0:T(8,128)(2,1)}, u32[]{:S(2)}, u32[]{:S(2)}) collective-permute-start(bf16[8,128,1024]{2,1,0:T(8,128)(2,1)S(1)} %bitcast_dynamic-update-slice_fusion.own_ref), channel_id=1, source_target_pairs={{0,1},{1,0},{2,3},{3,2},{4,5},{5,4},{6,7},{7,6},{8,9},{9,8},{10,11... | collective-permute-start | bytes 6291464 | tf_op jit(solution)/shard_map/weights/ppermute | solution.py:261
  71.4 1.0 copy-start.4
  72.4 1.0 copy-start.6
  73.5 1.0 copy-start.11
  80.6 2.0 %copy-start = (bf16[2,8,128,1024]{3,2,1,0:T(8,128)(2,1)}, bf16[2,8,128,1024]{3,2,1,0:T(8,128)(2,1)S(1)}, u32[]{:S(2)}) copy-start(bf16[2,8,128,1024]{3,2,1,0:T(8,128)(2,1)S(1)} %get-tuple-element.22.w_ref.weights) | copy-start | bytes 12582916
  82.6 0.8 copy-start.7
  83.4 0.8 copy-start.9
  84.2 32.7 %collective-permute-start.8 = (bf16[1024,256]{1,0:T(8,128)(2,1)}, bf16[1024,256]{1,0:T(8,128)(2,1)}, u32[]{:S(2)}, u32[]{:S(2)}) collective-permute-start(bf16[1024,256]{1,0:T(8,128)(2,1)} %get-tuple-element.20), channel_id=1, source_target_pairs={{0,1},{1,0},{2,3},{3,2},{4,5},{5,4},{6,7},{7,6},{8,9},{9,8},{10,11... | collective-permute-start | bytes 1572872 | tf_op jit(solution)/shard_map/gradient_sums/ppermute | solution.py:300
  101.9 2.2 %copy-start.1 = (bf16[2,8,128,1024]{3,2,1,0:T(8,128)(2,1)S(1)}, bf16[2,8,128,1024]{3,2,1,0:T(8,128)(2,1)}, u32[]{:S(2)}) copy-start(bf16[2,8,128,1024]{3,2,1,0:T(8,128)(2,1)} %copy-done) | copy-start | bytes 12582916
  104.1 12.8 %copy-start.10 = (bf16[1024,256]{1,0:T(8,128)(2,1)S(1)}, bf16[1024,256]{1,0:T(8,128)(2,1)}, u32[]{:S(2)}) copy-start(bf16[1024,256]{1,0:T(8,128)(2,1)} %copy-done.9) | copy-start | bytes 1572868
  110.1 18.5 %collective-permute-start.15 = (bf16[1024,256]{1,0:T(8,128)(2,1)S(1)}, bf16[1024,256]{1,0:T(8,128)(2,1)S(1)}, u32[]{:S(2)}, u32[]{:S(2)}) collective-permute-start(bf16[1024,256]{1,0:T(8,128)(2,1)S(1)} %get-tuple-element.24), channel_id=1, source_target_pairs={{0,1},{1,0},{2,3},{3,2},{4,5},{5,4},{6,7},{7,6},{8,9},{9,8},{10,11... | collective-permute-start | bytes 1572872 | tf_op jit(solution)/shard_map/gradient_sums/ppermute | solution.py:300
  112.1 50.9 %all-to-all-start.1 = ((bf16[64,8,512]{2,1,0:T(8,128)(2,1)}), bf16[64,8,512]{2,1,0:T(8,128)(2,1)S(1)}, u32[]{:S(2)}, u32[]{:S(2)}) async-start(bf16[64,8,512]{2,1,0:T(8,128)(2,1)} %bitcast.24), calls=%async_computation.1 | async-start | bytes 1048576 | tf_op jit(solution)/shard_map/from_columns/all_to_all | solution.py:295
  118.2 16.7 %collective-permute-start.10 = (bf16[256,256]{1,0:T(8,128)(2,1)S(1)}, bf16[256,256]{1,0:T(8,128)(2,1)S(1)}, u32[]{:S(2)}, u32[]{:S(2)}) collective-permute-start(bf16[256,256]{1,0:T(8,128)(2,1)S(1)} %get-tuple-element.32), channel_id=1, source_target_pairs={{0,384},{128,0},{256,128},{384,256},{1,385},{129,1},{257,129},{385... | collective-permute-start | bytes 393224 | tf_op jit(solution)/shard_map/gradient_sums/ppermute | solution.py:309
  120.6 17.6 %collective-permute-start.11 = (bf16[256,256]{1,0:T(8,128)(2,1)S(1)}, bf16[256,256]{1,0:T(8,128)(2,1)S(1)}, u32[]{:S(2)}, u32[]{:S(2)}) collective-permute-start(bf16[256,256]{1,0:T(8,128)(2,1)S(1)} %get-tuple-element.31), channel_id=1, source_target_pairs={{0,256},{128,384},{256,0},{384,128},{1,257},{129,385},{257,1},{385... | collective-permute-start | bytes 393224 | tf_op jit(solution)/shard_map/gradient_sums/ppermute | solution.py:309
  124.9 13.3 %collective-permute-start.9 = (bf16[256,256]{1,0:T(8,128)(2,1)S(1)}, bf16[256,256]{1,0:T(8,128)(2,1)S(1)}, u32[]{:S(2)}, u32[]{:S(2)}) collective-permute-start(bf16[256,256]{1,0:T(8,128)(2,1)S(1)} %get-tuple-element.30), channel_id=1, source_target_pairs={{0,128},{128,256},{256,384},{384,0},{1,129},{129,257},{257,385},{3... | collective-permute-start | bytes 393224 | tf_op jit(solution)/shard_map/gradient_sums/ppermute | solution.py:309
  128.8 47.6 %copy-start.8 = (bf16[256,1024]{1,0:T(8,128)(2,1)S(1)}, bf16[256,1024]{1,0:T(8,128)(2,1)}, u32[]{:S(2)}) copy-start(bf16[256,1024]{1,0:T(8,128)(2,1)} %copy-done.7) | copy-start | bytes 1572868
  128.9 16.4 %collective-permute-start.16 = (bf16[256,256]{1,0:T(8,128)(2,1)S(1)}, bf16[256,256]{1,0:T(8,128)(2,1)S(1)}, u32[]{:S(2)}, u32[]{:S(2)}) collective-permute-start(bf16[256,256]{1,0:T(8,128)(2,1)S(1)} %get-tuple-element.33), channel_id=1, source_target_pairs={{0,128},{128,256},{256,384},{384,0},{1,129},{129,257},{257,385},{3... | collective-permute-start | bytes 393224 | tf_op jit(solution)/shard_map/gradient_sums/ppermute | solution.py:309
  130.9 17.9 %collective-permute-start.17 = (bf16[256,256]{1,0:T(8,128)(2,1)S(1)}, bf16[256,256]{1,0:T(8,128)(2,1)S(1)}, u32[]{:S(2)}, u32[]{:S(2)}) collective-permute-start(bf16[256,256]{1,0:T(8,128)(2,1)S(1)} %get-tuple-element.35), channel_id=1, source_target_pairs={{0,384},{128,0},{256,128},{384,256},{1,385},{129,1},{257,129},{385... | collective-permute-start | bytes 393224 | tf_op jit(solution)/shard_map/gradient_sums/ppermute | solution.py:309
  134.9 13.9 %collective-permute-start.18 = (bf16[256,256]{1,0:T(8,128)(2,1)S(1)}, bf16[256,256]{1,0:T(8,128)(2,1)S(1)}, u32[]{:S(2)}, u32[]{:S(2)}) collective-permute-start(bf16[256,256]{1,0:T(8,128)(2,1)S(1)} %get-tuple-element.34), channel_id=1, source_target_pairs={{0,256},{128,384},{256,0},{384,128},{1,257},{129,385},{257,1},{385... | collective-permute-start | bytes 393224 | tf_op jit(solution)/shard_map/gradient_sums/ppermute | solution.py:309
  138.3 17.6 %collective-permute-start.12 = (bf16[128,128]{1,0:T(8,128)(2,1)S(1)}, bf16[128,128]{1,0:T(8,128)(2,1)S(1)}, u32[]{:S(2)}, u32[]{:S(2)}) collective-permute-start(bf16[128,128]{1,0:T(8,128)(2,1)S(1)} %get-tuple-element.36), channel_id=1, source_target_pairs={{0,2},{2,0},{64,66},{66,64},{1,3},{3,1},{65,67},{67,65},{4,6},{6,4... | collective-permute-start | bytes 98312 | tf_op jit(solution)/shard_map/gradient_sums/ppermute | solution.py:318
  141.6 17.9 %collective-permute-start.13 = (bf16[128,128]{1,0:T(8,128)(2,1)S(1)}, bf16[128,128]{1,0:T(8,128)(2,1)S(1)}, u32[]{:S(2)}, u32[]{:S(2)}) collective-permute-start(bf16[128,128]{1,0:T(8,128)(2,1)S(1)} %get-tuple-element.38), channel_id=1, source_target_pairs={{0,64},{2,66},{64,0},{66,2},{1,65},{3,67},{65,1},{67,3},{4,68},{6,... | collective-permute-start | bytes 98312 | tf_op jit(solution)/shard_map/gradient_sums/ppermute | solution.py:318
  145.3 14.1 %collective-permute-start.14 = (bf16[128,128]{1,0:T(8,128)(2,1)S(1)}, bf16[128,128]{1,0:T(8,128)(2,1)S(1)}, u32[]{:S(2)}, u32[]{:S(2)}) collective-permute-start(bf16[128,128]{1,0:T(8,128)(2,1)S(1)} %get-tuple-element.37), channel_id=1, source_target_pairs={{0,66},{2,64},{64,2},{66,0},{1,67},{3,65},{65,3},{67,1},{4,70},{6,... | collective-permute-start | bytes 98312 | tf_op jit(solution)/shard_map/gradient_sums/ppermute | solution.py:318
  148.9 10.5 %collective-permute-start.19 = (bf16[128,128]{1,0:T(8,128)(2,1)S(1)}, bf16[128,128]{1,0:T(8,128)(2,1)S(1)}, u32[]{:S(2)}, u32[]{:S(2)}) collective-permute-start(bf16[128,128]{1,0:T(8,128)(2,1)S(1)} %get-tuple-element.39), channel_id=1, source_target_pairs={{0,2},{2,0},{64,66},{66,64},{1,3},{3,1},{65,67},{67,65},{4,6},{6,4... | collective-permute-start | bytes 98312 | tf_op jit(solution)/shard_map/gradient_sums/ppermute | solution.py:318
  150.9 8.5 %collective-permute-start.20 = (bf16[128,128]{1,0:T(8,128)(2,1)S(1)}, bf16[128,128]{1,0:T(8,128)(2,1)S(1)}, u32[]{:S(2)}, u32[]{:S(2)}) collective-permute-start(bf16[128,128]{1,0:T(8,128)(2,1)S(1)} %get-tuple-element.41), channel_id=1, source_target_pairs={{0,64},{2,66},{64,0},{66,2},{1,65},{3,67},{65,1},{67,3},{4,68},{6,... | collective-permute-start | bytes 98312 | tf_op jit(solution)/shard_map/gradient_sums/ppermute | solution.py:318
  155.9 7.0 %collective-permute-start.21 = (bf16[128,128]{1,0:T(8,128)(2,1)S(1)}, bf16[128,128]{1,0:T(8,128)(2,1)S(1)}, u32[]{:S(2)}, u32[]{:S(2)}) collective-permute-start(bf16[128,128]{1,0:T(8,128)(2,1)S(1)} %get-tuple-element.40), channel_id=1, source_target_pairs={{0,66},{2,64},{64,2},{66,0},{1,67},{3,65},{65,3},{67,1},{4,70},{6,... | collective-permute-start | bytes 98312 | tf_op jit(solution)/shard_map/gradient_sums/ppermute | solution.py:318
  163.7 29.7 %all-to-all-start.2 = ((f32[64,2,256]{2,1,0:T(2,128)}), f32[64,2,256]{2,1,0:T(2,128)S(1)}, u32[]{:S(2)}, u32[]{:S(2)}) async-start(f32[64,2,256]{2,1,0:T(2,128)} %reshape.153), calls=%async_computation.2 | async-start | bytes 262144 | tf_op jit(solution)/shard_map/gradient_sums/all_to_all | solution.py:324
  176.4 2.2 %copy-start.2 = (bf16[2,8,128,1024]{3,2,1,0:T(8,128)(2,1)S(1)}, bf16[2,8,128,1024]{3,2,1,0:T(8,128)(2,1)}, u32[]{:S(2)}) copy-start(bf16[2,8,128,1024]{3,2,1,0:T(8,128)(2,1)} %copy-done) | copy-start | bytes 12582916

commit v3 on v2

--- a/solution.py
+++ b/solution.py
@@ -18,7 +18,7 @@
 VMEM = pl.BlockSpec(memory_space=pltpu.VMEM)
 SMEM = pl.BlockSpec(memory_space=pltpu.SMEM)
 ANYWHERE = pl.BlockSpec(memory_space=pl.ANY)
-PARAMS = pltpu.CompilerParams(vmem_limit_bytes=24 * 1024 * 1024)
+PARAMS = pltpu.CompilerParams(vmem_limit_bytes=60 * 1024 * 1024)
 OFFSETS = [(dx, dy) for dx in range(4) for dy in range(2)]
 SWAP = [(0, 1), (1, 0)]
 
@@ -57,21 +57,22 @@
         copy.wait()
 
 
-def prepare_kernel(
-    place, x_ref, ct_ref, wq_ref, wk_ref, wv_ref, wo_ref, packed_ref, sent_ref, x, ct, sems
-):
+def interleave_kernel(x_ref, ct_ref, sent_ref, x, ct, sems):
+    wait_for(start_copies(((x_ref, x), (ct_ref, ct)), sems))
+    sent_ref[...] = interleave(x[...], ct[...])
+
+
+def pack_kernel(place, wq_ref, wk_ref, wv_ref, wo_ref, after_ref, packed_ref, sems):
+    del after_ref
     core = place[0]
     here = pl.ds(pl.multiple_of(core * 256, 256), 256)
-    pairs = [(x_ref, x), (ct_ref, ct)]
+    pairs = []
     for i, ref in enumerate((wq_ref, wk_ref, wv_ref)):
         pairs.append((ref.at[:, here], packed_ref.at[:, pl.ds(i * 256, 256)]))
     for b in range(2):
         there = pl.ds(pl.multiple_of(core * 512 + b * 256, 256), 256)
         pairs.append((wo_ref.at[:, there], packed_ref.at[pl.ds(b * 64, 64), pl.ds(768, 256)]))
-    copies = start_copies(pairs, sems)
-    wait_for(copies[:2])
-    sent_ref[...] = interleave(x[...], ct[...])
-    wait_for(copies[2:])
+    wait_for(start_copies(pairs, sems))
 
 
 def attention(x, ct, weights, kind, bias_ref):
@@ -106,18 +107,17 @@
 
 
 def store_gradients(core, x, ct, out, dv, keep_ref, send_ref):
-    grad_value = product(x, dv, FIRST).astype(BF)
-    grad_out = product(ct, out, FIRST).astype(BF)
-
-    @pl.when(core == 0)
-    def _():
-        keep_ref[...] = grad_value
-        send_ref[...] = grad_out
-
-    @pl.when(core != 0)
-    def _():
-        keep_ref[...] = grad_out
-        send_ref[...] = grad_value
+    gradients = jnp.concatenate(
+        [product(x, dv, FIRST).astype(BF), product(ct, out, FIRST).astype(BF)], axis=1
+    )
+    new = lax.broadcasted_iota(jnp.int32, (128, 128), 0)
+    old = lax.broadcasted_iota(jnp.int32, (128, 128), 1)
+    source = ((new >> 1) & 15) * 8 + ((new >> 5) & 1) * 4 + ((new >> 6) ^ core) * 2 + (new & 1)
+    order = (old == source).astype(F32).astype(BF)
+    for block in range(8):
+        moved = product(order, gradients[block * 128 : (block + 1) * 128]).astype(BF)
+        keep_ref[block * 64 : (block + 1) * 64, :] = moved[:64]
+        send_ref[block * 64 : (block + 1) * 64, :] = moved[64:]
 
 
 def row_kernel(
@@ -239,16 +239,26 @@
     cot_flat = cotangent.reshape(256, 1024)
     seq = ("z", "yl", "c")
 
-    packed, sent = pl.pallas_call(
-        prepare_kernel,
-        out_shape=(shape(128, 1024), shape(512, 1024)),
-        in_specs=[SMEM] + [ANYWHERE] * 6,
-        out_specs=(VMEM, VMEM),
-        scratch_shapes=[buffer(256, 1024), buffer(256, 1024), pltpu.SemaphoreType.DMA((7,))],
-        compiler_params=PARAMS,
-        cost_estimate=cost(540000000, 4000000),
-        name="prepare",
-    )(place, flat, cot_flat, w_query, w_key, w_value, w_out)
+    sent = pl.pallas_call(
+        interleave_kernel,
+        out_shape=shape(512, 1024),
+        in_specs=[ANYWHERE] * 2,
+        out_specs=VMEM,
+        scratch_shapes=[buffer(256, 1024), buffer(256, 1024), pltpu.SemaphoreType.DMA((2,))],
+        compiler_params=PARAMS,
+        cost_estimate=cost(540000000, 2000000),
+        name="interleave",
+    )(flat, cot_flat)
+    packed = pl.pallas_call(
+        pack_kernel,
+        out_shape=shape(128, 1024),
+        in_specs=[SMEM] + [ANYWHERE] * 5,
+        out_specs=VMEM,
+        scratch_shapes=[pltpu.SemaphoreType.DMA((5,))],
+        compiler_params=PARAMS,
+        cost_estimate=cost(90000000000, 2000000),
+        name="pack",
+    )(place, w_query, w_key, w_value, w_out, sent)
     with jax.named_scope("to_columns"):
         both = lax.all_to_all(
             sent.reshape(64, 8, 1024), seq, split_axis=0, concat_axis=0, tiled=True
@@ -263,7 +273,7 @@
         row_bias, col_bias = biases(row_mask, column_mask)
     row_parts, row_keep, row_send, weights = pl.pallas_call(
         row_kernel,
-        out_shape=(shape(256, 1024), shape(1024, 256), shape(1024, 256), shape(2, 8, 128, 1024)),
+        out_shape=(shape(256, 1024), shape(512, 512), shape(512, 512), shape(2, 8, 128, 1024)),
         in_specs=[SMEM] + [ANYWHERE] * 5,
         out_specs=(VMEM,) * 4,
         scratch_shapes=[
@@ -278,7 +288,7 @@
     )(place, flat, cot_flat, row_bias, own, other)
     col_parts, col_keep, col_send = pl.pallas_call(
         column_kernel,
-        out_shape=(shape(512, 512), shape(1024, 256), shape(1024, 256)),
+        out_shape=(shape(512, 512),) * 3,
         in_specs=[SMEM] + [ANYWHERE] * 3,
         out_specs=(VMEM,) * 3,
         scratch_shapes=[
@@ -296,37 +306,39 @@
             col_parts.reshape(64, 8, 512), seq, split_axis=0, concat_axis=0, tiled=True
         ).reshape(512, 512)
 
-    def plane_sum(keep, send):
+    def core_sum(keep, send):
         got = lax.ppermute(send, "c", SWAP)
-        held = (keep.astype(F32) + got.astype(F32)).astype(BF)
-
-        def rows_of(step):
-            return lax.dynamic_slice_in_dim(held, ((across + step) & 3) * 256, 256, axis=0)
-
-        terms = [rows_of(0)]
+        return (keep.astype(F32) + got.astype(F32)).astype(BF)
+
+    def plane_sum(held):
+        def x_rows(step):
+            return lax.dynamic_slice_in_dim(held, ((across + step) & 3) * 128, 128, axis=0)
+
+        terms = [x_rows(0)]
         for step in (1, 3, 2):
             pairs = [(x, (x + step) % 4) for x in range(4)]
-            terms.append(lax.ppermute(rows_of(step), "x", pairs))
-        held_rows = sum(term.astype(F32) for term in terms).astype(BF)
-
-        def block_of(dh, dl):
-            return lax.dynamic_slice(held_rows, ((high ^ dh) * 128, (low ^ dl) * 128), (128, 128))
-
-        terms = [block_of(0, 0)]
-        for dh, dl in ((0, 1), (1, 0), (1, 1)):
-            pairs = [(h * 2 + l, (h ^ dh) * 2 + (l ^ dl)) for h in range(2) for l in range(2)]
-            terms.append(lax.ppermute(block_of(dh, dl), ("yh", "yl"), pairs))
+            terms.append(lax.ppermute(x_rows(step), "x", pairs))
+        line = sum(term.astype(F32) for term in terms).astype(BF)
+        mine = high * 2 + low
+        terms = [lax.dynamic_slice_in_dim(line, mine * 32, 32, axis=0)]
+        for step in (1, 2, 3):
+            pairs = [(y, y ^ step) for y in range(4)]
+            rows = lax.dynamic_slice_in_dim(line, (mine ^ step) * 32, 32, axis=0)
+            terms.append(lax.ppermute(rows, ("yh", "yl"), pairs))
         return sum(term.astype(F32) for term in terms)
 
     with jax.named_scope("gradient_sums"):
-        plane = jnp.concatenate([plane_sum(row_keep, row_send), plane_sum(col_keep, col_send)], axis=1)
+        held = jnp.concatenate([core_sum(row_keep, row_send), core_sum(col_keep, col_send)], axis=1)
+        plane = plane_sum(held)
         plane, returned = lax.optimization_barrier((plane, returned))
         line = lax.all_to_all(
-            plane.reshape(64, 2, 256), seq, split_axis=0, concat_axis=0, tiled=True
+            plane.reshape(16, 2, 1024), "z", split_axis=0, concat_axis=0, tiled=True
         )
-        line = jnp.sum(line.reshape(16, 2, 2, 2, 2, 128), axis=0)
-        grad_value = jnp.transpose(line[:, 0], (1, 2, 0, 3)).reshape(2, 512)
-        grad_output = jnp.transpose(line[:, 1], (2, 0, 3, 1)).reshape(512, 2)
+        line = jnp.sum(line, axis=0)
+        grad_value = jnp.concatenate([line[:, 0:256], line[:, 512:768]], axis=1)
+        grad_output = jnp.transpose(
+            jnp.concatenate([line[:, 256:512], line[:, 768:1024]], axis=1)
+        )
     mixed, grad_tokens = pl.pallas_call(
         final_kernel,
         out_shape=(shape(256, 1024), shape(256, 1024)),

time: 199 us -> 175 us (0.88); the launches traced: 195 us -> 174 us
  local copies, waits for them, and re-layouts: 24.1 us -> 3.14 us
  starting transfers between devices: 108 us -> 94.7 us
  Pallas kernels: 17.5 us -> 26.7 us
  waiting for transfers between devices: 40.2 us -> 43.2 us
    ppermute x14 -> x8, starting transfers between devices: 44.6 us -> 24.5 us  [the longest x3 10.4 us: plane_sum(): terms.append(lax.ppermute(rows, ('yh', 'yl'), pairs))]
    unnamed x43 -> x23, local copies, waits for them, and re-layouts: 21.6 us -> 2.16 us
    ppermute x14 -> x8, waiting for transfers between devices: 3.5 us -> 18.4 us  [the longest x3 11.3 us: plane_sum(): terms.append(lax.ppermute(x_rows(step), 'x', pairs))]
    all_to_all x1, waiting for transfers between devices: 15.1 us -> 1.44 us  [body(): lax.all_to_all(sent.reshape(64, 8, 1024), seq, split_axis=0, concat_axis=...]
    all_to_all x1, starting transfers between devices: 4.82 us -> 12.4 us  [body(): lax.all_to_all(col_parts.reshape(64, 8, 512), seq, split_axis=0, concat_a...]
    pallas_call x3 -> x4, Pallas kernels: 14.6 us -> 22.1 us  [the longest x1 8.83 us: body(): pl.pallas_call(row_kernel, out_shape=(shape(256, 1024), shape(512, 512),...]
    ppermute x7, waiting for transfers between devices: 7.22 us -> 13.6 us  [body(): lax.ppermute(packed, ('x', 'yh'), shifted(dx, dy))]
    all_to_all x1, waiting for transfers between devices: 11.9 us -> 8.63 us  [body(): lax.all_to_all(plane.reshape(16, 2, 1024), 'z', split_axis=0, concat_axis...]
  transfers between devices with their start and end apart: 25 -> 19, of which waited for: 6 -> 11; matrix products, arithmetic and copies ran while one was open for 5% -> 3% of each run, Pallas kernels for 8% -> 12%
where the time goes in v3:
time: 175 us; the launch traced here: 174 us
  starting transfers between devices  94.7 us (54%)
  waiting for transfers between devices  43.2 us (25%)
  Pallas kernels  26.7 us (15%)
  local copies, waits for them, and re-layouts  3.14 us (2%)
  matrix products  2.84 us (2%)
  other arithmetic  2.63 us (2%)
    ppermute x7, starting transfers between devices, body(): lax.ppermute(packed, ('x', 'yh'), shifted(dx, dy))  27.9 us
    all_to_all x1, starting transfers between devices, body(): lax.all_to_all(sent.reshape(64, 8, 1024), seq, split_axis=0, concat_axis=...  16.2 us
    ppermute x7, waiting for transfers between devices, body(): lax.ppermute(packed, ('x', 'yh'), shifted(dx, dy))  13.6 us
    all_to_all x1, starting transfers between devices, body(): lax.all_to_all(col_parts.reshape(64, 8, 512), seq, split_axis=0, concat_a...  12.4 us
    all_to_all x1, starting transfers between devices, body(): lax.all_to_all(plane.reshape(16, 2, 1024), 'z', split_axis=0, concat_axis...  11.7 us
    ppermute x3, waiting for transfers between devices, plane_sum(): terms.append(lax.ppermute(x_rows(step), 'x', pairs))  11.3 us
    ppermute x3, starting transfers between devices, plane_sum(): terms.append(lax.ppermute(rows, ('yh', 'yl'), pairs))  10.4 us
    ppermute x3, starting transfers between devices, plane_sum(): terms.append(lax.ppermute(x_rows(step), 'x', pairs))  10.1 us
  transfers between devices with their start and end apart: 19, of which 11 were waited for; matrix products, arithmetic and copies ran while one was open for 3% of the time, Pallas kernels for 12%

profile of v3, /device:TPU:6, one launch (start us, length us, event | category | flops | bytes accessed | tf_op | source)
XLA Modules:
  0.0 174.4 jit_solution(12934819392245297368)
XLA Ops:
  0.6 3.0 %interleave.1.after_ref = bf16[512,1024]{1,0:T(8,128)(2,1)} custom-call(bf16[256,1024]{1,0:T(8,128)(2,1)} %bitcast.57, bf16[256,1024]{1,0:T(8,128)(2,1)} %bitcast.59), custom_call_target="tpu_custom_call" | custom-call | flops 540000000 | bytes 2000000 | tf_op jit(solution)/shard_map/interleave/pallas_call | solution.py:242
  3.6 0.7 pad_add_fusion.place
  4.3 2.3 %pack.1 = bf16[128,1024]{1,0:T(8,128)(2,1)} custom-call(s32[3]{0:T(128)} %pad_add_fusion.place, bf16[128,512]{1,0:T(8,128)(2,1)} %wq_ref.1, bf16[128,512]{1,0:T(8,128)(2,1)} %wk_ref.1, bf16[128,512]{1,0:T(8,128)(2,1)} %wv_ref.1, bf16[64,1024]{1,0:T(8,128)(2,1)} %wo_ref.1, bf16[512,1024]{1,0:T(8,128)(2,1)} %interleave.1.after_ref), custom_call_target="tpu_custom_call" | custom-call | flops 89999998976 | bytes 2000000 | tf_op jit(solution)/shard_map/pack/pallas_call | solution.py:252
  6.6 0.0 copy-start.5
  6.6 5.2 %collective-permute-start = (bf16[128,1024]{1,0:T(8,128)(2,1)}, bf16[128,1024]{1,0:T(8,128)(2,1)}, u32[]{:S(2)}, u32[]{:S(2)}) collective-permute-start(bf16[128,1024]{1,0:T(8,128)(2,1)} %pack.1), channel_id=1, source_target_pairs={{0,64},{64,0},{128,192},{192,128},{256,320},{320,256},{384,448},{4... | collective-permute-start | bytes 786440 | tf_op jit(solution)/shard_map/weights/ppermute | solution.py:269
  11.9 16.2 %all-to-all-start = ((bf16[64,8,1024]{2,1,0:T(8,128)(2,1)}), bf16[64,8,1024]{2,1,0:T(8,128)(2,1)S(1)}, u32[]{:S(2)}, u32[]{:S(2)}) async-start(bf16[64,8,1024]{2,1,0:T(8,128)(2,1)} %bitcast.18), calls=%async_computation | async-start | bytes 2097152 | tf_op jit(solution)/shard_map/to_columns/all_to_all | solution.py:263
  28.1 0.0 copy-done.5
  28.1 0.0 copy-start.6
  28.1 2.4 %collective-permute-start.1 = (bf16[128,1024]{1,0:T(8,128)(2,1)S(1)}, bf16[128,1024]{1,0:T(8,128)(2,1)S(1)}, u32[]{:S(2)}, u32[]{:S(2)}) collective-permute-start(bf16[128,1024]{1,0:T(8,128)(2,1)S(1)} %copy-done.5), channel_id=1, source_target_pairs={{0,128},{64,192},{128,256},{192,320},{256,384},{320,448},{384,0},{... | collective-permute-start | bytes 786440 | tf_op jit(solution)/shard_map/weights/ppermute | solution.py:269
  30.5 4.7 %collective-permute-start.2 = (bf16[128,1024]{1,0:T(8,128)(2,1)S(1)}, bf16[128,1024]{1,0:T(8,128)(2,1)S(1)}, u32[]{:S(2)}, u32[]{:S(2)}) collective-permute-start(bf16[128,1024]{1,0:T(8,128)(2,1)S(1)} %copy-done.5), channel_id=1, source_target_pairs={{0,192},{64,128},{128,320},{192,256},{256,448},{320,384},{384,64},... | collective-permute-start | bytes 786440 | tf_op jit(solution)/shard_map/weights/ppermute | solution.py:269
  35.2 4.0 %collective-permute-start.3 = (bf16[128,1024]{1,0:T(8,128)(2,1)S(1)}, bf16[128,1024]{1,0:T(8,128)(2,1)S(1)}, u32[]{:S(2)}, u32[]{:S(2)}) collective-permute-start(bf16[128,1024]{1,0:T(8,128)(2,1)S(1)} %copy-done.5), channel_id=1, source_target_pairs={{0,256},{64,320},{128,384},{192,448},{256,0},{320,64},{384,128},{4... | collective-permute-start | bytes 786440 | tf_op jit(solution)/shard_map/weights/ppermute | solution.py:269
  39.2 4.4 %collective-permute-start.4 = (bf16[128,1024]{1,0:T(8,128)(2,1)S(1)}, bf16[128,1024]{1,0:T(8,128)(2,1)S(1)}, u32[]{:S(2)}, u32[]{:S(2)}) collective-permute-start(bf16[128,1024]{1,0:T(8,128)(2,1)S(1)} %copy-done.5), channel_id=1, source_target_pairs={{0,320},{64,256},{128,448},{192,384},{256,64},{320,0},{384,192},{4... | collective-permute-start | bytes 786440 | tf_op jit(solution)/shard_map/weights/ppermute | solution.py:269
  43.7 0.0 collective-permute-done
  43.7 2.4 %collective-permute-start.5 = (bf16[128,1024]{1,0:T(8,128)(2,1)S(1)}, bf16[128,1024]{1,0:T(8,128)(2,1)S(1)}, u32[]{:S(2)}, u32[]{:S(2)}) collective-permute-start(bf16[128,1024]{1,0:T(8,128)(2,1)S(1)} %copy-done.5), channel_id=1, source_target_pairs={{0,384},{64,448},{128,0},{192,64},{256,128},{320,192},{384,256},{4... | collective-permute-start | bytes 786440 | tf_op jit(solution)/shard_map/weights/ppermute | solution.py:269
  46.2 1.0 bitcast_dynamic-update-slice_fusion.6
  47.1 0.0 collective-permute-done.1
  47.1 4.7 %collective-permute-start.6 = (bf16[128,1024]{1,0:T(8,128)(2,1)S(1)}, bf16[128,1024]{1,0:T(8,128)(2,1)S(1)}, u32[]{:S(2)}, u32[]{:S(2)}) collective-permute-start(bf16[128,1024]{1,0:T(8,128)(2,1)S(1)} %copy-done.5), channel_id=1, source_target_pairs={{0,448},{64,384},{128,64},{192,0},{256,192},{320,128},{384,320},{4... | collective-permute-start | bytes 786440 | tf_op jit(solution)/shard_map/weights/ppermute | solution.py:269
  51.9 0.0 copy-start.7
  51.9 0.0 collective-permute-done.2
  52.0 0.0 collective-permute-done.3
  52.0 2.9 %collective-permute-done.4 = bf16[128,1024]{1,0:T(8,128)(2,1)S(1)} collective-permute-done((bf16[128,1024]{1,0:T(8,128)(2,1)S(1)}, bf16[128,1024]{1,0:T(8,128)(2,1)S(1)}, u32[]{:S(2)}, u32[]{:S(2)}) %collective-permute-start.4) | collective-permute-done | bytes 262176 | tf_op jit(solution)/shard_map/weights/ppermute | solution.py:269
  55.0 2.7 %collective-permute-done.5 = bf16[128,1024]{1,0:T(8,128)(2,1)S(1)} collective-permute-done((bf16[128,1024]{1,0:T(8,128)(2,1)S(1)}, bf16[128,1024]{1,0:T(8,128)(2,1)S(1)}, u32[]{:S(2)}, u32[]{:S(2)}) %collective-permute-start.5) | collective-permute-done | bytes 262176 | tf_op jit(solution)/shard_map/weights/ppermute | solution.py:269
  57.7 8.0 %collective-permute-done.6 = bf16[128,1024]{1,0:T(8,128)(2,1)S(1)} collective-permute-done((bf16[128,1024]{1,0:T(8,128)(2,1)S(1)}, bf16[128,1024]{1,0:T(8,128)(2,1)S(1)}, u32[]{:S(2)}, u32[]{:S(2)}) %collective-permute-start.6) | collective-permute-done | bytes 262176 | tf_op jit(solution)/shard_map/weights/ppermute | solution.py:269
  65.7 0.0 copy-start
  65.7 1.9 %collective-permute-start.7 = (bf16[8,128,1024]{2,1,0:T(8,128)(2,1)S(1)}, bf16[8,128,1024]{2,1,0:T(8,128)(2,1)}, u32[]{:S(2)}, u32[]{:S(2)}) collective-permute-start(bf16[8,128,1024]{2,1,0:T(8,128)(2,1)S(1)} %bitcast_dynamic-update-slice_fusion.own_ref), channel_id=1, source_target_pairs={{0,1},{1,0},{2,3},{3,2},{4,5},{5,4},{6,7},{7,6},{8,9},{9,8},{10,11... | collective-permute-start | bytes 6291464 | tf_op jit(solution)/shard_map/weights/ppermute | solution.py:271
  67.6 0.0 copy-done.6
  67.7 0.1 copy.12
  67.8 0.1 broadcast_compare_fusion
  67.9 1.4 fusion.6.bias_ref
  69.3 1.5 fusion.3.bias_ref
  70.8 1.1 collective-permute-done.7.other_ref
  71.9 8.8 %row_heads.1 = (bf16[256,1024]{1,0:T(8,128)(2,1)}, bf16[512,512]{1,0:T(8,128)(2,1)}, bf16[512,512]{1,0:T(8,128)(2,1)}, bf16[2,8,128,1024]{3,2,1,0:T(8,128)(2,1)}) custom-call(s32[3]{0:T(128)} %pad_add_fusion.place, bf16[256,1024]{1,0:T(8,128)(2,1)} %bitcast.58, bf16[256,1024]{1,0:T(8,128)(2,1)} %bitcast.60, bf16[4,256,256]{2,1,0:T(8,128)(2,1)} %fusion.6.bias_ref, ...), custom_call_target="tpu_custom_call" | custom-call | flops 1400000000 | bytes 12000000 | tf_op jit(solution)/shard_map/row_heads/pallas_call | solution.py:274
  80.7 2.0 %collective-permute-start.8 = (bf16[512,512]{1,0:T(8,128)(2,1)}, bf16[512,512]{1,0:T(8,128)(2,1)S(1)}, u32[]{:S(2)}, u32[]{:S(2)}) collective-permute-start(bf16[512,512]{1,0:T(8,128)(2,1)} %get-tuple-element.17), channel_id=1, source_target_pairs={{0,1},{1,0},{2,3},{3,2},{4,5},{5,4},{6,7},{7,6},{8,9},{9,8},{10,11... | collective-permute-start | bytes 1572872 | tf_op jit(solution)/shard_map/gradient_sums/ppermute | solution.py:310
  82.8 1.4 all-to-all-done
  84.2 1.0 copy-done.2
  85.3 8.0 %column_heads.1 = (bf16[512,512]{1,0:T(8,128)(2,1)}, bf16[512,512]{1,0:T(8,128)(2,1)}, bf16[512,512]{1,0:T(8,128)(2,1)}) custom-call(s32[3]{0:T(128)} %pad_add_fusion.place, bf16[512,1024]{1,0:T(8,128)(2,1)} %bitcast.61, bf16[4,256,256]{2,1,0:T(8,128)(2,1)} %fusion.3.bias_ref, bf16[2,8,128,1024]{3,2,1,0:T(8,128)(2,1)} %get-tuple-element.18.w_ref.weights), custom_call_target="tpu_custom_call" | custom-call | flops 1900000000 | bytes 8000000 | tf_op jit(solution)/shard_map/column_heads/pallas_call | solution.py:289
  93.3 12.4 %all-to-all-start.1 = ((bf16[64,8,512]{2,1,0:T(8,128)(2,1)}), bf16[64,8,512]{2,1,0:T(8,128)(2,1)S(1)}, u32[]{:S(2)}, u32[]{:S(2)}) async-start(bf16[64,8,512]{2,1,0:T(8,128)(2,1)} %bitcast.62), calls=%async_computation.1 | async-start | bytes 1048576 | tf_op jit(solution)/shard_map/from_columns/all_to_all | solution.py:305
  105.7 2.0 %collective-permute-start.9 = (bf16[512,512]{1,0:T(8,128)(2,1)}, bf16[512,512]{1,0:T(8,128)(2,1)S(1)}, u32[]{:S(2)}, u32[]{:S(2)}) collective-permute-start(bf16[512,512]{1,0:T(8,128)(2,1)} %get-tuple-element.20), channel_id=1, source_target_pairs={{0,1},{1,0},{2,3},{3,2},{4,5},{5,4},{6,7},{7,6},{8,9},{9,8},{10,11... | collective-permute-start | bytes 1572872 | tf_op jit(solution)/shard_map/gradient_sums/ppermute | solution.py:310
  107.7 0.0 collective-permute-done.8
  107.7 0.1 add_convert_fusion.1
  107.9 1.9 %collective-permute-done.9 = bf16[512,512]{1,0:T(8,128)(2,1)S(1)} collective-permute-done((bf16[512,512]{1,0:T(8,128)(2,1)}, bf16[512,512]{1,0:T(8,128)(2,1)S(1)}, u32[]{:S(2)}, u32[]{:S(2)}) %collective-permute-start.9) | collective-permute-done | bytes 524320 | tf_op jit(solution)/shard_map/gradient_sums/ppermute | solution.py:310
  109.7 0.1 add_convert_fusion
  109.9 0.1 fusion.9
  110.0 4.6 %collective-permute-start.10 = (bf16[128,1024]{1,0:T(8,128)(2,1)S(1)}, bf16[128,1024]{1,0:T(8,128)(2,1)S(1)}, u32[]{:S(2)}, u32[]{:S(2)}) collective-permute-start(bf16[128,1024]{1,0:T(8,128)(2,1)S(1)} %get-tuple-element.26), channel_id=1, source_target_pairs={{0,128},{128,256},{256,384},{384,0},{1,129},{129,257},{257,385},{3... | collective-permute-start | bytes 786440 | tf_op jit(solution)/shard_map/gradient_sums/ppermute | solution.py:320
  114.6 1.9 %collective-permute-start.11 = (bf16[128,1024]{1,0:T(8,128)(2,1)S(1)}, bf16[128,1024]{1,0:T(8,128)(2,1)S(1)}, u32[]{:S(2)}, u32[]{:S(2)}) collective-permute-start(bf16[128,1024]{1,0:T(8,128)(2,1)S(1)} %get-tuple-element.27), channel_id=1, source_target_pairs={{0,384},{128,0},{256,128},{384,256},{1,385},{129,1},{257,129},{385... | collective-permute-start | bytes 786440 | tf_op jit(solution)/shard_map/gradient_sums/ppermute | solution.py:320
  116.6 3.6 %collective-permute-start.12 = (bf16[128,1024]{1,0:T(8,128)(2,1)S(1)}, bf16[128,1024]{1,0:T(8,128)(2,1)S(1)}, u32[]{:S(2)}, u32[]{:S(2)}) collective-permute-start(bf16[128,1024]{1,0:T(8,128)(2,1)S(1)} %get-tuple-element.28), channel_id=1, source_target_pairs={{0,256},{128,384},{256,0},{384,128},{1,257},{129,385},{257,1},{385... | collective-permute-start | bytes 786440 | tf_op jit(solution)/shard_map/gradient_sums/ppermute | solution.py:320
  120.2 0.3 collective-permute-done.10
  120.5 10.9 %collective-permute-done.11 = bf16[128,1024]{1,0:T(8,128)(2,1)S(1)} collective-permute-done((bf16[128,1024]{1,0:T(8,128)(2,1)S(1)}, bf16[128,1024]{1,0:T(8,128)(2,1)S(1)}, u32[]{:S(2)}, u32[]{:S(2)}) %collective-permute-start.11) | collective-permute-done | bytes 262176 | tf_op jit(solution)/shard_map/gradient_sums/ppermute | solution.py:320
  131.4 0.0 collective-permute-done.12
  131.4 0.2 add_convert_fusion.2
  131.6 3.5 %collective-permute-start.13 = (bf16[32,1024]{1,0:T(8,128)(2,1)S(1)}, bf16[32,1024]{1,0:T(8,128)(2,1)S(1)}, u32[]{:S(2)}, u32[]{:S(2)}) collective-permute-start(bf16[32,1024]{1,0:T(8,128)(2,1)S(1)} %get-tuple-element.29), channel_id=1, source_target_pairs={{0,2},{2,0},{64,66},{66,64},{1,3},{3,1},{65,67},{67,65},{4,6},{6,4... | collective-permute-start | bytes 196616 | tf_op jit(solution)/shard_map/gradient_sums/ppermute | solution.py:327
  135.1 4.8 %collective-permute-start.14 = (bf16[32,1024]{1,0:T(8,128)(2,1)S(1)}, bf16[32,1024]{1,0:T(8,128)(2,1)S(1)}, u32[]{:S(2)}, u32[]{:S(2)}) collective-permute-start(bf16[32,1024]{1,0:T(8,128)(2,1)S(1)} %get-tuple-element.31), channel_id=1, source_target_pairs={{0,64},{2,66},{64,0},{66,2},{1,65},{3,67},{65,1},{67,3},{4,68},{6,... | collective-permute-start | bytes 196616 | tf_op jit(solution)/shard_map/gradient_sums/ppermute | solution.py:327
  139.9 2.1 %collective-permute-start.15 = (bf16[32,1024]{1,0:T(8,128)(2,1)S(1)}, bf16[32,1024]{1,0:T(8,128)(2,1)S(1)}, u32[]{:S(2)}, u32[]{:S(2)}) collective-permute-start(bf16[32,1024]{1,0:T(8,128)(2,1)S(1)} %get-tuple-element.30), channel_id=1, source_target_pairs={{0,66},{2,64},{64,2},{66,0},{1,67},{3,65},{65,3},{67,1},{4,70},{6,... | collective-permute-start | bytes 196616 | tf_op jit(solution)/shard_map/gradient_sums/ppermute | solution.py:327
  142.1 0.0 collective-permute-done.13
  142.1 0.7 collective-permute-done.14
  142.8 4.5 %collective-permute-done.15 = bf16[32,1024]{1,0:T(8,128)(2,1)S(1)} collective-permute-done((bf16[32,1024]{1,0:T(8,128)(2,1)S(1)}, bf16[32,1024]{1,0:T(8,128)(2,1)S(1)}, u32[]{:S(2)}, u32[]{:S(2)}) %collective-permute-start.15) | collective-permute-done | bytes 65568 | tf_op jit(solution)/shard_map/gradient_sums/ppermute | solution.py:327
  147.3 0.0 all-to-all-done.1
  147.4 0.8 reshape.144
  148.2 11.7 %all-to-all-start.2 = ((f32[16,2,1024]{2,1,0:T(2,128)}), f32[16,2,1024]{2,1,0:T(2,128)S(1)}, u32[]{:S(2)}, u32[]{:S(2)}) async-start(f32[16,2,1024]{2,1,0:T(2,128)} %reshape.144), calls=%async_computation.2 | async-start | bytes 262144 | tf_op jit(solution)/shard_map/gradient_sums/all_to_all | solution.py:334
  159.9 4.6 %output_products.1 = (bf16[256,1024]{1,0:T(8,128)(2,1)}, bf16[256,1024]{1,0:T(8,128)(2,1)}) custom-call(bf16[256,1024]{1,0:T(8,128)(2,1)} %get-tuple-element.15.row_ref, bf16[512,512]{1,0:T(8,128)(2,1)} %bitcast.56, bf16[2,8,128,1024]{3,2,1,0:T(8,128)(2,1)} %get-tuple-element.18.w_ref.weights), custom_call_target="tpu_custom_call" | custom-call | flops 1200000000 | bytes 8000000 | tf_op jit(solution)/shard_map/output_products/pallas_call | solution.py:342
  164.5 8.6 %all-to-all-done.2 = f32[16,2,1024]{2,1,0:T(2,128)S(1)} async-done(((f32[16,2,1024]{2,1,0:T(2,128)}), f32[16,2,1024]{2,1,0:T(2,128)S(1)}, u32[]{:S(2)}, u32[]{:S(2)}) %all-to-all-start.2) | async-done | bytes 131104 | tf_op jit(solution)/shard_map/gradient_sums/all_to_all | solution.py:334
  173.1 0.1 reduce_sum.9
  173.2 0.6 maximum_bitcast_fusion
  173.8 0.6 pad_maximum_fusion
  (24 shorter events, 0.3 us)
Async XLA Ops:
  6.6 21.5 %copy-start.5 = (bf16[128,1024]{1,0:T(8,128)(2,1)S(1)}, bf16[128,1024]{1,0:T(8,128)(2,1)}, u32[]{:S(2)}) copy-start(bf16[128,1024]{1,0:T(8,128)(2,1)} %pack.1) | copy-start | bytes 786436
  6.6 37.1 %collective-permute-start = (bf16[128,1024]{1,0:T(8,128)(2,1)}, bf16[128,1024]{1,0:T(8,128)(2,1)}, u32[]{:S(2)}, u32[]{:S(2)}) collective-permute-start(bf16[128,1024]{1,0:T(8,128)(2,1)} %pack.1), channel_id=1, source_target_pairs={{0,64},{64,0},{128,192},{192,128},{256,320},{320,256},{384,448},{4... | collective-permute-start | bytes 786440 | tf_op jit(solution)/shard_map/weights/ppermute | solution.py:269
  11.9 72.4 %all-to-all-start = ((bf16[64,8,1024]{2,1,0:T(8,128)(2,1)}), bf16[64,8,1024]{2,1,0:T(8,128)(2,1)S(1)}, u32[]{:S(2)}, u32[]{:S(2)}) async-start(bf16[64,8,1024]{2,1,0:T(8,128)(2,1)} %bitcast.18), calls=%async_computation | async-start | bytes 2097152 | tf_op jit(solution)/shard_map/to_columns/all_to_all | solution.py:263
  28.1 39.5 %copy-start.6 = (s32[4,1,2,2]{0,3,2,1:T(2,128)S(1)}, s32[4,1,2,2]{0,3,2,1:T(2,128)}, u32[]{:S(2)}) copy-start(s32[4,1,2,2]{0,3,2,1:T(2,128)} %param.10) | copy-start | bytes 196
  28.1 19.0 %collective-permute-start.1 = (bf16[128,1024]{1,0:T(8,128)(2,1)S(1)}, bf16[128,1024]{1,0:T(8,128)(2,1)S(1)}, u32[]{:S(2)}, u32[]{:S(2)}) collective-permute-start(bf16[128,1024]{1,0:T(8,128)(2,1)S(1)} %copy-done.5), channel_id=1, source_target_pairs={{0,128},{64,192},{128,256},{192,320},{256,384},{320,448},{384,0},{... | collective-permute-start | bytes 786440 | tf_op jit(solution)/shard_map/weights/ppermute | solution.py:269
  30.5 21.4 %collective-permute-start.2 = (bf16[128,1024]{1,0:T(8,128)(2,1)S(1)}, bf16[128,1024]{1,0:T(8,128)(2,1)S(1)}, u32[]{:S(2)}, u32[]{:S(2)}) collective-permute-start(bf16[128,1024]{1,0:T(8,128)(2,1)S(1)} %copy-done.5), channel_id=1, source_target_pairs={{0,192},{64,128},{128,320},{192,256},{256,448},{320,384},{384,64},... | collective-permute-start | bytes 786440 | tf_op jit(solution)/shard_map/weights/ppermute | solution.py:269
  35.2 16.8 %collective-permute-start.3 = (bf16[128,1024]{1,0:T(8,128)(2,1)S(1)}, bf16[128,1024]{1,0:T(8,128)(2,1)S(1)}, u32[]{:S(2)}, u32[]{:S(2)}) collective-permute-start(bf16[128,1024]{1,0:T(8,128)(2,1)S(1)} %copy-done.5), channel_id=1, source_target_pairs={{0,256},{64,320},{128,384},{192,448},{256,0},{320,64},{384,128},{4... | collective-permute-start | bytes 786440 | tf_op jit(solution)/shard_map/weights/ppermute | solution.py:269
  39.2 15.7 %collective-permute-start.4 = (bf16[128,1024]{1,0:T(8,128)(2,1)S(1)}, bf16[128,1024]{1,0:T(8,128)(2,1)S(1)}, u32[]{:S(2)}, u32[]{:S(2)}) collective-permute-start(bf16[128,1024]{1,0:T(8,128)(2,1)S(1)} %copy-done.5), channel_id=1, source_target_pairs={{0,320},{64,256},{128,448},{192,384},{256,64},{320,0},{384,192},{4... | collective-permute-start | bytes 786440 | tf_op jit(solution)/shard_map/weights/ppermute | solution.py:269
  43.7 13.9 %collective-permute-start.5 = (bf16[128,1024]{1,0:T(8,128)(2,1)S(1)}, bf16[128,1024]{1,0:T(8,128)(2,1)S(1)}, u32[]{:S(2)}, u32[]{:S(2)}) collective-permute-start(bf16[128,1024]{1,0:T(8,128)(2,1)S(1)} %copy-done.5), channel_id=1, source_target_pairs={{0,384},{64,448},{128,0},{192,64},{256,128},{320,192},{384,256},{4... | collective-permute-start | bytes 786440 | tf_op jit(solution)/shard_map/weights/ppermute | solution.py:269
  47.1 18.5 %collective-permute-start.6 = (bf16[128,1024]{1,0:T(8,128)(2,1)S(1)}, bf16[128,1024]{1,0:T(8,128)(2,1)S(1)}, u32[]{:S(2)}, u32[]{:S(2)}) collective-permute-start(bf16[128,1024]{1,0:T(8,128)(2,1)S(1)} %copy-done.5), channel_id=1, source_target_pairs={{0,448},{64,384},{128,64},{192,0},{256,192},{320,128},{384,320},{4... | collective-permute-start | bytes 786440 | tf_op jit(solution)/shard_map/weights/ppermute | solution.py:269
  51.9 17.4 %copy-start.7 = (s32[4,4,8,8]{3,2,1,0:T(8,128)S(1)}, s32[4,4,8,8]{3,2,1,0:T(8,128)}, u32[]{:S(2)}) copy-start(s32[4,4,8,8]{3,2,1,0:T(8,128)} %param.11) | copy-start | bytes 12292
  65.7 6.2 %copy-start = (bf16[8,128,1024]{2,1,0:T(8,128)(2,1)}, bf16[8,128,1024]{2,1,0:T(8,128)(2,1)S(1)}, u32[]{:S(2)}) copy-start(bf16[8,128,1024]{2,1,0:T(8,128)(2,1)S(1)} %bitcast_dynamic-update-slice_fusion.own_ref) | copy-start | bytes 6291460
  65.7 6.2 %collective-permute-start.7 = (bf16[8,128,1024]{2,1,0:T(8,128)(2,1)S(1)}, bf16[8,128,1024]{2,1,0:T(8,128)(2,1)}, u32[]{:S(2)}, u32[]{:S(2)}) collective-permute-start(bf16[8,128,1024]{2,1,0:T(8,128)(2,1)S(1)} %bitcast_dynamic-update-slice_fusion.own_ref), channel_id=1, source_target_pairs={{0,1},{1,0},{2,3},{3,2},{4,5},{5,4},{6,7},{7,6},{8,9},{9,8},{10,11... | collective-permute-start | bytes 6291464 | tf_op jit(solution)/shard_map/weights/ppermute | solution.py:271
  80.7 27.0 %collective-permute-start.8 = (bf16[512,512]{1,0:T(8,128)(2,1)}, bf16[512,512]{1,0:T(8,128)(2,1)S(1)}, u32[]{:S(2)}, u32[]{:S(2)}) collective-permute-start(bf16[512,512]{1,0:T(8,128)(2,1)} %get-tuple-element.17), channel_id=1, source_target_pairs={{0,1},{1,0},{2,3},{3,2},{4,5},{5,4},{6,7},{7,6},{8,9},{9,8},{10,11... | collective-permute-start | bytes 1572872 | tf_op jit(solution)/shard_map/gradient_sums/ppermute | solution.py:310
  84.2 1.0 copy-start.2
  85.3 22.5 %copy-start.3 = (bf16[512,512]{1,0:T(8,128)(2,1)S(1)}, bf16[512,512]{1,0:T(8,128)(2,1)}, u32[]{:S(2)}) copy-start(bf16[512,512]{1,0:T(8,128)(2,1)} %get-tuple-element.16) | copy-start | bytes 1572868
  93.3 16.5 %copy-start.4 = (bf16[512,512]{1,0:T(8,128)(2,1)S(1)}, bf16[512,512]{1,0:T(8,128)(2,1)}, u32[]{:S(2)}) copy-start(bf16[512,512]{1,0:T(8,128)(2,1)} %get-tuple-element.19) | copy-start | bytes 1572868
  93.3 54.1 %all-to-all-start.1 = ((bf16[64,8,512]{2,1,0:T(8,128)(2,1)}), bf16[64,8,512]{2,1,0:T(8,128)(2,1)S(1)}, u32[]{:S(2)}, u32[]{:S(2)}) async-start(bf16[64,8,512]{2,1,0:T(8,128)(2,1)} %bitcast.62), calls=%async_computation.1 | async-start | bytes 1048576 | tf_op jit(solution)/shard_map/from_columns/all_to_all | solution.py:305
  105.7 4.0 %collective-permute-start.9 = (bf16[512,512]{1,0:T(8,128)(2,1)}, bf16[512,512]{1,0:T(8,128)(2,1)S(1)}, u32[]{:S(2)}, u32[]{:S(2)}) collective-permute-start(bf16[512,512]{1,0:T(8,128)(2,1)} %get-tuple-element.20), channel_id=1, source_target_pairs={{0,1},{1,0},{2,3},{3,2},{4,5},{5,4},{6,7},{7,6},{8,9},{9,8},{10,11... | collective-permute-start | bytes 1572872 | tf_op jit(solution)/shard_map/gradient_sums/ppermute | solution.py:310
  110.0 10.5 %collective-permute-start.10 = (bf16[128,1024]{1,0:T(8,128)(2,1)S(1)}, bf16[128,1024]{1,0:T(8,128)(2,1)S(1)}, u32[]{:S(2)}, u32[]{:S(2)}) collective-permute-start(bf16[128,1024]{1,0:T(8,128)(2,1)S(1)} %get-tuple-element.26), channel_id=1, source_target_pairs={{0,128},{128,256},{256,384},{384,0},{1,129},{129,257},{257,385},{3... | collective-permute-start | bytes 786440 | tf_op jit(solution)/shard_map/gradient_sums/ppermute | solution.py:320
  114.6 16.8 %collective-permute-start.11 = (bf16[128,1024]{1,0:T(8,128)(2,1)S(1)}, bf16[128,1024]{1,0:T(8,128)(2,1)S(1)}, u32[]{:S(2)}, u32[]{:S(2)}) collective-permute-start(bf16[128,1024]{1,0:T(8,128)(2,1)S(1)} %get-tuple-element.27), channel_id=1, source_target_pairs={{0,384},{128,0},{256,128},{384,256},{1,385},{129,1},{257,129},{385... | collective-permute-start | bytes 786440 | tf_op jit(solution)/shard_map/gradient_sums/ppermute | solution.py:320
  116.6 14.9 %collective-permute-start.12 = (bf16[128,1024]{1,0:T(8,128)(2,1)S(1)}, bf16[128,1024]{1,0:T(8,128)(2,1)S(1)}, u32[]{:S(2)}, u32[]{:S(2)}) collective-permute-start(bf16[128,1024]{1,0:T(8,128)(2,1)S(1)} %get-tuple-element.28), channel_id=1, source_target_pairs={{0,256},{128,384},{256,0},{384,128},{1,257},{129,385},{257,1},{385... | collective-permute-start | bytes 786440 | tf_op jit(solution)/shard_map/gradient_sums/ppermute | solution.py:320
  131.6 10.5 %collective-permute-start.13 = (bf16[32,1024]{1,0:T(8,128)(2,1)S(1)}, bf16[32,1024]{1,0:T(8,128)(2,1)S(1)}, u32[]{:S(2)}, u32[]{:S(2)}) collective-permute-start(bf16[32,1024]{1,0:T(8,128)(2,1)S(1)} %get-tuple-element.29), channel_id=1, source_target_pairs={{0,2},{2,0},{64,66},{66,64},{1,3},{3,1},{65,67},{67,65},{4,6},{6,4... | collective-permute-start | bytes 196616 | tf_op jit(solution)/shard_map/gradient_sums/ppermute | solution.py:327
  135.1 7.7 %collective-permute-start.14 = (bf16[32,1024]{1,0:T(8,128)(2,1)S(1)}, bf16[32,1024]{1,0:T(8,128)(2,1)S(1)}, u32[]{:S(2)}, u32[]{:S(2)}) collective-permute-start(bf16[32,1024]{1,0:T(8,128)(2,1)S(1)} %get-tuple-element.31), channel_id=1, source_target_pairs={{0,64},{2,66},{64,0},{66,2},{1,65},{3,67},{65,1},{67,3},{4,68},{6,... | collective-permute-start | bytes 196616 | tf_op jit(solution)/shard_map/gradient_sums/ppermute | solution.py:327
  139.9 7.4 %collective-permute-start.15 = (bf16[32,1024]{1,0:T(8,128)(2,1)S(1)}, bf16[32,1024]{1,0:T(8,128)(2,1)S(1)}, u32[]{:S(2)}, u32[]{:S(2)}) collective-permute-start(bf16[32,1024]{1,0:T(8,128)(2,1)S(1)} %get-tuple-element.30), channel_id=1, source_target_pairs={{0,66},{2,64},{64,2},{66,0},{1,67},{3,65},{65,3},{67,1},{4,70},{6,... | collective-permute-start | bytes 196616 | tf_op jit(solution)/shard_map/gradient_sums/ppermute | solution.py:327
  147.4 12.5 %copy-start.1 = (bf16[64,8,512]{2,1,0:T(8,128)(2,1)}, bf16[64,8,512]{2,1,0:T(8,128)(2,1)S(1)}, u32[]{:S(2)}) copy-start(bf16[64,8,512]{2,1,0:T(8,128)(2,1)S(1)} %all-to-all-done.1) | copy-start | bytes 1572868
  148.2 24.9 %all-to-all-start.2 = ((f32[16,2,1024]{2,1,0:T(2,128)}), f32[16,2,1024]{2,1,0:T(2,128)S(1)}, u32[]{:S(2)}, u32[]{:S(2)}) async-start(f32[16,2,1024]{2,1,0:T(2,128)} %reshape.144), calls=%async_computation.2 | async-start | bytes 262144 | tf_op jit(solution)/shard_map/gradient_sums/all_to_all | solution.py:334

commit v4 on v3

--- a/solution.py
+++ b/solution.py
@@ -16,10 +16,9 @@
 FIRST = (((0,), (0,)), ((), ()))
 MASKED = -1e30
 VMEM = pl.BlockSpec(memory_space=pltpu.VMEM)
-SMEM = pl.BlockSpec(memory_space=pltpu.SMEM)
 ANYWHERE = pl.BlockSpec(memory_space=pl.ANY)
 PARAMS = pltpu.CompilerParams(vmem_limit_bytes=60 * 1024 * 1024)
-OFFSETS = [(dx, dy) for dx in range(4) for dy in range(2)]
+STEPS = (0, 1, 3, 2)
 SWAP = [(0, 1), (1, 0)]
 
 
@@ -62,9 +61,9 @@
     sent_ref[...] = interleave(x[...], ct[...])
 
 
-def pack_kernel(place, wq_ref, wk_ref, wv_ref, wo_ref, after_ref, packed_ref, sems):
+def pack_kernel(wq_ref, wk_ref, wv_ref, wo_ref, after_ref, packed_ref, sems):
     del after_ref
-    core = place[0]
+    core = lax.axis_index("c")
     here = pl.ds(pl.multiple_of(core * 256, 256), 256)
     pairs = []
     for i, ref in enumerate((wq_ref, wk_ref, wv_ref)):
@@ -121,7 +120,6 @@
 
 
 def row_kernel(
-    place,
     x_ref,
     ct_ref,
     bias_ref,
@@ -136,12 +134,14 @@
     bias,
     sems,
 ):
-    core = place[0]
+    core = lax.axis_index("c")
     pairs = []
-    for index, (dx, dy) in enumerate(OFFSETS):
-        source = ((place[1] + 4 - dx) & 3) * 2 + ((place[2] + dy) & 1)
-        for half, ref in ((core, own_ref), (1 - core, other_ref)):
-            pairs.append((ref.at[index], w_ref.at[half, source]))
+    across, high = lax.axis_index("x"), lax.axis_index("yh")
+    for index, step in enumerate(STEPS):
+        for flip in range(2):
+            source = ((across + 4 - step) & 3) * 2 + (high ^ flip)
+            for half, ref in ((core, own_ref), (1 - core, other_ref)):
+                pairs.append((ref.at[index * 2 + flip], w_ref.at[half, source]))
     pairs += [(x_ref, x_here), (ct_ref, ct_here), (bias_ref, bias)]
     wait_for(start_copies(pairs, sems))
     x, ct = x_here[...], ct_here[...]
@@ -152,9 +152,15 @@
 
 
 def column_kernel(
-    place, both_ref, bias_ref, w_ref, parts_ref, keep_ref, send_ref, both, bias, weights, sems
+    both_ref, bias_ref, w_ref, parts_ref, keep_ref, send_ref, both, bias, weights, sems
 ):
-    copies = start_copies(((both_ref, both), (w_ref, weights), (bias_ref, bias)), sems)
+    pairs = [(both_ref, both), (bias_ref, bias)]
+    mine, right = pl.ds(0, 768), pl.ds(768, 256)
+    pairs.append((w_ref.at[1, :, :, mine], weights.at[1, :, :, mine]))
+    for half in range(2):
+        wanted = (half, pl.ds(4, 4), slice(None), right)
+        pairs.append((w_ref.at[wanted], weights.at[wanted]))
+    copies = start_copies(pairs, sems)
     wait_for(copies[:1])
     x, ct = separate(both[...])
     wait_for(copies[1:])
@@ -162,7 +168,7 @@
     parts_ref[...] = interleave(
         jnp.concatenate([out, dq], axis=1), jnp.concatenate([dk, dv], axis=1)
     )
-    store_gradients(place[0], x, ct, out, dv, keep_ref, send_ref)
+    store_gradients(lax.axis_index("c"), x, ct, out, dv, keep_ref, send_ref)
 
 
 def final_kernel(row_ref, col_ref, weights, mixed_ref, gt_ref, row, col, w_ref, sems):
@@ -226,15 +232,8 @@
     return row_bias, col_bias
 
 
-def shifted(dx, dy):
-    return [
-        (x * 2 + y, (x + dx) % 4 * 2 + (y + dy) % 2) for x in range(4) for y in range(2)
-    ]
-
-
 def body(tokens, cotangent, row_mask, column_mask, w_query, w_key, w_value, w_out):
-    core, across, high, low = (lax.axis_index(name) for name in ("c", "x", "yh", "yl"))
-    place = jnp.stack([core, across, high]).astype(jnp.int32)
+    across, high, low = (lax.axis_index(name) for name in ("x", "yh", "yl"))
     flat = tokens.reshape(256, 1024)
     cot_flat = cotangent.reshape(256, 1024)
     seq = ("z", "yl", "c")
@@ -252,21 +251,23 @@
     packed = pl.pallas_call(
         pack_kernel,
         out_shape=shape(128, 1024),
-        in_specs=[SMEM] + [ANYWHERE] * 5,
+        in_specs=[ANYWHERE] * 5,
         out_specs=VMEM,
         scratch_shapes=[pltpu.SemaphoreType.DMA((5,))],
         compiler_params=PARAMS,
         cost_estimate=cost(90000000000, 2000000),
         name="pack",
-    )(place, w_query, w_key, w_value, w_out, sent)
+    )(w_query, w_key, w_value, w_out, sent)
     with jax.named_scope("to_columns"):
         both = lax.all_to_all(
             sent.reshape(64, 8, 1024), seq, split_axis=0, concat_axis=0, tiled=True
         ).reshape(512, 1024)
     with jax.named_scope("weights"):
-        own = jnp.stack(
-            [packed]
-            + [lax.ppermute(packed, ("x", "yh"), shifted(dx, dy)) for dx, dy in OFFSETS[1:]]
+        flipped = lax.ppermute(packed, ("yh", "yl"), [(y, 3 - y) for y in range(4)])
+        pair = jnp.stack([packed, flipped])
+        own = jnp.concatenate(
+            [pair]
+            + [lax.ppermute(pair, "x", [(x, (x + dx) % 4) for x in range(4)]) for dx in STEPS[1:]]
         )
         other = lax.ppermute(own, "c", SWAP)
     with jax.named_scope("masks"):
@@ -274,7 +275,7 @@
     row_parts, row_keep, row_send, weights = pl.pallas_call(
         row_kernel,
         out_shape=(shape(256, 1024), shape(512, 512), shape(512, 512), shape(2, 8, 128, 1024)),
-        in_specs=[SMEM] + [ANYWHERE] * 5,
+        in_specs=[ANYWHERE] * 5,
         out_specs=(VMEM,) * 4,
         scratch_shapes=[
             buffer(256, 1024),
@@ -285,22 +286,22 @@
         compiler_params=PARAMS,
         cost_estimate=cost(1400000000, 12000000),
         name="row_heads",
-    )(place, flat, cot_flat, row_bias, own, other)
+    )(flat, cot_flat, row_bias, own, other)
     col_parts, col_keep, col_send = pl.pallas_call(
         column_kernel,
         out_shape=(shape(512, 512),) * 3,
-        in_specs=[SMEM] + [ANYWHERE] * 3,
+        in_specs=[ANYWHERE] * 3,
         out_specs=(VMEM,) * 3,
         scratch_shapes=[
             buffer(512, 1024),
             buffer(4, 256, 256),
             buffer(2, 8, 128, 1024),
-            pltpu.SemaphoreType.DMA((3,)),
+            pltpu.SemaphoreType.DMA((5,)),
         ],
         compiler_params=PARAMS,
         cost_estimate=cost(1900000000, 8000000),
         name="column_heads",
-    )(place, both, col_bias, weights)
+    )(both, col_bias, weights)
     with jax.named_scope("from_columns"):
         returned = lax.all_to_all(
             col_parts.reshape(64, 8, 512), seq, split_axis=0, concat_axis=0, tiled=True

time: 175 us -> 170 us (0.971)
  starting transfers between devices: 94.7 us -> 82.3 us
  waiting for transfers between devices: 43.2 us -> 52.8 us
  Pallas kernels: 26.7 us -> 24.1 us
    ppermute x7 -> x4, starting transfers between devices: 27.9 us -> 14.1 us  [the longest x3 9.15 us: body(): lax.ppermute(pair, 'x', [(x, (x + dx) % 4) for x in range(4)])]
    ppermute x7 -> x4, waiting for transfers between devices: 13.6 us -> 26.3 us  [the longest x3 19.5 us: body(): lax.ppermute(pair, 'x', [(x, (x + dx) % 4) for x in range(4)])]
    ppermute x3, waiting for transfers between devices: 11.3 us -> 9.51 us  [plane_sum(): terms.append(lax.ppermute(x_rows(step), 'x', pairs))]
  transfers between devices with their start and end apart: 19 -> 16, of which waited for: 11 -> 11; matrix products, arithmetic and copies ran while one was open for 3% -> 3% of each run, Pallas kernels for 12% -> 12%
where the time goes in v4:
time: 170 us; the launch traced here: 169 us
  starting transfers between devices  82.3 us (48%)
  waiting for transfers between devices  52.8 us (31%)
  Pallas kernels  24.1 us (14%)
  local copies, waits for them, and re-layouts  3.08 us (2%)
  other arithmetic  2.97 us (2%)
  matrix products  2.85 us (2%)
    ppermute x3, waiting for transfers between devices, body(): lax.ppermute(pair, 'x', [(x, (x + dx) % 4) for x in range(4)])  19.5 us
    all_to_all x1, starting transfers between devices, body(): lax.all_to_all(sent.reshape(64, 8, 1024), seq, split_axis=0, concat_axis=...  17.1 us
    all_to_all x1, starting transfers between devices, body(): lax.all_to_all(col_parts.reshape(64, 8, 512), seq, split_axis=0, concat_a...  12.7 us
    all_to_all x1, starting transfers between devices, body(): lax.all_to_all(plane.reshape(16, 2, 1024), 'z', split_axis=0, concat_axis...  11.7 us
    ppermute x3, starting transfers between devices, plane_sum(): terms.append(lax.ppermute(rows, ('yh', 'yl'), pairs))  11.1 us
    ppermute x3, starting transfers between devices, plane_sum(): terms.append(lax.ppermute(x_rows(step), 'x', pairs))  9.71 us
    ppermute x3, waiting for transfers between devices, plane_sum(): terms.append(lax.ppermute(x_rows(step), 'x', pairs))  9.51 us
    ppermute x3, starting transfers between devices, body(): lax.ppermute(pair, 'x', [(x, (x + dx) % 4) for x in range(4)])  9.15 us
  transfers between devices with their start and end apart: 16, of which 11 were waited for; matrix products, arithmetic and copies ran while one was open for 3% of the time, Pallas kernels for 12%

profile of v4, /device:TPU:6, one launch (start us, length us, event | category | flops | bytes accessed | tf_op | source)
XLA Modules:
  0.0 169.2 jit_solution(17548138715820822602)
XLA Ops:
  0.6 3.0 %interleave.1.after_ref = bf16[512,1024]{1,0:T(8,128)(2,1)} custom-call(bf16[256,1024]{1,0:T(8,128)(2,1)} %bitcast.43, bf16[256,1024]{1,0:T(8,128)(2,1)} %bitcast.45), custom_call_target="tpu_custom_call" | custom-call | flops 540000000 | bytes 2000000 | tf_op jit(solution)/shard_map/interleave/pallas_call | solution.py:241
  3.6 17.1 %all-to-all-start = ((bf16[64,8,1024]{2,1,0:T(8,128)(2,1)}), bf16[64,8,1024]{2,1,0:T(8,128)(2,1)S(1)}, u32[]{:S(2)}, u32[]{:S(2)}) async-start(bf16[64,8,1024]{2,1,0:T(8,128)(2,1)} %bitcast.41), calls=%async_computation | async-start | bytes 2097152 | tf_op jit(solution)/shard_map/to_columns/all_to_all | solution.py:262
  20.8 1.7 pack.1
  22.4 4.9 %collective-permute-start = (bf16[128,1024]{1,0:T(8,128)(2,1)}, bf16[128,1024]{1,0:T(8,128)(2,1)S(1)}, u32[]{:S(2)}, u32[]{:S(2)}) collective-permute-start(bf16[128,1024]{1,0:T(8,128)(2,1)} %pack.1), channel_id=1, source_target_pairs={{0,66},{2,64},{64,2},{66,0},{1,67},{3,65},{65,3},{67,1},{4,70},{6,... | collective-permute-start | bytes 786440 | tf_op jit(solution)/shard_map/weights/ppermute | solution.py:266
  27.4 6.8 %collective-permute-done = bf16[128,1024]{1,0:T(8,128)(2,1)S(1)} collective-permute-done((bf16[128,1024]{1,0:T(8,128)(2,1)}, bf16[128,1024]{1,0:T(8,128)(2,1)S(1)}, u32[]{:S(2)}, u32[]{:S(2)}) %collective-permute-start) | collective-permute-done | bytes 262176 | tf_op jit(solution)/shard_map/weights/ppermute | solution.py:266
  34.2 1.0 pad_maximum_fusion
  35.2 0.0 copy-start.5
  35.2 2.4 %collective-permute-start.1 = (bf16[2,128,1024]{2,1,0:T(8,128)(2,1)S(1)}, bf16[2,128,1024]{2,1,0:T(8,128)(2,1)S(1)}, u32[]{:S(2)}, u32[]{:S(2)}) collective-permute-start(bf16[2,128,1024]{2,1,0:T(8,128)(2,1)S(1)} %pad_maximum_fusion), channel_id=1, source_target_pairs={{0,128},{128,256},{256,384},{384,0},{1,129},{129,257},{257,385},{3... | collective-permute-start | bytes 1572872 | tf_op jit(solution)/shard_map/weights/ppermute | solution.py:270
  37.6 3.5 %collective-permute-start.2 = (bf16[2,128,1024]{2,1,0:T(8,128)(2,1)S(1)}, bf16[2,128,1024]{2,1,0:T(8,128)(2,1)S(1)}, u32[]{:S(2)}, u32[]{:S(2)}) collective-permute-start(bf16[2,128,1024]{2,1,0:T(8,128)(2,1)S(1)} %pad_maximum_fusion), channel_id=1, source_target_pairs={{0,384},{128,0},{256,128},{384,256},{1,385},{129,1},{257,129},{385... | collective-permute-start | bytes 1572872 | tf_op jit(solution)/shard_map/weights/ppermute | solution.py:270
  41.0 3.3 %collective-permute-start.3 = (bf16[2,128,1024]{2,1,0:T(8,128)(2,1)S(1)}, bf16[2,128,1024]{2,1,0:T(8,128)(2,1)S(1)}, u32[]{:S(2)}, u32[]{:S(2)}) collective-permute-start(bf16[2,128,1024]{2,1,0:T(8,128)(2,1)S(1)} %pad_maximum_fusion), channel_id=1, source_target_pairs={{0,256},{128,384},{256,0},{384,128},{1,257},{129,385},{257,1},{385... | collective-permute-start | bytes 1572872 | tf_op jit(solution)/shard_map/weights/ppermute | solution.py:270
  44.4 1.0 constant_dynamic-update-slice_fusion.4
  45.4 0.0 copy-start.6
  45.4 6.6 %collective-permute-done.1 = bf16[2,128,1024]{2,1,0:T(8,128)(2,1)S(1)} collective-permute-done((bf16[2,128,1024]{2,1,0:T(8,128)(2,1)S(1)}, bf16[2,128,1024]{2,1,0:T(8,128)(2,1)S(1)}, u32[]{:S(2)}, u32[]{:S(2)}) %collective-permute-start.1) | collective-permute-done | bytes 524320 | tf_op jit(solution)/shard_map/weights/ppermute | solution.py:270
  52.0 12.9 %collective-permute-done.2 = bf16[2,128,1024]{2,1,0:T(8,128)(2,1)S(1)} collective-permute-done((bf16[2,128,1024]{2,1,0:T(8,128)(2,1)S(1)}, bf16[2,128,1024]{2,1,0:T(8,128)(2,1)S(1)}, u32[]{:S(2)}, u32[]{:S(2)}) %collective-permute-start.2) | collective-permute-done | bytes 524320 | tf_op jit(solution)/shard_map/weights/ppermute | solution.py:270
  64.9 0.0 collective-permute-done.3
  65.0 0.0 copy-start
  65.0 1.9 %collective-permute-start.4 = (bf16[8,128,1024]{2,1,0:T(8,128)(2,1)S(1)}, bf16[8,128,1024]{2,1,0:T(8,128)(2,1)}, u32[]{:S(2)}, u32[]{:S(2)}) collective-permute-start(bf16[8,128,1024]{2,1,0:T(8,128)(2,1)S(1)} %constant_dynamic-update-slice_fusion.own_ref), channel_id=1, source_target_pairs={{0,1},{1,0},{2,3},{3,2},{4,5},{5,4},{6,7},{7,6},{8,9},{9,8},{10,11... | collective-permute-start | bytes 6291464 | tf_op jit(solution)/shard_map/weights/ppermute | solution.py:272
  66.9 0.0 copy-done.5
  66.9 0.1 copy.12
  67.1 0.1 broadcast_compare_fusion
  67.2 1.4 fusion.6.bias_ref
  68.6 0.0 copy-done.6
  68.6 1.5 fusion.3.bias_ref
  70.0 1.1 collective-permute-done.4.other_ref
  71.2 0.0 copy-done
  71.2 8.2 %row_heads.1 = (bf16[256,1024]{1,0:T(8,128)(2,1)}, bf16[512,512]{1,0:T(8,128)(2,1)}, bf16[512,512]{1,0:T(8,128)(2,1)}, bf16[2,8,128,1024]{3,2,1,0:T(8,128)(2,1)}) custom-call(bf16[256,1024]{1,0:T(8,128)(2,1)} %bitcast.44, bf16[256,1024]{1,0:T(8,128)(2,1)} %bitcast.46, bf16[4,256,256]{2,1,0:T(8,128)(2,1)} %fusion.6.bias_ref, bf16[8,128,1024]{2,1,0:T(8,128)(2,1)} %copy-done, ...), custom_call_target="tpu_custom_call" | custom-call | flops 1400000000 | bytes 12000000 | tf_op jit(solution)/shard_map/row_heads/pallas_call | solution.py:275
  79.3 2.0 %collective-permute-start.5 = (bf16[512,512]{1,0:T(8,128)(2,1)}, bf16[512,512]{1,0:T(8,128)(2,1)S(1)}, u32[]{:S(2)}, u32[]{:S(2)}) collective-permute-start(bf16[512,512]{1,0:T(8,128)(2,1)} %get-tuple-element.17), channel_id=1, source_target_pairs={{0,1},{1,0},{2,3},{3,2},{4,5},{5,4},{6,7},{7,6},{8,9},{9,8},{10,11... | collective-permute-start | bytes 1572872 | tf_op jit(solution)/shard_map/gradient_sums/ppermute | solution.py:311
  81.4 0.0 all-to-all-done
  81.4 0.0 copy-start.2
  81.4 1.0 copy-done.2
  82.4 6.7 %column_heads.1 = (bf16[512,512]{1,0:T(8,128)(2,1)}, bf16[512,512]{1,0:T(8,128)(2,1)}, bf16[512,512]{1,0:T(8,128)(2,1)}) custom-call(bf16[512,1024]{1,0:T(8,128)(2,1)} %bitcast.47, bf16[4,256,256]{2,1,0:T(8,128)(2,1)} %fusion.3.bias_ref, bf16[2,8,128,1024]{3,2,1,0:T(8,128)(2,1)} %get-tuple-element.18.w_ref.weights), custom_call_target="tpu_custom_call" | custom-call | flops 1900000000 | bytes 8000000 | tf_op jit(solution)/shard_map/column_heads/pallas_call | solution.py:290
  89.1 0.0 copy-start.4
  89.1 12.7 %all-to-all-start.1 = ((bf16[64,8,512]{2,1,0:T(8,128)(2,1)}), bf16[64,8,512]{2,1,0:T(8,128)(2,1)S(1)}, u32[]{:S(2)}, u32[]{:S(2)}) async-start(bf16[64,8,512]{2,1,0:T(8,128)(2,1)} %bitcast.50), calls=%async_computation.1 | async-start | bytes 1048576 | tf_op jit(solution)/shard_map/from_columns/all_to_all | solution.py:306
  101.8 2.0 %collective-permute-start.6 = (bf16[512,512]{1,0:T(8,128)(2,1)}, bf16[512,512]{1,0:T(8,128)(2,1)S(1)}, u32[]{:S(2)}, u32[]{:S(2)}) collective-permute-start(bf16[512,512]{1,0:T(8,128)(2,1)} %get-tuple-element.20), channel_id=1, source_target_pairs={{0,1},{1,0},{2,3},{3,2},{4,5},{5,4},{6,7},{7,6},{8,9},{9,8},{10,11... | collective-permute-start | bytes 1572872 | tf_op jit(solution)/shard_map/gradient_sums/ppermute | solution.py:311
  103.8 0.0 collective-permute-done.5
  103.8 0.0 copy-done.3
  103.8 0.1 add_convert_fusion.1
  104.0 1.9 %collective-permute-done.6 = bf16[512,512]{1,0:T(8,128)(2,1)S(1)} collective-permute-done((bf16[512,512]{1,0:T(8,128)(2,1)}, bf16[512,512]{1,0:T(8,128)(2,1)S(1)}, u32[]{:S(2)}, u32[]{:S(2)}) %collective-permute-start.6) | collective-permute-done | bytes 524320 | tf_op jit(solution)/shard_map/gradient_sums/ppermute | solution.py:311
  105.8 0.0 copy-done.4
  105.8 0.1 add_convert_fusion
  106.0 0.1 fusion.9
  106.1 1.9 %collective-permute-start.7 = (bf16[128,1024]{1,0:T(8,128)(2,1)S(1)}, bf16[128,1024]{1,0:T(8,128)(2,1)S(1)}, u32[]{:S(2)}, u32[]{:S(2)}) collective-permute-start(bf16[128,1024]{1,0:T(8,128)(2,1)S(1)} %get-tuple-element.26), channel_id=1, source_target_pairs={{0,128},{128,256},{256,384},{384,0},{1,129},{129,257},{257,385},{3... | collective-permute-start | bytes 786440 | tf_op jit(solution)/shard_map/gradient_sums/ppermute | solution.py:321
  108.0 3.9 %collective-permute-start.8 = (bf16[128,1024]{1,0:T(8,128)(2,1)S(1)}, bf16[128,1024]{1,0:T(8,128)(2,1)S(1)}, u32[]{:S(2)}, u32[]{:S(2)}) collective-permute-start(bf16[128,1024]{1,0:T(8,128)(2,1)S(1)} %get-tuple-element.27), channel_id=1, source_target_pairs={{0,384},{128,0},{256,128},{384,256},{1,385},{129,1},{257,129},{385... | collective-permute-start | bytes 786440 | tf_op jit(solution)/shard_map/gradient_sums/ppermute | solution.py:321
  112.0 3.9 %collective-permute-start.9 = (bf16[128,1024]{1,0:T(8,128)(2,1)S(1)}, bf16[128,1024]{1,0:T(8,128)(2,1)S(1)}, u32[]{:S(2)}, u32[]{:S(2)}) collective-permute-start(bf16[128,1024]{1,0:T(8,128)(2,1)S(1)} %get-tuple-element.28), channel_id=1, source_target_pairs={{0,256},{128,384},{256,0},{384,128},{1,257},{129,385},{257,1},{385... | collective-permute-start | bytes 786440 | tf_op jit(solution)/shard_map/gradient_sums/ppermute | solution.py:321
  115.9 0.5 collective-permute-done.7
  116.3 4.0 %collective-permute-done.8 = bf16[128,1024]{1,0:T(8,128)(2,1)S(1)} collective-permute-done((bf16[128,1024]{1,0:T(8,128)(2,1)S(1)}, bf16[128,1024]{1,0:T(8,128)(2,1)S(1)}, u32[]{:S(2)}, u32[]{:S(2)}) %collective-permute-start.8) | collective-permute-done | bytes 262176 | tf_op jit(solution)/shard_map/gradient_sums/ppermute | solution.py:321
  120.3 5.1 %collective-permute-done.9 = bf16[128,1024]{1,0:T(8,128)(2,1)S(1)} collective-permute-done((bf16[128,1024]{1,0:T(8,128)(2,1)S(1)}, bf16[128,1024]{1,0:T(8,128)(2,1)S(1)}, u32[]{:S(2)}, u32[]{:S(2)}) %collective-permute-start.9) | collective-permute-done | bytes 262176 | tf_op jit(solution)/shard_map/gradient_sums/ppermute | solution.py:321
  125.4 0.2 add_convert_fusion.2
  125.6 3.5 %collective-permute-start.10 = (bf16[32,1024]{1,0:T(8,128)(2,1)S(1)}, bf16[32,1024]{1,0:T(8,128)(2,1)S(1)}, u32[]{:S(2)}, u32[]{:S(2)}) collective-permute-start(bf16[32,1024]{1,0:T(8,128)(2,1)S(1)} %get-tuple-element.29), channel_id=1, source_target_pairs={{0,2},{2,0},{64,66},{66,64},{1,3},{3,1},{65,67},{67,65},{4,6},{6,4... | collective-permute-start | bytes 196616 | tf_op jit(solution)/shard_map/gradient_sums/ppermute | solution.py:328
  129.1 5.7 %collective-permute-start.11 = (bf16[32,1024]{1,0:T(8,128)(2,1)S(1)}, bf16[32,1024]{1,0:T(8,128)(2,1)S(1)}, u32[]{:S(2)}, u32[]{:S(2)}) collective-permute-start(bf16[32,1024]{1,0:T(8,128)(2,1)S(1)} %get-tuple-element.31), channel_id=1, source_target_pairs={{0,64},{2,66},{64,0},{66,2},{1,65},{3,67},{65,1},{67,3},{4,68},{6,... | collective-permute-start | bytes 196616 | tf_op jit(solution)/shard_map/gradient_sums/ppermute | solution.py:328
  134.8 1.9 %collective-permute-start.12 = (bf16[32,1024]{1,0:T(8,128)(2,1)S(1)}, bf16[32,1024]{1,0:T(8,128)(2,1)S(1)}, u32[]{:S(2)}, u32[]{:S(2)}) collective-permute-start(bf16[32,1024]{1,0:T(8,128)(2,1)S(1)} %get-tuple-element.30), channel_id=1, source_target_pairs={{0,66},{2,64},{64,2},{66,0},{1,67},{3,65},{65,3},{67,1},{4,70},{6,... | collective-permute-start | bytes 196616 | tf_op jit(solution)/shard_map/gradient_sums/ppermute | solution.py:328
  136.7 0.0 collective-permute-done.10
  136.8 0.3 collective-permute-done.11
  137.0 5.1 %collective-permute-done.12 = bf16[32,1024]{1,0:T(8,128)(2,1)S(1)} collective-permute-done((bf16[32,1024]{1,0:T(8,128)(2,1)S(1)}, bf16[32,1024]{1,0:T(8,128)(2,1)S(1)}, u32[]{:S(2)}, u32[]{:S(2)}) %collective-permute-start.12) | collective-permute-done | bytes 65568 | tf_op jit(solution)/shard_map/gradient_sums/ppermute | solution.py:328
  142.2 0.0 all-to-all-done.1
  142.2 0.0 copy-start.1
  142.2 0.8 reshape.144
  143.1 11.7 %all-to-all-start.2 = ((f32[16,2,1024]{2,1,0:T(2,128)}), f32[16,2,1024]{2,1,0:T(2,128)S(1)}, u32[]{:S(2)}, u32[]{:S(2)}) async-start(f32[16,2,1024]{2,1,0:T(2,128)} %reshape.144), calls=%async_computation.2 | async-start | bytes 262144 | tf_op jit(solution)/shard_map/gradient_sums/all_to_all | solution.py:335
  154.7 0.0 copy-done.1
  154.7 4.6 %output_products.1 = (bf16[256,1024]{1,0:T(8,128)(2,1)}, bf16[256,1024]{1,0:T(8,128)(2,1)}) custom-call(bf16[256,1024]{1,0:T(8,128)(2,1)} %get-tuple-element.15.row_ref, bf16[512,512]{1,0:T(8,128)(2,1)} %bitcast.42, bf16[2,8,128,1024]{3,2,1,0:T(8,128)(2,1)} %get-tuple-element.18.w_ref.weights), custom_call_target="tpu_custom_call" | custom-call | flops 1200000000 | bytes 8000000 | tf_op jit(solution)/shard_map/output_products/pallas_call | solution.py:343
  159.3 8.6 %all-to-all-done.2 = f32[16,2,1024]{2,1,0:T(2,128)S(1)} async-done(((f32[16,2,1024]{2,1,0:T(2,128)}), f32[16,2,1024]{2,1,0:T(2,128)S(1)}, u32[]{:S(2)}, u32[]{:S(2)}) %all-to-all-start.2) | async-done | bytes 131104 | tf_op jit(solution)/shard_map/gradient_sums/all_to_all | solution.py:335
  168.0 0.1 reduce_sum.9
  168.0 0.6 maximum_bitcast_fusion
  168.6 0.6 pad_maximum_fusion.1
  (13 shorter events, 0.2 us)
Async XLA Ops:
  3.6 77.8 %all-to-all-start = ((bf16[64,8,1024]{2,1,0:T(8,128)(2,1)}), bf16[64,8,1024]{2,1,0:T(8,128)(2,1)S(1)}, u32[]{:S(2)}, u32[]{:S(2)}) async-start(bf16[64,8,1024]{2,1,0:T(8,128)(2,1)} %bitcast.41), calls=%async_computation | async-start | bytes 2097152 | tf_op jit(solution)/shard_map/to_columns/all_to_all | solution.py:262
  22.4 11.7 %collective-permute-start = (bf16[128,1024]{1,0:T(8,128)(2,1)}, bf16[128,1024]{1,0:T(8,128)(2,1)S(1)}, u32[]{:S(2)}, u32[]{:S(2)}) collective-permute-start(bf16[128,1024]{1,0:T(8,128)(2,1)} %pack.1), channel_id=1, source_target_pairs={{0,66},{2,64},{64,2},{66,0},{1,67},{3,65},{65,3},{67,1},{4,70},{6,... | collective-permute-start | bytes 786440 | tf_op jit(solution)/shard_map/weights/ppermute | solution.py:266
  35.2 31.7 %copy-start.5 = (s32[4,1,2,2]{0,3,2,1:T(2,128)S(1)}, s32[4,1,2,2]{0,3,2,1:T(2,128)}, u32[]{:S(2)}) copy-start(s32[4,1,2,2]{0,3,2,1:T(2,128)} %param.10) | copy-start | bytes 196
  35.2 16.8 %collective-permute-start.1 = (bf16[2,128,1024]{2,1,0:T(8,128)(2,1)S(1)}, bf16[2,128,1024]{2,1,0:T(8,128)(2,1)S(1)}, u32[]{:S(2)}, u32[]{:S(2)}) collective-permute-start(bf16[2,128,1024]{2,1,0:T(8,128)(2,1)S(1)} %pad_maximum_fusion), channel_id=1, source_target_pairs={{0,128},{128,256},{256,384},{384,0},{1,129},{129,257},{257,385},{3... | collective-permute-start | bytes 1572872 | tf_op jit(solution)/shard_map/weights/ppermute | solution.py:270
  37.6 27.3 %collective-permute-start.2 = (bf16[2,128,1024]{2,1,0:T(8,128)(2,1)S(1)}, bf16[2,128,1024]{2,1,0:T(8,128)(2,1)S(1)}, u32[]{:S(2)}, u32[]{:S(2)}) collective-permute-start(bf16[2,128,1024]{2,1,0:T(8,128)(2,1)S(1)} %pad_maximum_fusion), channel_id=1, source_target_pairs={{0,384},{128,0},{256,128},{384,256},{1,385},{129,1},{257,129},{385... | collective-permute-start | bytes 1572872 | tf_op jit(solution)/shard_map/weights/ppermute | solution.py:270
  41.0 23.9 %collective-permute-start.3 = (bf16[2,128,1024]{2,1,0:T(8,128)(2,1)S(1)}, bf16[2,128,1024]{2,1,0:T(8,128)(2,1)S(1)}, u32[]{:S(2)}, u32[]{:S(2)}) collective-permute-start(bf16[2,128,1024]{2,1,0:T(8,128)(2,1)S(1)} %pad_maximum_fusion), channel_id=1, source_target_pairs={{0,256},{128,384},{256,0},{384,128},{1,257},{129,385},{257,1},{385... | collective-permute-start | bytes 1572872 | tf_op jit(solution)/shard_map/weights/ppermute | solution.py:270
  45.4 23.2 %copy-start.6 = (s32[4,4,8,8]{3,2,1,0:T(8,128)S(1)}, s32[4,4,8,8]{3,2,1,0:T(8,128)}, u32[]{:S(2)}) copy-start(s32[4,4,8,8]{3,2,1,0:T(8,128)} %param.11) | copy-start | bytes 12292
  65.0 6.2 %copy-start = (bf16[8,128,1024]{2,1,0:T(8,128)(2,1)}, bf16[8,128,1024]{2,1,0:T(8,128)(2,1)S(1)}, u32[]{:S(2)}) copy-start(bf16[8,128,1024]{2,1,0:T(8,128)(2,1)S(1)} %constant_dynamic-update-slice_fusion.own_ref) | copy-start | bytes 6291460
  65.0 6.2 %collective-permute-start.4 = (bf16[8,128,1024]{2,1,0:T(8,128)(2,1)S(1)}, bf16[8,128,1024]{2,1,0:T(8,128)(2,1)}, u32[]{:S(2)}, u32[]{:S(2)}) collective-permute-start(bf16[8,128,1024]{2,1,0:T(8,128)(2,1)S(1)} %constant_dynamic-update-slice_fusion.own_ref), channel_id=1, source_target_pairs={{0,1},{1,0},{2,3},{3,2},{4,5},{5,4},{6,7},{7,6},{8,9},{9,8},{10,11... | collective-permute-start | bytes 6291464 | tf_op jit(solution)/shard_map/weights/ppermute | solution.py:272
  79.3 24.5 %collective-permute-start.5 = (bf16[512,512]{1,0:T(8,128)(2,1)}, bf16[512,512]{1,0:T(8,128)(2,1)S(1)}, u32[]{:S(2)}, u32[]{:S(2)}) collective-permute-start(bf16[512,512]{1,0:T(8,128)(2,1)} %get-tuple-element.17), channel_id=1, source_target_pairs={{0,1},{1,0},{2,3},{3,2},{4,5},{5,4},{6,7},{7,6},{8,9},{9,8},{10,11... | collective-permute-start | bytes 1572872 | tf_op jit(solution)/shard_map/gradient_sums/ppermute | solution.py:311
  81.4 1.0 copy-start.2
  82.4 21.4 %copy-start.3 = (bf16[512,512]{1,0:T(8,128)(2,1)S(1)}, bf16[512,512]{1,0:T(8,128)(2,1)}, u32[]{:S(2)}) copy-start(bf16[512,512]{1,0:T(8,128)(2,1)} %get-tuple-element.16) | copy-start | bytes 1572868
  89.1 16.7 %copy-start.4 = (bf16[512,512]{1,0:T(8,128)(2,1)S(1)}, bf16[512,512]{1,0:T(8,128)(2,1)}, u32[]{:S(2)}) copy-start(bf16[512,512]{1,0:T(8,128)(2,1)} %get-tuple-element.19) | copy-start | bytes 1572868
  89.1 53.1 %all-to-all-start.1 = ((bf16[64,8,512]{2,1,0:T(8,128)(2,1)}), bf16[64,8,512]{2,1,0:T(8,128)(2,1)S(1)}, u32[]{:S(2)}, u32[]{:S(2)}) async-start(bf16[64,8,512]{2,1,0:T(8,128)(2,1)} %bitcast.50), calls=%async_computation.1 | async-start | bytes 1048576 | tf_op jit(solution)/shard_map/from_columns/all_to_all | solution.py:306
  101.8 4.0 %collective-permute-start.6 = (bf16[512,512]{1,0:T(8,128)(2,1)}, bf16[512,512]{1,0:T(8,128)(2,1)S(1)}, u32[]{:S(2)}, u32[]{:S(2)}) collective-permute-start(bf16[512,512]{1,0:T(8,128)(2,1)} %get-tuple-element.20), channel_id=1, source_target_pairs={{0,1},{1,0},{2,3},{3,2},{4,5},{5,4},{6,7},{7,6},{8,9},{9,8},{10,11... | collective-permute-start | bytes 1572872 | tf_op jit(solution)/shard_map/gradient_sums/ppermute | solution.py:311
  106.1 10.2 %collective-permute-start.7 = (bf16[128,1024]{1,0:T(8,128)(2,1)S(1)}, bf16[128,1024]{1,0:T(8,128)(2,1)S(1)}, u32[]{:S(2)}, u32[]{:S(2)}) collective-permute-start(bf16[128,1024]{1,0:T(8,128)(2,1)S(1)} %get-tuple-element.26), channel_id=1, source_target_pairs={{0,128},{128,256},{256,384},{384,0},{1,129},{129,257},{257,385},{3... | collective-permute-start | bytes 786440 | tf_op jit(solution)/shard_map/gradient_sums/ppermute | solution.py:321
  108.0 12.3 %collective-permute-start.8 = (bf16[128,1024]{1,0:T(8,128)(2,1)S(1)}, bf16[128,1024]{1,0:T(8,128)(2,1)S(1)}, u32[]{:S(2)}, u32[]{:S(2)}) collective-permute-start(bf16[128,1024]{1,0:T(8,128)(2,1)S(1)} %get-tuple-element.27), channel_id=1, source_target_pairs={{0,384},{128,0},{256,128},{384,256},{1,385},{129,1},{257,129},{385... | collective-permute-start | bytes 786440 | tf_op jit(solution)/shard_map/gradient_sums/ppermute | solution.py:321
  112.0 13.4 %collective-permute-start.9 = (bf16[128,1024]{1,0:T(8,128)(2,1)S(1)}, bf16[128,1024]{1,0:T(8,128)(2,1)S(1)}, u32[]{:S(2)}, u32[]{:S(2)}) collective-permute-start(bf16[128,1024]{1,0:T(8,128)(2,1)S(1)} %get-tuple-element.28), channel_id=1, source_target_pairs={{0,256},{128,384},{256,0},{384,128},{1,257},{129,385},{257,1},{385... | collective-permute-start | bytes 786440 | tf_op jit(solution)/shard_map/gradient_sums/ppermute | solution.py:321
  125.6 11.2 %collective-permute-start.10 = (bf16[32,1024]{1,0:T(8,128)(2,1)S(1)}, bf16[32,1024]{1,0:T(8,128)(2,1)S(1)}, u32[]{:S(2)}, u32[]{:S(2)}) collective-permute-start(bf16[32,1024]{1,0:T(8,128)(2,1)S(1)} %get-tuple-element.29), channel_id=1, source_target_pairs={{0,2},{2,0},{64,66},{66,64},{1,3},{3,1},{65,67},{67,65},{4,6},{6,4... | collective-permute-start | bytes 196616 | tf_op jit(solution)/shard_map/gradient_sums/ppermute | solution.py:328
  129.1 8.0 %collective-permute-start.11 = (bf16[32,1024]{1,0:T(8,128)(2,1)S(1)}, bf16[32,1024]{1,0:T(8,128)(2,1)S(1)}, u32[]{:S(2)}, u32[]{:S(2)}) collective-permute-start(bf16[32,1024]{1,0:T(8,128)(2,1)S(1)} %get-tuple-element.31), channel_id=1, source_target_pairs={{0,64},{2,66},{64,0},{66,2},{1,65},{3,67},{65,1},{67,3},{4,68},{6,... | collective-permute-start | bytes 196616 | tf_op jit(solution)/shard_map/gradient_sums/ppermute | solution.py:328
  134.8 7.4 %collective-permute-start.12 = (bf16[32,1024]{1,0:T(8,128)(2,1)S(1)}, bf16[32,1024]{1,0:T(8,128)(2,1)S(1)}, u32[]{:S(2)}, u32[]{:S(2)}) collective-permute-start(bf16[32,1024]{1,0:T(8,128)(2,1)S(1)} %get-tuple-element.30), channel_id=1, source_target_pairs={{0,66},{2,64},{64,2},{66,0},{1,67},{3,65},{65,3},{67,1},{4,70},{6,... | collective-permute-start | bytes 196616 | tf_op jit(solution)/shard_map/gradient_sums/ppermute | solution.py:328
  142.2 12.5 %copy-start.1 = (bf16[64,8,512]{2,1,0:T(8,128)(2,1)}, bf16[64,8,512]{2,1,0:T(8,128)(2,1)S(1)}, u32[]{:S(2)}) copy-start(bf16[64,8,512]{2,1,0:T(8,128)(2,1)S(1)} %all-to-all-done.1) | copy-start | bytes 1572868
  143.1 24.9 %all-to-all-start.2 = ((f32[16,2,1024]{2,1,0:T(2,128)}), f32[16,2,1024]{2,1,0:T(2,128)S(1)}, u32[]{:S(2)}, u32[]{:S(2)}) async-start(f32[16,2,1024]{2,1,0:T(2,128)} %reshape.144), calls=%async_computation.2 | async-start | bytes 262144 | tf_op jit(solution)/shard_map/gradient_sums/all_to_all | solution.py:335

commit v5 on v4

--- a/solution.py
+++ b/solution.py
@@ -16,10 +16,15 @@
 FIRST = (((0,), (0,)), ((), ()))
 MASKED = -1e30
 VMEM = pl.BlockSpec(memory_space=pltpu.VMEM)
-ANYWHERE = pl.BlockSpec(memory_space=pl.ANY)
-PARAMS = pltpu.CompilerParams(vmem_limit_bytes=60 * 1024 * 1024)
-STEPS = (0, 1, 3, 2)
+HBM = pl.BlockSpec(memory_space=pltpu.HBM)
+
+
+def room(mebibytes):
+    return pltpu.CompilerParams(vmem_limit_bytes=mebibytes * 1024 * 1024)
+
+
 SWAP = [(0, 1), (1, 0)]
+PACK, PAIR, PICK = 1000000000, 30000000000, 10000000000
 
 
 def product(a, b, dims=(((1,), (0,)), ((), ()))):
@@ -61,8 +66,7 @@
     sent_ref[...] = interleave(x[...], ct[...])
 
 
-def pack_kernel(wq_ref, wk_ref, wv_ref, wo_ref, after_ref, packed_ref, sems):
-    del after_ref
+def pack_kernel(wq_ref, wk_ref, wv_ref, wo_ref, packed_ref, sems):
     core = lax.axis_index("c")
     here = pl.ds(pl.multiple_of(core * 256, 256), 256)
     pairs = []
@@ -72,6 +76,11 @@
         there = pl.ds(pl.multiple_of(core * 512 + b * 256, 256), 256)
         pairs.append((wo_ref.at[:, there], packed_ref.at[pl.ds(b * 64, 64), pl.ds(768, 256)]))
     wait_for(start_copies(pairs, sems))
+
+
+def pair_kernel(packed_ref, flipped_ref, pair_ref):
+    pair_ref[0] = packed_ref[...]
+    pair_ref[1] = flipped_ref[...]
 
 
 def attention(x, ct, weights, kind, bias_ref):
@@ -111,7 +120,7 @@
     )
     new = lax.broadcasted_iota(jnp.int32, (128, 128), 0)
     old = lax.broadcasted_iota(jnp.int32, (128, 128), 1)
-    source = ((new >> 1) & 15) * 8 + ((new >> 5) & 1) * 4 + ((new >> 6) ^ core) * 2 + (new & 1)
+    source = ((new >> 1) & 31) * 4 + ((new >> 6) ^ core) * 2 + (new & 1)
     order = (old == source).astype(F32).astype(BF)
     for block in range(8):
         moved = product(order, gradients[block * 128 : (block + 1) * 128]).astype(BF)
@@ -119,63 +128,96 @@
         send_ref[block * 64 : (block + 1) * 64, :] = moved[64:]
 
 
-def row_kernel(
-    x_ref,
-    ct_ref,
-    bias_ref,
-    own_ref,
-    other_ref,
-    parts_ref,
-    keep_ref,
-    send_ref,
-    w_ref,
-    x_here,
-    ct_here,
-    bias,
-    sems,
-):
+def weight_copies(refs, w_ref, sems, kinds):
+    core, across, high = (lax.axis_index(name) for name in ("c", "x", "yh"))
+    right = pl.ds(768, 256)
+    pairs, sides = [], ([], [])
+    for step in range(4):
+        for flip in range(2):
+            shard = ((across + 4 - step) & 3) * 2 + (high ^ flip)
+            for side, ref in enumerate((refs[step], refs[4 + step])):
+                half = core ^ side
+                if kinds == 2:
+                    pairs.append((ref.at[flip], w_ref.at[half, shard]))
+                else:
+                    pairs.append((ref.at[flip, :, right], w_ref.at[half, shard, :, right]))
+                    left = pl.ds(0, 768)
+                    sides[side].append((ref.at[flip, :, left], w_ref.at[half, shard, :, left]))
+    return pairs, sides
+
+
+def kind_copies(kind, refs, w_ref, sems, first):
+    pairs, sides = weight_copies(refs, w_ref, sems, 1)
     core = lax.axis_index("c")
-    pairs = []
-    across, high = lax.axis_index("x"), lax.axis_index("yh")
-    for index, step in enumerate(STEPS):
-        for flip in range(2):
-            source = ((across + 4 - step) & 3) * 2 + (high ^ flip)
-            for half, ref in ((core, own_ref), (1 - core, other_ref)):
-                pairs.append((ref.at[index * 2 + flip], w_ref.at[half, source]))
-    pairs += [(x_ref, x_here), (ct_ref, ct_here), (bias_ref, bias)]
-    wait_for(start_copies(pairs, sems))
+    for side in range(2):
+
+        @pl.when((core ^ side) == kind)
+        def _(side=side):
+            start_copies(sides[side], sems, first)
+
+    waits = [
+        pltpu.make_async_copy(source, target, sems.at[first + i])
+        for i, (source, target) in enumerate(sides[0])
+    ]
+    return waits + start_copies(pairs, sems, first + 8)
+
+
+def row_kernel(x_ref, ct_ref, bias_ref, *refs):
+    weights, (parts_ref, keep_ref, send_ref, x_here, ct_here, bias, w_ref, sems) = refs[:8], refs[8:]
+    copies = start_copies(((x_ref, x_here), (ct_ref, ct_here), (bias_ref, bias)), sems)
+    wait_for(kind_copies(0, weights, w_ref, sems, 3) + copies)
     x, ct = x_here[...], ct_here[...]
     out, dq, dk, dv = attention(x, ct, w_ref, 0, bias)
     for i, part in enumerate((out, dq, dk, dv)):
         parts_ref[:, i * 256 : (i + 1) * 256] = part
-    store_gradients(core, x, ct, out, dv, keep_ref, send_ref)
-
-
-def column_kernel(
-    both_ref, bias_ref, w_ref, parts_ref, keep_ref, send_ref, both, bias, weights, sems
-):
-    pairs = [(both_ref, both), (bias_ref, bias)]
-    mine, right = pl.ds(0, 768), pl.ds(768, 256)
-    pairs.append((w_ref.at[1, :, :, mine], weights.at[1, :, :, mine]))
-    for half in range(2):
-        wanted = (half, pl.ds(4, 4), slice(None), right)
-        pairs.append((w_ref.at[wanted], weights.at[wanted]))
-    copies = start_copies(pairs, sems)
-    wait_for(copies[:1])
-    x, ct = separate(both[...])
-    wait_for(copies[1:])
-    out, dq, dk, dv = attention(x, ct, weights, 1, bias)
+    store_gradients(lax.axis_index("c"), x, ct, out, dv, keep_ref, send_ref)
+
+
+def column_kernel(both_ref, bias_ref, *refs):
+    weights, (parts_ref, keep_ref, send_ref, bias, w_ref, sems) = refs[:8], refs[8:]
+    copies = kind_copies(1, weights, w_ref, sems, 1) + start_copies(((bias_ref, bias),), sems)
+    x, ct = separate(both_ref[...])
+    wait_for(copies)
+    out, dq, dk, dv = attention(x, ct, w_ref, 1, bias)
     parts_ref[...] = interleave(
         jnp.concatenate([out, dq], axis=1), jnp.concatenate([dk, dv], axis=1)
     )
     store_gradients(lax.axis_index("c"), x, ct, out, dv, keep_ref, send_ref)
 
 
-def final_kernel(row_ref, col_ref, weights, mixed_ref, gt_ref, row, col, w_ref, sems):
-    copies = start_copies(((col_ref, col), (row_ref, row), (weights, w_ref)), sems)
-    wait_for(copies[:2])
-    first, second = separate(col[...])
-    wait_for(copies[2:])
+def pick_kernel(row_keep, row_got, col_keep, col_got, *terms):
+    across = lax.axis_index("x")
+    for step, term in enumerate(terms):
+        rows = pl.ds(pl.multiple_of(((across + step) & 3) * 128, 128), 128)
+        for i, (keep, got) in enumerate(((row_keep, row_got), (col_keep, col_got))):
+            total = keep[rows, :].astype(F32) + got[rows, :].astype(F32)
+            term[:, i * 512 : (i + 1) * 512] = total.astype(BF)
+
+
+def line_kernel(*refs):
+    given, out_ref = refs[:4], refs[4]
+    total = sum(ref[...].astype(F32) for ref in given).astype(BF)
+    row = lax.broadcasted_iota(jnp.int32, (512, 128), 0)
+    col = lax.broadcasted_iota(jnp.int32, (512, 128), 1)
+    out = jnp.zeros((512, 256), F32)
+    for b in range(4):
+        here = (col == (row >> 3) * 2 + (row & 1)) & ((row & 6) == 2 * b)
+        out += product(here.astype(F32).astype(BF), total[:, b * 256 : (b + 1) * 256])
+    out_ref[...] = out.astype(BF)
+
+
+def last_kernel(line_ref, value_ref, out_ref):
+    total = jnp.sum(line_ref[...].astype(F32).reshape(64, 8, 256), axis=0)
+    for kind in range(2):
+        value_ref[:, kind * 256 : (kind + 1) * 256] = total[kind * 4 : kind * 4 + 2]
+        out_ref[:, kind * 256 : (kind + 1) * 256] = total[kind * 4 + 2 : kind * 4 + 4]
+
+
+def final_kernel(row_ref, col_ref, *refs):
+    weights, (mixed_ref, gt_ref, row, w_ref, sems) = refs[:8], refs[8:]
+    copies = start_copies(weight_copies(weights, w_ref, sems, 2)[0] + [(row_ref, row)], sems)
+    first, second = separate(col_ref[...])
+    wait_for(copies)
     sides = (
         (row[:, 0:256], row[:, 256:1024]),
         (first[:, 0:256], jnp.concatenate([first[:, 256:512], second], axis=1)),
@@ -233,7 +275,6 @@
 
 
 def body(tokens, cotangent, row_mask, column_mask, w_query, w_key, w_value, w_out):
-    across, high, low = (lax.axis_index(name) for name in ("x", "yh", "yl"))
     flat = tokens.reshape(256, 1024)
     cot_flat = cotangent.reshape(256, 1024)
     seq = ("z", "yl", "c")
@@ -241,120 +282,134 @@
     sent = pl.pallas_call(
         interleave_kernel,
         out_shape=shape(512, 1024),
-        in_specs=[ANYWHERE] * 2,
+        in_specs=[HBM] * 2,
         out_specs=VMEM,
         scratch_shapes=[buffer(256, 1024), buffer(256, 1024), pltpu.SemaphoreType.DMA((2,))],
-        compiler_params=PARAMS,
+        compiler_params=room(60),
         cost_estimate=cost(540000000, 2000000),
         name="interleave",
     )(flat, cot_flat)
     packed = pl.pallas_call(
         pack_kernel,
         out_shape=shape(128, 1024),
-        in_specs=[ANYWHERE] * 5,
+        in_specs=[HBM] * 4,
         out_specs=VMEM,
         scratch_shapes=[pltpu.SemaphoreType.DMA((5,))],
-        compiler_params=PARAMS,
-        cost_estimate=cost(90000000000, 2000000),
+        compiler_params=room(60),
+        cost_estimate=cost(PACK, 2000000),
         name="pack",
-    )(w_query, w_key, w_value, w_out, sent)
+    )(w_query, w_key, w_value, w_out)
     with jax.named_scope("to_columns"):
         both = lax.all_to_all(
             sent.reshape(64, 8, 1024), seq, split_axis=0, concat_axis=0, tiled=True
         ).reshape(512, 1024)
+    with jax.named_scope("masks"):
+        row_bias, col_bias = biases(row_mask, column_mask)
     with jax.named_scope("weights"):
         flipped = lax.ppermute(packed, ("yh", "yl"), [(y, 3 - y) for y in range(4)])
-        pair = jnp.stack([packed, flipped])
-        own = jnp.concatenate(
-            [pair]
-            + [lax.ppermute(pair, "x", [(x, (x + dx) % 4) for x in range(4)]) for dx in STEPS[1:]]
-        )
-        other = lax.ppermute(own, "c", SWAP)
-    with jax.named_scope("masks"):
-        row_bias, col_bias = biases(row_mask, column_mask)
-    row_parts, row_keep, row_send, weights = pl.pallas_call(
+        pair = pl.pallas_call(
+            pair_kernel,
+            out_shape=shape(2, 128, 1024),
+            in_specs=[VMEM] * 2,
+            out_specs=VMEM,
+            compiler_params=room(16),
+            cost_estimate=cost(PAIR, 1000000),
+            name="pair",
+        )(packed, flipped)
+        weights = [pair] + [
+            lax.ppermute(pair, "x", [(x, (x + step) % 4) for x in range(4)]) for step in (1, 2, 3)
+        ]
+        weights[3], row_bias, col_bias = lax.optimization_barrier((weights[3], row_bias, col_bias))
+        weights += [lax.ppermute(part, "c", SWAP) for part in weights]
+    row_parts, row_keep, row_send = pl.pallas_call(
         row_kernel,
-        out_shape=(shape(256, 1024), shape(512, 512), shape(512, 512), shape(2, 8, 128, 1024)),
-        in_specs=[ANYWHERE] * 5,
-        out_specs=(VMEM,) * 4,
+        out_shape=(shape(256, 1024), shape(512, 512), shape(512, 512)),
+        in_specs=[HBM] * 11,
+        out_specs=(VMEM,) * 3,
         scratch_shapes=[
             buffer(256, 1024),
             buffer(256, 1024),
             buffer(4, 256, 256),
-            pltpu.SemaphoreType.DMA((19,)),
+            buffer(2, 8, 128, 1024),
+            pltpu.SemaphoreType.DMA((27,)),
         ],
-        compiler_params=PARAMS,
+        compiler_params=room(58),
         cost_estimate=cost(1400000000, 12000000),
         name="row_heads",
-    )(flat, cot_flat, row_bias, own, other)
+    )(flat, cot_flat, row_bias, *weights)
+    row_got = lax.ppermute(row_send, "c", SWAP)
+    both, row_keep = lax.optimization_barrier((both, row_keep))
     col_parts, col_keep, col_send = pl.pallas_call(
         column_kernel,
         out_shape=(shape(512, 512),) * 3,
-        in_specs=[ANYWHERE] * 3,
+        in_specs=[VMEM] + [HBM] * 9,
         out_specs=(VMEM,) * 3,
         scratch_shapes=[
-            buffer(512, 1024),
             buffer(4, 256, 256),
             buffer(2, 8, 128, 1024),
-            pltpu.SemaphoreType.DMA((5,)),
+            pltpu.SemaphoreType.DMA((25,)),
         ],
-        compiler_params=PARAMS,
+        compiler_params=room(58),
         cost_estimate=cost(1900000000, 8000000),
         name="column_heads",
-    )(both, col_bias, weights)
+    )(both, col_bias, *weights)
+    col_got = lax.ppermute(col_send, "c", SWAP)
     with jax.named_scope("from_columns"):
         returned = lax.all_to_all(
             col_parts.reshape(64, 8, 512), seq, split_axis=0, concat_axis=0, tiled=True
         ).reshape(512, 512)
 
-    def core_sum(keep, send):
-        got = lax.ppermute(send, "c", SWAP)
-        return (keep.astype(F32) + got.astype(F32)).astype(BF)
-
-    def plane_sum(held):
-        def x_rows(step):
-            return lax.dynamic_slice_in_dim(held, ((across + step) & 3) * 128, 128, axis=0)
-
-        terms = [x_rows(0)]
-        for step in (1, 3, 2):
-            pairs = [(x, (x + step) % 4) for x in range(4)]
-            terms.append(lax.ppermute(x_rows(step), "x", pairs))
-        line = sum(term.astype(F32) for term in terms).astype(BF)
-        mine = high * 2 + low
-        terms = [lax.dynamic_slice_in_dim(line, mine * 32, 32, axis=0)]
-        for step in (1, 2, 3):
-            pairs = [(y, y ^ step) for y in range(4)]
-            rows = lax.dynamic_slice_in_dim(line, (mine ^ step) * 32, 32, axis=0)
-            terms.append(lax.ppermute(rows, ("yh", "yl"), pairs))
-        return sum(term.astype(F32) for term in terms)
-
     with jax.named_scope("gradient_sums"):
-        held = jnp.concatenate([core_sum(row_keep, row_send), core_sum(col_keep, col_send)], axis=1)
-        plane = plane_sum(held)
-        plane, returned = lax.optimization_barrier((plane, returned))
+        terms = pl.pallas_call(
+            pick_kernel,
+            out_shape=(shape(128, 1024),) * 4,
+            in_specs=[VMEM] * 4,
+            out_specs=(VMEM,) * 4,
+            compiler_params=room(16),
+            cost_estimate=cost(PICK, 3000000),
+            name="pick",
+        )(row_keep, row_got, col_keep, col_got)
+        moved = [
+            lax.ppermute(terms[step], "x", [(x, (x + step) % 4) for x in range(4)])
+            for step in (1, 2, 3)
+        ]
+        line = pl.pallas_call(
+            line_kernel,
+            out_shape=shape(512, 256),
+            in_specs=[VMEM] * 4,
+            out_specs=VMEM,
+            compiler_params=room(16),
+            cost_estimate=cost(10000000, 300000),
+            name="line",
+        )(terms[0], *moved)
+        line, returned = lax.optimization_barrier((line, returned))
         line = lax.all_to_all(
-            plane.reshape(16, 2, 1024), "z", split_axis=0, concat_axis=0, tiled=True
+            line.reshape(64, 8, 256), ("yh", "z", "yl"), split_axis=0, concat_axis=0, tiled=True
         )
-        line = jnp.sum(line, axis=0)
-        grad_value = jnp.concatenate([line[:, 0:256], line[:, 512:768]], axis=1)
-        grad_output = jnp.transpose(
-            jnp.concatenate([line[:, 256:512], line[:, 768:1024]], axis=1)
-        )
+        grad_value, grad_output = pl.pallas_call(
+            last_kernel,
+            out_shape=(jax.ShapeDtypeStruct((2, 512), F32),) * 2,
+            in_specs=[VMEM],
+            out_specs=(VMEM,) * 2,
+            compiler_params=room(16),
+            cost_estimate=cost(100000, 100000),
+            name="last",
+        )(line.reshape(512, 256))
+        grad_output = jnp.transpose(grad_output)
     mixed, grad_tokens = pl.pallas_call(
         final_kernel,
         out_shape=(shape(256, 1024), shape(256, 1024)),
-        in_specs=[ANYWHERE] * 3,
+        in_specs=[HBM, VMEM] + [HBM] * 8,
         out_specs=(VMEM, VMEM),
         scratch_shapes=[
             buffer(256, 1024),
-            buffer(512, 512),
             buffer(2, 8, 128, 1024),
-            pltpu.SemaphoreType.DMA((3,)),
+            pltpu.SemaphoreType.DMA((17,)),
         ],
-        compiler_params=PARAMS,
+        compiler_params=room(58),
         cost_estimate=cost(1200000000, 8000000),
         name="output_products",
-    )(row_parts, returned, weights)
+    )(row_parts, returned, *weights)
     return (
         mixed.reshape(tokens.shape),
         grad_tokens.reshape(tokens.shape),

time: 170 us -> 162 us (0.953)
  starting transfers between devices: 82.3 us -> 64 us
  waiting for transfers between devices: 52.8 us -> 63.3 us
  Pallas kernels: 24.1 us -> 27.2 us
  other arithmetic: 2.97 us -> 0.12 us
    all_to_all x1, waiting for transfers between devices: 0.01 us -> 11 us  [body(): lax.all_to_all(sent.reshape(64, 8, 1024), seq, split_axis=0, concat_axis=...]
    ppermute x12, waiting for transfers between devices: 37.4 us -> 28.6 us  [the longest x3 14.3 us: body(): lax.ppermute(pair, 'x', [(x, (x + step) % 4) for x in range(4)])]
    all_to_all x1, waiting for transfers between devices: 8.62 us -> 17.3 us  [body(): lax.all_to_all(line.reshape(64, 8, 256), ('yh', 'z', 'yl'), split_axis=0,...]
    all_to_all x1, starting transfers between devices: 12.7 us -> 4.78 us  [body(): lax.all_to_all(col_parts.reshape(64, 8, 512), seq, split_axis=0, concat_a...]
    ppermute x1, waiting for transfers between devices: 6.81 us -> 0.01 us  [body(): flipped = lax.ppermute(packed, ('yh', 'yl'), [(y, 3 - y) for y in range(4)])]
    all_to_all x1, waiting for transfers between devices: 0.01 us -> 6.41 us  [body(): lax.all_to_all(col_parts.reshape(64, 8, 512), seq, split_axis=0, concat_a...]
    ppermute x12, starting transfers between devices: 35.9 us -> 30.7 us  [the longest x3 9.24 us: body(): lax.ppermute(pair, 'x', [(x, (x + step) % 4) for x in range(4)])]
    all_to_all x1, starting transfers between devices: 11.7 us -> 7.17 us  [body(): lax.all_to_all(line.reshape(64, 8, 256), ('yh', 'z', 'yl'), split_axis=0,...]
  transfers between devices with their start and end apart: 16 -> 16, of which waited for: 11 -> 9; matrix products, arithmetic and copies ran while one was open for 3% -> 2% of each run, Pallas kernels for 12% -> 10%
where the time goes in v5:
time: 162 us; the launch traced here: 160 us
  starting transfers between devices  64 us (40%)
  waiting for transfers between devices  63.3 us (39%)
  Pallas kernels  27.2 us (17%)
  matrix products  2.82 us (2%)
    all_to_all x1, waiting for transfers between devices, body(): lax.all_to_all(line.reshape(64, 8, 256), ('yh', 'z', 'yl'), split_axis=0,...  17.3 us
    all_to_all x1, starting transfers between devices, body(): lax.all_to_all(sent.reshape(64, 8, 1024), seq, split_axis=0, concat_axis=...  16.5 us
    ppermute x3, waiting for transfers between devices, body(): lax.ppermute(pair, 'x', [(x, (x + step) % 4) for x in range(4)])  14.3 us
    ppermute x3, waiting for transfers between devices, body(): lax.ppermute(terms[step], 'x', [(x, (x + step) % 4) for x in range(4)])  11 us
    all_to_all x1, waiting for transfers between devices, body(): lax.all_to_all(sent.reshape(64, 8, 1024), seq, split_axis=0, concat_axis=...  11 us
    ppermute x3, starting transfers between devices, body(): lax.ppermute(pair, 'x', [(x, (x + step) % 4) for x in range(4)])  9.24 us
    ppermute x3, starting transfers between devices, body(): lax.ppermute(terms[step], 'x', [(x, (x + step) % 4) for x in range(4)])  8.65 us
    ppermute x4, starting transfers between devices, body(): weights += [lax.ppermute(part, 'c', SWAP) for part in weights]  8.26 us
  transfers between devices with their start and end apart: 16, of which 9 were waited for; matrix products, arithmetic and copies ran while one was open for 2% of the time, Pallas kernels for 10%

profile of v5, /device:TPU:6, one launch (start us, length us, event | category | flops | bytes accessed | tf_op | source)
XLA Modules:
  0.0 160.0 jit_solution(14959726899332074581)
XLA Ops:
  0.6 1.7 %pack.1.packed_ref = bf16[128,1024]{1,0:T(8,128)(2,1)} custom-call(bf16[128,512]{1,0:T(8,128)(2,1)} %wq_ref.1, bf16[128,512]{1,0:T(8,128)(2,1)} %wk_ref.1, bf16[128,512]{1,0:T(8,128)(2,1)} %wv_ref.1, bf16[64,1024]{1,0:T(8,128)(2,1)} %wo_ref.1), custom_call_target="tpu_custom_call" | custom-call | flops 1000000000 | bytes 2000000 | tf_op jit(solution)/shard_map/pack/pallas_call | solution.py:292
  2.3 4.9 %collective-permute-start = (bf16[128,1024]{1,0:T(8,128)(2,1)}, bf16[128,1024]{1,0:T(8,128)(2,1)S(1)}, u32[]{:S(2)}, u32[]{:S(2)}) collective-permute-start(bf16[128,1024]{1,0:T(8,128)(2,1)} %pack.1.packed_ref), channel_id=1, source_target_pairs={{0,66},{2,64},{64,2},{66,0},{1,67},{3,65},{65,3},{67,1},{4,70},{6,... | collective-permute-start | bytes 786440 | tf_op jit(solution)/shard_map/weights/ppermute | solution.py:309
  7.2 2.9 %interleave.1 = bf16[512,1024]{1,0:T(8,128)(2,1)} custom-call(bf16[256,1024]{1,0:T(8,128)(2,1)} %bitcast.41, bf16[256,1024]{1,0:T(8,128)(2,1)} %bitcast.43), custom_call_target="tpu_custom_call" | custom-call | flops 540000000 | bytes 2000000 | tf_op jit(solution)/shard_map/interleave/pallas_call | solution.py:282
  10.1 0.0 copy-start.2
  10.2 16.5 %all-to-all-start = ((bf16[64,8,1024]{2,1,0:T(8,128)(2,1)}), bf16[64,8,1024]{2,1,0:T(8,128)(2,1)}, u32[]{:S(2)}, u32[]{:S(2)}) async-start(bf16[64,8,1024]{2,1,0:T(8,128)(2,1)} %bitcast.39), calls=%async_computation | async-start | bytes 2097152 | tf_op jit(solution)/shard_map/to_columns/all_to_all | solution.py:303
  26.7 0.0 copy-start.12
  26.7 0.1 iota_compare_fusion
  26.8 0.6 copy-done.12
  27.4 0.0 collective-permute-done.flipped_ref
  27.4 0.0 copy-done.2
  27.4 0.0 copy-start
  27.5 3.3 %collective-permute-start.3 = (bf16[2,128,1024]{2,1,0:T(8,128)(2,1)S(1)}, bf16[2,128,1024]{2,1,0:T(8,128)(2,1)S(1)}, u32[]{:S(2)}, u32[]{:S(2)}) collective-permute-start(bf16[2,128,1024]{2,1,0:T(8,128)(2,1)S(1)} %pair.1.refs_0_), channel_id=1, source_target_pairs={{0,256},{128,384},{256,0},{384,128},{1,257},{129,385},{257,1},{385... | collective-permute-start | bytes 1572872 | tf_op jit(solution)/shard_map/weights/ppermute | solution.py:320
  30.8 4.0 %collective-permute-start.2 = (bf16[2,128,1024]{2,1,0:T(8,128)(2,1)S(1)}, bf16[2,128,1024]{2,1,0:T(8,128)(2,1)S(1)}, u32[]{:S(2)}, u32[]{:S(2)}) collective-permute-start(bf16[2,128,1024]{2,1,0:T(8,128)(2,1)S(1)} %pair.1.refs_0_), channel_id=1, source_target_pairs={{0,128},{128,256},{256,384},{384,0},{1,129},{129,257},{257,385},{3... | collective-permute-start | bytes 1572872 | tf_op jit(solution)/shard_map/weights/ppermute | solution.py:320
  34.8 1.9 %collective-permute-start.1 = (bf16[2,128,1024]{2,1,0:T(8,128)(2,1)S(1)}, bf16[2,128,1024]{2,1,0:T(8,128)(2,1)S(1)}, u32[]{:S(2)}, u32[]{:S(2)}) collective-permute-start(bf16[2,128,1024]{2,1,0:T(8,128)(2,1)S(1)} %pair.1.refs_0_), channel_id=1, source_target_pairs={{0,384},{128,0},{256,128},{384,256},{1,385},{129,1},{257,129},{385... | collective-permute-start | bytes 1572872 | tf_op jit(solution)/shard_map/weights/ppermute | solution.py:320
  36.7 0.1 copy.12
  36.8 1.4 fusion.6.bias_ref
  38.2 0.0 copy-done.14
  38.2 1.4 fusion.3.bias_ref
  39.7 0.0 copy-done
  39.7 1.9 %collective-permute-start.4 = (bf16[2,128,1024]{2,1,0:T(8,128)(2,1)S(1)}, bf16[2,128,1024]{2,1,0:T(8,128)(2,1)S(1)}, u32[]{:S(2)}, u32[]{:S(2)}) collective-permute-start(bf16[2,128,1024]{2,1,0:T(8,128)(2,1)S(1)} %pair.1.refs_0_), channel_id=1, source_target_pairs={{0,1},{1,0},{2,3},{3,2},{4,5},{5,4},{6,7},{7,6},{8,9},{9,8},{10,11... | collective-permute-start | bytes 1572872 | tf_op jit(solution)/shard_map/weights/ppermute | solution.py:323
  41.6 14.3 %collective-permute-done.1.refs_3_ = bf16[2,128,1024]{2,1,0:T(8,128)(2,1)S(1)} collective-permute-done((bf16[2,128,1024]{2,1,0:T(8,128)(2,1)S(1)}, bf16[2,128,1024]{2,1,0:T(8,128)(2,1)S(1)}, u32[]{:S(2)}, u32[]{:S(2)}) %collective-permute-start.1) | collective-permute-done | bytes 524320 | tf_op jit(solution)/shard_map/weights/ppermute | solution.py:320
  55.9 0.0 collective-permute-done.3.refs_2_
  55.9 2.0 %collective-permute-start.6 = (bf16[2,128,1024]{2,1,0:T(8,128)(2,1)S(1)}, bf16[2,128,1024]{2,1,0:T(8,128)(2,1)S(1)}, u32[]{:S(2)}, u32[]{:S(2)}) collective-permute-start(bf16[2,128,1024]{2,1,0:T(8,128)(2,1)S(1)} %collective-permute-done.3.refs_2_), channel_id=1, source_target_pairs={{0,1},{1,0},{2,3},{3,2},{4,5},{5,4},{6,7},{7,6},{8,9},{9,8},{10,11... | collective-permute-start | bytes 1572872 | tf_op jit(solution)/shard_map/weights/ppermute | solution.py:323
  57.9 0.0 collective-permute-done.2.refs_1_
  57.9 0.0 copy-start.6
  58.0 2.3 %collective-permute-start.5 = (bf16[2,128,1024]{2,1,0:T(8,128)(2,1)S(1)}, bf16[2,128,1024]{2,1,0:T(8,128)(2,1)S(1)}, u32[]{:S(2)}, u32[]{:S(2)}) collective-permute-start(bf16[2,128,1024]{2,1,0:T(8,128)(2,1)S(1)} %collective-permute-done.2.refs_1_), channel_id=1, source_target_pairs={{0,1},{1,0},{2,3},{3,2},{4,5},{5,4},{6,7},{7,6},{8,9},{9,8},{10,11... | collective-permute-start | bytes 1572872 | tf_op jit(solution)/shard_map/weights/ppermute | solution.py:323
  60.3 2.0 %collective-permute-start.7 = (bf16[2,128,1024]{2,1,0:T(8,128)(2,1)S(1)}, bf16[2,128,1024]{2,1,0:T(8,128)(2,1)S(1)}, u32[]{:S(2)}, u32[]{:S(2)}) collective-permute-start(bf16[2,128,1024]{2,1,0:T(8,128)(2,1)S(1)} %collective-permute-done.1.refs_3_), channel_id=1, source_target_pairs={{0,1},{1,0},{2,3},{3,2},{4,5},{5,4},{6,7},{7,6},{8,9},{9,8},{10,11... | collective-permute-start | bytes 1572872 | tf_op jit(solution)/shard_map/weights/ppermute | solution.py:323
  62.3 0.0 collective-permute-done.4.refs_4_
  62.3 0.0 copy-start.8
  62.3 0.0 collective-permute-done.6.refs_6_
  62.3 0.0 copy-start.9
  62.3 0.0 collective-permute-done.5.refs_5_
  62.3 0.0 copy-start.10
  62.4 1.7 %collective-permute-done.7.refs_7_ = bf16[2,128,1024]{2,1,0:T(8,128)(2,1)S(1)} collective-permute-done((bf16[2,128,1024]{2,1,0:T(8,128)(2,1)S(1)}, bf16[2,128,1024]{2,1,0:T(8,128)(2,1)S(1)}, u32[]{:S(2)}, u32[]{:S(2)}) %collective-permute-start.7) | collective-permute-done | bytes 524320 | tf_op jit(solution)/shard_map/weights/ppermute | solution.py:323
  64.1 0.0 copy-done.7
  64.1 0.0 copy-done.5
  64.1 0.0 copy-done.6
  64.1 0.0 copy-done.8
  64.1 0.0 copy-done.9
  64.1 0.0 copy-done.10
  64.1 0.8 copy-done.11
  64.9 6.7 %row_heads.1 = (bf16[256,1024]{1,0:T(8,128)(2,1)}, bf16[512,512]{1,0:T(8,128)(2,1)}, bf16[512,512]{1,0:T(8,128)(2,1)}) custom-call(bf16[256,1024]{1,0:T(8,128)(2,1)} %bitcast.42, bf16[256,1024]{1,0:T(8,128)(2,1)} %bitcast.44, bf16[4,256,256]{2,1,0:T(8,128)(2,1)} %fusion.6.bias_ref, bf16[2,128,1024]{2,1,0:T(8,128)(2,1)} %copy-done, ...), custom_call_target="tpu_custom_call" | custom-call | flops 1400000000 | bytes 12000000 | tf_op jit(solution)/shard_map/row_heads/pallas_call | solution.py:324
  71.6 11.0 %all-to-all-done = bf16[64,8,1024]{2,1,0:T(8,128)(2,1)} async-done(((bf16[64,8,1024]{2,1,0:T(8,128)(2,1)}), bf16[64,8,1024]{2,1,0:T(8,128)(2,1)}, u32[]{:S(2)}, u32[]{:S(2)}) %all-to-all-start) | async-done | bytes 1048608 | tf_op jit(solution)/shard_map/to_columns/all_to_all | solution.py:303
  82.7 8.1 %column_heads.1 = (bf16[512,512]{1,0:T(8,128)(2,1)}, bf16[512,512]{1,0:T(8,128)(2,1)}, bf16[512,512]{1,0:T(8,128)(2,1)}) custom-call(bf16[512,1024]{1,0:T(8,128)(2,1)} %bitcast.11.both_ref, bf16[4,256,256]{2,1,0:T(8,128)(2,1)} %fusion.3.bias_ref, bf16[2,128,1024]{2,1,0:T(8,128)(2,1)} %copy-done, bf16[2,128,1024]{2,1,0:T(8,128)(2,1)} %copy-done.6, ...), custom_call_target="tpu_custom_call" | custom-call | flops 1900000000 | bytes 8000000 | tf_op jit(solution)/shard_map/column_heads/pallas_call | solution.py:342
  90.8 0.0 copy-start.1
  90.8 4.8 %all-to-all-start.1 = ((bf16[64,8,512]{2,1,0:T(8,128)(2,1)}), bf16[64,8,512]{2,1,0:T(8,128)(2,1)S(1)}, u32[]{:S(2)}, u32[]{:S(2)}) async-start(bf16[64,8,512]{2,1,0:T(8,128)(2,1)} %bitcast.45), calls=%async_computation.1 | async-start | bytes 1048576 | tf_op jit(solution)/shard_map/from_columns/all_to_all | solution.py:358
  95.6 1.9 %collective-permute-start.8 = (bf16[512,512]{1,0:T(8,128)(2,1)S(1)}, bf16[512,512]{1,0:T(8,128)(2,1)S(1)}, u32[]{:S(2)}, u32[]{:S(2)}) collective-permute-start(bf16[512,512]{1,0:T(8,128)(2,1)S(1)} %copy-done.13), channel_id=1, source_target_pairs={{0,1},{1,0},{2,3},{3,2},{4,5},{5,4},{6,7},{7,6},{8,9},{9,8},{10,11... | collective-permute-start | bytes 1572872 | tf_op jit(solution)/shard_map/ppermute | solution.py:340
  97.5 2.6 %collective-permute-start.9 = (bf16[512,512]{1,0:T(8,128)(2,1)}, bf16[512,512]{1,0:T(8,128)(2,1)S(1)}, u32[]{:S(2)}, u32[]{:S(2)}) collective-permute-start(bf16[512,512]{1,0:T(8,128)(2,1)} %get-tuple-element.34), channel_id=1, source_target_pairs={{0,1},{1,0},{2,3},{3,2},{4,5},{5,4},{6,7},{7,6},{8,9},{9,8},{10,11... | collective-permute-start | bytes 1572872 | tf_op jit(solution)/shard_map/ppermute | solution.py:356
  100.1 0.0 collective-permute-done.8.row_got
  100.1 1.5 collective-permute-done.9.col_got
  101.7 0.0 copy-done.1
  101.7 0.2 pick.1
  101.9 2.4 %collective-permute-start.10 = (bf16[128,1024]{1,0:T(8,128)(2,1)S(1)}, bf16[128,1024]{1,0:T(8,128)(2,1)S(1)}, u32[]{:S(2)}, u32[]{:S(2)}) collective-permute-start(bf16[128,1024]{1,0:T(8,128)(2,1)S(1)} %get-tuple-element.36), channel_id=1, source_target_pairs={{0,128},{128,256},{256,384},{384,0},{1,129},{129,257},{257,385},{3... | collective-permute-start | bytes 786440 | tf_op jit(solution)/shard_map/gradient_sums/ppermute | solution.py:373
  104.3 4.3 %collective-permute-start.11 = (bf16[128,1024]{1,0:T(8,128)(2,1)S(1)}, bf16[128,1024]{1,0:T(8,128)(2,1)S(1)}, u32[]{:S(2)}, u32[]{:S(2)}) collective-permute-start(bf16[128,1024]{1,0:T(8,128)(2,1)S(1)} %get-tuple-element.37), channel_id=1, source_target_pairs={{0,256},{128,384},{256,0},{384,128},{1,257},{129,385},{257,1},{385... | collective-permute-start | bytes 786440 | tf_op jit(solution)/shard_map/gradient_sums/ppermute | solution.py:373
  108.7 1.9 %collective-permute-start.12 = (bf16[128,1024]{1,0:T(8,128)(2,1)S(1)}, bf16[128,1024]{1,0:T(8,128)(2,1)S(1)}, u32[]{:S(2)}, u32[]{:S(2)}) collective-permute-start(bf16[128,1024]{1,0:T(8,128)(2,1)S(1)} %get-tuple-element.38), channel_id=1, source_target_pairs={{0,384},{128,0},{256,128},{384,256},{1,385},{129,1},{257,129},{385... | collective-permute-start | bytes 786440 | tf_op jit(solution)/shard_map/gradient_sums/ppermute | solution.py:373
  110.6 2.4 %collective-permute-done.10.refs_1_ = bf16[128,1024]{1,0:T(8,128)(2,1)S(1)} collective-permute-done((bf16[128,1024]{1,0:T(8,128)(2,1)S(1)}, bf16[128,1024]{1,0:T(8,128)(2,1)S(1)}, u32[]{:S(2)}, u32[]{:S(2)}) %collective-permute-start.10) | collective-permute-done | bytes 262176 | tf_op jit(solution)/shard_map/gradient_sums/ppermute | solution.py:373
  112.9 3.9 %collective-permute-done.11.refs_2_ = bf16[128,1024]{1,0:T(8,128)(2,1)S(1)} collective-permute-done((bf16[128,1024]{1,0:T(8,128)(2,1)S(1)}, bf16[128,1024]{1,0:T(8,128)(2,1)S(1)}, u32[]{:S(2)}, u32[]{:S(2)}) %collective-permute-start.11) | collective-permute-done | bytes 262176 | tf_op jit(solution)/shard_map/gradient_sums/ppermute | solution.py:373
  116.9 4.7 %collective-permute-done.12.refs_3_ = bf16[128,1024]{1,0:T(8,128)(2,1)S(1)} collective-permute-done((bf16[128,1024]{1,0:T(8,128)(2,1)S(1)}, bf16[128,1024]{1,0:T(8,128)(2,1)S(1)}, u32[]{:S(2)}, u32[]{:S(2)}) %collective-permute-start.12) | collective-permute-done | bytes 262176 | tf_op jit(solution)/shard_map/gradient_sums/ppermute | solution.py:373
  121.6 1.2 line.1
  122.9 6.4 %all-to-all-done.1 = bf16[64,8,512]{2,1,0:T(8,128)(2,1)S(1)} async-done(((bf16[64,8,512]{2,1,0:T(8,128)(2,1)}), bf16[64,8,512]{2,1,0:T(8,128)(2,1)S(1)}, u32[]{:S(2)}, u32[]{:S(2)}) %all-to-all-start.1) | async-done | bytes 524320 | tf_op jit(solution)/shard_map/from_columns/all_to_all | solution.py:358
  129.3 7.2 %all-to-all-start.2 = ((bf16[64,8,256]{2,1,0:T(8,128)(2,1)}), bf16[64,8,256]{2,1,0:T(8,128)(2,1)S(1)}, u32[]{:S(2)}, u32[]{:S(2)}) async-start(bf16[64,8,256]{2,1,0:T(8,128)(2,1)} %bitcast.16), calls=%async_computation.2 | async-start | bytes 524288 | tf_op jit(solution)/shard_map/gradient_sums/all_to_all | solution.py:386
  136.5 5.6 %output_products.1 = (bf16[256,1024]{1,0:T(8,128)(2,1)}, bf16[256,1024]{1,0:T(8,128)(2,1)}) custom-call(bf16[256,1024]{1,0:T(8,128)(2,1)} %get-tuple-element.27.row_ref, bf16[512,512]{1,0:T(8,128)(2,1)} %bitcast.40, bf16[2,128,1024]{2,1,0:T(8,128)(2,1)} %copy-done, bf16[2,128,1024]{2,1,0:T(8,128)(2,1)} %copy-done.6, bf16[2,128,1024]{2,1,0:T(8,128)(2,1)} %copy-done.5, ...), custom_call_target="tpu_custom_call" | custom-call | flops 1200000000 | bytes 8000000 | tf_op jit(solution)/shard_map/output_products/pallas_call | solution.py:399
  142.1 17.3 %all-to-all-done.2 = bf16[64,8,256]{2,1,0:T(8,128)(2,1)S(1)} async-done(((bf16[64,8,256]{2,1,0:T(8,128)(2,1)}), bf16[64,8,256]{2,1,0:T(8,128)(2,1)S(1)}, u32[]{:S(2)}, u32[]{:S(2)}) %all-to-all-start.2) | async-done | bytes 262176 | tf_op jit(solution)/shard_map/gradient_sums/all_to_all | solution.py:386
  159.3 0.7 last.1
  (15 shorter events, 0.1 us)
Async XLA Ops:
  2.3 25.1 %collective-permute-start = (bf16[128,1024]{1,0:T(8,128)(2,1)}, bf16[128,1024]{1,0:T(8,128)(2,1)S(1)}, u32[]{:S(2)}, u32[]{:S(2)}) collective-permute-start(bf16[128,1024]{1,0:T(8,128)(2,1)} %pack.1.packed_ref), channel_id=1, source_target_pairs={{0,66},{2,64},{64,2},{66,0},{1,67},{3,65},{65,3},{67,1},{4,70},{6,... | collective-permute-start | bytes 786440 | tf_op jit(solution)/shard_map/weights/ppermute | solution.py:309
  10.1 17.2 %copy-start.2 = (bf16[128,1024]{1,0:T(8,128)(2,1)S(1)}, bf16[128,1024]{1,0:T(8,128)(2,1)}, u32[]{:S(2)}) copy-start(bf16[128,1024]{1,0:T(8,128)(2,1)} %pack.1.packed_ref) | copy-start | bytes 786436
  10.2 72.5 %all-to-all-start = ((bf16[64,8,1024]{2,1,0:T(8,128)(2,1)}), bf16[64,8,1024]{2,1,0:T(8,128)(2,1)}, u32[]{:S(2)}, u32[]{:S(2)}) async-start(bf16[64,8,1024]{2,1,0:T(8,128)(2,1)} %bitcast.39), calls=%async_computation | async-start | bytes 2097152 | tf_op jit(solution)/shard_map/to_columns/all_to_all | solution.py:303
  26.7 0.7 copy-start.12
  27.4 12.2 %copy-start = (bf16[2,128,1024]{2,1,0:T(8,128)(2,1)}, bf16[2,128,1024]{2,1,0:T(8,128)(2,1)S(1)}, u32[]{:S(2)}) copy-start(bf16[2,128,1024]{2,1,0:T(8,128)(2,1)S(1)} %pair.1.refs_0_) | copy-start | bytes 1572868
  27.5 28.4 %collective-permute-start.3 = (bf16[2,128,1024]{2,1,0:T(8,128)(2,1)S(1)}, bf16[2,128,1024]{2,1,0:T(8,128)(2,1)S(1)}, u32[]{:S(2)}, u32[]{:S(2)}) collective-permute-start(bf16[2,128,1024]{2,1,0:T(8,128)(2,1)S(1)} %pair.1.refs_0_), channel_id=1, source_target_pairs={{0,256},{128,384},{256,0},{384,128},{1,257},{129,385},{257,1},{385... | collective-permute-start | bytes 1572872 | tf_op jit(solution)/shard_map/weights/ppermute | solution.py:320
  30.8 27.2 %collective-permute-start.2 = (bf16[2,128,1024]{2,1,0:T(8,128)(2,1)S(1)}, bf16[2,128,1024]{2,1,0:T(8,128)(2,1)S(1)}, u32[]{:S(2)}, u32[]{:S(2)}) collective-permute-start(bf16[2,128,1024]{2,1,0:T(8,128)(2,1)S(1)} %pair.1.refs_0_), channel_id=1, source_target_pairs={{0,128},{128,256},{256,384},{384,0},{1,129},{129,257},{257,385},{3... | collective-permute-start | bytes 1572872 | tf_op jit(solution)/shard_map/weights/ppermute | solution.py:320
  34.8 21.1 %collective-permute-start.1 = (bf16[2,128,1024]{2,1,0:T(8,128)(2,1)S(1)}, bf16[2,128,1024]{2,1,0:T(8,128)(2,1)S(1)}, u32[]{:S(2)}, u32[]{:S(2)}) collective-permute-start(bf16[2,128,1024]{2,1,0:T(8,128)(2,1)S(1)} %pair.1.refs_0_), channel_id=1, source_target_pairs={{0,384},{128,0},{256,128},{384,256},{1,385},{129,1},{257,129},{385... | collective-permute-start | bytes 1572872 | tf_op jit(solution)/shard_map/weights/ppermute | solution.py:320
  36.8 1.4 copy-start.14
  39.7 22.6 %collective-permute-start.4 = (bf16[2,128,1024]{2,1,0:T(8,128)(2,1)S(1)}, bf16[2,128,1024]{2,1,0:T(8,128)(2,1)S(1)}, u32[]{:S(2)}, u32[]{:S(2)}) collective-permute-start(bf16[2,128,1024]{2,1,0:T(8,128)(2,1)S(1)} %pair.1.refs_0_), channel_id=1, source_target_pairs={{0,1},{1,0},{2,3},{3,2},{4,5},{5,4},{6,7},{7,6},{8,9},{9,8},{10,11... | collective-permute-start | bytes 1572872 | tf_op jit(solution)/shard_map/weights/ppermute | solution.py:323
  55.9 8.2 %copy-start.7 = (bf16[2,128,1024]{2,1,0:T(8,128)(2,1)}, bf16[2,128,1024]{2,1,0:T(8,128)(2,1)S(1)}, u32[]{:S(2)}) copy-start(bf16[2,128,1024]{2,1,0:T(8,128)(2,1)S(1)} %collective-permute-done.1.refs_3_) | copy-start | bytes 1572868
  55.9 8.2 %copy-start.5 = (bf16[2,128,1024]{2,1,0:T(8,128)(2,1)}, bf16[2,128,1024]{2,1,0:T(8,128)(2,1)S(1)}, u32[]{:S(2)}) copy-start(bf16[2,128,1024]{2,1,0:T(8,128)(2,1)S(1)} %collective-permute-done.3.refs_2_) | copy-start | bytes 1572868
  55.9 6.4 %collective-permute-start.6 = (bf16[2,128,1024]{2,1,0:T(8,128)(2,1)S(1)}, bf16[2,128,1024]{2,1,0:T(8,128)(2,1)S(1)}, u32[]{:S(2)}, u32[]{:S(2)}) collective-permute-start(bf16[2,128,1024]{2,1,0:T(8,128)(2,1)S(1)} %collective-permute-done.3.refs_2_), channel_id=1, source_target_pairs={{0,1},{1,0},{2,3},{3,2},{4,5},{5,4},{6,7},{7,6},{8,9},{9,8},{10,11... | collective-permute-start | bytes 1572872 | tf_op jit(solution)/shard_map/weights/ppermute | solution.py:323
  57.9 6.1 %copy-start.6 = (bf16[2,128,1024]{2,1,0:T(8,128)(2,1)}, bf16[2,128,1024]{2,1,0:T(8,128)(2,1)S(1)}, u32[]{:S(2)}) copy-start(bf16[2,128,1024]{2,1,0:T(8,128)(2,1)S(1)} %collective-permute-done.2.refs_1_) | copy-start | bytes 1572868
  58.0 4.4 %collective-permute-start.5 = (bf16[2,128,1024]{2,1,0:T(8,128)(2,1)S(1)}, bf16[2,128,1024]{2,1,0:T(8,128)(2,1)S(1)}, u32[]{:S(2)}, u32[]{:S(2)}) collective-permute-start(bf16[2,128,1024]{2,1,0:T(8,128)(2,1)S(1)} %collective-permute-done.2.refs_1_), channel_id=1, source_target_pairs={{0,1},{1,0},{2,3},{3,2},{4,5},{5,4},{6,7},{7,6},{8,9},{9,8},{10,11... | collective-permute-start | bytes 1572872 | tf_op jit(solution)/shard_map/weights/ppermute | solution.py:323
  60.3 3.8 %collective-permute-start.7 = (bf16[2,128,1024]{2,1,0:T(8,128)(2,1)S(1)}, bf16[2,128,1024]{2,1,0:T(8,128)(2,1)S(1)}, u32[]{:S(2)}, u32[]{:S(2)}) collective-permute-start(bf16[2,128,1024]{2,1,0:T(8,128)(2,1)S(1)} %collective-permute-done.1.refs_3_), channel_id=1, source_target_pairs={{0,1},{1,0},{2,3},{3,2},{4,5},{5,4},{6,7},{7,6},{8,9},{9,8},{10,11... | collective-permute-start | bytes 1572872 | tf_op jit(solution)/shard_map/weights/ppermute | solution.py:323
  62.3 1.8 %copy-start.8 = (bf16[2,128,1024]{2,1,0:T(8,128)(2,1)}, bf16[2,128,1024]{2,1,0:T(8,128)(2,1)S(1)}, u32[]{:S(2)}) copy-start(bf16[2,128,1024]{2,1,0:T(8,128)(2,1)S(1)} %collective-permute-done.4.refs_4_) | copy-start | bytes 1572868
  62.3 1.8 %copy-start.9 = (bf16[2,128,1024]{2,1,0:T(8,128)(2,1)}, bf16[2,128,1024]{2,1,0:T(8,128)(2,1)S(1)}, u32[]{:S(2)}) copy-start(bf16[2,128,1024]{2,1,0:T(8,128)(2,1)S(1)} %collective-permute-done.6.refs_6_) | copy-start | bytes 1572868
  62.3 1.7 %copy-start.10 = (bf16[2,128,1024]{2,1,0:T(8,128)(2,1)}, bf16[2,128,1024]{2,1,0:T(8,128)(2,1)S(1)}, u32[]{:S(2)}) copy-start(bf16[2,128,1024]{2,1,0:T(8,128)(2,1)S(1)} %collective-permute-done.5.refs_5_) | copy-start | bytes 1572868
  64.1 0.8 copy-start.11
  82.7 12.9 %copy-start.13 = (bf16[512,512]{1,0:T(8,128)(2,1)S(1)}, bf16[512,512]{1,0:T(8,128)(2,1)}, u32[]{:S(2)}) copy-start(bf16[512,512]{1,0:T(8,128)(2,1)} %get-tuple-element.30) | copy-start | bytes 1572868
  90.8 10.9 %copy-start.1 = (bf16[512,512]{1,0:T(8,128)(2,1)S(1)}, bf16[512,512]{1,0:T(8,128)(2,1)}, u32[]{:S(2)}) copy-start(bf16[512,512]{1,0:T(8,128)(2,1)} %get-tuple-element.29.row_keep) | copy-start | bytes 1572868
  90.8 10.9 %copy-start.3 = (bf16[512,512]{1,0:T(8,128)(2,1)S(1)}, bf16[512,512]{1,0:T(8,128)(2,1)}, u32[]{:S(2)}) copy-start(bf16[512,512]{1,0:T(8,128)(2,1)} %get-tuple-element.33.col_keep) | copy-start | bytes 1572868
  90.8 38.5 %all-to-all-start.1 = ((bf16[64,8,512]{2,1,0:T(8,128)(2,1)}), bf16[64,8,512]{2,1,0:T(8,128)(2,1)S(1)}, u32[]{:S(2)}, u32[]{:S(2)}) async-start(bf16[64,8,512]{2,1,0:T(8,128)(2,1)} %bitcast.45), calls=%async_computation.1 | async-start | bytes 1048576 | tf_op jit(solution)/shard_map/from_columns/all_to_all | solution.py:358
  95.6 4.5 %collective-permute-start.8 = (bf16[512,512]{1,0:T(8,128)(2,1)S(1)}, bf16[512,512]{1,0:T(8,128)(2,1)S(1)}, u32[]{:S(2)}, u32[]{:S(2)}) collective-permute-start(bf16[512,512]{1,0:T(8,128)(2,1)S(1)} %copy-done.13), channel_id=1, source_target_pairs={{0,1},{1,0},{2,3},{3,2},{4,5},{5,4},{6,7},{7,6},{8,9},{9,8},{10,11... | collective-permute-start | bytes 1572872 | tf_op jit(solution)/shard_map/ppermute | solution.py:340
  97.5 4.1 %collective-permute-start.9 = (bf16[512,512]{1,0:T(8,128)(2,1)}, bf16[512,512]{1,0:T(8,128)(2,1)S(1)}, u32[]{:S(2)}, u32[]{:S(2)}) collective-permute-start(bf16[512,512]{1,0:T(8,128)(2,1)} %get-tuple-element.34), channel_id=1, source_target_pairs={{0,1},{1,0},{2,3},{3,2},{4,5},{5,4},{6,7},{7,6},{8,9},{9,8},{10,11... | collective-permute-start | bytes 1572872 | tf_op jit(solution)/shard_map/ppermute | solution.py:356
  101.9 11.0 %collective-permute-start.10 = (bf16[128,1024]{1,0:T(8,128)(2,1)S(1)}, bf16[128,1024]{1,0:T(8,128)(2,1)S(1)}, u32[]{:S(2)}, u32[]{:S(2)}) collective-permute-start(bf16[128,1024]{1,0:T(8,128)(2,1)S(1)} %get-tuple-element.36), channel_id=1, source_target_pairs={{0,128},{128,256},{256,384},{384,0},{1,129},{129,257},{257,385},{3... | collective-permute-start | bytes 786440 | tf_op jit(solution)/shard_map/gradient_sums/ppermute | solution.py:373
  104.3 12.6 %collective-permute-start.11 = (bf16[128,1024]{1,0:T(8,128)(2,1)S(1)}, bf16[128,1024]{1,0:T(8,128)(2,1)S(1)}, u32[]{:S(2)}, u32[]{:S(2)}) collective-permute-start(bf16[128,1024]{1,0:T(8,128)(2,1)S(1)} %get-tuple-element.37), channel_id=1, source_target_pairs={{0,256},{128,384},{256,0},{384,128},{1,257},{129,385},{257,1},{385... | collective-permute-start | bytes 786440 | tf_op jit(solution)/shard_map/gradient_sums/ppermute | solution.py:373
  108.7 13.0 %collective-permute-start.12 = (bf16[128,1024]{1,0:T(8,128)(2,1)S(1)}, bf16[128,1024]{1,0:T(8,128)(2,1)S(1)}, u32[]{:S(2)}, u32[]{:S(2)}) collective-permute-start(bf16[128,1024]{1,0:T(8,128)(2,1)S(1)} %get-tuple-element.38), channel_id=1, source_target_pairs={{0,384},{128,0},{256,128},{384,256},{1,385},{129,1},{257,129},{385... | collective-permute-start | bytes 786440 | tf_op jit(solution)/shard_map/gradient_sums/ppermute | solution.py:373
  129.3 7.2 %copy-start.4 = (bf16[64,8,512]{2,1,0:T(8,128)(2,1)}, bf16[64,8,512]{2,1,0:T(8,128)(2,1)S(1)}, u32[]{:S(2)}) copy-start(bf16[64,8,512]{2,1,0:T(8,128)(2,1)S(1)} %all-to-all-done.1) | copy-start | bytes 1572868
  129.3 30.1 %all-to-all-start.2 = ((bf16[64,8,256]{2,1,0:T(8,128)(2,1)}), bf16[64,8,256]{2,1,0:T(8,128)(2,1)S(1)}, u32[]{:S(2)}, u32[]{:S(2)}) async-start(bf16[64,8,256]{2,1,0:T(8,128)(2,1)} %bitcast.16), calls=%async_computation.2 | async-start | bytes 524288 | tf_op jit(solution)/shard_map/gradient_sums/all_to_all | solution.py:386

commit v6 on v5

--- a/solution.py
+++ b/solution.py
@@ -24,22 +24,25 @@
 
 
 SWAP = [(0, 1), (1, 0)]
-PACK, PAIR, PICK = 1000000000, 30000000000, 10000000000
+PAIR, PICK = 30000000000, 14000000000
 
 
 def product(a, b, dims=(((1,), (0,)), ((), ()))):
     return lax.dot_general(a, b, dims, preferred_element_type=F32)
 
 
-def eights(first):
-    row = lax.broadcasted_iota(jnp.int32, (512, 256), 0)
-    col = lax.broadcasted_iota(jnp.int32, (512, 256), 1)
+def eights(first, rows=256):
+    row = lax.broadcasted_iota(jnp.int32, (2 * rows, rows), 0)
+    col = lax.broadcasted_iota(jnp.int32, (2 * rows, rows), 1)
     inside = (row & 4) == (0 if first else 4)
     return ((col == (row >> 3) * 4 + (row & 3)) & inside).astype(F32).astype(BF)
 
 
-def interleave(first, second):
-    return (product(eights(True), first) + product(eights(False), second)).astype(BF)
+def interleave(first, second, dims=(((1,), (0,)), ((), ()))):
+    rows = first.shape[dims[0][1][0]]
+    return (
+        product(eights(True, rows), first, dims) + product(eights(False, rows), second, dims)
+    ).astype(BF)
 
 
 def separate(both):
@@ -61,9 +64,17 @@
         copy.wait()
 
 
-def interleave_kernel(x_ref, ct_ref, sent_ref, x, ct, sems):
-    wait_for(start_copies(((x_ref, x), (ct_ref, ct)), sems))
-    sent_ref[...] = interleave(x[...], ct[...])
+def interleave_kernel(x_ref, ct_ref, sent_ref, x, ct, sent, sems):
+    pieces = [(pl.ds(i * 64, 64), pl.ds(i * 128, 128)) for i in range(4)]
+    loads, stores = [], []
+    for rows, _ in pieces:
+        loads += [(x_ref.at[rows], x.at[rows]), (ct_ref.at[rows], ct.at[rows])]
+    copies = start_copies(loads, sems)
+    for i, (rows, out) in enumerate(pieces):
+        wait_for(copies[2 * i : 2 * i + 2])
+        sent[out] = interleave(x[rows], ct[rows])
+        stores += start_copies([(sent.at[out], sent_ref.at[out])], sems, 8 + i)
+    wait_for(stores)
 
 
 def pack_kernel(wq_ref, wk_ref, wv_ref, wo_ref, packed_ref, sems):
@@ -83,9 +94,18 @@
     pair_ref[1] = flipped_ref[...]
 
 
-def attention(x, ct, weights, kind, bias_ref):
-    qkv = product(x, weights[kind, :, :, 0:768].reshape(1024, 768)).astype(BF)
+def attention(x_ref, ct_ref, weights, copies, kind, bias_ref):
+    across = lax.axis_index("x")
+    qkv = jnp.zeros((256, 768), F32)
+    for step in range(4):
+        wait_for(copies[2 * step : 2 * step + 2])
+        source = (across + 4 - step) & 3
+        left = x_ref[:, pl.ds(pl.multiple_of(source * 256, 256), 256)]
+        qkv += product(left, weights[kind, pl.ds(source * 2, 2), :, 0:768].reshape(256, 768))
+    qkv = qkv.astype(BF)
     q, k, v = qkv[:, :256], qkv[:, 256:512], qkv[:, 512:]
+    wait_for(copies[8:])
+    ct = ct_ref[...]
     do = jnp.zeros((256, 256), F32)
     for half in range(2):
         for b in range(2):
@@ -93,39 +113,40 @@
             start = half * 512 + b * 256
             do += product(ct[:, start : start + 256], block.reshape(256, 256), LAST)
     do = do.astype(BF)
+    q = q * jnp.asarray(0.125, BF)
+    qt, kt, vt, ot = q.T, (k * jnp.asarray(0.125, BF)).T, v.T, do.T
     lane = lax.broadcasted_iota(jnp.int32, (256, 256), 1) // HEAD_DIM
     zero = jnp.zeros_like(q)
-    out = jnp.zeros((256, 256), F32)
-    dq, dk, dv = out, out, out
-    for h in range(4):
-        mine = lane == h
-        kh, vh = jnp.where(mine, k, zero), jnp.where(mine, v, zero)
-        qh, doh = jnp.where(mine, q, zero), jnp.where(mine, do, zero)
-        s = product(q, kh, LAST) * 0.125 + bias_ref[h].astype(F32)
-        e = jnp.exp(s - jnp.max(s, axis=-1, keepdims=True))
-        w = e * (1.0 / jnp.sum(e, axis=-1, keepdims=True))
-        p = w.astype(BF)
-        out += product(p, vh)
-        dp = product(do, vh, LAST).astype(BF).astype(F32)
-        ds = (w * (dp - jnp.sum(dp * w, axis=-1, keepdims=True)) * 0.125).astype(BF)
-        dq += product(ds, kh)
-        dk += product(ds, qh, FIRST)
-        dv += product(p, doh, FIRST)
-    return tuple(a.astype(BF) for a in (out, dq, dk, dv))
-
-
-def store_gradients(core, x, ct, out, dv, keep_ref, send_ref):
-    gradients = jnp.concatenate(
-        [product(x, dv, FIRST).astype(BF), product(ct, out, FIRST).astype(BF)], axis=1
+    heads = range(4)
+    s = [product(jnp.where(lane == h, q, zero), k, LAST) + bias_ref[h].astype(F32) for h in heads]
+    e = [jnp.exp(a - jnp.max(a, axis=-1, keepdims=True)) for a in s]
+    w = [a * (1.0 / jnp.sum(a, axis=-1, keepdims=True)) for a in e]
+    p = [a.astype(BF) for a in w]
+    dp = [product(jnp.where(lane == h, do, zero), v, LAST) for h in heads]
+    ds = [(a * (b - jnp.sum(b * a, axis=-1, keepdims=True))).astype(BF) for a, b in zip(w, dp)]
+    rows = [slice(h * HEAD_DIM, (h + 1) * HEAD_DIM) for h in heads]
+    results = (
+        [product(vt[rows[h]], p[h], LAST) for h in heads],
+        [product(kt[rows[h]], ds[h], LAST) for h in heads],
+        [product(qt[rows[h]], ds[h]) for h in heads],
+        [product(ot[rows[h]], p[h]) for h in heads],
     )
+    return tuple(jnp.concatenate(a, axis=0).astype(BF) for a in results)
+
+
+def store_gradients(core, x, ct, outt, dvt, keep_ref, send_ref, done=lambda block: None):
+    gradients = (product(dvt, x).astype(BF), product(outt, ct).astype(BF))
     new = lax.broadcasted_iota(jnp.int32, (128, 128), 0)
     old = lax.broadcasted_iota(jnp.int32, (128, 128), 1)
     source = ((new >> 1) & 31) * 4 + ((new >> 6) ^ core) * 2 + (new & 1)
     order = (old == source).astype(F32).astype(BF)
     for block in range(8):
-        moved = product(order, gradients[block * 128 : (block + 1) * 128]).astype(BF)
-        keep_ref[block * 64 : (block + 1) * 64, :] = moved[:64]
-        send_ref[block * 64 : (block + 1) * 64, :] = moved[64:]
+        rows = slice(block * 64, (block + 1) * 64)
+        for i, part in enumerate(gradients):
+            moved = product(order, part[:, block * 128 : (block + 1) * 128], LAST).astype(BF)
+            keep_ref[rows, i * 256 : (i + 1) * 256] = moved[:64]
+            send_ref[rows, i * 256 : (i + 1) * 256] = moved[64:]
+        done(block)
 
 
 def weight_copies(refs, w_ref, sems, kinds):
@@ -135,14 +156,15 @@
     for step in range(4):
         for flip in range(2):
             shard = ((across + 4 - step) & 3) * 2 + (high ^ flip)
-            for side, ref in enumerate((refs[step], refs[4 + step])):
+            for side in range(2):
+                ref = refs[4 * side + step].at[flip]
                 half = core ^ side
                 if kinds == 2:
-                    pairs.append((ref.at[flip], w_ref.at[half, shard]))
+                    pairs.append((ref, w_ref.at[half, shard]))
                 else:
-                    pairs.append((ref.at[flip, :, right], w_ref.at[half, shard, :, right]))
+                    pairs.append((ref.at[:, right], w_ref.at[half, shard, :, right]))
                     left = pl.ds(0, 768)
-                    sides[side].append((ref.at[flip, :, left], w_ref.at[half, shard, :, left]))
+                    sides[side].append((ref.at[:, left], w_ref.at[half, shard, :, left]))
     return pairs, sides
 
 
@@ -165,24 +187,33 @@
 def row_kernel(x_ref, ct_ref, bias_ref, *refs):
     weights, (parts_ref, keep_ref, send_ref, x_here, ct_here, bias, w_ref, sems) = refs[:8], refs[8:]
     copies = start_copies(((x_ref, x_here), (ct_ref, ct_here), (bias_ref, bias)), sems)
-    wait_for(kind_copies(0, weights, w_ref, sems, 3) + copies)
-    x, ct = x_here[...], ct_here[...]
-    out, dq, dk, dv = attention(x, ct, w_ref, 0, bias)
+    more = kind_copies(0, weights, w_ref, sems, 3)
+    wait_for(copies[:1])
+    out, dq, dk, dv = attention(x_here, ct_here, w_ref, more + copies[1:], 0, bias)
     for i, part in enumerate((out, dq, dk, dv)):
-        parts_ref[:, i * 256 : (i + 1) * 256] = part
-    store_gradients(lax.axis_index("c"), x, ct, out, dv, keep_ref, send_ref)
+        parts_ref[:, i * 256 : (i + 1) * 256] = part.T
+    store_gradients(lax.axis_index("c"), x_here[...], ct_here[...], out, dv, keep_ref, send_ref)
 
 
 def column_kernel(both_ref, bias_ref, *refs):
-    weights, (parts_ref, keep_ref, send_ref, bias, w_ref, sems) = refs[:8], refs[8:]
+    weights, refs = refs[:8], refs[8:]
+    parts_ref, keep_ref, send_ref, parts, keep, send, x, ct, bias, w_ref, sems = refs
     copies = kind_copies(1, weights, w_ref, sems, 1) + start_copies(((bias_ref, bias),), sems)
-    x, ct = separate(both_ref[...])
-    wait_for(copies)
-    out, dq, dk, dv = attention(x, ct, w_ref, 1, bias)
-    parts_ref[...] = interleave(
-        jnp.concatenate([out, dq], axis=1), jnp.concatenate([dk, dv], axis=1)
-    )
-    store_gradients(lax.axis_index("c"), x, ct, out, dv, keep_ref, send_ref)
+    x[...], ct[...] = separate(both_ref[...])
+    out, dq, dk, dv = attention(x, ct, w_ref, copies, 1, bias)
+    parts[:, 0:256] = interleave(out, dk, LAST)
+    parts[:, 256:512] = interleave(dq, dv, LAST)
+    stores = start_copies(((parts, parts_ref),), sems)
+
+
+    def store(block):
+        if block in (3, 7):
+            rows = pl.ds((block - 3) * 64, 256)
+            pairs = [(keep.at[rows], keep_ref.at[rows]), (send.at[rows], send_ref.at[rows])]
+            stores.extend(start_copies(pairs, sems, block - 2))
+
+    store_gradients(lax.axis_index("c"), x[...], ct[...], out, dv, keep, send, store)
+    wait_for(stores)
 
 
 def pick_kernel(row_keep, row_got, col_keep, col_got, *terms):
@@ -194,12 +225,19 @@
             term[:, i * 512 : (i + 1) * 512] = total.astype(BF)
 
 
-def line_kernel(*refs):
-    given, out_ref = refs[:4], refs[4]
-    total = sum(ref[...].astype(F32) for ref in given).astype(BF)
-    row = lax.broadcasted_iota(jnp.int32, (512, 128), 0)
-    col = lax.broadcasted_iota(jnp.int32, (512, 128), 1)
-    out = jnp.zeros((512, 256), F32)
+def spread_kernel(*refs):
+    given, keep_ref, send_ref, total = refs[:4], refs[4], refs[5], refs[6]
+    total[...] = sum(ref[...].astype(F32) for ref in given).astype(BF)
+    high = lax.axis_index("yh")
+    keep_ref[...] = total[pl.ds(pl.multiple_of(high * 64, 64), 64), :]
+    send_ref[...] = total[pl.ds(pl.multiple_of((high ^ 1) * 64, 64), 64), :]
+
+
+def line_kernel(keep_ref, got_ref, out_ref):
+    total = (keep_ref[...].astype(F32) + got_ref[...].astype(F32)).astype(BF)
+    row = lax.broadcasted_iota(jnp.int32, (256, 64), 0)
+    col = lax.broadcasted_iota(jnp.int32, (256, 64), 1)
+    out = jnp.zeros((256, 256), F32)
     for b in range(4):
         here = (col == (row >> 3) * 2 + (row & 1)) & ((row & 6) == 2 * b)
         out += product(here.astype(F32).astype(BF), total[:, b * 256 : (b + 1) * 256])
@@ -207,7 +245,7 @@
 
 
 def last_kernel(line_ref, value_ref, out_ref):
-    total = jnp.sum(line_ref[...].astype(F32).reshape(64, 8, 256), axis=0)
+    total = jnp.sum(line_ref[...].astype(F32).reshape(32, 8, 256), axis=0)
     for kind in range(2):
         value_ref[:, kind * 256 : (kind + 1) * 256] = total[kind * 4 : kind * 4 + 2]
         out_ref[:, kind * 256 : (kind + 1) * 256] = total[kind * 4 + 2 : kind * 4 + 4]
@@ -283,8 +321,13 @@
         interleave_kernel,
         out_shape=shape(512, 1024),
         in_specs=[HBM] * 2,
-        out_specs=VMEM,
-        scratch_shapes=[buffer(256, 1024), buffer(256, 1024), pltpu.SemaphoreType.DMA((2,))],
+        out_specs=HBM,
+        scratch_shapes=[
+            buffer(256, 1024),
+            buffer(256, 1024),
+            buffer(512, 1024),
+            pltpu.SemaphoreType.DMA((12,)),
+        ],
         compiler_params=room(60),
         cost_estimate=cost(540000000, 2000000),
         name="interleave",
@@ -296,7 +339,7 @@
         out_specs=VMEM,
         scratch_shapes=[pltpu.SemaphoreType.DMA((5,))],
         compiler_params=room(60),
-        cost_estimate=cost(PACK, 2000000),
+        cost_estimate=cost(1000000000, 2000000),
         name="pack",
     )(w_query, w_key, w_value, w_out)
     with jax.named_scope("to_columns"):
@@ -343,8 +386,13 @@
         column_kernel,
         out_shape=(shape(512, 512),) * 3,
         in_specs=[VMEM] + [HBM] * 9,
-        out_specs=(VMEM,) * 3,
+        out_specs=(HBM,) * 3,
         scratch_shapes=[
+            buffer(512, 512),
+            buffer(512, 512),
+            buffer(512, 512),
+            buffer(256, 1024),
+            buffer(256, 1024),
             buffer(4, 256, 256),
             buffer(2, 8, 128, 1024),
             pltpu.SemaphoreType.DMA((25,)),
@@ -371,20 +419,31 @@
         )(row_keep, row_got, col_keep, col_got)
         moved = [
             lax.ppermute(terms[step], "x", [(x, (x + step) % 4) for x in range(4)])
-            for step in (1, 2, 3)
+            for step in (2, 1, 3)
         ]
+        line_keep, line_send = pl.pallas_call(
+            spread_kernel,
+            out_shape=(shape(64, 1024),) * 2,
+            in_specs=[VMEM] * 4,
+            out_specs=(VMEM,) * 2,
+            scratch_shapes=[buffer(128, 1024)],
+            compiler_params=room(16),
+            cost_estimate=cost(10000000, 1000000),
+            name="spread",
+        )(terms[0], *moved)
+        line_got = lax.ppermute(line_send, ("yh", "yl"), [(y, 3 - y) for y in range(4)])
         line = pl.pallas_call(
             line_kernel,
-            out_shape=shape(512, 256),
-            in_specs=[VMEM] * 4,
+            out_shape=shape(256, 256),
+            in_specs=[VMEM] * 2,
             out_specs=VMEM,
             compiler_params=room(16),
             cost_estimate=cost(10000000, 300000),
             name="line",
-        )(terms[0], *moved)
+        )(line_keep, line_got)
         line, returned = lax.optimization_barrier((line, returned))
         line = lax.all_to_all(
-            line.reshape(64, 8, 256), ("yh", "z", "yl"), split_axis=0, concat_axis=0, tiled=True
+            line.reshape(32, 8, 256), ("z", "yl"), split_axis=0, concat_axis=0, tiled=True
         )
         grad_value, grad_output = pl.pallas_call(
             last_kernel,
@@ -394,7 +453,7 @@
             compiler_params=room(16),
             cost_estimate=cost(100000, 100000),
             name="last",
-        )(line.reshape(512, 256))
+        )(line.reshape(256, 256))
         grad_output = jnp.transpose(grad_output)
     mixed, grad_tokens = pl.pallas_call(
         final_kernel,

time: 162 us -> 153 us (0.944)
  waiting for transfers between devices: 63.3 us -> 54.9 us
  Pallas kernels: 27.2 us -> 24.9 us
  starting transfers between devices: 64 us -> 66.2 us
    all_to_all x1, waiting for transfers between devices: 17.3 us -> 9.34 us  [body(): lax.all_to_all(line.reshape(32, 8, 256), ('z', 'yl'), split_axis=0, conca...]
    ppermute x0 -> x1, waiting for transfers between devices: none -> 4.95 us  [body(): lax.ppermute(line_send, ('yh', 'yl'), [(y, 3 - y) for y in range(4)])]
    ppermute x0 -> x1, starting transfers between devices: none -> 3.11 us  [body(): lax.ppermute(line_send, ('yh', 'yl'), [(y, 3 - y) for y in range(4)])]
    ppermute x3, waiting for transfers between devices: 11 us -> 8.89 us  [body(): lax.ppermute(terms[step], 'x', [(x, (x + step) % 4) for x in range(4)])]
  transfers between devices with their start and end apart: 16 -> 17, of which waited for: 9 -> 9; matrix products, arithmetic and copies ran while one was open for 2% -> 2% of each run, Pallas kernels for 10% -> 15%
where the time goes in v6:
time: 153 us; the launch traced here: 152 us
  starting transfers between devices  66.2 us (43%)
  waiting for transfers between devices  54.9 us (36%)
  Pallas kernels  24.9 us (16%)
  matrix products  2.82 us (2%)
  local copies, waits for them, and re-layouts  1.54 us (1%)
    all_to_all x1, starting transfers between devices, body(): lax.all_to_all(sent.reshape(64, 8, 1024), seq, split_axis=0, concat_axis=...  16.5 us
    ppermute x3, waiting for transfers between devices, body(): lax.ppermute(pair, 'x', [(x, (x + step) % 4) for x in range(4)])  14.3 us
    all_to_all x1, waiting for transfers between devices, body(): lax.all_to_all(sent.reshape(64, 8, 1024), seq, split_axis=0, concat_axis=...  9.76 us
    all_to_all x1, waiting for transfers between devices, body(): lax.all_to_all(line.reshape(32, 8, 256), ('z', 'yl'), split_axis=0, conca...  9.34 us
    ppermute x3, starting transfers between devices, body(): lax.ppermute(terms[step], 'x', [(x, (x + step) % 4) for x in range(4)])  9.24 us
    ppermute x3, starting transfers between devices, body(): lax.ppermute(pair, 'x', [(x, (x + step) % 4) for x in range(4)])  9.24 us
    ppermute x3, waiting for transfers between devices, body(): lax.ppermute(terms[step], 'x', [(x, (x + step) % 4) for x in range(4)])  8.89 us
    ppermute x4, starting transfers between devices, body(): weights += [lax.ppermute(part, 'c', SWAP) for part in weights]  8.26 us
  transfers between devices with their start and end apart: 17, of which 9 were waited for; matrix products, arithmetic and copies ran while one was open for 2% of the time, Pallas kernels for 15%

profile of v6, /device:TPU:6, one launch (start us, length us, event | category | flops | bytes accessed | tf_op | source)
XLA Modules:
  0.0 151.6 jit_solution(15743572302440381665)
XLA Ops:
  0.6 1.7 %pack.1.packed_ref = bf16[128,1024]{1,0:T(8,128)(2,1)} custom-call(bf16[128,512]{1,0:T(8,128)(2,1)} %wq_ref.1, bf16[128,512]{1,0:T(8,128)(2,1)} %wk_ref.1, bf16[128,512]{1,0:T(8,128)(2,1)} %wv_ref.1, bf16[64,1024]{1,0:T(8,128)(2,1)} %wo_ref.1), custom_call_target="tpu_custom_call" | custom-call | flops 1000000000 | bytes 2000000 | tf_op jit(solution)/shard_map/pack/pallas_call | solution.py:335
  2.3 4.9 %collective-permute-start = (bf16[128,1024]{1,0:T(8,128)(2,1)}, bf16[128,1024]{1,0:T(8,128)(2,1)S(1)}, u32[]{:S(2)}, u32[]{:S(2)}) collective-permute-start(bf16[128,1024]{1,0:T(8,128)(2,1)} %pack.1.packed_ref), channel_id=1, source_target_pairs={{0,66},{2,64},{64,2},{66,0},{1,67},{3,65},{65,3},{67,1},{4,70},{6,... | collective-permute-start | bytes 786440 | tf_op jit(solution)/shard_map/weights/ppermute | solution.py:352
  7.2 2.9 %interleave.1 = bf16[512,1024]{1,0:T(8,128)(2,1)} custom-call(bf16[256,1024]{1,0:T(8,128)(2,1)} %bitcast.41, bf16[256,1024]{1,0:T(8,128)(2,1)} %bitcast.43), custom_call_target="tpu_custom_call" | custom-call | flops 540000000 | bytes 2000000 | tf_op jit(solution)/shard_map/interleave/pallas_call | solution.py:320
  10.1 0.0 copy-start.2
  10.1 16.5 %all-to-all-start = ((bf16[64,8,1024]{2,1,0:T(8,128)(2,1)}), bf16[64,8,1024]{2,1,0:T(8,128)(2,1)}, u32[]{:S(2)}, u32[]{:S(2)}) async-start(bf16[64,8,1024]{2,1,0:T(8,128)(2,1)} %bitcast.39), calls=%async_computation | async-start | bytes 2097152 | tf_op jit(solution)/shard_map/to_columns/all_to_all | solution.py:346
  26.7 0.0 copy-start.12
  26.7 0.1 iota_compare_fusion
  26.8 0.6 copy-done.12
  27.4 0.0 collective-permute-done.flipped_ref
  27.4 0.0 copy-done.2
  27.4 0.0 copy-start
  27.4 3.3 %collective-permute-start.3 = (bf16[2,128,1024]{2,1,0:T(8,128)(2,1)S(1)}, bf16[2,128,1024]{2,1,0:T(8,128)(2,1)S(1)}, u32[]{:S(2)}, u32[]{:S(2)}) collective-permute-start(bf16[2,128,1024]{2,1,0:T(8,128)(2,1)S(1)} %pair.1.refs_0_), channel_id=1, source_target_pairs={{0,256},{128,384},{256,0},{384,128},{1,257},{129,385},{257,1},{385... | collective-permute-start | bytes 1572872 | tf_op jit(solution)/shard_map/weights/ppermute | solution.py:363
  30.7 4.0 %collective-permute-start.2 = (bf16[2,128,1024]{2,1,0:T(8,128)(2,1)S(1)}, bf16[2,128,1024]{2,1,0:T(8,128)(2,1)S(1)}, u32[]{:S(2)}, u32[]{:S(2)}) collective-permute-start(bf16[2,128,1024]{2,1,0:T(8,128)(2,1)S(1)} %pair.1.refs_0_), channel_id=1, source_target_pairs={{0,128},{128,256},{256,384},{384,0},{1,129},{129,257},{257,385},{3... | collective-permute-start | bytes 1572872 | tf_op jit(solution)/shard_map/weights/ppermute | solution.py:363
  34.8 1.9 %collective-permute-start.1 = (bf16[2,128,1024]{2,1,0:T(8,128)(2,1)S(1)}, bf16[2,128,1024]{2,1,0:T(8,128)(2,1)S(1)}, u32[]{:S(2)}, u32[]{:S(2)}) collective-permute-start(bf16[2,128,1024]{2,1,0:T(8,128)(2,1)S(1)} %pair.1.refs_0_), channel_id=1, source_target_pairs={{0,384},{128,0},{256,128},{384,256},{1,385},{129,1},{257,129},{385... | collective-permute-start | bytes 1572872 | tf_op jit(solution)/shard_map/weights/ppermute | solution.py:363
  36.7 0.1 copy.12
  36.8 1.4 fusion.6.bias_ref
  38.2 0.0 copy-done.13
  38.2 1.4 fusion.3.bias_ref
  39.6 0.0 copy-done
  39.6 1.9 %collective-permute-start.4 = (bf16[2,128,1024]{2,1,0:T(8,128)(2,1)S(1)}, bf16[2,128,1024]{2,1,0:T(8,128)(2,1)S(1)}, u32[]{:S(2)}, u32[]{:S(2)}) collective-permute-start(bf16[2,128,1024]{2,1,0:T(8,128)(2,1)S(1)} %pair.1.refs_0_), channel_id=1, source_target_pairs={{0,1},{1,0},{2,3},{3,2},{4,5},{5,4},{6,7},{7,6},{8,9},{9,8},{10,11... | collective-permute-start | bytes 1572872 | tf_op jit(solution)/shard_map/weights/ppermute | solution.py:366
  41.6 14.3 %collective-permute-done.1.refs_3_ = bf16[2,128,1024]{2,1,0:T(8,128)(2,1)S(1)} collective-permute-done((bf16[2,128,1024]{2,1,0:T(8,128)(2,1)S(1)}, bf16[2,128,1024]{2,1,0:T(8,128)(2,1)S(1)}, u32[]{:S(2)}, u32[]{:S(2)}) %collective-permute-start.1) | collective-permute-done | bytes 524320 | tf_op jit(solution)/shard_map/weights/ppermute | solution.py:363
  55.9 0.0 collective-permute-done.3.refs_2_
  55.9 2.0 %collective-permute-start.6 = (bf16[2,128,1024]{2,1,0:T(8,128)(2,1)S(1)}, bf16[2,128,1024]{2,1,0:T(8,128)(2,1)S(1)}, u32[]{:S(2)}, u32[]{:S(2)}) collective-permute-start(bf16[2,128,1024]{2,1,0:T(8,128)(2,1)S(1)} %collective-permute-done.3.refs_2_), channel_id=1, source_target_pairs={{0,1},{1,0},{2,3},{3,2},{4,5},{5,4},{6,7},{7,6},{8,9},{9,8},{10,11... | collective-permute-start | bytes 1572872 | tf_op jit(solution)/shard_map/weights/ppermute | solution.py:366
  57.9 0.0 collective-permute-done.2.refs_1_
  57.9 0.0 copy-start.6
  57.9 2.3 %collective-permute-start.5 = (bf16[2,128,1024]{2,1,0:T(8,128)(2,1)S(1)}, bf16[2,128,1024]{2,1,0:T(8,128)(2,1)S(1)}, u32[]{:S(2)}, u32[]{:S(2)}) collective-permute-start(bf16[2,128,1024]{2,1,0:T(8,128)(2,1)S(1)} %collective-permute-done.2.refs_1_), channel_id=1, source_target_pairs={{0,1},{1,0},{2,3},{3,2},{4,5},{5,4},{6,7},{7,6},{8,9},{9,8},{10,11... | collective-permute-start | bytes 1572872 | tf_op jit(solution)/shard_map/weights/ppermute | solution.py:366
  60.2 2.0 %collective-permute-start.7 = (bf16[2,128,1024]{2,1,0:T(8,128)(2,1)S(1)}, bf16[2,128,1024]{2,1,0:T(8,128)(2,1)S(1)}, u32[]{:S(2)}, u32[]{:S(2)}) collective-permute-start(bf16[2,128,1024]{2,1,0:T(8,128)(2,1)S(1)} %collective-permute-done.1.refs_3_), channel_id=1, source_target_pairs={{0,1},{1,0},{2,3},{3,2},{4,5},{5,4},{6,7},{7,6},{8,9},{9,8},{10,11... | collective-permute-start | bytes 1572872 | tf_op jit(solution)/shard_map/weights/ppermute | solution.py:366
  62.3 0.0 collective-permute-done.4.refs_4_
  62.3 0.0 copy-start.8
  62.3 0.0 collective-permute-done.6.refs_6_
  62.3 0.0 copy-start.9
  62.3 0.0 collective-permute-done.5.refs_5_
  62.3 0.0 copy-start.10
  62.3 1.7 %collective-permute-done.7.refs_7_ = bf16[2,128,1024]{2,1,0:T(8,128)(2,1)S(1)} collective-permute-done((bf16[2,128,1024]{2,1,0:T(8,128)(2,1)S(1)}, bf16[2,128,1024]{2,1,0:T(8,128)(2,1)S(1)}, u32[]{:S(2)}, u32[]{:S(2)}) %collective-permute-start.7) | collective-permute-done | bytes 524320 | tf_op jit(solution)/shard_map/weights/ppermute | solution.py:366
  64.0 0.0 copy-done.8
  64.1 0.0 copy-done.9
  64.1 0.0 copy-done.10
  64.1 0.0 copy-start.11
  64.1 0.8 copy-done.11
  64.9 5.9 %row_heads.1 = (bf16[256,1024]{1,0:T(8,128)(2,1)}, bf16[512,512]{1,0:T(8,128)(2,1)}, bf16[512,512]{1,0:T(8,128)(2,1)}) custom-call(bf16[256,1024]{1,0:T(8,128)(2,1)} %bitcast.42, bf16[256,1024]{1,0:T(8,128)(2,1)} %bitcast.44, bf16[4,256,256]{2,1,0:T(8,128)(2,1)} %fusion.6.bias_ref, bf16[2,128,1024]{2,1,0:T(8,128)(2,1)} %copy-done, ...), custom_call_target="tpu_custom_call" | custom-call | flops 1400000000 | bytes 12000000 | tf_op jit(solution)/shard_map/row_heads/pallas_call | solution.py:367
  70.8 2.0 %collective-permute-start.8 = (bf16[512,512]{1,0:T(8,128)(2,1)}, bf16[512,512]{1,0:T(8,128)(2,1)S(1)}, u32[]{:S(2)}, u32[]{:S(2)}) collective-permute-start(bf16[512,512]{1,0:T(8,128)(2,1)} %get-tuple-element.32), channel_id=1, source_target_pairs={{0,1},{1,0},{2,3},{3,2},{4,5},{5,4},{6,7},{7,6},{8,9},{9,8},{10,11... | collective-permute-start | bytes 1572872 | tf_op jit(solution)/shard_map/ppermute | solution.py:383
  72.9 9.8 %all-to-all-done = bf16[64,8,1024]{2,1,0:T(8,128)(2,1)} async-done(((bf16[64,8,1024]{2,1,0:T(8,128)(2,1)}), bf16[64,8,1024]{2,1,0:T(8,128)(2,1)}, u32[]{:S(2)}, u32[]{:S(2)}) %all-to-all-start) | async-done | bytes 1048608 | tf_op jit(solution)/shard_map/to_columns/all_to_all | solution.py:346
  82.6 6.7 %column_heads.1 = (bf16[512,512]{1,0:T(8,128)(2,1)}, bf16[512,512]{1,0:T(8,128)(2,1)}, bf16[512,512]{1,0:T(8,128)(2,1)}) custom-call(bf16[512,1024]{1,0:T(8,128)(2,1)} %bitcast.11.both_ref, bf16[4,256,256]{2,1,0:T(8,128)(2,1)} %fusion.3.bias_ref, bf16[2,128,1024]{2,1,0:T(8,128)(2,1)} %copy-done, bf16[2,128,1024]{2,1,0:T(8,128)(2,1)} %copy-done.6, ...), custom_call_target="tpu_custom_call" | custom-call | flops 1900000000 | bytes 8000000 | tf_op jit(solution)/shard_map/column_heads/pallas_call | solution.py:385
  89.4 1.9 %collective-permute-start.9 = (bf16[512,512]{1,0:T(8,128)(2,1)}, bf16[512,512]{1,0:T(8,128)(2,1)S(1)}, u32[]{:S(2)}, u32[]{:S(2)}) collective-permute-start(bf16[512,512]{1,0:T(8,128)(2,1)} %get-tuple-element.36), channel_id=1, source_target_pairs={{0,1},{1,0},{2,3},{3,2},{4,5},{5,4},{6,7},{7,6},{8,9},{9,8},{10,11... | collective-permute-start | bytes 1572872 | tf_op jit(solution)/shard_map/ppermute | solution.py:404
  91.3 0.0 copy-start.1
  91.3 4.8 %all-to-all-start.1 = ((bf16[64,8,512]{2,1,0:T(8,128)(2,1)}), bf16[64,8,512]{2,1,0:T(8,128)(2,1)S(1)}, u32[]{:S(2)}, u32[]{:S(2)}) async-start(bf16[64,8,512]{2,1,0:T(8,128)(2,1)} %bitcast.45), calls=%async_computation.1 | async-start | bytes 1048576 | tf_op jit(solution)/shard_map/from_columns/all_to_all | solution.py:406
  96.1 0.0 collective-permute-done.8.row_got
  96.1 0.0 collective-permute-done.9.col_got
  96.1 0.3 pick.1
  96.4 3.3 %collective-permute-start.10 = (bf16[128,1024]{1,0:T(8,128)(2,1)S(1)}, bf16[128,1024]{1,0:T(8,128)(2,1)S(1)}, u32[]{:S(2)}, u32[]{:S(2)}) collective-permute-start(bf16[128,1024]{1,0:T(8,128)(2,1)S(1)} %get-tuple-element.38), channel_id=1, source_target_pairs={{0,256},{128,384},{256,0},{384,128},{1,257},{129,385},{257,1},{385... | collective-permute-start | bytes 786440 | tf_op jit(solution)/shard_map/gradient_sums/ppermute | solution.py:421
  99.7 4.0 %collective-permute-start.11 = (bf16[128,1024]{1,0:T(8,128)(2,1)S(1)}, bf16[128,1024]{1,0:T(8,128)(2,1)S(1)}, u32[]{:S(2)}, u32[]{:S(2)}) collective-permute-start(bf16[128,1024]{1,0:T(8,128)(2,1)S(1)} %get-tuple-element.39), channel_id=1, source_target_pairs={{0,128},{128,256},{256,384},{384,0},{1,129},{129,257},{257,385},{3... | collective-permute-start | bytes 786440 | tf_op jit(solution)/shard_map/gradient_sums/ppermute | solution.py:421
  103.7 1.9 %collective-permute-start.12 = (bf16[128,1024]{1,0:T(8,128)(2,1)S(1)}, bf16[128,1024]{1,0:T(8,128)(2,1)S(1)}, u32[]{:S(2)}, u32[]{:S(2)}) collective-permute-start(bf16[128,1024]{1,0:T(8,128)(2,1)S(1)} %get-tuple-element.40), channel_id=1, source_target_pairs={{0,384},{128,0},{256,128},{384,256},{1,385},{129,1},{257,129},{385... | collective-permute-start | bytes 786440 | tf_op jit(solution)/shard_map/gradient_sums/ppermute | solution.py:421
  105.7 2.7 %collective-permute-done.10.refs_1_ = bf16[128,1024]{1,0:T(8,128)(2,1)S(1)} collective-permute-done((bf16[128,1024]{1,0:T(8,128)(2,1)S(1)}, bf16[128,1024]{1,0:T(8,128)(2,1)S(1)}, u32[]{:S(2)}, u32[]{:S(2)}) %collective-permute-start.10) | collective-permute-done | bytes 262176 | tf_op jit(solution)/shard_map/gradient_sums/ppermute | solution.py:421
  108.3 3.2 %collective-permute-done.11.refs_2_ = bf16[128,1024]{1,0:T(8,128)(2,1)S(1)} collective-permute-done((bf16[128,1024]{1,0:T(8,128)(2,1)S(1)}, bf16[128,1024]{1,0:T(8,128)(2,1)S(1)}, u32[]{:S(2)}, u32[]{:S(2)}) %collective-permute-start.11) | collective-permute-done | bytes 262176 | tf_op jit(solution)/shard_map/gradient_sums/ppermute | solution.py:421
  111.5 3.1 %collective-permute-done.12.refs_3_ = bf16[128,1024]{1,0:T(8,128)(2,1)S(1)} collective-permute-done((bf16[128,1024]{1,0:T(8,128)(2,1)S(1)}, bf16[128,1024]{1,0:T(8,128)(2,1)S(1)}, u32[]{:S(2)}, u32[]{:S(2)}) %collective-permute-start.12) | collective-permute-done | bytes 262176 | tf_op jit(solution)/shard_map/gradient_sums/ppermute | solution.py:421
  114.6 0.2 spread.1
  114.8 3.1 %collective-permute-start.13 = (bf16[64,1024]{1,0:T(8,128)(2,1)S(1)}, bf16[64,1024]{1,0:T(8,128)(2,1)S(1)}, u32[]{:S(2)}, u32[]{:S(2)}) collective-permute-start(bf16[64,1024]{1,0:T(8,128)(2,1)S(1)} %get-tuple-element.42), channel_id=1, source_target_pairs={{0,66},{2,64},{64,2},{66,0},{1,67},{3,65},{65,3},{67,1},{4,70},{6,... | collective-permute-start | bytes 393224 | tf_op jit(solution)/shard_map/gradient_sums/ppermute | solution.py:434
  117.9 5.0 %collective-permute-done.13.got_ref = bf16[64,1024]{1,0:T(8,128)(2,1)S(1)} collective-permute-done((bf16[64,1024]{1,0:T(8,128)(2,1)S(1)}, bf16[64,1024]{1,0:T(8,128)(2,1)S(1)}, u32[]{:S(2)}, u32[]{:S(2)}) %collective-permute-start.13) | collective-permute-done | bytes 131104 | tf_op jit(solution)/shard_map/gradient_sums/ppermute | solution.py:434
  122.9 1.0 line.1
  123.8 6.0 %all-to-all-done.1 = bf16[64,8,512]{2,1,0:T(8,128)(2,1)S(1)} async-done(((bf16[64,8,512]{2,1,0:T(8,128)(2,1)}), bf16[64,8,512]{2,1,0:T(8,128)(2,1)S(1)}, u32[]{:S(2)}, u32[]{:S(2)}) %all-to-all-start.1) | async-done | bytes 524320 | tf_op jit(solution)/shard_map/from_columns/all_to_all | solution.py:406
  129.8 6.2 %all-to-all-start.2 = ((bf16[32,8,256]{2,1,0:T(8,128)(2,1)}), bf16[32,8,256]{2,1,0:T(8,128)(2,1)S(1)}, u32[]{:S(2)}, u32[]{:S(2)}) async-start(bf16[32,8,256]{2,1,0:T(8,128)(2,1)} %bitcast.16), calls=%async_computation.2 | async-start | bytes 262144 | tf_op jit(solution)/shard_map/gradient_sums/all_to_all | solution.py:445
  136.0 5.6 %output_products.1 = (bf16[256,1024]{1,0:T(8,128)(2,1)}, bf16[256,1024]{1,0:T(8,128)(2,1)}) custom-call(bf16[256,1024]{1,0:T(8,128)(2,1)} %get-tuple-element.29.row_ref, bf16[512,512]{1,0:T(8,128)(2,1)} %bitcast.40, bf16[2,128,1024]{2,1,0:T(8,128)(2,1)} %copy-done, bf16[2,128,1024]{2,1,0:T(8,128)(2,1)} %copy-done.6, bf16[2,128,1024]{2,1,0:T(8,128)(2,1)} %copy-done.5, ...), custom_call_target="tpu_custom_call" | custom-call | flops 1200000000 | bytes 8000000 | tf_op jit(solution)/shard_map/output_products/pallas_call | solution.py:458
  141.6 9.3 %all-to-all-done.2 = bf16[32,8,256]{2,1,0:T(8,128)(2,1)S(1)} async-done(((bf16[32,8,256]{2,1,0:T(8,128)(2,1)}), bf16[32,8,256]{2,1,0:T(8,128)(2,1)S(1)}, u32[]{:S(2)}, u32[]{:S(2)}) %all-to-all-start.2) | async-done | bytes 131104 | tf_op jit(solution)/shard_map/gradient_sums/all_to_all | solution.py:445
  150.9 0.6 last.1
  (16 shorter events, 0.1 us)
Async XLA Ops:
  2.3 25.1 %collective-permute-start = (bf16[128,1024]{1,0:T(8,128)(2,1)}, bf16[128,1024]{1,0:T(8,128)(2,1)S(1)}, u32[]{:S(2)}, u32[]{:S(2)}) collective-permute-start(bf16[128,1024]{1,0:T(8,128)(2,1)} %pack.1.packed_ref), channel_id=1, source_target_pairs={{0,66},{2,64},{64,2},{66,0},{1,67},{3,65},{65,3},{67,1},{4,70},{6,... | collective-permute-start | bytes 786440 | tf_op jit(solution)/shard_map/weights/ppermute | solution.py:352
  10.1 17.2 %copy-start.2 = (bf16[128,1024]{1,0:T(8,128)(2,1)S(1)}, bf16[128,1024]{1,0:T(8,128)(2,1)}, u32[]{:S(2)}) copy-start(bf16[128,1024]{1,0:T(8,128)(2,1)} %pack.1.packed_ref) | copy-start | bytes 786436
  10.1 72.5 %all-to-all-start = ((bf16[64,8,1024]{2,1,0:T(8,128)(2,1)}), bf16[64,8,1024]{2,1,0:T(8,128)(2,1)}, u32[]{:S(2)}, u32[]{:S(2)}) async-start(bf16[64,8,1024]{2,1,0:T(8,128)(2,1)} %bitcast.39), calls=%async_computation | async-start | bytes 2097152 | tf_op jit(solution)/shard_map/to_columns/all_to_all | solution.py:346
  26.7 0.7 copy-start.12
  27.4 12.2 %copy-start = (bf16[2,128,1024]{2,1,0:T(8,128)(2,1)}, bf16[2,128,1024]{2,1,0:T(8,128)(2,1)S(1)}, u32[]{:S(2)}) copy-start(bf16[2,128,1024]{2,1,0:T(8,128)(2,1)S(1)} %pair.1.refs_0_) | copy-start | bytes 1572868
  27.4 28.4 %collective-permute-start.3 = (bf16[2,128,1024]{2,1,0:T(8,128)(2,1)S(1)}, bf16[2,128,1024]{2,1,0:T(8,128)(2,1)S(1)}, u32[]{:S(2)}, u32[]{:S(2)}) collective-permute-start(bf16[2,128,1024]{2,1,0:T(8,128)(2,1)S(1)} %pair.1.refs_0_), channel_id=1, source_target_pairs={{0,256},{128,384},{256,0},{384,128},{1,257},{129,385},{257,1},{385... | collective-permute-start | bytes 1572872 | tf_op jit(solution)/shard_map/weights/ppermute | solution.py:363
  30.7 27.2 %collective-permute-start.2 = (bf16[2,128,1024]{2,1,0:T(8,128)(2,1)S(1)}, bf16[2,128,1024]{2,1,0:T(8,128)(2,1)S(1)}, u32[]{:S(2)}, u32[]{:S(2)}) collective-permute-start(bf16[2,128,1024]{2,1,0:T(8,128)(2,1)S(1)} %pair.1.refs_0_), channel_id=1, source_target_pairs={{0,128},{128,256},{256,384},{384,0},{1,129},{129,257},{257,385},{3... | collective-permute-start | bytes 1572872 | tf_op jit(solution)/shard_map/weights/ppermute | solution.py:363
  34.8 21.1 %collective-permute-start.1 = (bf16[2,128,1024]{2,1,0:T(8,128)(2,1)S(1)}, bf16[2,128,1024]{2,1,0:T(8,128)(2,1)S(1)}, u32[]{:S(2)}, u32[]{:S(2)}) collective-permute-start(bf16[2,128,1024]{2,1,0:T(8,128)(2,1)S(1)} %pair.1.refs_0_), channel_id=1, source_target_pairs={{0,384},{128,0},{256,128},{384,256},{1,385},{129,1},{257,129},{385... | collective-permute-start | bytes 1572872 | tf_op jit(solution)/shard_map/weights/ppermute | solution.py:363
  36.8 1.4 copy-start.13
  39.6 22.6 %collective-permute-start.4 = (bf16[2,128,1024]{2,1,0:T(8,128)(2,1)S(1)}, bf16[2,128,1024]{2,1,0:T(8,128)(2,1)S(1)}, u32[]{:S(2)}, u32[]{:S(2)}) collective-permute-start(bf16[2,128,1024]{2,1,0:T(8,128)(2,1)S(1)} %pair.1.refs_0_), channel_id=1, source_target_pairs={{0,1},{1,0},{2,3},{3,2},{4,5},{5,4},{6,7},{7,6},{8,9},{9,8},{10,11... | collective-permute-start | bytes 1572872 | tf_op jit(solution)/shard_map/weights/ppermute | solution.py:366
  55.9 8.2 %copy-start.7 = (bf16[2,128,1024]{2,1,0:T(8,128)(2,1)}, bf16[2,128,1024]{2,1,0:T(8,128)(2,1)S(1)}, u32[]{:S(2)}) copy-start(bf16[2,128,1024]{2,1,0:T(8,128)(2,1)S(1)} %collective-permute-done.1.refs_3_) | copy-start | bytes 1572868
  55.9 8.2 %copy-start.5 = (bf16[2,128,1024]{2,1,0:T(8,128)(2,1)}, bf16[2,128,1024]{2,1,0:T(8,128)(2,1)S(1)}, u32[]{:S(2)}) copy-start(bf16[2,128,1024]{2,1,0:T(8,128)(2,1)S(1)} %collective-permute-done.3.refs_2_) | copy-start | bytes 1572868
  55.9 6.4 %collective-permute-start.6 = (bf16[2,128,1024]{2,1,0:T(8,128)(2,1)S(1)}, bf16[2,128,1024]{2,1,0:T(8,128)(2,1)S(1)}, u32[]{:S(2)}, u32[]{:S(2)}) collective-permute-start(bf16[2,128,1024]{2,1,0:T(8,128)(2,1)S(1)} %collective-permute-done.3.refs_2_), channel_id=1, source_target_pairs={{0,1},{1,0},{2,3},{3,2},{4,5},{5,4},{6,7},{7,6},{8,9},{9,8},{10,11... | collective-permute-start | bytes 1572872 | tf_op jit(solution)/shard_map/weights/ppermute | solution.py:366
  57.9 6.1 %copy-start.6 = (bf16[2,128,1024]{2,1,0:T(8,128)(2,1)}, bf16[2,128,1024]{2,1,0:T(8,128)(2,1)S(1)}, u32[]{:S(2)}) copy-start(bf16[2,128,1024]{2,1,0:T(8,128)(2,1)S(1)} %collective-permute-done.2.refs_1_) | copy-start | bytes 1572868
  57.9 4.4 %collective-permute-start.5 = (bf16[2,128,1024]{2,1,0:T(8,128)(2,1)S(1)}, bf16[2,128,1024]{2,1,0:T(8,128)(2,1)S(1)}, u32[]{:S(2)}, u32[]{:S(2)}) collective-permute-start(bf16[2,128,1024]{2,1,0:T(8,128)(2,1)S(1)} %collective-permute-done.2.refs_1_), channel_id=1, source_target_pairs={{0,1},{1,0},{2,3},{3,2},{4,5},{5,4},{6,7},{7,6},{8,9},{9,8},{10,11... | collective-permute-start | bytes 1572872 | tf_op jit(solution)/shard_map/weights/ppermute | solution.py:366
  60.2 3.8 %collective-permute-start.7 = (bf16[2,128,1024]{2,1,0:T(8,128)(2,1)S(1)}, bf16[2,128,1024]{2,1,0:T(8,128)(2,1)S(1)}, u32[]{:S(2)}, u32[]{:S(2)}) collective-permute-start(bf16[2,128,1024]{2,1,0:T(8,128)(2,1)S(1)} %collective-permute-done.1.refs_3_), channel_id=1, source_target_pairs={{0,1},{1,0},{2,3},{3,2},{4,5},{5,4},{6,7},{7,6},{8,9},{9,8},{10,11... | collective-permute-start | bytes 1572872 | tf_op jit(solution)/shard_map/weights/ppermute | solution.py:366
  62.3 1.8 %copy-start.8 = (bf16[2,128,1024]{2,1,0:T(8,128)(2,1)}, bf16[2,128,1024]{2,1,0:T(8,128)(2,1)S(1)}, u32[]{:S(2)}) copy-start(bf16[2,128,1024]{2,1,0:T(8,128)(2,1)S(1)} %collective-permute-done.4.refs_4_) | copy-start | bytes 1572868
  62.3 1.8 %copy-start.9 = (bf16[2,128,1024]{2,1,0:T(8,128)(2,1)}, bf16[2,128,1024]{2,1,0:T(8,128)(2,1)S(1)}, u32[]{:S(2)}) copy-start(bf16[2,128,1024]{2,1,0:T(8,128)(2,1)S(1)} %collective-permute-done.6.refs_6_) | copy-start | bytes 1572868
  62.3 1.7 %copy-start.10 = (bf16[2,128,1024]{2,1,0:T(8,128)(2,1)}, bf16[2,128,1024]{2,1,0:T(8,128)(2,1)S(1)}, u32[]{:S(2)}) copy-start(bf16[2,128,1024]{2,1,0:T(8,128)(2,1)S(1)} %collective-permute-done.5.refs_5_) | copy-start | bytes 1572868
  64.1 0.8 copy-start.11
  70.8 25.3 %collective-permute-start.8 = (bf16[512,512]{1,0:T(8,128)(2,1)}, bf16[512,512]{1,0:T(8,128)(2,1)S(1)}, u32[]{:S(2)}, u32[]{:S(2)}) collective-permute-start(bf16[512,512]{1,0:T(8,128)(2,1)} %get-tuple-element.32), channel_id=1, source_target_pairs={{0,1},{1,0},{2,3},{3,2},{4,5},{5,4},{6,7},{7,6},{8,9},{9,8},{10,11... | collective-permute-start | bytes 1572872 | tf_op jit(solution)/shard_map/ppermute | solution.py:383
  89.4 6.7 %collective-permute-start.9 = (bf16[512,512]{1,0:T(8,128)(2,1)}, bf16[512,512]{1,0:T(8,128)(2,1)S(1)}, u32[]{:S(2)}, u32[]{:S(2)}) collective-permute-start(bf16[512,512]{1,0:T(8,128)(2,1)} %get-tuple-element.36), channel_id=1, source_target_pairs={{0,1},{1,0},{2,3},{3,2},{4,5},{5,4},{6,7},{7,6},{8,9},{9,8},{10,11... | collective-permute-start | bytes 1572872 | tf_op jit(solution)/shard_map/ppermute | solution.py:404
  91.3 4.8 %copy-start.1 = (bf16[512,512]{1,0:T(8,128)(2,1)S(1)}, bf16[512,512]{1,0:T(8,128)(2,1)}, u32[]{:S(2)}) copy-start(bf16[512,512]{1,0:T(8,128)(2,1)} %get-tuple-element.31.row_keep) | copy-start | bytes 1572868
  91.3 4.8 %copy-start.3 = (bf16[512,512]{1,0:T(8,128)(2,1)S(1)}, bf16[512,512]{1,0:T(8,128)(2,1)}, u32[]{:S(2)}) copy-start(bf16[512,512]{1,0:T(8,128)(2,1)} %get-tuple-element.35.col_keep) | copy-start | bytes 1572868
  91.3 38.5 %all-to-all-start.1 = ((bf16[64,8,512]{2,1,0:T(8,128)(2,1)}), bf16[64,8,512]{2,1,0:T(8,128)(2,1)S(1)}, u32[]{:S(2)}, u32[]{:S(2)}) async-start(bf16[64,8,512]{2,1,0:T(8,128)(2,1)} %bitcast.45), calls=%async_computation.1 | async-start | bytes 1048576 | tf_op jit(solution)/shard_map/from_columns/all_to_all | solution.py:406
  96.4 11.9 %collective-permute-start.10 = (bf16[128,1024]{1,0:T(8,128)(2,1)S(1)}, bf16[128,1024]{1,0:T(8,128)(2,1)S(1)}, u32[]{:S(2)}, u32[]{:S(2)}) collective-permute-start(bf16[128,1024]{1,0:T(8,128)(2,1)S(1)} %get-tuple-element.38), channel_id=1, source_target_pairs={{0,256},{128,384},{256,0},{384,128},{1,257},{129,385},{257,1},{385... | collective-permute-start | bytes 786440 | tf_op jit(solution)/shard_map/gradient_sums/ppermute | solution.py:421
  99.7 11.8 %collective-permute-start.11 = (bf16[128,1024]{1,0:T(8,128)(2,1)S(1)}, bf16[128,1024]{1,0:T(8,128)(2,1)S(1)}, u32[]{:S(2)}, u32[]{:S(2)}) collective-permute-start(bf16[128,1024]{1,0:T(8,128)(2,1)S(1)} %get-tuple-element.39), channel_id=1, source_target_pairs={{0,128},{128,256},{256,384},{384,0},{1,129},{129,257},{257,385},{3... | collective-permute-start | bytes 786440 | tf_op jit(solution)/shard_map/gradient_sums/ppermute | solution.py:421
  103.7 10.8 %collective-permute-start.12 = (bf16[128,1024]{1,0:T(8,128)(2,1)S(1)}, bf16[128,1024]{1,0:T(8,128)(2,1)S(1)}, u32[]{:S(2)}, u32[]{:S(2)}) collective-permute-start(bf16[128,1024]{1,0:T(8,128)(2,1)S(1)} %get-tuple-element.40), channel_id=1, source_target_pairs={{0,384},{128,0},{256,128},{384,256},{1,385},{129,1},{257,129},{385... | collective-permute-start | bytes 786440 | tf_op jit(solution)/shard_map/gradient_sums/ppermute | solution.py:421
  114.8 8.1 %collective-permute-start.13 = (bf16[64,1024]{1,0:T(8,128)(2,1)S(1)}, bf16[64,1024]{1,0:T(8,128)(2,1)S(1)}, u32[]{:S(2)}, u32[]{:S(2)}) collective-permute-start(bf16[64,1024]{1,0:T(8,128)(2,1)S(1)} %get-tuple-element.42), channel_id=1, source_target_pairs={{0,66},{2,64},{64,2},{66,0},{1,67},{3,65},{65,3},{67,1},{4,70},{6,... | collective-permute-start | bytes 393224 | tf_op jit(solution)/shard_map/gradient_sums/ppermute | solution.py:434
  129.8 6.2 %copy-start.4 = (bf16[64,8,512]{2,1,0:T(8,128)(2,1)}, bf16[64,8,512]{2,1,0:T(8,128)(2,1)S(1)}, u32[]{:S(2)}) copy-start(bf16[64,8,512]{2,1,0:T(8,128)(2,1)S(1)} %all-to-all-done.1) | copy-start | bytes 1572868
  129.8 21.1 %all-to-all-start.2 = ((bf16[32,8,256]{2,1,0:T(8,128)(2,1)}), bf16[32,8,256]{2,1,0:T(8,128)(2,1)S(1)}, u32[]{:S(2)}, u32[]{:S(2)}) async-start(bf16[32,8,256]{2,1,0:T(8,128)(2,1)} %bitcast.16), calls=%async_computation.2 | async-start | bytes 262144 | tf_op jit(solution)/shard_map/gradient_sums/all_to_all | solution.py:445

commit v7 on v6

--- a/solution.py
+++ b/solution.py
@@ -34,6 +34,7 @@
 def eights(first, rows=256):
     row = lax.broadcasted_iota(jnp.int32, (2 * rows, rows), 0)
     col = lax.broadcasted_iota(jnp.int32, (2 * rows, rows), 1)
+    row = row ^ (256 if rows == 256 else 0)
     inside = (row & 4) == (0 if first else 4)
     return ((col == (row >> 3) * 4 + (row & 3)) & inside).astype(F32).astype(BF)
 
@@ -64,16 +65,12 @@
         copy.wait()
 
 
-def interleave_kernel(x_ref, ct_ref, sent_ref, x, ct, sent, sems):
-    pieces = [(pl.ds(i * 64, 64), pl.ds(i * 128, 128)) for i in range(4)]
-    loads, stores = [], []
-    for rows, _ in pieces:
-        loads += [(x_ref.at[rows], x.at[rows]), (ct_ref.at[rows], ct.at[rows])]
-    copies = start_copies(loads, sems)
-    for i, (rows, out) in enumerate(pieces):
-        wait_for(copies[2 * i : 2 * i + 2])
-        sent[out] = interleave(x[rows], ct[rows])
-        stores += start_copies([(sent.at[out], sent_ref.at[out])], sems, 8 + i)
+def interleave_kernel(x_ref, ct_ref, sent_ref, sent, sems):
+    stores = []
+    for i in range(4):
+        rows, out = pl.ds(i * 64, 64), pl.ds((i ^ 2) * 128, 128)
+        sent[out] = interleave(x_ref[rows], ct_ref[rows])
+        stores += start_copies([(sent.at[out], sent_ref.at[out])], sems, i)
     wait_for(stores)
 
 
@@ -239,7 +236,7 @@
     col = lax.broadcasted_iota(jnp.int32, (256, 64), 1)
     out = jnp.zeros((256, 256), F32)
     for b in range(4):
-        here = (col == (row >> 3) * 2 + (row & 1)) & ((row & 6) == 2 * b)
+        here = (col == ((row >> 3) ^ 16) * 2 + (row & 1)) & ((row & 6) == 2 * b)
         out += product(here.astype(F32).astype(BF), total[:, b * 256 : (b + 1) * 256])
     out_ref[...] = out.astype(BF)
 
@@ -320,15 +317,10 @@
     sent = pl.pallas_call(
         interleave_kernel,
         out_shape=shape(512, 1024),
-        in_specs=[HBM] * 2,
+        in_specs=[VMEM] * 2,
         out_specs=HBM,
-        scratch_shapes=[
-            buffer(256, 1024),
-            buffer(256, 1024),
-            buffer(512, 1024),
-            pltpu.SemaphoreType.DMA((12,)),
-        ],
-        compiler_params=room(60),
+        scratch_shapes=[buffer(512, 1024), pltpu.SemaphoreType.DMA((4,))],
+        compiler_params=room(16),
         cost_estimate=cost(540000000, 2000000),
         name="interleave",
     )(flat, cot_flat)
@@ -344,7 +336,7 @@
     )(w_query, w_key, w_value, w_out)
     with jax.named_scope("to_columns"):
         both = lax.all_to_all(
-            sent.reshape(64, 8, 1024), seq, split_axis=0, concat_axis=0, tiled=True
+            sent.reshape(64, 8, 1024), seq, split_axis=0, concat_axis=0, tiled=True, axis_index_groups=[[p ^ 32 for p in range(64)]]
         ).reshape(512, 1024)
     with jax.named_scope("masks"):
         row_bias, col_bias = biases(row_mask, column_mask)
@@ -404,7 +396,7 @@
     col_got = lax.ppermute(col_send, "c", SWAP)
     with jax.named_scope("from_columns"):
         returned = lax.all_to_all(
-            col_parts.reshape(64, 8, 512), seq, split_axis=0, concat_axis=0, tiled=True
+            col_parts.reshape(64, 8, 512), seq, split_axis=0, concat_axis=0, tiled=True, axis_index_groups=[[p ^ 32 for p in range(64)]]
         ).reshape(512, 512)
 
     with jax.named_scope("gradient_sums"):
@@ -443,7 +435,7 @@
         )(line_keep, line_got)
         line, returned = lax.optimization_barrier((line, returned))
         line = lax.all_to_all(
-            line.reshape(32, 8, 256), ("z", "yl"), split_axis=0, concat_axis=0, tiled=True
+            line.reshape(32, 8, 256), ("z", "yl"), split_axis=0, concat_axis=0, tiled=True, axis_index_groups=[[p ^ 16 for p in range(32)]]
         )
         grad_value, grad_output = pl.pallas_call(
             last_kernel,

time: 153 us -> 146 us (0.954)
  waiting for transfers between devices: 54.9 us -> 30.4 us
  starting transfers between devices: 66.2 us -> 85.1 us
    all_to_all x1, waiting for transfers between devices: 9.76 us -> 0.02 us  [body(): lax.all_to_all(sent.reshape(64, 8, 1024), seq, split_axis=0, concat_axis=...]
    all_to_all x1, starting transfers between devices: 4.78 us -> 14.1 us  [body(): lax.all_to_all(col_parts.reshape(64, 8, 512), seq, split_axis=0, concat_a...]
    all_to_all x1, waiting for transfers between devices: 9.34 us -> 0.17 us  [body(): lax.all_to_all(line.reshape(32, 8, 256), ('z', 'yl'), split_axis=0, conca...]
    all_to_all x1, starting transfers between devices: 6.18 us -> 12.2 us  [body(): lax.all_to_all(line.reshape(32, 8, 256), ('z', 'yl'), split_axis=0, conca...]
    all_to_all x1, waiting for transfers between devices: 5.96 us -> 0.01 us  [body(): lax.all_to_all(col_parts.reshape(64, 8, 512), seq, split_axis=0, concat_a...]
    all_to_all x1, starting transfers between devices: 16.5 us -> 19.8 us  [body(): lax.all_to_all(sent.reshape(64, 8, 1024), seq, split_axis=0, concat_axis=...]
  transfers between devices with their start and end apart: 17 -> 17, of which waited for: 9 -> 7; matrix products, arithmetic and copies ran while one was open for 2% -> 2% of each run, Pallas kernels for 15% -> 15%
where the time goes in v7:
time: 146 us; the launch traced here: 145 us
  starting transfers between devices  85.1 us (58%)
  waiting for transfers between devices  30.4 us (21%)
  Pallas kernels  23.5 us (16%)
  matrix products  2.83 us (2%)
  local copies, waits for them, and re-layouts  1.55 us (1%)
    all_to_all x1, starting transfers between devices, body(): lax.all_to_all(sent.reshape(64, 8, 1024), seq, split_axis=0, concat_axis=...  19.8 us
    ppermute x3, waiting for transfers between devices, body(): lax.ppermute(pair, 'x', [(x, (x + step) % 4) for x in range(4)])  14.5 us
    all_to_all x1, starting transfers between devices, body(): lax.all_to_all(col_parts.reshape(64, 8, 512), seq, split_axis=0, concat_a...  14.1 us
    all_to_all x1, starting transfers between devices, body(): lax.all_to_all(line.reshape(32, 8, 256), ('z', 'yl'), split_axis=0, conca...  12.2 us
    ppermute x3, starting transfers between devices, body(): lax.ppermute(pair, 'x', [(x, (x + step) % 4) for x in range(4)])  9.24 us
    ppermute x3, starting transfers between devices, body(): lax.ppermute(terms[step], 'x', [(x, (x + step) % 4) for x in range(4)])  9.24 us
    ppermute x3, waiting for transfers between devices, body(): lax.ppermute(terms[step], 'x', [(x, (x + step) % 4) for x in range(4)])  8.97 us
    ppermute x4, starting transfers between devices, body(): weights += [lax.ppermute(part, 'c', SWAP) for part in weights]  8.26 us
  transfers between devices with their start and end apart: 17, of which 7 were waited for; matrix products, arithmetic and copies ran while one was open for 2% of the time, Pallas kernels for 15%

profile of v7, /device:TPU:6, one launch (start us, length us, event | category | flops | bytes accessed | tf_op | source)
XLA Modules:
  0.0 144.6 jit_solution(15153724405060053254)
XLA Ops:
  0.6 0.0 copy-start.2
  0.6 0.0 copy-start.1
  0.7 1.7 %pack.1.packed_ref = bf16[128,1024]{1,0:T(8,128)(2,1)} custom-call(bf16[128,512]{1,0:T(8,128)(2,1)} %wq_ref.1, bf16[128,512]{1,0:T(8,128)(2,1)} %wk_ref.1, bf16[128,512]{1,0:T(8,128)(2,1)} %wv_ref.1, bf16[64,1024]{1,0:T(8,128)(2,1)} %wo_ref.1), custom_call_target="tpu_custom_call" | custom-call | flops 1000000000 | bytes 2000000 | tf_op jit(solution)/shard_map/pack/pallas_call | solution.py:327
  2.4 4.9 %collective-permute-start = (bf16[128,1024]{1,0:T(8,128)(2,1)}, bf16[128,1024]{1,0:T(8,128)(2,1)S(1)}, u32[]{:S(2)}, u32[]{:S(2)}) collective-permute-start(bf16[128,1024]{1,0:T(8,128)(2,1)} %pack.1.packed_ref), channel_id=1, source_target_pairs={{0,66},{2,64},{64,2},{66,0},{1,67},{3,65},{65,3},{67,1},{4,70},{6,... | collective-permute-start | bytes 786440 | tf_op jit(solution)/shard_map/weights/ppermute | solution.py:344
  7.3 0.0 copy-done.2
  7.3 0.0 copy-done.1
  7.4 1.4 %interleave.1 = bf16[512,1024]{1,0:T(8,128)(2,1)} custom-call(bf16[256,1024]{1,0:T(8,128)(2,1)S(1)} %bitcast.39, bf16[256,1024]{1,0:T(8,128)(2,1)S(1)} %bitcast.41), custom_call_target="tpu_custom_call" | custom-call | flops 540000000 | bytes 2000000 | tf_op jit(solution)/shard_map/interleave/pallas_call | solution.py:317
  8.8 0.0 copy-start.4
  8.8 19.8 %all-to-all-start = ((bf16[64,8,1024]{2,1,0:T(8,128)(2,1)}), bf16[64,8,1024]{2,1,0:T(8,128)(2,1)}, u32[]{:S(2)}, u32[]{:S(2)}) async-start(bf16[64,8,1024]{2,1,0:T(8,128)(2,1)} %bitcast.10), calls=%async_computation | async-start | bytes 2097152 | tf_op jit(solution)/shard_map/to_columns/all_to_all | solution.py:338
  28.7 0.0 copy-start.14
  28.7 0.1 iota_compare_fusion
  28.8 0.6 copy-done.14
  29.4 0.0 collective-permute-done.flipped_ref
  29.4 0.0 copy-done.4
  29.4 0.0 copy-start
  29.4 3.3 %collective-permute-start.3 = (bf16[2,128,1024]{2,1,0:T(8,128)(2,1)S(1)}, bf16[2,128,1024]{2,1,0:T(8,128)(2,1)S(1)}, u32[]{:S(2)}, u32[]{:S(2)}) collective-permute-start(bf16[2,128,1024]{2,1,0:T(8,128)(2,1)S(1)} %pair.1.refs_0_), channel_id=1, source_target_pairs={{0,256},{128,384},{256,0},{384,128},{1,257},{129,385},{257,1},{385... | collective-permute-start | bytes 1572872 | tf_op jit(solution)/shard_map/weights/ppermute | solution.py:355
  32.7 4.0 %collective-permute-start.2 = (bf16[2,128,1024]{2,1,0:T(8,128)(2,1)S(1)}, bf16[2,128,1024]{2,1,0:T(8,128)(2,1)S(1)}, u32[]{:S(2)}, u32[]{:S(2)}) collective-permute-start(bf16[2,128,1024]{2,1,0:T(8,128)(2,1)S(1)} %pair.1.refs_0_), channel_id=1, source_target_pairs={{0,128},{128,256},{256,384},{384,0},{1,129},{129,257},{257,385},{3... | collective-permute-start | bytes 1572872 | tf_op jit(solution)/shard_map/weights/ppermute | solution.py:355
  36.8 1.9 %collective-permute-start.1 = (bf16[2,128,1024]{2,1,0:T(8,128)(2,1)S(1)}, bf16[2,128,1024]{2,1,0:T(8,128)(2,1)S(1)}, u32[]{:S(2)}, u32[]{:S(2)}) collective-permute-start(bf16[2,128,1024]{2,1,0:T(8,128)(2,1)S(1)} %pair.1.refs_0_), channel_id=1, source_target_pairs={{0,384},{128,0},{256,128},{384,256},{1,385},{129,1},{257,129},{385... | collective-permute-start | bytes 1572872 | tf_op jit(solution)/shard_map/weights/ppermute | solution.py:355
  38.7 0.1 copy.12
  38.8 1.4 fusion.6.bias_ref
  40.2 0.0 copy-done.15
  40.2 1.5 %fusion.3.bias_ref = bf16[4,256,256]{2,1,0:T(8,128)(2,1)} fusion(pred[256,256]{1,0:T(8,128)(4,1)S(1)} %get-tuple-element.51, pred[256,256]{1,0:T(8,128)(4,1)S(1)} %get-tuple-element.50, s32[256]{0:T(256)S(1)} %get-tuple-element.53, s32[4,4,8,8]{3,2,1,0:T(8,128)S(1)} %copy-done.15, s32[256]{0:T(256)S(1)} %get-tuple-element.52), kind=kOutput, calls=%fused_computation.5 | convolution fusion | flops 6564864 | bytes 661504 | tf_op jit(solution)/shard_map/masks/ia,hab,jb->hij/dot_general | solution.py:300
  41.6 0.0 copy-done
  41.6 1.9 %collective-permute-start.4 = (bf16[2,128,1024]{2,1,0:T(8,128)(2,1)S(1)}, bf16[2,128,1024]{2,1,0:T(8,128)(2,1)S(1)}, u32[]{:S(2)}, u32[]{:S(2)}) collective-permute-start(bf16[2,128,1024]{2,1,0:T(8,128)(2,1)S(1)} %pair.1.refs_0_), channel_id=1, source_target_pairs={{0,1},{1,0},{2,3},{3,2},{4,5},{5,4},{6,7},{7,6},{8,9},{9,8},{10,11... | collective-permute-start | bytes 1572872 | tf_op jit(solution)/shard_map/weights/ppermute | solution.py:358
  43.6 14.5 %collective-permute-done.1.refs_3_ = bf16[2,128,1024]{2,1,0:T(8,128)(2,1)S(1)} collective-permute-done((bf16[2,128,1024]{2,1,0:T(8,128)(2,1)S(1)}, bf16[2,128,1024]{2,1,0:T(8,128)(2,1)S(1)}, u32[]{:S(2)}, u32[]{:S(2)}) %collective-permute-start.1) | collective-permute-done | bytes 524320 | tf_op jit(solution)/shard_map/weights/ppermute | solution.py:355
  58.0 0.0 collective-permute-done.3.refs_2_
  58.0 2.0 %collective-permute-start.6 = (bf16[2,128,1024]{2,1,0:T(8,128)(2,1)S(1)}, bf16[2,128,1024]{2,1,0:T(8,128)(2,1)S(1)}, u32[]{:S(2)}, u32[]{:S(2)}) collective-permute-start(bf16[2,128,1024]{2,1,0:T(8,128)(2,1)S(1)} %collective-permute-done.3.refs_2_), channel_id=1, source_target_pairs={{0,1},{1,0},{2,3},{3,2},{4,5},{5,4},{6,7},{7,6},{8,9},{9,8},{10,11... | collective-permute-start | bytes 1572872 | tf_op jit(solution)/shard_map/weights/ppermute | solution.py:358
  60.1 0.0 collective-permute-done.2.refs_1_
  60.1 0.0 copy-start.8
  60.1 2.3 %collective-permute-start.5 = (bf16[2,128,1024]{2,1,0:T(8,128)(2,1)S(1)}, bf16[2,128,1024]{2,1,0:T(8,128)(2,1)S(1)}, u32[]{:S(2)}, u32[]{:S(2)}) collective-permute-start(bf16[2,128,1024]{2,1,0:T(8,128)(2,1)S(1)} %collective-permute-done.2.refs_1_), channel_id=1, source_target_pairs={{0,1},{1,0},{2,3},{3,2},{4,5},{5,4},{6,7},{7,6},{8,9},{9,8},{10,11... | collective-permute-start | bytes 1572872 | tf_op jit(solution)/shard_map/weights/ppermute | solution.py:358
  62.4 2.0 %collective-permute-start.7 = (bf16[2,128,1024]{2,1,0:T(8,128)(2,1)S(1)}, bf16[2,128,1024]{2,1,0:T(8,128)(2,1)S(1)}, u32[]{:S(2)}, u32[]{:S(2)}) collective-permute-start(bf16[2,128,1024]{2,1,0:T(8,128)(2,1)S(1)} %collective-permute-done.1.refs_3_), channel_id=1, source_target_pairs={{0,1},{1,0},{2,3},{3,2},{4,5},{5,4},{6,7},{7,6},{8,9},{9,8},{10,11... | collective-permute-start | bytes 1572872 | tf_op jit(solution)/shard_map/weights/ppermute | solution.py:358
  64.4 0.0 collective-permute-done.4.refs_4_
  64.5 0.0 collective-permute-done.6.refs_6_
  64.5 0.0 collective-permute-done.5.refs_5_
  64.5 0.0 copy-start.12
  64.5 1.7 %collective-permute-done.7.refs_7_ = bf16[2,128,1024]{2,1,0:T(8,128)(2,1)S(1)} collective-permute-done((bf16[2,128,1024]{2,1,0:T(8,128)(2,1)S(1)}, bf16[2,128,1024]{2,1,0:T(8,128)(2,1)S(1)}, u32[]{:S(2)}, u32[]{:S(2)}) %collective-permute-start.7) | collective-permute-done | bytes 524320 | tf_op jit(solution)/shard_map/weights/ppermute | solution.py:358
  66.3 0.8 copy-done.13
  67.1 5.9 %row_heads.1 = (bf16[256,1024]{1,0:T(8,128)(2,1)}, bf16[512,512]{1,0:T(8,128)(2,1)}, bf16[512,512]{1,0:T(8,128)(2,1)}) custom-call(bf16[256,1024]{1,0:T(8,128)(2,1)} %bitcast.38, bf16[256,1024]{1,0:T(8,128)(2,1)} %bitcast.40, bf16[4,256,256]{2,1,0:T(8,128)(2,1)} %fusion.6.bias_ref, bf16[2,128,1024]{2,1,0:T(8,128)(2,1)} %copy-done, ...), custom_call_target="tpu_custom_call" | custom-call | flops 1400000000 | bytes 12000000 | tf_op jit(solution)/shard_map/row_heads/pallas_call | solution.py:359
  73.0 2.0 %collective-permute-start.8 = (bf16[512,512]{1,0:T(8,128)(2,1)}, bf16[512,512]{1,0:T(8,128)(2,1)S(1)}, u32[]{:S(2)}, u32[]{:S(2)}) collective-permute-start(bf16[512,512]{1,0:T(8,128)(2,1)} %get-tuple-element.32), channel_id=1, source_target_pairs={{0,1},{1,0},{2,3},{3,2},{4,5},{5,4},{6,7},{7,6},{8,9},{9,8},{10,11... | collective-permute-start | bytes 1572872 | tf_op jit(solution)/shard_map/ppermute | solution.py:375
  75.0 0.0 all-to-all-done
  75.1 6.7 %column_heads.1 = (bf16[512,512]{1,0:T(8,128)(2,1)}, bf16[512,512]{1,0:T(8,128)(2,1)}, bf16[512,512]{1,0:T(8,128)(2,1)}) custom-call(bf16[512,1024]{1,0:T(8,128)(2,1)} %bitcast.11.both_ref, bf16[4,256,256]{2,1,0:T(8,128)(2,1)} %fusion.3.bias_ref, bf16[2,128,1024]{2,1,0:T(8,128)(2,1)} %copy-done, bf16[2,128,1024]{2,1,0:T(8,128)(2,1)} %copy-done.8, ...), custom_call_target="tpu_custom_call" | custom-call | flops 1900000000 | bytes 8000000 | tf_op jit(solution)/shard_map/column_heads/pallas_call | solution.py:377
  81.8 2.3 %collective-permute-start.9 = (bf16[512,512]{1,0:T(8,128)(2,1)}, bf16[512,512]{1,0:T(8,128)(2,1)S(1)}, u32[]{:S(2)}, u32[]{:S(2)}) collective-permute-start(bf16[512,512]{1,0:T(8,128)(2,1)} %get-tuple-element.36), channel_id=1, source_target_pairs={{0,1},{1,0},{2,3},{3,2},{4,5},{5,4},{6,7},{7,6},{8,9},{9,8},{10,11... | collective-permute-start | bytes 1572872 | tf_op jit(solution)/shard_map/ppermute | solution.py:396
  84.1 0.0 copy-start.3
  84.1 14.1 %all-to-all-start.1 = ((bf16[64,8,512]{2,1,0:T(8,128)(2,1)}), bf16[64,8,512]{2,1,0:T(8,128)(2,1)S(1)}, u32[]{:S(2)}, u32[]{:S(2)}) async-start(bf16[64,8,512]{2,1,0:T(8,128)(2,1)} %bitcast.44), calls=%async_computation.1 | async-start | bytes 1048576 | tf_op jit(solution)/shard_map/from_columns/all_to_all | solution.py:398
  98.2 0.0 collective-permute-done.8.row_got
  98.2 0.0 collective-permute-done.9.col_got
  98.2 0.0 copy-done.3
  98.2 0.0 copy-done.5
  98.2 0.3 pick.1
  98.5 3.3 %collective-permute-start.10 = (bf16[128,1024]{1,0:T(8,128)(2,1)S(1)}, bf16[128,1024]{1,0:T(8,128)(2,1)S(1)}, u32[]{:S(2)}, u32[]{:S(2)}) collective-permute-start(bf16[128,1024]{1,0:T(8,128)(2,1)S(1)} %get-tuple-element.38), channel_id=1, source_target_pairs={{0,256},{128,384},{256,0},{384,128},{1,257},{129,385},{257,1},{385... | collective-permute-start | bytes 786440 | tf_op jit(solution)/shard_map/gradient_sums/ppermute | solution.py:413
  101.8 4.0 %collective-permute-start.11 = (bf16[128,1024]{1,0:T(8,128)(2,1)S(1)}, bf16[128,1024]{1,0:T(8,128)(2,1)S(1)}, u32[]{:S(2)}, u32[]{:S(2)}) collective-permute-start(bf16[128,1024]{1,0:T(8,128)(2,1)S(1)} %get-tuple-element.39), channel_id=1, source_target_pairs={{0,128},{128,256},{256,384},{384,0},{1,129},{129,257},{257,385},{3... | collective-permute-start | bytes 786440 | tf_op jit(solution)/shard_map/gradient_sums/ppermute | solution.py:413
  105.8 1.9 %collective-permute-start.12 = (bf16[128,1024]{1,0:T(8,128)(2,1)S(1)}, bf16[128,1024]{1,0:T(8,128)(2,1)S(1)}, u32[]{:S(2)}, u32[]{:S(2)}) collective-permute-start(bf16[128,1024]{1,0:T(8,128)(2,1)S(1)} %get-tuple-element.40), channel_id=1, source_target_pairs={{0,384},{128,0},{256,128},{384,256},{1,385},{129,1},{257,129},{385... | collective-permute-start | bytes 786440 | tf_op jit(solution)/shard_map/gradient_sums/ppermute | solution.py:413
  107.7 2.7 %collective-permute-done.10.refs_1_ = bf16[128,1024]{1,0:T(8,128)(2,1)S(1)} collective-permute-done((bf16[128,1024]{1,0:T(8,128)(2,1)S(1)}, bf16[128,1024]{1,0:T(8,128)(2,1)S(1)}, u32[]{:S(2)}, u32[]{:S(2)}) %collective-permute-start.10) | collective-permute-done | bytes 262176 | tf_op jit(solution)/shard_map/gradient_sums/ppermute | solution.py:413
  110.5 3.2 %collective-permute-done.11.refs_2_ = bf16[128,1024]{1,0:T(8,128)(2,1)S(1)} collective-permute-done((bf16[128,1024]{1,0:T(8,128)(2,1)S(1)}, bf16[128,1024]{1,0:T(8,128)(2,1)S(1)}, u32[]{:S(2)}, u32[]{:S(2)}) %collective-permute-start.11) | collective-permute-done | bytes 262176 | tf_op jit(solution)/shard_map/gradient_sums/ppermute | solution.py:413
  113.7 3.1 %collective-permute-done.12.refs_3_ = bf16[128,1024]{1,0:T(8,128)(2,1)S(1)} collective-permute-done((bf16[128,1024]{1,0:T(8,128)(2,1)S(1)}, bf16[128,1024]{1,0:T(8,128)(2,1)S(1)}, u32[]{:S(2)}, u32[]{:S(2)}) %collective-permute-start.12) | collective-permute-done | bytes 262176 | tf_op jit(solution)/shard_map/gradient_sums/ppermute | solution.py:413
  116.7 0.2 spread.1
  117.0 3.1 %collective-permute-start.13 = (bf16[64,1024]{1,0:T(8,128)(2,1)S(1)}, bf16[64,1024]{1,0:T(8,128)(2,1)S(1)}, u32[]{:S(2)}, u32[]{:S(2)}) collective-permute-start(bf16[64,1024]{1,0:T(8,128)(2,1)S(1)} %get-tuple-element.42), channel_id=1, source_target_pairs={{0,66},{2,64},{64,2},{66,0},{1,67},{3,65},{65,3},{67,1},{4,70},{6,... | collective-permute-start | bytes 393224 | tf_op jit(solution)/shard_map/gradient_sums/ppermute | solution.py:426
  120.0 5.0 %collective-permute-done.13.got_ref = bf16[64,1024]{1,0:T(8,128)(2,1)S(1)} collective-permute-done((bf16[64,1024]{1,0:T(8,128)(2,1)S(1)}, bf16[64,1024]{1,0:T(8,128)(2,1)S(1)}, u32[]{:S(2)}, u32[]{:S(2)}) %collective-permute-start.13) | collective-permute-done | bytes 131104 | tf_op jit(solution)/shard_map/gradient_sums/ppermute | solution.py:426
  125.0 0.9 line.1
  126.0 0.0 all-to-all-done.1
  126.0 12.2 %all-to-all-start.2 = ((bf16[32,8,256]{2,1,0:T(8,128)(2,1)}), bf16[32,8,256]{2,1,0:T(8,128)(2,1)S(1)}, u32[]{:S(2)}, u32[]{:S(2)}) async-start(bf16[32,8,256]{2,1,0:T(8,128)(2,1)} %bitcast.16), calls=%async_computation.2 | async-start | bytes 262144 | tf_op jit(solution)/shard_map/gradient_sums/all_to_all | solution.py:437
  138.2 5.6 %output_products.1 = (bf16[256,1024]{1,0:T(8,128)(2,1)}, bf16[256,1024]{1,0:T(8,128)(2,1)}) custom-call(bf16[256,1024]{1,0:T(8,128)(2,1)} %get-tuple-element.29.row_ref, bf16[512,512]{1,0:T(8,128)(2,1)} %bitcast.43, bf16[2,128,1024]{2,1,0:T(8,128)(2,1)} %copy-done, bf16[2,128,1024]{2,1,0:T(8,128)(2,1)} %copy-done.8, bf16[2,128,1024]{2,1,0:T(8,128)(2,1)} %copy-done.7, ...), custom_call_target="tpu_custom_call" | custom-call | flops 1200000000 | bytes 8000000 | tf_op jit(solution)/shard_map/output_products/pallas_call | solution.py:450
  143.8 0.2 all-to-all-done.2
  143.9 0.6 last.1
  (20 shorter events, 0.1 us)
Async XLA Ops:
  0.6 6.7 %copy-start.2 = (bf16[1,1,256,1024]{3,2,1,0:T(8,128)(2,1)S(1)}, bf16[1,1,256,1024]{3,2,1,0:T(8,128)(2,1)}, u32[]{:S(2)}) copy-start(bf16[1,1,256,1024]{3,2,1,0:T(8,128)(2,1)} %param.9) | copy-start | bytes 1572868
  0.6 6.7 %copy-start.1 = (bf16[1,1,256,1024]{3,2,1,0:T(8,128)(2,1)S(1)}, bf16[1,1,256,1024]{3,2,1,0:T(8,128)(2,1)}, u32[]{:S(2)}) copy-start(bf16[1,1,256,1024]{3,2,1,0:T(8,128)(2,1)} %param.8) | copy-start | bytes 1572868
  2.4 26.9 %collective-permute-start = (bf16[128,1024]{1,0:T(8,128)(2,1)}, bf16[128,1024]{1,0:T(8,128)(2,1)S(1)}, u32[]{:S(2)}, u32[]{:S(2)}) collective-permute-start(bf16[128,1024]{1,0:T(8,128)(2,1)} %pack.1.packed_ref), channel_id=1, source_target_pairs={{0,66},{2,64},{64,2},{66,0},{1,67},{3,65},{65,3},{67,1},{4,70},{6,... | collective-permute-start | bytes 786440 | tf_op jit(solution)/shard_map/weights/ppermute | solution.py:344
  8.8 20.5 %copy-start.4 = (bf16[128,1024]{1,0:T(8,128)(2,1)S(1)}, bf16[128,1024]{1,0:T(8,128)(2,1)}, u32[]{:S(2)}) copy-start(bf16[128,1024]{1,0:T(8,128)(2,1)} %pack.1.packed_ref) | copy-start | bytes 786436
  8.8 66.2 %all-to-all-start = ((bf16[64,8,1024]{2,1,0:T(8,128)(2,1)}), bf16[64,8,1024]{2,1,0:T(8,128)(2,1)}, u32[]{:S(2)}, u32[]{:S(2)}) async-start(bf16[64,8,1024]{2,1,0:T(8,128)(2,1)} %bitcast.10), calls=%async_computation | async-start | bytes 2097152 | tf_op jit(solution)/shard_map/to_columns/all_to_all | solution.py:338
  28.7 0.7 copy-start.14
  29.4 12.2 %copy-start = (bf16[2,128,1024]{2,1,0:T(8,128)(2,1)}, bf16[2,128,1024]{2,1,0:T(8,128)(2,1)S(1)}, u32[]{:S(2)}) copy-start(bf16[2,128,1024]{2,1,0:T(8,128)(2,1)S(1)} %pair.1.refs_0_) | copy-start | bytes 1572868
  29.4 28.6 %collective-permute-start.3 = (bf16[2,128,1024]{2,1,0:T(8,128)(2,1)S(1)}, bf16[2,128,1024]{2,1,0:T(8,128)(2,1)S(1)}, u32[]{:S(2)}, u32[]{:S(2)}) collective-permute-start(bf16[2,128,1024]{2,1,0:T(8,128)(2,1)S(1)} %pair.1.refs_0_), channel_id=1, source_target_pairs={{0,256},{128,384},{256,0},{384,128},{1,257},{129,385},{257,1},{385... | collective-permute-start | bytes 1572872 | tf_op jit(solution)/shard_map/weights/ppermute | solution.py:355
  32.7 27.3 %collective-permute-start.2 = (bf16[2,128,1024]{2,1,0:T(8,128)(2,1)S(1)}, bf16[2,128,1024]{2,1,0:T(8,128)(2,1)S(1)}, u32[]{:S(2)}, u32[]{:S(2)}) collective-permute-start(bf16[2,128,1024]{2,1,0:T(8,128)(2,1)S(1)} %pair.1.refs_0_), channel_id=1, source_target_pairs={{0,128},{128,256},{256,384},{384,0},{1,129},{129,257},{257,385},{3... | collective-permute-start | bytes 1572872 | tf_op jit(solution)/shard_map/weights/ppermute | solution.py:355
  36.8 21.3 %collective-permute-start.1 = (bf16[2,128,1024]{2,1,0:T(8,128)(2,1)S(1)}, bf16[2,128,1024]{2,1,0:T(8,128)(2,1)S(1)}, u32[]{:S(2)}, u32[]{:S(2)}) collective-permute-start(bf16[2,128,1024]{2,1,0:T(8,128)(2,1)S(1)} %pair.1.refs_0_), channel_id=1, source_target_pairs={{0,384},{128,0},{256,128},{384,256},{1,385},{129,1},{257,129},{385... | collective-permute-start | bytes 1572872 | tf_op jit(solution)/shard_map/weights/ppermute | solution.py:355
  38.8 1.4 copy-start.15
  41.6 22.8 %collective-permute-start.4 = (bf16[2,128,1024]{2,1,0:T(8,128)(2,1)S(1)}, bf16[2,128,1024]{2,1,0:T(8,128)(2,1)S(1)}, u32[]{:S(2)}, u32[]{:S(2)}) collective-permute-start(bf16[2,128,1024]{2,1,0:T(8,128)(2,1)S(1)} %pair.1.refs_0_), channel_id=1, source_target_pairs={{0,1},{1,0},{2,3},{3,2},{4,5},{5,4},{6,7},{7,6},{8,9},{9,8},{10,11... | collective-permute-start | bytes 1572872 | tf_op jit(solution)/shard_map/weights/ppermute | solution.py:358
  58.0 8.2 %copy-start.9 = (bf16[2,128,1024]{2,1,0:T(8,128)(2,1)}, bf16[2,128,1024]{2,1,0:T(8,128)(2,1)S(1)}, u32[]{:S(2)}) copy-start(bf16[2,128,1024]{2,1,0:T(8,128)(2,1)S(1)} %collective-permute-done.1.refs_3_) | copy-start | bytes 1572868
  58.0 8.2 %copy-start.7 = (bf16[2,128,1024]{2,1,0:T(8,128)(2,1)}, bf16[2,128,1024]{2,1,0:T(8,128)(2,1)S(1)}, u32[]{:S(2)}) copy-start(bf16[2,128,1024]{2,1,0:T(8,128)(2,1)S(1)} %collective-permute-done.3.refs_2_) | copy-start | bytes 1572868
  58.0 6.4 %collective-permute-start.6 = (bf16[2,128,1024]{2,1,0:T(8,128)(2,1)S(1)}, bf16[2,128,1024]{2,1,0:T(8,128)(2,1)S(1)}, u32[]{:S(2)}, u32[]{:S(2)}) collective-permute-start(bf16[2,128,1024]{2,1,0:T(8,128)(2,1)S(1)} %collective-permute-done.3.refs_2_), channel_id=1, source_target_pairs={{0,1},{1,0},{2,3},{3,2},{4,5},{5,4},{6,7},{7,6},{8,9},{9,8},{10,11... | collective-permute-start | bytes 1572872 | tf_op jit(solution)/shard_map/weights/ppermute | solution.py:358
  60.1 6.1 %copy-start.8 = (bf16[2,128,1024]{2,1,0:T(8,128)(2,1)}, bf16[2,128,1024]{2,1,0:T(8,128)(2,1)S(1)}, u32[]{:S(2)}) copy-start(bf16[2,128,1024]{2,1,0:T(8,128)(2,1)S(1)} %collective-permute-done.2.refs_1_) | copy-start | bytes 1572868
  60.1 4.4 %collective-permute-start.5 = (bf16[2,128,1024]{2,1,0:T(8,128)(2,1)S(1)}, bf16[2,128,1024]{2,1,0:T(8,128)(2,1)S(1)}, u32[]{:S(2)}, u32[]{:S(2)}) collective-permute-start(bf16[2,128,1024]{2,1,0:T(8,128)(2,1)S(1)} %collective-permute-done.2.refs_1_), channel_id=1, source_target_pairs={{0,1},{1,0},{2,3},{3,2},{4,5},{5,4},{6,7},{7,6},{8,9},{9,8},{10,11... | collective-permute-start | bytes 1572872 | tf_op jit(solution)/shard_map/weights/ppermute | solution.py:358
  62.4 3.8 %collective-permute-start.7 = (bf16[2,128,1024]{2,1,0:T(8,128)(2,1)S(1)}, bf16[2,128,1024]{2,1,0:T(8,128)(2,1)S(1)}, u32[]{:S(2)}, u32[]{:S(2)}) collective-permute-start(bf16[2,128,1024]{2,1,0:T(8,128)(2,1)S(1)} %collective-permute-done.1.refs_3_), channel_id=1, source_target_pairs={{0,1},{1,0},{2,3},{3,2},{4,5},{5,4},{6,7},{7,6},{8,9},{9,8},{10,11... | collective-permute-start | bytes 1572872 | tf_op jit(solution)/shard_map/weights/ppermute | solution.py:358
  64.4 1.8 %copy-start.10 = (bf16[2,128,1024]{2,1,0:T(8,128)(2,1)}, bf16[2,128,1024]{2,1,0:T(8,128)(2,1)S(1)}, u32[]{:S(2)}) copy-start(bf16[2,128,1024]{2,1,0:T(8,128)(2,1)S(1)} %collective-permute-done.4.refs_4_) | copy-start | bytes 1572868
  64.5 1.8 %copy-start.11 = (bf16[2,128,1024]{2,1,0:T(8,128)(2,1)}, bf16[2,128,1024]{2,1,0:T(8,128)(2,1)S(1)}, u32[]{:S(2)}) copy-start(bf16[2,128,1024]{2,1,0:T(8,128)(2,1)S(1)} %collective-permute-done.6.refs_6_) | copy-start | bytes 1572868
  64.5 1.7 %copy-start.12 = (bf16[2,128,1024]{2,1,0:T(8,128)(2,1)}, bf16[2,128,1024]{2,1,0:T(8,128)(2,1)S(1)}, u32[]{:S(2)}) copy-start(bf16[2,128,1024]{2,1,0:T(8,128)(2,1)S(1)} %collective-permute-done.5.refs_5_) | copy-start | bytes 1572868
  66.2 0.8 copy-start.13
  73.0 25.2 %collective-permute-start.8 = (bf16[512,512]{1,0:T(8,128)(2,1)}, bf16[512,512]{1,0:T(8,128)(2,1)S(1)}, u32[]{:S(2)}, u32[]{:S(2)}) collective-permute-start(bf16[512,512]{1,0:T(8,128)(2,1)} %get-tuple-element.32), channel_id=1, source_target_pairs={{0,1},{1,0},{2,3},{3,2},{4,5},{5,4},{6,7},{7,6},{8,9},{9,8},{10,11... | collective-permute-start | bytes 1572872 | tf_op jit(solution)/shard_map/ppermute | solution.py:375
  81.8 16.4 %collective-permute-start.9 = (bf16[512,512]{1,0:T(8,128)(2,1)}, bf16[512,512]{1,0:T(8,128)(2,1)S(1)}, u32[]{:S(2)}, u32[]{:S(2)}) collective-permute-start(bf16[512,512]{1,0:T(8,128)(2,1)} %get-tuple-element.36), channel_id=1, source_target_pairs={{0,1},{1,0},{2,3},{3,2},{4,5},{5,4},{6,7},{7,6},{8,9},{9,8},{10,11... | collective-permute-start | bytes 1572872 | tf_op jit(solution)/shard_map/ppermute | solution.py:396
  84.1 14.1 %copy-start.3 = (bf16[512,512]{1,0:T(8,128)(2,1)S(1)}, bf16[512,512]{1,0:T(8,128)(2,1)}, u32[]{:S(2)}) copy-start(bf16[512,512]{1,0:T(8,128)(2,1)} %get-tuple-element.31.row_keep) | copy-start | bytes 1572868
  84.1 14.1 %copy-start.5 = (bf16[512,512]{1,0:T(8,128)(2,1)S(1)}, bf16[512,512]{1,0:T(8,128)(2,1)}, u32[]{:S(2)}) copy-start(bf16[512,512]{1,0:T(8,128)(2,1)} %get-tuple-element.35.col_keep) | copy-start | bytes 1572868
  84.1 41.9 %all-to-all-start.1 = ((bf16[64,8,512]{2,1,0:T(8,128)(2,1)}), bf16[64,8,512]{2,1,0:T(8,128)(2,1)S(1)}, u32[]{:S(2)}, u32[]{:S(2)}) async-start(bf16[64,8,512]{2,1,0:T(8,128)(2,1)} %bitcast.44), calls=%async_computation.1 | async-start | bytes 1048576 | tf_op jit(solution)/shard_map/from_columns/all_to_all | solution.py:398
  98.5 12.0 %collective-permute-start.10 = (bf16[128,1024]{1,0:T(8,128)(2,1)S(1)}, bf16[128,1024]{1,0:T(8,128)(2,1)S(1)}, u32[]{:S(2)}, u32[]{:S(2)}) collective-permute-start(bf16[128,1024]{1,0:T(8,128)(2,1)S(1)} %get-tuple-element.38), channel_id=1, source_target_pairs={{0,256},{128,384},{256,0},{384,128},{1,257},{129,385},{257,1},{385... | collective-permute-start | bytes 786440 | tf_op jit(solution)/shard_map/gradient_sums/ppermute | solution.py:413
  101.8 11.9 %collective-permute-start.11 = (bf16[128,1024]{1,0:T(8,128)(2,1)S(1)}, bf16[128,1024]{1,0:T(8,128)(2,1)S(1)}, u32[]{:S(2)}, u32[]{:S(2)}) collective-permute-start(bf16[128,1024]{1,0:T(8,128)(2,1)S(1)} %get-tuple-element.39), channel_id=1, source_target_pairs={{0,128},{128,256},{256,384},{384,0},{1,129},{129,257},{257,385},{3... | collective-permute-start | bytes 786440 | tf_op jit(solution)/shard_map/gradient_sums/ppermute | solution.py:413
  105.8 10.9 %collective-permute-start.12 = (bf16[128,1024]{1,0:T(8,128)(2,1)S(1)}, bf16[128,1024]{1,0:T(8,128)(2,1)S(1)}, u32[]{:S(2)}, u32[]{:S(2)}) collective-permute-start(bf16[128,1024]{1,0:T(8,128)(2,1)S(1)} %get-tuple-element.40), channel_id=1, source_target_pairs={{0,384},{128,0},{256,128},{384,256},{1,385},{129,1},{257,129},{385... | collective-permute-start | bytes 786440 | tf_op jit(solution)/shard_map/gradient_sums/ppermute | solution.py:413
  117.0 8.1 %collective-permute-start.13 = (bf16[64,1024]{1,0:T(8,128)(2,1)S(1)}, bf16[64,1024]{1,0:T(8,128)(2,1)S(1)}, u32[]{:S(2)}, u32[]{:S(2)}) collective-permute-start(bf16[64,1024]{1,0:T(8,128)(2,1)S(1)} %get-tuple-element.42), channel_id=1, source_target_pairs={{0,66},{2,64},{64,2},{66,0},{1,67},{3,65},{65,3},{67,1},{4,70},{6,... | collective-permute-start | bytes 393224 | tf_op jit(solution)/shard_map/gradient_sums/ppermute | solution.py:426
  126.0 12.2 %copy-start.6 = (bf16[64,8,512]{2,1,0:T(8,128)(2,1)}, bf16[64,8,512]{2,1,0:T(8,128)(2,1)S(1)}, u32[]{:S(2)}) copy-start(bf16[64,8,512]{2,1,0:T(8,128)(2,1)S(1)} %all-to-all-done.1) | copy-start | bytes 1572868
  126.0 18.0 %all-to-all-start.2 = ((bf16[32,8,256]{2,1,0:T(8,128)(2,1)}), bf16[32,8,256]{2,1,0:T(8,128)(2,1)S(1)}, u32[]{:S(2)}, u32[]{:S(2)}) async-start(bf16[32,8,256]{2,1,0:T(8,128)(2,1)} %bitcast.16), calls=%async_computation.2 | async-start | bytes 262144 | tf_op jit(solution)/shard_map/gradient_sums/all_to_all | solution.py:437

commit v8 on v7

--- a/solution.py
+++ b/solution.py
@@ -24,6 +24,7 @@
 
 
 SWAP = [(0, 1), (1, 0)]
+BEGIN, BEGIN_LAST = 10, 9
 PAIR, PICK = 30000000000, 14000000000
 
 
@@ -31,18 +32,25 @@
     return lax.dot_general(a, b, dims, preferred_element_type=F32)
 
 
-def eights(first, rows=256):
-    row = lax.broadcasted_iota(jnp.int32, (2 * rows, rows), 0)
-    col = lax.broadcasted_iota(jnp.int32, (2 * rows, rows), 1)
-    row = row ^ (256 if rows == 256 else 0)
+def member(place, rest, begin):
+    return (place + begin * rest) & (16 * rest - 1)
+
+
+def groups(rest, begin):
+    return [[member(place, rest, begin) for place in range(16 * rest)]]
+
+
+def eights(first, start=0, rows=512):
+    row = lax.broadcasted_iota(jnp.int32, (rows, 256), 0) + start
+    col = lax.broadcasted_iota(jnp.int32, (rows, 256), 1)
     inside = (row & 4) == (0 if first else 4)
-    return ((col == (row >> 3) * 4 + (row & 3)) & inside).astype(F32).astype(BF)
-
-
-def interleave(first, second, dims=(((1,), (0,)), ((), ()))):
-    rows = first.shape[dims[0][1][0]]
+    return ((col == member(row >> 3, 4, BEGIN) * 4 + (row & 3)) & inside).astype(F32).astype(BF)
+
+
+def interleave(first, second, dims=(((1,), (0,)), ((), ())), start=0, rows=512):
     return (
-        product(eights(True, rows), first, dims) + product(eights(False, rows), second, dims)
+        product(eights(True, start, rows), first, dims)
+        + product(eights(False, start, rows), second, dims)
     ).astype(BF)
 
 
@@ -68,8 +76,8 @@
 def interleave_kernel(x_ref, ct_ref, sent_ref, sent, sems):
     stores = []
     for i in range(4):
-        rows, out = pl.ds(i * 64, 64), pl.ds((i ^ 2) * 128, 128)
-        sent[out] = interleave(x_ref[rows], ct_ref[rows])
+        out = pl.ds(i * 128, 128)
+        sent[out] = interleave(x_ref[...], ct_ref[...], start=i * 128, rows=128)
         stores += start_copies([(sent.at[out], sent_ref.at[out])], sems, i)
     wait_for(stores)
 
@@ -194,9 +202,11 @@
 
 def column_kernel(both_ref, bias_ref, *refs):
     weights, refs = refs[:8], refs[8:]
-    parts_ref, keep_ref, send_ref, parts, keep, send, x, ct, bias, w_ref, sems = refs
+    parts_ref, keep_ref, send_ref, parts, keep, send, both, x, ct, bias, w_ref, sems = refs
+    first = start_copies(((both_ref, both),), sems, 25)
     copies = kind_copies(1, weights, w_ref, sems, 1) + start_copies(((bias_ref, bias),), sems)
-    x[...], ct[...] = separate(both_ref[...])
+    wait_for(first)
+    x[...], ct[...] = separate(both[...])
     out, dq, dk, dv = attention(x, ct, w_ref, copies, 1, bias)
     parts[:, 0:256] = interleave(out, dk, LAST)
     parts[:, 256:512] = interleave(dq, dv, LAST)
@@ -236,7 +246,7 @@
     col = lax.broadcasted_iota(jnp.int32, (256, 64), 1)
     out = jnp.zeros((256, 256), F32)
     for b in range(4):
-        here = (col == ((row >> 3) ^ 16) * 2 + (row & 1)) & ((row & 6) == 2 * b)
+        here = (col == member(row >> 3, 2, BEGIN_LAST) * 2 + (row & 1)) & ((row & 6) == 2 * b)
         out += product(here.astype(F32).astype(BF), total[:, b * 256 : (b + 1) * 256])
     out_ref[...] = out.astype(BF)
 
@@ -336,7 +346,7 @@
     )(w_query, w_key, w_value, w_out)
     with jax.named_scope("to_columns"):
         both = lax.all_to_all(
-            sent.reshape(64, 8, 1024), seq, split_axis=0, concat_axis=0, tiled=True, axis_index_groups=[[p ^ 32 for p in range(64)]]
+            sent.reshape(64, 8, 1024), seq, split_axis=0, concat_axis=0, tiled=True, axis_index_groups=groups(4, BEGIN)
         ).reshape(512, 1024)
     with jax.named_scope("masks"):
         row_bias, col_bias = biases(row_mask, column_mask)
@@ -377,17 +387,18 @@
     col_parts, col_keep, col_send = pl.pallas_call(
         column_kernel,
         out_shape=(shape(512, 512),) * 3,
-        in_specs=[VMEM] + [HBM] * 9,
+        in_specs=[HBM] * 10,
         out_specs=(HBM,) * 3,
         scratch_shapes=[
             buffer(512, 512),
             buffer(512, 512),
             buffer(512, 512),
+            buffer(512, 1024),
             buffer(256, 1024),
             buffer(256, 1024),
             buffer(4, 256, 256),
             buffer(2, 8, 128, 1024),
-            pltpu.SemaphoreType.DMA((25,)),
+            pltpu.SemaphoreType.DMA((26,)),
         ],
         compiler_params=room(58),
         cost_estimate=cost(1900000000, 8000000),
@@ -396,7 +407,7 @@
     col_got = lax.ppermute(col_send, "c", SWAP)
     with jax.named_scope("from_columns"):
         returned = lax.all_to_all(
-            col_parts.reshape(64, 8, 512), seq, split_axis=0, concat_axis=0, tiled=True, axis_index_groups=[[p ^ 32 for p in range(64)]]
+            col_parts.reshape(64, 8, 512), seq, split_axis=0, concat_axis=0, tiled=True, axis_index_groups=groups(4, BEGIN)
         ).reshape(512, 512)
 
     with jax.named_scope("gradient_sums"):
@@ -435,7 +446,7 @@
         )(line_keep, line_got)
         line, returned = lax.optimization_barrier((line, returned))
         line = lax.all_to_all(
-            line.reshape(32, 8, 256), ("z", "yl"), split_axis=0, concat_axis=0, tiled=True, axis_index_groups=[[p ^ 16 for p in range(32)]]
+            line.reshape(32, 8, 256), ("z", "yl"), split_axis=0, concat_axis=0, tiled=True, axis_index_groups=groups(2, BEGIN_LAST)
         )
         grad_value, grad_output = pl.pallas_call(
             last_kernel,

time: 146 us -> 145 us (level)
  starting transfers between devices: 85.1 us -> 82.3 us
  waiting for transfers between devices: 30.4 us -> 32.3 us
    all_to_all x1, starting transfers between devices: 19.8 us -> 18.1 us  [body(): lax.all_to_all(sent.reshape(64, 8, 1024), seq, split_axis=0, concat_axis=...]
  transfers between devices with their start and end apart: 17 -> 17, of which waited for: 7 -> 8; matrix products, arithmetic and copies ran while one was open for 2% -> 2% of each run, Pallas kernels for 15% -> 14%
where the time goes in v8:
time: 145 us; the launch traced here: 143 us
  starting transfers between devices  82.3 us (57%)
  waiting for transfers between devices  32.3 us (22%)
  Pallas kernels  23.1 us (16%)
  matrix products  2.83 us (2%)
  local copies, waits for them, and re-layouts  1.55 us (1%)
    all_to_all x1, starting transfers between devices, body(): lax.all_to_all(sent.reshape(64, 8, 1024), seq, split_axis=0, concat_axis=...  18.1 us
    ppermute x3, waiting for transfers between devices, body(): lax.ppermute(pair, 'x', [(x, (x + step) % 4) for x in range(4)])  14.5 us
    all_to_all x1, starting transfers between devices, body(): lax.all_to_all(col_parts.reshape(64, 8, 512), seq, split_axis=0, concat_a...  13.2 us
    all_to_all x1, starting transfers between devices, body(): lax.all_to_all(line.reshape(32, 8, 256), ('z', 'yl'), split_axis=0, conca...  12.2 us
    ppermute x3, starting transfers between devices, body(): lax.ppermute(terms[step], 'x', [(x, (x + step) % 4) for x in range(4)])  9.43 us
    ppermute x3, starting transfers between devices, body(): lax.ppermute(pair, 'x', [(x, (x + step) % 4) for x in range(4)])  9.24 us
    ppermute x3, waiting for transfers between devices, body(): lax.ppermute(terms[step], 'x', [(x, (x + step) % 4) for x in range(4)])  8.79 us
    ppermute x4, starting transfers between devices, body(): weights += [lax.ppermute(part, 'c', SWAP) for part in weights]  8.26 us
  transfers between devices with their start and end apart: 17, of which 8 were waited for; matrix products, arithmetic and copies ran while one was open for 2% of the time, Pallas kernels for 14%

profile of v8, /device:TPU:6, one launch (start us, length us, event | category | flops | bytes accessed | tf_op | source)
XLA Modules:
  0.0 143.3 jit_solution(1074933175566840084)
XLA Ops:
  0.6 0.0 copy-start.2
  0.6 0.0 copy-start.1
  0.7 1.7 %pack.1.packed_ref = bf16[128,1024]{1,0:T(8,128)(2,1)} custom-call(bf16[128,512]{1,0:T(8,128)(2,1)} %wq_ref.1, bf16[128,512]{1,0:T(8,128)(2,1)} %wk_ref.1, bf16[128,512]{1,0:T(8,128)(2,1)} %wv_ref.1, bf16[64,1024]{1,0:T(8,128)(2,1)} %wo_ref.1), custom_call_target="tpu_custom_call" | custom-call | flops 1000000000 | bytes 2000000 | tf_op jit(solution)/shard_map/pack/pallas_call | solution.py:337
  2.4 4.9 %collective-permute-start = (bf16[128,1024]{1,0:T(8,128)(2,1)}, bf16[128,1024]{1,0:T(8,128)(2,1)S(1)}, u32[]{:S(2)}, u32[]{:S(2)}) collective-permute-start(bf16[128,1024]{1,0:T(8,128)(2,1)} %pack.1.packed_ref), channel_id=1, source_target_pairs={{0,66},{2,64},{64,2},{66,0},{1,67},{3,65},{65,3},{67,1},{4,70},{6,... | collective-permute-start | bytes 786440 | tf_op jit(solution)/shard_map/weights/ppermute | solution.py:354
  7.3 0.0 copy-done.2
  7.3 0.0 copy-done.1
  7.4 1.5 %interleave.1 = bf16[512,1024]{1,0:T(8,128)(2,1)} custom-call(bf16[256,1024]{1,0:T(8,128)(2,1)S(1)} %bitcast.39, bf16[256,1024]{1,0:T(8,128)(2,1)S(1)} %bitcast.41), custom_call_target="tpu_custom_call" | custom-call | flops 540000000 | bytes 2000000 | tf_op jit(solution)/shard_map/interleave/pallas_call | solution.py:327
  8.8 0.0 copy-start.4
  8.8 18.1 %all-to-all-start = ((bf16[64,8,1024]{2,1,0:T(8,128)(2,1)}), bf16[64,8,1024]{2,1,0:T(8,128)(2,1)}, u32[]{:S(2)}, u32[]{:S(2)}) async-start(bf16[64,8,1024]{2,1,0:T(8,128)(2,1)} %bitcast.10), calls=%async_computation | async-start | bytes 2097152 | tf_op jit(solution)/shard_map/to_columns/all_to_all | solution.py:348
  27.0 0.0 copy-start.14
  27.0 0.1 iota_compare_fusion
  27.1 0.6 copy-done.14
  27.7 0.0 collective-permute-done.flipped_ref
  27.7 0.0 copy-done.4
  27.7 0.0 copy-start
  27.7 3.3 %collective-permute-start.3 = (bf16[2,128,1024]{2,1,0:T(8,128)(2,1)S(1)}, bf16[2,128,1024]{2,1,0:T(8,128)(2,1)S(1)}, u32[]{:S(2)}, u32[]{:S(2)}) collective-permute-start(bf16[2,128,1024]{2,1,0:T(8,128)(2,1)S(1)} %pair.1.refs_0_), channel_id=1, source_target_pairs={{0,256},{128,384},{256,0},{384,128},{1,257},{129,385},{257,1},{385... | collective-permute-start | bytes 1572872 | tf_op jit(solution)/shard_map/weights/ppermute | solution.py:365
  31.0 4.0 %collective-permute-start.2 = (bf16[2,128,1024]{2,1,0:T(8,128)(2,1)S(1)}, bf16[2,128,1024]{2,1,0:T(8,128)(2,1)S(1)}, u32[]{:S(2)}, u32[]{:S(2)}) collective-permute-start(bf16[2,128,1024]{2,1,0:T(8,128)(2,1)S(1)} %pair.1.refs_0_), channel_id=1, source_target_pairs={{0,128},{128,256},{256,384},{384,0},{1,129},{129,257},{257,385},{3... | collective-permute-start | bytes 1572872 | tf_op jit(solution)/shard_map/weights/ppermute | solution.py:365
  35.1 1.9 %collective-permute-start.1 = (bf16[2,128,1024]{2,1,0:T(8,128)(2,1)S(1)}, bf16[2,128,1024]{2,1,0:T(8,128)(2,1)S(1)}, u32[]{:S(2)}, u32[]{:S(2)}) collective-permute-start(bf16[2,128,1024]{2,1,0:T(8,128)(2,1)S(1)} %pair.1.refs_0_), channel_id=1, source_target_pairs={{0,384},{128,0},{256,128},{384,256},{1,385},{129,1},{257,129},{385... | collective-permute-start | bytes 1572872 | tf_op jit(solution)/shard_map/weights/ppermute | solution.py:365
  37.0 0.1 copy.12
  37.1 1.4 fusion.6.bias_ref
  38.5 0.0 copy-done.15
  38.5 1.5 %fusion.3.bias_ref = bf16[4,256,256]{2,1,0:T(8,128)(2,1)} fusion(pred[256,256]{1,0:T(8,128)(4,1)S(1)} %get-tuple-element.51, pred[256,256]{1,0:T(8,128)(4,1)S(1)} %get-tuple-element.50, s32[256]{0:T(256)S(1)} %get-tuple-element.53, s32[4,4,8,8]{3,2,1,0:T(8,128)S(1)} %copy-done.15, s32[256]{0:T(256)S(1)} %get-tuple-element.52), kind=kOutput, calls=%fused_computation.5 | convolution fusion | flops 6564864 | bytes 661504 | tf_op jit(solution)/shard_map/masks/ia,hab,jb->hij/dot_general | solution.py:310
  39.9 1.9 %collective-permute-start.4 = (bf16[2,128,1024]{2,1,0:T(8,128)(2,1)S(1)}, bf16[2,128,1024]{2,1,0:T(8,128)(2,1)S(1)}, u32[]{:S(2)}, u32[]{:S(2)}) collective-permute-start(bf16[2,128,1024]{2,1,0:T(8,128)(2,1)S(1)} %pair.1.refs_0_), channel_id=1, source_target_pairs={{0,1},{1,0},{2,3},{3,2},{4,5},{5,4},{6,7},{7,6},{8,9},{9,8},{10,11... | collective-permute-start | bytes 1572872 | tf_op jit(solution)/shard_map/weights/ppermute | solution.py:368
  41.9 14.5 %collective-permute-done.1.refs_3_ = bf16[2,128,1024]{2,1,0:T(8,128)(2,1)S(1)} collective-permute-done((bf16[2,128,1024]{2,1,0:T(8,128)(2,1)S(1)}, bf16[2,128,1024]{2,1,0:T(8,128)(2,1)S(1)}, u32[]{:S(2)}, u32[]{:S(2)}) %collective-permute-start.1) | collective-permute-done | bytes 524320 | tf_op jit(solution)/shard_map/weights/ppermute | solution.py:365
  56.3 0.0 collective-permute-done.3.refs_2_
  56.3 2.0 %collective-permute-start.6 = (bf16[2,128,1024]{2,1,0:T(8,128)(2,1)S(1)}, bf16[2,128,1024]{2,1,0:T(8,128)(2,1)S(1)}, u32[]{:S(2)}, u32[]{:S(2)}) collective-permute-start(bf16[2,128,1024]{2,1,0:T(8,128)(2,1)S(1)} %collective-permute-done.3.refs_2_), channel_id=1, source_target_pairs={{0,1},{1,0},{2,3},{3,2},{4,5},{5,4},{6,7},{7,6},{8,9},{9,8},{10,11... | collective-permute-start | bytes 1572872 | tf_op jit(solution)/shard_map/weights/ppermute | solution.py:368
  58.4 0.0 collective-permute-done.2.refs_1_
  58.4 2.3 %collective-permute-start.5 = (bf16[2,128,1024]{2,1,0:T(8,128)(2,1)S(1)}, bf16[2,128,1024]{2,1,0:T(8,128)(2,1)S(1)}, u32[]{:S(2)}, u32[]{:S(2)}) collective-permute-start(bf16[2,128,1024]{2,1,0:T(8,128)(2,1)S(1)} %collective-permute-done.2.refs_1_), channel_id=1, source_target_pairs={{0,1},{1,0},{2,3},{3,2},{4,5},{5,4},{6,7},{7,6},{8,9},{9,8},{10,11... | collective-permute-start | bytes 1572872 | tf_op jit(solution)/shard_map/weights/ppermute | solution.py:368
  60.7 2.0 %collective-permute-start.7 = (bf16[2,128,1024]{2,1,0:T(8,128)(2,1)S(1)}, bf16[2,128,1024]{2,1,0:T(8,128)(2,1)S(1)}, u32[]{:S(2)}, u32[]{:S(2)}) collective-permute-start(bf16[2,128,1024]{2,1,0:T(8,128)(2,1)S(1)} %collective-permute-done.1.refs_3_), channel_id=1, source_target_pairs={{0,1},{1,0},{2,3},{3,2},{4,5},{5,4},{6,7},{7,6},{8,9},{9,8},{10,11... | collective-permute-start | bytes 1572872 | tf_op jit(solution)/shard_map/weights/ppermute | solution.py:368
  62.7 0.0 collective-permute-done.4.refs_4_
  62.8 0.0 collective-permute-done.6.refs_6_
  62.8 0.0 copy-start.11
  62.8 0.0 collective-permute-done.5.refs_5_
  62.8 1.7 %collective-permute-done.7.refs_7_ = bf16[2,128,1024]{2,1,0:T(8,128)(2,1)S(1)} collective-permute-done((bf16[2,128,1024]{2,1,0:T(8,128)(2,1)S(1)}, bf16[2,128,1024]{2,1,0:T(8,128)(2,1)S(1)}, u32[]{:S(2)}, u32[]{:S(2)}) %collective-permute-start.7) | collective-permute-done | bytes 524320 | tf_op jit(solution)/shard_map/weights/ppermute | solution.py:368
  64.5 0.0 copy-done.7
  64.6 0.8 copy-done.13
  65.4 5.9 %row_heads.1 = (bf16[256,1024]{1,0:T(8,128)(2,1)}, bf16[512,512]{1,0:T(8,128)(2,1)}, bf16[512,512]{1,0:T(8,128)(2,1)}) custom-call(bf16[256,1024]{1,0:T(8,128)(2,1)} %bitcast.38, bf16[256,1024]{1,0:T(8,128)(2,1)} %bitcast.40, bf16[4,256,256]{2,1,0:T(8,128)(2,1)} %fusion.6.bias_ref, bf16[2,128,1024]{2,1,0:T(8,128)(2,1)} %copy-done, ...), custom_call_target="tpu_custom_call" | custom-call | flops 1400000000 | bytes 12000000 | tf_op jit(solution)/shard_map/row_heads/pallas_call | solution.py:369
  71.3 2.0 %collective-permute-start.8 = (bf16[512,512]{1,0:T(8,128)(2,1)}, bf16[512,512]{1,0:T(8,128)(2,1)S(1)}, u32[]{:S(2)}, u32[]{:S(2)}) collective-permute-start(bf16[512,512]{1,0:T(8,128)(2,1)} %get-tuple-element.32), channel_id=1, source_target_pairs={{0,1},{1,0},{2,3},{3,2},{4,5},{5,4},{6,7},{7,6},{8,9},{9,8},{10,11... | collective-permute-start | bytes 1572872 | tf_op jit(solution)/shard_map/ppermute | solution.py:385
  73.3 1.2 all-to-all-done
  74.6 6.3 %column_heads.1 = (bf16[512,512]{1,0:T(8,128)(2,1)}, bf16[512,512]{1,0:T(8,128)(2,1)}, bf16[512,512]{1,0:T(8,128)(2,1)}) custom-call(bf16[512,1024]{1,0:T(8,128)(2,1)} %bitcast.11.both_ref, bf16[4,256,256]{2,1,0:T(8,128)(2,1)} %fusion.3.bias_ref, bf16[2,128,1024]{2,1,0:T(8,128)(2,1)} %copy-done, bf16[2,128,1024]{2,1,0:T(8,128)(2,1)} %copy-done.8, ...), custom_call_target="tpu_custom_call" | custom-call | flops 1900000000 | bytes 8000000 | tf_op jit(solution)/shard_map/column_heads/pallas_call | solution.py:387
  80.9 1.9 %collective-permute-start.9 = (bf16[512,512]{1,0:T(8,128)(2,1)}, bf16[512,512]{1,0:T(8,128)(2,1)S(1)}, u32[]{:S(2)}, u32[]{:S(2)}) collective-permute-start(bf16[512,512]{1,0:T(8,128)(2,1)} %get-tuple-element.36), channel_id=1, source_target_pairs={{0,1},{1,0},{2,3},{3,2},{4,5},{5,4},{6,7},{7,6},{8,9},{9,8},{10,11... | collective-permute-start | bytes 1572872 | tf_op jit(solution)/shard_map/ppermute | solution.py:407
  82.8 0.0 copy-start.3
  82.8 0.0 copy-start.5
  82.8 13.2 %all-to-all-start.1 = ((bf16[64,8,512]{2,1,0:T(8,128)(2,1)}), bf16[64,8,512]{2,1,0:T(8,128)(2,1)S(1)}, u32[]{:S(2)}, u32[]{:S(2)}) async-start(bf16[64,8,512]{2,1,0:T(8,128)(2,1)} %bitcast.44), calls=%async_computation.1 | async-start | bytes 1048576 | tf_op jit(solution)/shard_map/from_columns/all_to_all | solution.py:409
  96.1 0.0 collective-permute-done.8.row_got
  96.1 0.0 collective-permute-done.9.col_got
  96.1 0.0 copy-done.3
  96.1 0.0 copy-done.5
  96.1 0.3 pick.1
  96.4 3.3 %collective-permute-start.10 = (bf16[128,1024]{1,0:T(8,128)(2,1)S(1)}, bf16[128,1024]{1,0:T(8,128)(2,1)S(1)}, u32[]{:S(2)}, u32[]{:S(2)}) collective-permute-start(bf16[128,1024]{1,0:T(8,128)(2,1)S(1)} %get-tuple-element.38), channel_id=1, source_target_pairs={{0,256},{128,384},{256,0},{384,128},{1,257},{129,385},{257,1},{385... | collective-permute-start | bytes 786440 | tf_op jit(solution)/shard_map/gradient_sums/ppermute | solution.py:424
  99.7 4.0 %collective-permute-start.11 = (bf16[128,1024]{1,0:T(8,128)(2,1)S(1)}, bf16[128,1024]{1,0:T(8,128)(2,1)S(1)}, u32[]{:S(2)}, u32[]{:S(2)}) collective-permute-start(bf16[128,1024]{1,0:T(8,128)(2,1)S(1)} %get-tuple-element.39), channel_id=1, source_target_pairs={{0,128},{128,256},{256,384},{384,0},{1,129},{129,257},{257,385},{3... | collective-permute-start | bytes 786440 | tf_op jit(solution)/shard_map/gradient_sums/ppermute | solution.py:424
  103.7 2.1 %collective-permute-start.12 = (bf16[128,1024]{1,0:T(8,128)(2,1)S(1)}, bf16[128,1024]{1,0:T(8,128)(2,1)S(1)}, u32[]{:S(2)}, u32[]{:S(2)}) collective-permute-start(bf16[128,1024]{1,0:T(8,128)(2,1)S(1)} %get-tuple-element.40), channel_id=1, source_target_pairs={{0,384},{128,0},{256,128},{384,256},{1,385},{129,1},{257,129},{385... | collective-permute-start | bytes 786440 | tf_op jit(solution)/shard_map/gradient_sums/ppermute | solution.py:424
  105.8 2.6 %collective-permute-done.10.refs_1_ = bf16[128,1024]{1,0:T(8,128)(2,1)S(1)} collective-permute-done((bf16[128,1024]{1,0:T(8,128)(2,1)S(1)}, bf16[128,1024]{1,0:T(8,128)(2,1)S(1)}, u32[]{:S(2)}, u32[]{:S(2)}) %collective-permute-start.10) | collective-permute-done | bytes 262176 | tf_op jit(solution)/shard_map/gradient_sums/ppermute | solution.py:424
  108.4 3.2 %collective-permute-done.11.refs_2_ = bf16[128,1024]{1,0:T(8,128)(2,1)S(1)} collective-permute-done((bf16[128,1024]{1,0:T(8,128)(2,1)S(1)}, bf16[128,1024]{1,0:T(8,128)(2,1)S(1)}, u32[]{:S(2)}, u32[]{:S(2)}) %collective-permute-start.11) | collective-permute-done | bytes 262176 | tf_op jit(solution)/shard_map/gradient_sums/ppermute | solution.py:424
  111.6 3.1 %collective-permute-done.12.refs_3_ = bf16[128,1024]{1,0:T(8,128)(2,1)S(1)} collective-permute-done((bf16[128,1024]{1,0:T(8,128)(2,1)S(1)}, bf16[128,1024]{1,0:T(8,128)(2,1)S(1)}, u32[]{:S(2)}, u32[]{:S(2)}) %collective-permute-start.12) | collective-permute-done | bytes 262176 | tf_op jit(solution)/shard_map/gradient_sums/ppermute | solution.py:424
  114.6 0.2 spread.1
  114.9 2.9 %collective-permute-start.13 = (bf16[64,1024]{1,0:T(8,128)(2,1)S(1)}, bf16[64,1024]{1,0:T(8,128)(2,1)S(1)}, u32[]{:S(2)}, u32[]{:S(2)}) collective-permute-start(bf16[64,1024]{1,0:T(8,128)(2,1)S(1)} %get-tuple-element.42), channel_id=1, source_target_pairs={{0,66},{2,64},{64,2},{66,0},{1,67},{3,65},{65,3},{67,1},{4,70},{6,... | collective-permute-start | bytes 393224 | tf_op jit(solution)/shard_map/gradient_sums/ppermute | solution.py:437
  117.8 5.2 %collective-permute-done.13.got_ref = bf16[64,1024]{1,0:T(8,128)(2,1)S(1)} collective-permute-done((bf16[64,1024]{1,0:T(8,128)(2,1)S(1)}, bf16[64,1024]{1,0:T(8,128)(2,1)S(1)}, u32[]{:S(2)}, u32[]{:S(2)}) %collective-permute-start.13) | collective-permute-done | bytes 131104 | tf_op jit(solution)/shard_map/gradient_sums/ppermute | solution.py:437
  123.0 0.9 line.1
  123.9 0.0 all-to-all-done.1
  123.9 12.2 %all-to-all-start.2 = ((bf16[32,8,256]{2,1,0:T(8,128)(2,1)}), bf16[32,8,256]{2,1,0:T(8,128)(2,1)S(1)}, u32[]{:S(2)}, u32[]{:S(2)}) async-start(bf16[32,8,256]{2,1,0:T(8,128)(2,1)} %bitcast.16), calls=%async_computation.2 | async-start | bytes 262144 | tf_op jit(solution)/shard_map/gradient_sums/all_to_all | solution.py:448
  136.2 5.6 %output_products.1 = (bf16[256,1024]{1,0:T(8,128)(2,1)}, bf16[256,1024]{1,0:T(8,128)(2,1)}) custom-call(bf16[256,1024]{1,0:T(8,128)(2,1)} %get-tuple-element.29.row_ref, bf16[512,512]{1,0:T(8,128)(2,1)} %bitcast.43, bf16[2,128,1024]{2,1,0:T(8,128)(2,1)} %copy-done, bf16[2,128,1024]{2,1,0:T(8,128)(2,1)} %copy-done.8, bf16[2,128,1024]{2,1,0:T(8,128)(2,1)} %copy-done.7, ...), custom_call_target="tpu_custom_call" | custom-call | flops 1200000000 | bytes 8000000 | tf_op jit(solution)/shard_map/output_products/pallas_call | solution.py:461
  141.8 0.9 all-to-all-done.2
  142.7 0.6 last.1
  (20 shorter events, 0.1 us)
Async XLA Ops:
  0.6 6.7 %copy-start.2 = (bf16[1,1,256,1024]{3,2,1,0:T(8,128)(2,1)S(1)}, bf16[1,1,256,1024]{3,2,1,0:T(8,128)(2,1)}, u32[]{:S(2)}) copy-start(bf16[1,1,256,1024]{3,2,1,0:T(8,128)(2,1)} %param.9) | copy-start | bytes 1572868
  0.6 6.7 %copy-start.1 = (bf16[1,1,256,1024]{3,2,1,0:T(8,128)(2,1)S(1)}, bf16[1,1,256,1024]{3,2,1,0:T(8,128)(2,1)}, u32[]{:S(2)}) copy-start(bf16[1,1,256,1024]{3,2,1,0:T(8,128)(2,1)} %param.8) | copy-start | bytes 1572868
  2.4 25.2 %collective-permute-start = (bf16[128,1024]{1,0:T(8,128)(2,1)}, bf16[128,1024]{1,0:T(8,128)(2,1)S(1)}, u32[]{:S(2)}, u32[]{:S(2)}) collective-permute-start(bf16[128,1024]{1,0:T(8,128)(2,1)} %pack.1.packed_ref), channel_id=1, source_target_pairs={{0,66},{2,64},{64,2},{66,0},{1,67},{3,65},{65,3},{67,1},{4,70},{6,... | collective-permute-start | bytes 786440 | tf_op jit(solution)/shard_map/weights/ppermute | solution.py:354
  8.8 18.8 %copy-start.4 = (bf16[128,1024]{1,0:T(8,128)(2,1)S(1)}, bf16[128,1024]{1,0:T(8,128)(2,1)}, u32[]{:S(2)}) copy-start(bf16[128,1024]{1,0:T(8,128)(2,1)} %pack.1.packed_ref) | copy-start | bytes 786436
  8.8 65.7 %all-to-all-start = ((bf16[64,8,1024]{2,1,0:T(8,128)(2,1)}), bf16[64,8,1024]{2,1,0:T(8,128)(2,1)}, u32[]{:S(2)}, u32[]{:S(2)}) async-start(bf16[64,8,1024]{2,1,0:T(8,128)(2,1)} %bitcast.10), calls=%async_computation | async-start | bytes 2097152 | tf_op jit(solution)/shard_map/to_columns/all_to_all | solution.py:348
  27.0 0.7 copy-start.14
  27.7 12.2 %copy-start = (bf16[2,128,1024]{2,1,0:T(8,128)(2,1)}, bf16[2,128,1024]{2,1,0:T(8,128)(2,1)S(1)}, u32[]{:S(2)}) copy-start(bf16[2,128,1024]{2,1,0:T(8,128)(2,1)S(1)} %pair.1.refs_0_) | copy-start | bytes 1572868
  27.7 28.6 %collective-permute-start.3 = (bf16[2,128,1024]{2,1,0:T(8,128)(2,1)S(1)}, bf16[2,128,1024]{2,1,0:T(8,128)(2,1)S(1)}, u32[]{:S(2)}, u32[]{:S(2)}) collective-permute-start(bf16[2,128,1024]{2,1,0:T(8,128)(2,1)S(1)} %pair.1.refs_0_), channel_id=1, source_target_pairs={{0,256},{128,384},{256,0},{384,128},{1,257},{129,385},{257,1},{385... | collective-permute-start | bytes 1572872 | tf_op jit(solution)/shard_map/weights/ppermute | solution.py:365
  31.0 27.3 %collective-permute-start.2 = (bf16[2,128,1024]{2,1,0:T(8,128)(2,1)S(1)}, bf16[2,128,1024]{2,1,0:T(8,128)(2,1)S(1)}, u32[]{:S(2)}, u32[]{:S(2)}) collective-permute-start(bf16[2,128,1024]{2,1,0:T(8,128)(2,1)S(1)} %pair.1.refs_0_), channel_id=1, source_target_pairs={{0,128},{128,256},{256,384},{384,0},{1,129},{129,257},{257,385},{3... | collective-permute-start | bytes 1572872 | tf_op jit(solution)/shard_map/weights/ppermute | solution.py:365
  35.1 21.3 %collective-permute-start.1 = (bf16[2,128,1024]{2,1,0:T(8,128)(2,1)S(1)}, bf16[2,128,1024]{2,1,0:T(8,128)(2,1)S(1)}, u32[]{:S(2)}, u32[]{:S(2)}) collective-permute-start(bf16[2,128,1024]{2,1,0:T(8,128)(2,1)S(1)} %pair.1.refs_0_), channel_id=1, source_target_pairs={{0,384},{128,0},{256,128},{384,256},{1,385},{129,1},{257,129},{385... | collective-permute-start | bytes 1572872 | tf_op jit(solution)/shard_map/weights/ppermute | solution.py:365
  37.1 1.4 copy-start.15
  39.9 22.8 %collective-permute-start.4 = (bf16[2,128,1024]{2,1,0:T(8,128)(2,1)S(1)}, bf16[2,128,1024]{2,1,0:T(8,128)(2,1)S(1)}, u32[]{:S(2)}, u32[]{:S(2)}) collective-permute-start(bf16[2,128,1024]{2,1,0:T(8,128)(2,1)S(1)} %pair.1.refs_0_), channel_id=1, source_target_pairs={{0,1},{1,0},{2,3},{3,2},{4,5},{5,4},{6,7},{7,6},{8,9},{9,8},{10,11... | collective-permute-start | bytes 1572872 | tf_op jit(solution)/shard_map/weights/ppermute | solution.py:368
  56.3 8.2 %copy-start.9 = (bf16[2,128,1024]{2,1,0:T(8,128)(2,1)}, bf16[2,128,1024]{2,1,0:T(8,128)(2,1)S(1)}, u32[]{:S(2)}) copy-start(bf16[2,128,1024]{2,1,0:T(8,128)(2,1)S(1)} %collective-permute-done.1.refs_3_) | copy-start | bytes 1572868
  56.3 8.2 %copy-start.7 = (bf16[2,128,1024]{2,1,0:T(8,128)(2,1)}, bf16[2,128,1024]{2,1,0:T(8,128)(2,1)S(1)}, u32[]{:S(2)}) copy-start(bf16[2,128,1024]{2,1,0:T(8,128)(2,1)S(1)} %collective-permute-done.3.refs_2_) | copy-start | bytes 1572868
  56.3 6.4 %collective-permute-start.6 = (bf16[2,128,1024]{2,1,0:T(8,128)(2,1)S(1)}, bf16[2,128,1024]{2,1,0:T(8,128)(2,1)S(1)}, u32[]{:S(2)}, u32[]{:S(2)}) collective-permute-start(bf16[2,128,1024]{2,1,0:T(8,128)(2,1)S(1)} %collective-permute-done.3.refs_2_), channel_id=1, source_target_pairs={{0,1},{1,0},{2,3},{3,2},{4,5},{5,4},{6,7},{7,6},{8,9},{9,8},{10,11... | collective-permute-start | bytes 1572872 | tf_op jit(solution)/shard_map/weights/ppermute | solution.py:368
  58.4 6.1 %copy-start.8 = (bf16[2,128,1024]{2,1,0:T(8,128)(2,1)}, bf16[2,128,1024]{2,1,0:T(8,128)(2,1)S(1)}, u32[]{:S(2)}) copy-start(bf16[2,128,1024]{2,1,0:T(8,128)(2,1)S(1)} %collective-permute-done.2.refs_1_) | copy-start | bytes 1572868
  58.4 4.4 %collective-permute-start.5 = (bf16[2,128,1024]{2,1,0:T(8,128)(2,1)S(1)}, bf16[2,128,1024]{2,1,0:T(8,128)(2,1)S(1)}, u32[]{:S(2)}, u32[]{:S(2)}) collective-permute-start(bf16[2,128,1024]{2,1,0:T(8,128)(2,1)S(1)} %collective-permute-done.2.refs_1_), channel_id=1, source_target_pairs={{0,1},{1,0},{2,3},{3,2},{4,5},{5,4},{6,7},{7,6},{8,9},{9,8},{10,11... | collective-permute-start | bytes 1572872 | tf_op jit(solution)/shard_map/weights/ppermute | solution.py:368
  60.7 3.8 %collective-permute-start.7 = (bf16[2,128,1024]{2,1,0:T(8,128)(2,1)S(1)}, bf16[2,128,1024]{2,1,0:T(8,128)(2,1)S(1)}, u32[]{:S(2)}, u32[]{:S(2)}) collective-permute-start(bf16[2,128,1024]{2,1,0:T(8,128)(2,1)S(1)} %collective-permute-done.1.refs_3_), channel_id=1, source_target_pairs={{0,1},{1,0},{2,3},{3,2},{4,5},{5,4},{6,7},{7,6},{8,9},{9,8},{10,11... | collective-permute-start | bytes 1572872 | tf_op jit(solution)/shard_map/weights/ppermute | solution.py:368
  62.7 1.8 %copy-start.10 = (bf16[2,128,1024]{2,1,0:T(8,128)(2,1)}, bf16[2,128,1024]{2,1,0:T(8,128)(2,1)S(1)}, u32[]{:S(2)}) copy-start(bf16[2,128,1024]{2,1,0:T(8,128)(2,1)S(1)} %collective-permute-done.4.refs_4_) | copy-start | bytes 1572868
  62.8 1.8 %copy-start.11 = (bf16[2,128,1024]{2,1,0:T(8,128)(2,1)}, bf16[2,128,1024]{2,1,0:T(8,128)(2,1)S(1)}, u32[]{:S(2)}) copy-start(bf16[2,128,1024]{2,1,0:T(8,128)(2,1)S(1)} %collective-permute-done.6.refs_6_) | copy-start | bytes 1572868
  62.8 1.7 %copy-start.12 = (bf16[2,128,1024]{2,1,0:T(8,128)(2,1)}, bf16[2,128,1024]{2,1,0:T(8,128)(2,1)S(1)}, u32[]{:S(2)}) copy-start(bf16[2,128,1024]{2,1,0:T(8,128)(2,1)S(1)} %collective-permute-done.5.refs_5_) | copy-start | bytes 1572868
  64.5 0.8 copy-start.13
  71.3 24.8 %collective-permute-start.8 = (bf16[512,512]{1,0:T(8,128)(2,1)}, bf16[512,512]{1,0:T(8,128)(2,1)S(1)}, u32[]{:S(2)}, u32[]{:S(2)}) collective-permute-start(bf16[512,512]{1,0:T(8,128)(2,1)} %get-tuple-element.32), channel_id=1, source_target_pairs={{0,1},{1,0},{2,3},{3,2},{4,5},{5,4},{6,7},{7,6},{8,9},{9,8},{10,11... | collective-permute-start | bytes 1572872 | tf_op jit(solution)/shard_map/ppermute | solution.py:385
  80.9 15.2 %collective-permute-start.9 = (bf16[512,512]{1,0:T(8,128)(2,1)}, bf16[512,512]{1,0:T(8,128)(2,1)S(1)}, u32[]{:S(2)}, u32[]{:S(2)}) collective-permute-start(bf16[512,512]{1,0:T(8,128)(2,1)} %get-tuple-element.36), channel_id=1, source_target_pairs={{0,1},{1,0},{2,3},{3,2},{4,5},{5,4},{6,7},{7,6},{8,9},{9,8},{10,11... | collective-permute-start | bytes 1572872 | tf_op jit(solution)/shard_map/ppermute | solution.py:407
  82.8 13.3 %copy-start.3 = (bf16[512,512]{1,0:T(8,128)(2,1)S(1)}, bf16[512,512]{1,0:T(8,128)(2,1)}, u32[]{:S(2)}) copy-start(bf16[512,512]{1,0:T(8,128)(2,1)} %get-tuple-element.31.row_keep) | copy-start | bytes 1572868
  82.8 13.3 %copy-start.5 = (bf16[512,512]{1,0:T(8,128)(2,1)S(1)}, bf16[512,512]{1,0:T(8,128)(2,1)}, u32[]{:S(2)}) copy-start(bf16[512,512]{1,0:T(8,128)(2,1)} %get-tuple-element.35.col_keep) | copy-start | bytes 1572868
  82.8 41.1 %all-to-all-start.1 = ((bf16[64,8,512]{2,1,0:T(8,128)(2,1)}), bf16[64,8,512]{2,1,0:T(8,128)(2,1)S(1)}, u32[]{:S(2)}, u32[]{:S(2)}) async-start(bf16[64,8,512]{2,1,0:T(8,128)(2,1)} %bitcast.44), calls=%async_computation.1 | async-start | bytes 1048576 | tf_op jit(solution)/shard_map/from_columns/all_to_all | solution.py:409
  96.4 12.0 %collective-permute-start.10 = (bf16[128,1024]{1,0:T(8,128)(2,1)S(1)}, bf16[128,1024]{1,0:T(8,128)(2,1)S(1)}, u32[]{:S(2)}, u32[]{:S(2)}) collective-permute-start(bf16[128,1024]{1,0:T(8,128)(2,1)S(1)} %get-tuple-element.38), channel_id=1, source_target_pairs={{0,256},{128,384},{256,0},{384,128},{1,257},{129,385},{257,1},{385... | collective-permute-start | bytes 786440 | tf_op jit(solution)/shard_map/gradient_sums/ppermute | solution.py:424
  99.7 11.9 %collective-permute-start.11 = (bf16[128,1024]{1,0:T(8,128)(2,1)S(1)}, bf16[128,1024]{1,0:T(8,128)(2,1)S(1)}, u32[]{:S(2)}, u32[]{:S(2)}) collective-permute-start(bf16[128,1024]{1,0:T(8,128)(2,1)S(1)} %get-tuple-element.39), channel_id=1, source_target_pairs={{0,128},{128,256},{256,384},{384,0},{1,129},{129,257},{257,385},{3... | collective-permute-start | bytes 786440 | tf_op jit(solution)/shard_map/gradient_sums/ppermute | solution.py:424
  103.7 10.9 %collective-permute-start.12 = (bf16[128,1024]{1,0:T(8,128)(2,1)S(1)}, bf16[128,1024]{1,0:T(8,128)(2,1)S(1)}, u32[]{:S(2)}, u32[]{:S(2)}) collective-permute-start(bf16[128,1024]{1,0:T(8,128)(2,1)S(1)} %get-tuple-element.40), channel_id=1, source_target_pairs={{0,384},{128,0},{256,128},{384,256},{1,385},{129,1},{257,129},{385... | collective-permute-start | bytes 786440 | tf_op jit(solution)/shard_map/gradient_sums/ppermute | solution.py:424
  114.9 8.1 %collective-permute-start.13 = (bf16[64,1024]{1,0:T(8,128)(2,1)S(1)}, bf16[64,1024]{1,0:T(8,128)(2,1)S(1)}, u32[]{:S(2)}, u32[]{:S(2)}) collective-permute-start(bf16[64,1024]{1,0:T(8,128)(2,1)S(1)} %get-tuple-element.42), channel_id=1, source_target_pairs={{0,66},{2,64},{64,2},{66,0},{1,67},{3,65},{65,3},{67,1},{4,70},{6,... | collective-permute-start | bytes 393224 | tf_op jit(solution)/shard_map/gradient_sums/ppermute | solution.py:437
  123.9 12.2 %copy-start.6 = (bf16[64,8,512]{2,1,0:T(8,128)(2,1)}, bf16[64,8,512]{2,1,0:T(8,128)(2,1)S(1)}, u32[]{:S(2)}) copy-start(bf16[64,8,512]{2,1,0:T(8,128)(2,1)S(1)} %all-to-all-done.1) | copy-start | bytes 1572868
  123.9 18.8 %all-to-all-start.2 = ((bf16[32,8,256]{2,1,0:T(8,128)(2,1)}), bf16[32,8,256]{2,1,0:T(8,128)(2,1)S(1)}, u32[]{:S(2)}, u32[]{:S(2)}) async-start(bf16[32,8,256]{2,1,0:T(8,128)(2,1)} %bitcast.16), calls=%async_computation.2 | async-start | bytes 262144 | tf_op jit(solution)/shard_map/gradient_sums/all_to_all | solution.py:448

commit v9 on v8

--- a/solution.py
+++ b/solution.py
@@ -24,7 +24,7 @@
 
 
 SWAP = [(0, 1), (1, 0)]
-BEGIN, BEGIN_LAST = 10, 9
+BEGIN, BEGIN_LAST = 10, 8
 PAIR, PICK = 30000000000, 14000000000
 
 

time: 145 us -> 144 us (level)
  transfers between devices with their start and end apart: 17 -> 17, of which waited for: 8 -> 8; matrix products, arithmetic and copies ran while one was open for 2% -> 2% of each run, Pallas kernels for 14% -> 15%
where the time goes in v9:
time: 144 us; the launch traced here: 143 us
  starting transfers between devices  82.3 us (57%)
  waiting for transfers between devices  31.7 us (22%)
  Pallas kernels  23.1 us (16%)
  matrix products  2.83 us (2%)
  local copies, waits for them, and re-layouts  1.55 us (1%)
    all_to_all x1, starting transfers between devices, body(): lax.all_to_all(sent.reshape(64, 8, 1024), seq, split_axis=0, concat_axis=...  18.1 us
    ppermute x3, waiting for transfers between devices, body(): lax.ppermute(pair, 'x', [(x, (x + step) % 4) for x in range(4)])  14.5 us
    all_to_all x1, starting transfers between devices, body(): lax.all_to_all(col_parts.reshape(64, 8, 512), seq, split_axis=0, concat_a...  13.2 us
    all_to_all x1, starting transfers between devices, body(): lax.all_to_all(line.reshape(32, 8, 256), ('z', 'yl'), split_axis=0, conca...  12.2 us
    ppermute x3, starting transfers between devices, body(): lax.ppermute(terms[step], 'x', [(x, (x + step) % 4) for x in range(4)])  9.43 us
    ppermute x3, starting transfers between devices, body(): lax.ppermute(pair, 'x', [(x, (x + step) % 4) for x in range(4)])  9.24 us
    ppermute x3, waiting for transfers between devices, body(): lax.ppermute(terms[step], 'x', [(x, (x + step) % 4) for x in range(4)])  8.79 us
    ppermute x4, starting transfers between devices, body(): weights += [lax.ppermute(part, 'c', SWAP) for part in weights]  8.26 us
  transfers between devices with their start and end apart: 17, of which 8 were waited for; matrix products, arithmetic and copies ran while one was open for 2% of the time, Pallas kernels for 15%

profile of v9, /device:TPU:6, one launch (start us, length us, event | category | flops | bytes accessed | tf_op | source)
XLA Modules:
  0.0 142.7 jit_solution(13868221482193880232)
XLA Ops:
  0.6 0.0 copy-start.2
  0.6 0.0 copy-start.1
  0.7 1.7 %pack.1.packed_ref = bf16[128,1024]{1,0:T(8,128)(2,1)} custom-call(bf16[128,512]{1,0:T(8,128)(2,1)} %wq_ref.1, bf16[128,512]{1,0:T(8,128)(2,1)} %wk_ref.1, bf16[128,512]{1,0:T(8,128)(2,1)} %wv_ref.1, bf16[64,1024]{1,0:T(8,128)(2,1)} %wo_ref.1), custom_call_target="tpu_custom_call" | custom-call | flops 1000000000 | bytes 2000000 | tf_op jit(solution)/shard_map/pack/pallas_call | solution.py:337
  2.4 4.9 %collective-permute-start = (bf16[128,1024]{1,0:T(8,128)(2,1)}, bf16[128,1024]{1,0:T(8,128)(2,1)S(1)}, u32[]{:S(2)}, u32[]{:S(2)}) collective-permute-start(bf16[128,1024]{1,0:T(8,128)(2,1)} %pack.1.packed_ref), channel_id=1, source_target_pairs={{0,66},{2,64},{64,2},{66,0},{1,67},{3,65},{65,3},{67,1},{4,70},{6,... | collective-permute-start | bytes 786440 | tf_op jit(solution)/shard_map/weights/ppermute | solution.py:354
  7.3 0.0 copy-done.2
  7.3 0.0 copy-done.1
  7.4 1.5 %interleave.1 = bf16[512,1024]{1,0:T(8,128)(2,1)} custom-call(bf16[256,1024]{1,0:T(8,128)(2,1)S(1)} %bitcast.39, bf16[256,1024]{1,0:T(8,128)(2,1)S(1)} %bitcast.41), custom_call_target="tpu_custom_call" | custom-call | flops 540000000 | bytes 2000000 | tf_op jit(solution)/shard_map/interleave/pallas_call | solution.py:327
  8.8 0.0 copy-start.4
  8.8 18.1 %all-to-all-start = ((bf16[64,8,1024]{2,1,0:T(8,128)(2,1)}), bf16[64,8,1024]{2,1,0:T(8,128)(2,1)}, u32[]{:S(2)}, u32[]{:S(2)}) async-start(bf16[64,8,1024]{2,1,0:T(8,128)(2,1)} %bitcast.10), calls=%async_computation | async-start | bytes 2097152 | tf_op jit(solution)/shard_map/to_columns/all_to_all | solution.py:348
  27.0 0.0 copy-start.14
  27.0 0.1 iota_compare_fusion
  27.1 0.6 copy-done.14
  27.7 0.0 collective-permute-done.flipped_ref
  27.7 0.0 copy-done.4
  27.7 0.0 copy-start
  27.7 3.3 %collective-permute-start.3 = (bf16[2,128,1024]{2,1,0:T(8,128)(2,1)S(1)}, bf16[2,128,1024]{2,1,0:T(8,128)(2,1)S(1)}, u32[]{:S(2)}, u32[]{:S(2)}) collective-permute-start(bf16[2,128,1024]{2,1,0:T(8,128)(2,1)S(1)} %pair.1.refs_0_), channel_id=1, source_target_pairs={{0,256},{128,384},{256,0},{384,128},{1,257},{129,385},{257,1},{385... | collective-permute-start | bytes 1572872 | tf_op jit(solution)/shard_map/weights/ppermute | solution.py:365
  31.0 4.0 %collective-permute-start.2 = (bf16[2,128,1024]{2,1,0:T(8,128)(2,1)S(1)}, bf16[2,128,1024]{2,1,0:T(8,128)(2,1)S(1)}, u32[]{:S(2)}, u32[]{:S(2)}) collective-permute-start(bf16[2,128,1024]{2,1,0:T(8,128)(2,1)S(1)} %pair.1.refs_0_), channel_id=1, source_target_pairs={{0,128},{128,256},{256,384},{384,0},{1,129},{129,257},{257,385},{3... | collective-permute-start | bytes 1572872 | tf_op jit(solution)/shard_map/weights/ppermute | solution.py:365
  35.1 1.9 %collective-permute-start.1 = (bf16[2,128,1024]{2,1,0:T(8,128)(2,1)S(1)}, bf16[2,128,1024]{2,1,0:T(8,128)(2,1)S(1)}, u32[]{:S(2)}, u32[]{:S(2)}) collective-permute-start(bf16[2,128,1024]{2,1,0:T(8,128)(2,1)S(1)} %pair.1.refs_0_), channel_id=1, source_target_pairs={{0,384},{128,0},{256,128},{384,256},{1,385},{129,1},{257,129},{385... | collective-permute-start | bytes 1572872 | tf_op jit(solution)/shard_map/weights/ppermute | solution.py:365
  37.0 0.1 copy.12
  37.1 1.4 fusion.6.bias_ref
  38.5 1.5 %fusion.3.bias_ref = bf16[4,256,256]{2,1,0:T(8,128)(2,1)} fusion(pred[256,256]{1,0:T(8,128)(4,1)S(1)} %get-tuple-element.51, pred[256,256]{1,0:T(8,128)(4,1)S(1)} %get-tuple-element.50, s32[256]{0:T(256)S(1)} %get-tuple-element.53, s32[4,4,8,8]{3,2,1,0:T(8,128)S(1)} %copy-done.15, s32[256]{0:T(256)S(1)} %get-tuple-element.52), kind=kOutput, calls=%fused_computation.5 | convolution fusion | flops 6564864 | bytes 661504 | tf_op jit(solution)/shard_map/masks/ia,hab,jb->hij/dot_general | solution.py:310
  39.9 1.9 %collective-permute-start.4 = (bf16[2,128,1024]{2,1,0:T(8,128)(2,1)S(1)}, bf16[2,128,1024]{2,1,0:T(8,128)(2,1)S(1)}, u32[]{:S(2)}, u32[]{:S(2)}) collective-permute-start(bf16[2,128,1024]{2,1,0:T(8,128)(2,1)S(1)} %pair.1.refs_0_), channel_id=1, source_target_pairs={{0,1},{1,0},{2,3},{3,2},{4,5},{5,4},{6,7},{7,6},{8,9},{9,8},{10,11... | collective-permute-start | bytes 1572872 | tf_op jit(solution)/shard_map/weights/ppermute | solution.py:368
  41.9 14.5 %collective-permute-done.1.refs_3_ = bf16[2,128,1024]{2,1,0:T(8,128)(2,1)S(1)} collective-permute-done((bf16[2,128,1024]{2,1,0:T(8,128)(2,1)S(1)}, bf16[2,128,1024]{2,1,0:T(8,128)(2,1)S(1)}, u32[]{:S(2)}, u32[]{:S(2)}) %collective-permute-start.1) | collective-permute-done | bytes 524320 | tf_op jit(solution)/shard_map/weights/ppermute | solution.py:365
  56.3 0.0 collective-permute-done.3.refs_2_
  56.3 2.0 %collective-permute-start.6 = (bf16[2,128,1024]{2,1,0:T(8,128)(2,1)S(1)}, bf16[2,128,1024]{2,1,0:T(8,128)(2,1)S(1)}, u32[]{:S(2)}, u32[]{:S(2)}) collective-permute-start(bf16[2,128,1024]{2,1,0:T(8,128)(2,1)S(1)} %collective-permute-done.3.refs_2_), channel_id=1, source_target_pairs={{0,1},{1,0},{2,3},{3,2},{4,5},{5,4},{6,7},{7,6},{8,9},{9,8},{10,11... | collective-permute-start | bytes 1572872 | tf_op jit(solution)/shard_map/weights/ppermute | solution.py:368
  58.4 0.0 collective-permute-done.2.refs_1_
  58.4 2.3 %collective-permute-start.5 = (bf16[2,128,1024]{2,1,0:T(8,128)(2,1)S(1)}, bf16[2,128,1024]{2,1,0:T(8,128)(2,1)S(1)}, u32[]{:S(2)}, u32[]{:S(2)}) collective-permute-start(bf16[2,128,1024]{2,1,0:T(8,128)(2,1)S(1)} %collective-permute-done.2.refs_1_), channel_id=1, source_target_pairs={{0,1},{1,0},{2,3},{3,2},{4,5},{5,4},{6,7},{7,6},{8,9},{9,8},{10,11... | collective-permute-start | bytes 1572872 | tf_op jit(solution)/shard_map/weights/ppermute | solution.py:368
  60.7 2.0 %collective-permute-start.7 = (bf16[2,128,1024]{2,1,0:T(8,128)(2,1)S(1)}, bf16[2,128,1024]{2,1,0:T(8,128)(2,1)S(1)}, u32[]{:S(2)}, u32[]{:S(2)}) collective-permute-start(bf16[2,128,1024]{2,1,0:T(8,128)(2,1)S(1)} %collective-permute-done.1.refs_3_), channel_id=1, source_target_pairs={{0,1},{1,0},{2,3},{3,2},{4,5},{5,4},{6,7},{7,6},{8,9},{9,8},{10,11... | collective-permute-start | bytes 1572872 | tf_op jit(solution)/shard_map/weights/ppermute | solution.py:368
  62.7 0.0 collective-permute-done.4.refs_4_
  62.8 0.0 collective-permute-done.6.refs_6_
  62.8 0.0 copy-start.11
  62.8 0.0 collective-permute-done.5.refs_5_
  62.8 1.7 %collective-permute-done.7.refs_7_ = bf16[2,128,1024]{2,1,0:T(8,128)(2,1)S(1)} collective-permute-done((bf16[2,128,1024]{2,1,0:T(8,128)(2,1)S(1)}, bf16[2,128,1024]{2,1,0:T(8,128)(2,1)S(1)}, u32[]{:S(2)}, u32[]{:S(2)}) %collective-permute-start.7) | collective-permute-done | bytes 524320 | tf_op jit(solution)/shard_map/weights/ppermute | solution.py:368
  64.5 0.0 copy-done.7
  64.6 0.8 copy-done.13
  65.4 5.9 %row_heads.1 = (bf16[256,1024]{1,0:T(8,128)(2,1)}, bf16[512,512]{1,0:T(8,128)(2,1)}, bf16[512,512]{1,0:T(8,128)(2,1)}) custom-call(bf16[256,1024]{1,0:T(8,128)(2,1)} %bitcast.38, bf16[256,1024]{1,0:T(8,128)(2,1)} %bitcast.40, bf16[4,256,256]{2,1,0:T(8,128)(2,1)} %fusion.6.bias_ref, bf16[2,128,1024]{2,1,0:T(8,128)(2,1)} %copy-done, ...), custom_call_target="tpu_custom_call" | custom-call | flops 1400000000 | bytes 12000000 | tf_op jit(solution)/shard_map/row_heads/pallas_call | solution.py:369
  71.3 2.0 %collective-permute-start.8 = (bf16[512,512]{1,0:T(8,128)(2,1)}, bf16[512,512]{1,0:T(8,128)(2,1)S(1)}, u32[]{:S(2)}, u32[]{:S(2)}) collective-permute-start(bf16[512,512]{1,0:T(8,128)(2,1)} %get-tuple-element.32), channel_id=1, source_target_pairs={{0,1},{1,0},{2,3},{3,2},{4,5},{5,4},{6,7},{7,6},{8,9},{9,8},{10,11... | collective-permute-start | bytes 1572872 | tf_op jit(solution)/shard_map/ppermute | solution.py:385
  73.3 1.2 all-to-all-done
  74.6 6.3 %column_heads.1 = (bf16[512,512]{1,0:T(8,128)(2,1)}, bf16[512,512]{1,0:T(8,128)(2,1)}, bf16[512,512]{1,0:T(8,128)(2,1)}) custom-call(bf16[512,1024]{1,0:T(8,128)(2,1)} %bitcast.11.both_ref, bf16[4,256,256]{2,1,0:T(8,128)(2,1)} %fusion.3.bias_ref, bf16[2,128,1024]{2,1,0:T(8,128)(2,1)} %copy-done, bf16[2,128,1024]{2,1,0:T(8,128)(2,1)} %copy-done.8, ...), custom_call_target="tpu_custom_call" | custom-call | flops 1900000000 | bytes 8000000 | tf_op jit(solution)/shard_map/column_heads/pallas_call | solution.py:387
  80.9 1.9 %collective-permute-start.9 = (bf16[512,512]{1,0:T(8,128)(2,1)}, bf16[512,512]{1,0:T(8,128)(2,1)S(1)}, u32[]{:S(2)}, u32[]{:S(2)}) collective-permute-start(bf16[512,512]{1,0:T(8,128)(2,1)} %get-tuple-element.36), channel_id=1, source_target_pairs={{0,1},{1,0},{2,3},{3,2},{4,5},{5,4},{6,7},{7,6},{8,9},{9,8},{10,11... | collective-permute-start | bytes 1572872 | tf_op jit(solution)/shard_map/ppermute | solution.py:407
  82.8 0.0 copy-start.3
  82.8 0.0 copy-start.5
  82.8 13.2 %all-to-all-start.1 = ((bf16[64,8,512]{2,1,0:T(8,128)(2,1)}), bf16[64,8,512]{2,1,0:T(8,128)(2,1)S(1)}, u32[]{:S(2)}, u32[]{:S(2)}) async-start(bf16[64,8,512]{2,1,0:T(8,128)(2,1)} %bitcast.44), calls=%async_computation.1 | async-start | bytes 1048576 | tf_op jit(solution)/shard_map/from_columns/all_to_all | solution.py:409
  96.1 0.0 collective-permute-done.8.row_got
  96.1 0.0 collective-permute-done.9.col_got
  96.1 0.0 copy-done.3
  96.1 0.0 copy-done.5
  96.1 0.3 pick.1
  96.4 3.3 %collective-permute-start.10 = (bf16[128,1024]{1,0:T(8,128)(2,1)S(1)}, bf16[128,1024]{1,0:T(8,128)(2,1)S(1)}, u32[]{:S(2)}, u32[]{:S(2)}) collective-permute-start(bf16[128,1024]{1,0:T(8,128)(2,1)S(1)} %get-tuple-element.38), channel_id=1, source_target_pairs={{0,256},{128,384},{256,0},{384,128},{1,257},{129,385},{257,1},{385... | collective-permute-start | bytes 786440 | tf_op jit(solution)/shard_map/gradient_sums/ppermute | solution.py:424
  99.7 4.0 %collective-permute-start.11 = (bf16[128,1024]{1,0:T(8,128)(2,1)S(1)}, bf16[128,1024]{1,0:T(8,128)(2,1)S(1)}, u32[]{:S(2)}, u32[]{:S(2)}) collective-permute-start(bf16[128,1024]{1,0:T(8,128)(2,1)S(1)} %get-tuple-element.39), channel_id=1, source_target_pairs={{0,128},{128,256},{256,384},{384,0},{1,129},{129,257},{257,385},{3... | collective-permute-start | bytes 786440 | tf_op jit(solution)/shard_map/gradient_sums/ppermute | solution.py:424
  103.7 2.1 %collective-permute-start.12 = (bf16[128,1024]{1,0:T(8,128)(2,1)S(1)}, bf16[128,1024]{1,0:T(8,128)(2,1)S(1)}, u32[]{:S(2)}, u32[]{:S(2)}) collective-permute-start(bf16[128,1024]{1,0:T(8,128)(2,1)S(1)} %get-tuple-element.40), channel_id=1, source_target_pairs={{0,384},{128,0},{256,128},{384,256},{1,385},{129,1},{257,129},{385... | collective-permute-start | bytes 786440 | tf_op jit(solution)/shard_map/gradient_sums/ppermute | solution.py:424
  105.8 2.6 %collective-permute-done.10.refs_1_ = bf16[128,1024]{1,0:T(8,128)(2,1)S(1)} collective-permute-done((bf16[128,1024]{1,0:T(8,128)(2,1)S(1)}, bf16[128,1024]{1,0:T(8,128)(2,1)S(1)}, u32[]{:S(2)}, u32[]{:S(2)}) %collective-permute-start.10) | collective-permute-done | bytes 262176 | tf_op jit(solution)/shard_map/gradient_sums/ppermute | solution.py:424
  108.4 3.2 %collective-permute-done.11.refs_2_ = bf16[128,1024]{1,0:T(8,128)(2,1)S(1)} collective-permute-done((bf16[128,1024]{1,0:T(8,128)(2,1)S(1)}, bf16[128,1024]{1,0:T(8,128)(2,1)S(1)}, u32[]{:S(2)}, u32[]{:S(2)}) %collective-permute-start.11) | collective-permute-done | bytes 262176 | tf_op jit(solution)/shard_map/gradient_sums/ppermute | solution.py:424
  111.6 3.1 %collective-permute-done.12.refs_3_ = bf16[128,1024]{1,0:T(8,128)(2,1)S(1)} collective-permute-done((bf16[128,1024]{1,0:T(8,128)(2,1)S(1)}, bf16[128,1024]{1,0:T(8,128)(2,1)S(1)}, u32[]{:S(2)}, u32[]{:S(2)}) %collective-permute-start.12) | collective-permute-done | bytes 262176 | tf_op jit(solution)/shard_map/gradient_sums/ppermute | solution.py:424
  114.6 0.2 spread.1
  114.9 2.9 %collective-permute-start.13 = (bf16[64,1024]{1,0:T(8,128)(2,1)S(1)}, bf16[64,1024]{1,0:T(8,128)(2,1)S(1)}, u32[]{:S(2)}, u32[]{:S(2)}) collective-permute-start(bf16[64,1024]{1,0:T(8,128)(2,1)S(1)} %get-tuple-element.42), channel_id=1, source_target_pairs={{0,66},{2,64},{64,2},{66,0},{1,67},{3,65},{65,3},{67,1},{4,70},{6,... | collective-permute-start | bytes 393224 | tf_op jit(solution)/shard_map/gradient_sums/ppermute | solution.py:437
  117.8 5.2 %collective-permute-done.13.got_ref = bf16[64,1024]{1,0:T(8,128)(2,1)S(1)} collective-permute-done((bf16[64,1024]{1,0:T(8,128)(2,1)S(1)}, bf16[64,1024]{1,0:T(8,128)(2,1)S(1)}, u32[]{:S(2)}, u32[]{:S(2)}) %collective-permute-start.13) | collective-permute-done | bytes 131104 | tf_op jit(solution)/shard_map/gradient_sums/ppermute | solution.py:437
  123.0 0.9 line.1
  123.9 0.0 all-to-all-done.1
  123.9 12.2 %all-to-all-start.2 = ((bf16[32,8,256]{2,1,0:T(8,128)(2,1)}), bf16[32,8,256]{2,1,0:T(8,128)(2,1)S(1)}, u32[]{:S(2)}, u32[]{:S(2)}) async-start(bf16[32,8,256]{2,1,0:T(8,128)(2,1)} %bitcast.16), calls=%async_computation.2 | async-start | bytes 262144 | tf_op jit(solution)/shard_map/gradient_sums/all_to_all | solution.py:448
  136.1 0.0 copy-done.6
  136.2 5.6 %output_products.1 = (bf16[256,1024]{1,0:T(8,128)(2,1)}, bf16[256,1024]{1,0:T(8,128)(2,1)}) custom-call(bf16[256,1024]{1,0:T(8,128)(2,1)} %get-tuple-element.29.row_ref, bf16[512,512]{1,0:T(8,128)(2,1)} %bitcast.43, bf16[2,128,1024]{2,1,0:T(8,128)(2,1)} %copy-done, bf16[2,128,1024]{2,1,0:T(8,128)(2,1)} %copy-done.8, bf16[2,128,1024]{2,1,0:T(8,128)(2,1)} %copy-done.7, ...), custom_call_target="tpu_custom_call" | custom-call | flops 1200000000 | bytes 8000000 | tf_op jit(solution)/shard_map/output_products/pallas_call | solution.py:461
  141.8 0.3 all-to-all-done.2
  142.1 0.6 last.1
  (20 shorter events, 0.1 us)
Async XLA Ops:
  0.6 6.7 %copy-start.2 = (bf16[1,1,256,1024]{3,2,1,0:T(8,128)(2,1)S(1)}, bf16[1,1,256,1024]{3,2,1,0:T(8,128)(2,1)}, u32[]{:S(2)}) copy-start(bf16[1,1,256,1024]{3,2,1,0:T(8,128)(2,1)} %param.9) | copy-start | bytes 1572868
  0.6 6.7 %copy-start.1 = (bf16[1,1,256,1024]{3,2,1,0:T(8,128)(2,1)S(1)}, bf16[1,1,256,1024]{3,2,1,0:T(8,128)(2,1)}, u32[]{:S(2)}) copy-start(bf16[1,1,256,1024]{3,2,1,0:T(8,128)(2,1)} %param.8) | copy-start | bytes 1572868
  2.4 25.2 %collective-permute-start = (bf16[128,1024]{1,0:T(8,128)(2,1)}, bf16[128,1024]{1,0:T(8,128)(2,1)S(1)}, u32[]{:S(2)}, u32[]{:S(2)}) collective-permute-start(bf16[128,1024]{1,0:T(8,128)(2,1)} %pack.1.packed_ref), channel_id=1, source_target_pairs={{0,66},{2,64},{64,2},{66,0},{1,67},{3,65},{65,3},{67,1},{4,70},{6,... | collective-permute-start | bytes 786440 | tf_op jit(solution)/shard_map/weights/ppermute | solution.py:354
  8.8 18.8 %copy-start.4 = (bf16[128,1024]{1,0:T(8,128)(2,1)S(1)}, bf16[128,1024]{1,0:T(8,128)(2,1)}, u32[]{:S(2)}) copy-start(bf16[128,1024]{1,0:T(8,128)(2,1)} %pack.1.packed_ref) | copy-start | bytes 786436
  8.8 65.7 %all-to-all-start = ((bf16[64,8,1024]{2,1,0:T(8,128)(2,1)}), bf16[64,8,1024]{2,1,0:T(8,128)(2,1)}, u32[]{:S(2)}, u32[]{:S(2)}) async-start(bf16[64,8,1024]{2,1,0:T(8,128)(2,1)} %bitcast.10), calls=%async_computation | async-start | bytes 2097152 | tf_op jit(solution)/shard_map/to_columns/all_to_all | solution.py:348
  27.0 0.7 copy-start.14
  27.7 12.2 %copy-start = (bf16[2,128,1024]{2,1,0:T(8,128)(2,1)}, bf16[2,128,1024]{2,1,0:T(8,128)(2,1)S(1)}, u32[]{:S(2)}) copy-start(bf16[2,128,1024]{2,1,0:T(8,128)(2,1)S(1)} %pair.1.refs_0_) | copy-start | bytes 1572868
  27.7 28.6 %collective-permute-start.3 = (bf16[2,128,1024]{2,1,0:T(8,128)(2,1)S(1)}, bf16[2,128,1024]{2,1,0:T(8,128)(2,1)S(1)}, u32[]{:S(2)}, u32[]{:S(2)}) collective-permute-start(bf16[2,128,1024]{2,1,0:T(8,128)(2,1)S(1)} %pair.1.refs_0_), channel_id=1, source_target_pairs={{0,256},{128,384},{256,0},{384,128},{1,257},{129,385},{257,1},{385... | collective-permute-start | bytes 1572872 | tf_op jit(solution)/shard_map/weights/ppermute | solution.py:365
  31.0 27.3 %collective-permute-start.2 = (bf16[2,128,1024]{2,1,0:T(8,128)(2,1)S(1)}, bf16[2,128,1024]{2,1,0:T(8,128)(2,1)S(1)}, u32[]{:S(2)}, u32[]{:S(2)}) collective-permute-start(bf16[2,128,1024]{2,1,0:T(8,128)(2,1)S(1)} %pair.1.refs_0_), channel_id=1, source_target_pairs={{0,128},{128,256},{256,384},{384,0},{1,129},{129,257},{257,385},{3... | collective-permute-start | bytes 1572872 | tf_op jit(solution)/shard_map/weights/ppermute | solution.py:365
  35.1 21.3 %collective-permute-start.1 = (bf16[2,128,1024]{2,1,0:T(8,128)(2,1)S(1)}, bf16[2,128,1024]{2,1,0:T(8,128)(2,1)S(1)}, u32[]{:S(2)}, u32[]{:S(2)}) collective-permute-start(bf16[2,128,1024]{2,1,0:T(8,128)(2,1)S(1)} %pair.1.refs_0_), channel_id=1, source_target_pairs={{0,384},{128,0},{256,128},{384,256},{1,385},{129,1},{257,129},{385... | collective-permute-start | bytes 1572872 | tf_op jit(solution)/shard_map/weights/ppermute | solution.py:365
  37.1 1.4 copy-start.15
  39.9 22.8 %collective-permute-start.4 = (bf16[2,128,1024]{2,1,0:T(8,128)(2,1)S(1)}, bf16[2,128,1024]{2,1,0:T(8,128)(2,1)S(1)}, u32[]{:S(2)}, u32[]{:S(2)}) collective-permute-start(bf16[2,128,1024]{2,1,0:T(8,128)(2,1)S(1)} %pair.1.refs_0_), channel_id=1, source_target_pairs={{0,1},{1,0},{2,3},{3,2},{4,5},{5,4},{6,7},{7,6},{8,9},{9,8},{10,11... | collective-permute-start | bytes 1572872 | tf_op jit(solution)/shard_map/weights/ppermute | solution.py:368
  56.3 8.2 %copy-start.9 = (bf16[2,128,1024]{2,1,0:T(8,128)(2,1)}, bf16[2,128,1024]{2,1,0:T(8,128)(2,1)S(1)}, u32[]{:S(2)}) copy-start(bf16[2,128,1024]{2,1,0:T(8,128)(2,1)S(1)} %collective-permute-done.1.refs_3_) | copy-start | bytes 1572868
  56.3 8.2 %copy-start.7 = (bf16[2,128,1024]{2,1,0:T(8,128)(2,1)}, bf16[2,128,1024]{2,1,0:T(8,128)(2,1)S(1)}, u32[]{:S(2)}) copy-start(bf16[2,128,1024]{2,1,0:T(8,128)(2,1)S(1)} %collective-permute-done.3.refs_2_) | copy-start | bytes 1572868
  56.3 6.4 %collective-permute-start.6 = (bf16[2,128,1024]{2,1,0:T(8,128)(2,1)S(1)}, bf16[2,128,1024]{2,1,0:T(8,128)(2,1)S(1)}, u32[]{:S(2)}, u32[]{:S(2)}) collective-permute-start(bf16[2,128,1024]{2,1,0:T(8,128)(2,1)S(1)} %collective-permute-done.3.refs_2_), channel_id=1, source_target_pairs={{0,1},{1,0},{2,3},{3,2},{4,5},{5,4},{6,7},{7,6},{8,9},{9,8},{10,11... | collective-permute-start | bytes 1572872 | tf_op jit(solution)/shard_map/weights/ppermute | solution.py:368
  58.4 6.1 %copy-start.8 = (bf16[2,128,1024]{2,1,0:T(8,128)(2,1)}, bf16[2,128,1024]{2,1,0:T(8,128)(2,1)S(1)}, u32[]{:S(2)}) copy-start(bf16[2,128,1024]{2,1,0:T(8,128)(2,1)S(1)} %collective-permute-done.2.refs_1_) | copy-start | bytes 1572868
  58.4 4.4 %collective-permute-start.5 = (bf16[2,128,1024]{2,1,0:T(8,128)(2,1)S(1)}, bf16[2,128,1024]{2,1,0:T(8,128)(2,1)S(1)}, u32[]{:S(2)}, u32[]{:S(2)}) collective-permute-start(bf16[2,128,1024]{2,1,0:T(8,128)(2,1)S(1)} %collective-permute-done.2.refs_1_), channel_id=1, source_target_pairs={{0,1},{1,0},{2,3},{3,2},{4,5},{5,4},{6,7},{7,6},{8,9},{9,8},{10,11... | collective-permute-start | bytes 1572872 | tf_op jit(solution)/shard_map/weights/ppermute | solution.py:368
  60.7 3.8 %collective-permute-start.7 = (bf16[2,128,1024]{2,1,0:T(8,128)(2,1)S(1)}, bf16[2,128,1024]{2,1,0:T(8,128)(2,1)S(1)}, u32[]{:S(2)}, u32[]{:S(2)}) collective-permute-start(bf16[2,128,1024]{2,1,0:T(8,128)(2,1)S(1)} %collective-permute-done.1.refs_3_), channel_id=1, source_target_pairs={{0,1},{1,0},{2,3},{3,2},{4,5},{5,4},{6,7},{7,6},{8,9},{9,8},{10,11... | collective-permute-start | bytes 1572872 | tf_op jit(solution)/shard_map/weights/ppermute | solution.py:368
  62.7 1.8 %copy-start.10 = (bf16[2,128,1024]{2,1,0:T(8,128)(2,1)}, bf16[2,128,1024]{2,1,0:T(8,128)(2,1)S(1)}, u32[]{:S(2)}) copy-start(bf16[2,128,1024]{2,1,0:T(8,128)(2,1)S(1)} %collective-permute-done.4.refs_4_) | copy-start | bytes 1572868
  62.8 1.8 %copy-start.11 = (bf16[2,128,1024]{2,1,0:T(8,128)(2,1)}, bf16[2,128,1024]{2,1,0:T(8,128)(2,1)S(1)}, u32[]{:S(2)}) copy-start(bf16[2,128,1024]{2,1,0:T(8,128)(2,1)S(1)} %collective-permute-done.6.refs_6_) | copy-start | bytes 1572868
  62.8 1.7 %copy-start.12 = (bf16[2,128,1024]{2,1,0:T(8,128)(2,1)}, bf16[2,128,1024]{2,1,0:T(8,128)(2,1)S(1)}, u32[]{:S(2)}) copy-start(bf16[2,128,1024]{2,1,0:T(8,128)(2,1)S(1)} %collective-permute-done.5.refs_5_) | copy-start | bytes 1572868
  64.5 0.8 copy-start.13
  71.3 24.8 %collective-permute-start.8 = (bf16[512,512]{1,0:T(8,128)(2,1)}, bf16[512,512]{1,0:T(8,128)(2,1)S(1)}, u32[]{:S(2)}, u32[]{:S(2)}) collective-permute-start(bf16[512,512]{1,0:T(8,128)(2,1)} %get-tuple-element.32), channel_id=1, source_target_pairs={{0,1},{1,0},{2,3},{3,2},{4,5},{5,4},{6,7},{7,6},{8,9},{9,8},{10,11... | collective-permute-start | bytes 1572872 | tf_op jit(solution)/shard_map/ppermute | solution.py:385
  80.9 15.2 %collective-permute-start.9 = (bf16[512,512]{1,0:T(8,128)(2,1)}, bf16[512,512]{1,0:T(8,128)(2,1)S(1)}, u32[]{:S(2)}, u32[]{:S(2)}) collective-permute-start(bf16[512,512]{1,0:T(8,128)(2,1)} %get-tuple-element.36), channel_id=1, source_target_pairs={{0,1},{1,0},{2,3},{3,2},{4,5},{5,4},{6,7},{7,6},{8,9},{9,8},{10,11... | collective-permute-start | bytes 1572872 | tf_op jit(solution)/shard_map/ppermute | solution.py:407
  82.8 13.3 %copy-start.3 = (bf16[512,512]{1,0:T(8,128)(2,1)S(1)}, bf16[512,512]{1,0:T(8,128)(2,1)}, u32[]{:S(2)}) copy-start(bf16[512,512]{1,0:T(8,128)(2,1)} %get-tuple-element.31.row_keep) | copy-start | bytes 1572868
  82.8 13.3 %copy-start.5 = (bf16[512,512]{1,0:T(8,128)(2,1)S(1)}, bf16[512,512]{1,0:T(8,128)(2,1)}, u32[]{:S(2)}) copy-start(bf16[512,512]{1,0:T(8,128)(2,1)} %get-tuple-element.35.col_keep) | copy-start | bytes 1572868
  82.8 41.1 %all-to-all-start.1 = ((bf16[64,8,512]{2,1,0:T(8,128)(2,1)}), bf16[64,8,512]{2,1,0:T(8,128)(2,1)S(1)}, u32[]{:S(2)}, u32[]{:S(2)}) async-start(bf16[64,8,512]{2,1,0:T(8,128)(2,1)} %bitcast.44), calls=%async_computation.1 | async-start | bytes 1048576 | tf_op jit(solution)/shard_map/from_columns/all_to_all | solution.py:409
  96.4 12.0 %collective-permute-start.10 = (bf16[128,1024]{1,0:T(8,128)(2,1)S(1)}, bf16[128,1024]{1,0:T(8,128)(2,1)S(1)}, u32[]{:S(2)}, u32[]{:S(2)}) collective-permute-start(bf16[128,1024]{1,0:T(8,128)(2,1)S(1)} %get-tuple-element.38), channel_id=1, source_target_pairs={{0,256},{128,384},{256,0},{384,128},{1,257},{129,385},{257,1},{385... | collective-permute-start | bytes 786440 | tf_op jit(solution)/shard_map/gradient_sums/ppermute | solution.py:424
  99.7 11.9 %collective-permute-start.11 = (bf16[128,1024]{1,0:T(8,128)(2,1)S(1)}, bf16[128,1024]{1,0:T(8,128)(2,1)S(1)}, u32[]{:S(2)}, u32[]{:S(2)}) collective-permute-start(bf16[128,1024]{1,0:T(8,128)(2,1)S(1)} %get-tuple-element.39), channel_id=1, source_target_pairs={{0,128},{128,256},{256,384},{384,0},{1,129},{129,257},{257,385},{3... | collective-permute-start | bytes 786440 | tf_op jit(solution)/shard_map/gradient_sums/ppermute | solution.py:424
  103.7 10.9 %collective-permute-start.12 = (bf16[128,1024]{1,0:T(8,128)(2,1)S(1)}, bf16[128,1024]{1,0:T(8,128)(2,1)S(1)}, u32[]{:S(2)}, u32[]{:S(2)}) collective-permute-start(bf16[128,1024]{1,0:T(8,128)(2,1)S(1)} %get-tuple-element.40), channel_id=1, source_target_pairs={{0,384},{128,0},{256,128},{384,256},{1,385},{129,1},{257,129},{385... | collective-permute-start | bytes 786440 | tf_op jit(solution)/shard_map/gradient_sums/ppermute | solution.py:424
  114.9 8.1 %collective-permute-start.13 = (bf16[64,1024]{1,0:T(8,128)(2,1)S(1)}, bf16[64,1024]{1,0:T(8,128)(2,1)S(1)}, u32[]{:S(2)}, u32[]{:S(2)}) collective-permute-start(bf16[64,1024]{1,0:T(8,128)(2,1)S(1)} %get-tuple-element.42), channel_id=1, source_target_pairs={{0,66},{2,64},{64,2},{66,0},{1,67},{3,65},{65,3},{67,1},{4,70},{6,... | collective-permute-start | bytes 393224 | tf_op jit(solution)/shard_map/gradient_sums/ppermute | solution.py:437
  123.9 12.2 %copy-start.6 = (bf16[64,8,512]{2,1,0:T(8,128)(2,1)}, bf16[64,8,512]{2,1,0:T(8,128)(2,1)S(1)}, u32[]{:S(2)}) copy-start(bf16[64,8,512]{2,1,0:T(8,128)(2,1)S(1)} %all-to-all-done.1) | copy-start | bytes 1572868
  123.9 18.2 %all-to-all-start.2 = ((bf16[32,8,256]{2,1,0:T(8,128)(2,1)}), bf16[32,8,256]{2,1,0:T(8,128)(2,1)S(1)}, u32[]{:S(2)}, u32[]{:S(2)}) async-start(bf16[32,8,256]{2,1,0:T(8,128)(2,1)} %bitcast.16), calls=%async_computation.2 | async-start | bytes 262144 | tf_op jit(solution)/shard_map/gradient_sums/all_to_all | solution.py:448

commit v10 on v9

--- a/solution.py
+++ b/solution.py
@@ -214,9 +214,10 @@
 
 
     def store(block):
-        if block in (3, 7):
-            rows = pl.ds((block - 3) * 64, 256)
-            pairs = [(keep.at[rows], keep_ref.at[rows]), (send.at[rows], send_ref.at[rows])]
+        if block in (3, 5, 7):
+            first = {3: 0, 5: 256, 7: 384}[block]
+            rows = pl.ds(first, (block + 1) * 64 - first)
+            pairs = [(send.at[rows], send_ref.at[rows]), (keep.at[rows], keep_ref.at[rows])]
             stores.extend(start_copies(pairs, sems, block - 2))
 
     store_gradients(lax.axis_index("c"), x[...], ct[...], out, dv, keep, send, store)

time: 144 us -> 144 us (level)
  no operation moved by 1% of the time
where the time goes in v10:
time: 144 us; the launch traced here: 143 us
  starting transfers between devices  82.3 us (57%)
  waiting for transfers between devices  31.7 us (22%)
  Pallas kernels  23.2 us (16%)
  matrix products  2.83 us (2%)
  local copies, waits for them, and re-layouts  1.55 us (1%)
    all_to_all x1, starting transfers between devices, body(): lax.all_to_all(sent.reshape(64, 8, 1024), seq, split_axis=0, concat_axis=...  18.1 us
    ppermute x3, waiting for transfers between devices, body(): lax.ppermute(pair, 'x', [(x, (x + step) % 4) for x in range(4)])  14.5 us
    all_to_all x1, starting transfers between devices, body(): lax.all_to_all(col_parts.reshape(64, 8, 512), seq, split_axis=0, concat_a...  13.2 us
    all_to_all x1, starting transfers between devices, body(): lax.all_to_all(line.reshape(32, 8, 256), ('z', 'yl'), split_axis=0, conca...  12.2 us
    ppermute x3, starting transfers between devices, body(): lax.ppermute(terms[step], 'x', [(x, (x + step) % 4) for x in range(4)])  9.43 us
    ppermute x3, starting transfers between devices, body(): lax.ppermute(pair, 'x', [(x, (x + step) % 4) for x in range(4)])  9.24 us
    ppermute x3, waiting for transfers between devices, body(): lax.ppermute(terms[step], 'x', [(x, (x + step) % 4) for x in range(4)])  8.79 us
    ppermute x4, starting transfers between devices, body(): weights += [lax.ppermute(part, 'c', SWAP) for part in weights]  8.26 us
  transfers between devices with their start and end apart: 17, of which 8 were waited for; matrix products, arithmetic and copies ran while one was open for 2% of the time, Pallas kernels for 15%

profile of v10, /device:TPU:6, one launch (start us, length us, event | category | flops | bytes accessed | tf_op | source)
XLA Modules:
  0.0 142.7 jit_solution(11162678969608282127)
XLA Ops:
  0.6 0.0 copy-start.2
  0.6 0.0 copy-start.1
  0.7 1.7 %pack.1.packed_ref = bf16[128,1024]{1,0:T(8,128)(2,1)} custom-call(bf16[128,512]{1,0:T(8,128)(2,1)} %wq_ref.1, bf16[128,512]{1,0:T(8,128)(2,1)} %wk_ref.1, bf16[128,512]{1,0:T(8,128)(2,1)} %wv_ref.1, bf16[64,1024]{1,0:T(8,128)(2,1)} %wo_ref.1), custom_call_target="tpu_custom_call" | custom-call | flops 1000000000 | bytes 2000000 | tf_op jit(solution)/shard_map/pack/pallas_call | solution.py:338
  2.4 4.9 %collective-permute-start = (bf16[128,1024]{1,0:T(8,128)(2,1)}, bf16[128,1024]{1,0:T(8,128)(2,1)S(1)}, u32[]{:S(2)}, u32[]{:S(2)}) collective-permute-start(bf16[128,1024]{1,0:T(8,128)(2,1)} %pack.1.packed_ref), channel_id=1, source_target_pairs={{0,66},{2,64},{64,2},{66,0},{1,67},{3,65},{65,3},{67,1},{4,70},{6,... | collective-permute-start | bytes 786440 | tf_op jit(solution)/shard_map/weights/ppermute | solution.py:355
  7.3 0.0 copy-done.2
  7.3 0.0 copy-done.1
  7.4 1.5 %interleave.1 = bf16[512,1024]{1,0:T(8,128)(2,1)} custom-call(bf16[256,1024]{1,0:T(8,128)(2,1)S(1)} %bitcast.39, bf16[256,1024]{1,0:T(8,128)(2,1)S(1)} %bitcast.41), custom_call_target="tpu_custom_call" | custom-call | flops 540000000 | bytes 2000000 | tf_op jit(solution)/shard_map/interleave/pallas_call | solution.py:328
  8.8 0.0 copy-start.4
  8.8 18.1 %all-to-all-start = ((bf16[64,8,1024]{2,1,0:T(8,128)(2,1)}), bf16[64,8,1024]{2,1,0:T(8,128)(2,1)}, u32[]{:S(2)}, u32[]{:S(2)}) async-start(bf16[64,8,1024]{2,1,0:T(8,128)(2,1)} %bitcast.10), calls=%async_computation | async-start | bytes 2097152 | tf_op jit(solution)/shard_map/to_columns/all_to_all | solution.py:349
  27.0 0.0 copy-start.14
  27.0 0.1 iota_compare_fusion
  27.1 0.6 copy-done.14
  27.7 0.0 collective-permute-done.flipped_ref
  27.7 0.0 copy-done.4
  27.7 3.3 %collective-permute-start.3 = (bf16[2,128,1024]{2,1,0:T(8,128)(2,1)S(1)}, bf16[2,128,1024]{2,1,0:T(8,128)(2,1)S(1)}, u32[]{:S(2)}, u32[]{:S(2)}) collective-permute-start(bf16[2,128,1024]{2,1,0:T(8,128)(2,1)S(1)} %pair.1.refs_0_), channel_id=1, source_target_pairs={{0,256},{128,384},{256,0},{384,128},{1,257},{129,385},{257,1},{385... | collective-permute-start | bytes 1572872 | tf_op jit(solution)/shard_map/weights/ppermute | solution.py:366
  31.0 4.0 %collective-permute-start.2 = (bf16[2,128,1024]{2,1,0:T(8,128)(2,1)S(1)}, bf16[2,128,1024]{2,1,0:T(8,128)(2,1)S(1)}, u32[]{:S(2)}, u32[]{:S(2)}) collective-permute-start(bf16[2,128,1024]{2,1,0:T(8,128)(2,1)S(1)} %pair.1.refs_0_), channel_id=1, source_target_pairs={{0,128},{128,256},{256,384},{384,0},{1,129},{129,257},{257,385},{3... | collective-permute-start | bytes 1572872 | tf_op jit(solution)/shard_map/weights/ppermute | solution.py:366
  35.1 1.9 %collective-permute-start.1 = (bf16[2,128,1024]{2,1,0:T(8,128)(2,1)S(1)}, bf16[2,128,1024]{2,1,0:T(8,128)(2,1)S(1)}, u32[]{:S(2)}, u32[]{:S(2)}) collective-permute-start(bf16[2,128,1024]{2,1,0:T(8,128)(2,1)S(1)} %pair.1.refs_0_), channel_id=1, source_target_pairs={{0,384},{128,0},{256,128},{384,256},{1,385},{129,1},{257,129},{385... | collective-permute-start | bytes 1572872 | tf_op jit(solution)/shard_map/weights/ppermute | solution.py:366
  37.0 0.1 copy.12
  37.1 1.4 fusion.6.bias_ref
  38.5 0.0 copy-done.15
  38.5 1.5 %fusion.3.bias_ref = bf16[4,256,256]{2,1,0:T(8,128)(2,1)} fusion(pred[256,256]{1,0:T(8,128)(4,1)S(1)} %get-tuple-element.51, pred[256,256]{1,0:T(8,128)(4,1)S(1)} %get-tuple-element.50, s32[256]{0:T(256)S(1)} %get-tuple-element.53, s32[4,4,8,8]{3,2,1,0:T(8,128)S(1)} %copy-done.15, s32[256]{0:T(256)S(1)} %get-tuple-element.52), kind=kOutput, calls=%fused_computation.5 | convolution fusion | flops 6564864 | bytes 661504 | tf_op jit(solution)/shard_map/masks/ia,hab,jb->hij/dot_general | solution.py:311
  39.9 1.9 %collective-permute-start.4 = (bf16[2,128,1024]{2,1,0:T(8,128)(2,1)S(1)}, bf16[2,128,1024]{2,1,0:T(8,128)(2,1)S(1)}, u32[]{:S(2)}, u32[]{:S(2)}) collective-permute-start(bf16[2,128,1024]{2,1,0:T(8,128)(2,1)S(1)} %pair.1.refs_0_), channel_id=1, source_target_pairs={{0,1},{1,0},{2,3},{3,2},{4,5},{5,4},{6,7},{7,6},{8,9},{9,8},{10,11... | collective-permute-start | bytes 1572872 | tf_op jit(solution)/shard_map/weights/ppermute | solution.py:369
  41.9 14.5 %collective-permute-done.1.refs_3_ = bf16[2,128,1024]{2,1,0:T(8,128)(2,1)S(1)} collective-permute-done((bf16[2,128,1024]{2,1,0:T(8,128)(2,1)S(1)}, bf16[2,128,1024]{2,1,0:T(8,128)(2,1)S(1)}, u32[]{:S(2)}, u32[]{:S(2)}) %collective-permute-start.1) | collective-permute-done | bytes 524320 | tf_op jit(solution)/shard_map/weights/ppermute | solution.py:366
  56.3 0.0 collective-permute-done.3.refs_2_
  56.3 2.0 %collective-permute-start.6 = (bf16[2,128,1024]{2,1,0:T(8,128)(2,1)S(1)}, bf16[2,128,1024]{2,1,0:T(8,128)(2,1)S(1)}, u32[]{:S(2)}, u32[]{:S(2)}) collective-permute-start(bf16[2,128,1024]{2,1,0:T(8,128)(2,1)S(1)} %collective-permute-done.3.refs_2_), channel_id=1, source_target_pairs={{0,1},{1,0},{2,3},{3,2},{4,5},{5,4},{6,7},{7,6},{8,9},{9,8},{10,11... | collective-permute-start | bytes 1572872 | tf_op jit(solution)/shard_map/weights/ppermute | solution.py:369
  58.4 0.0 collective-permute-done.2.refs_1_
  58.4 2.3 %collective-permute-start.5 = (bf16[2,128,1024]{2,1,0:T(8,128)(2,1)S(1)}, bf16[2,128,1024]{2,1,0:T(8,128)(2,1)S(1)}, u32[]{:S(2)}, u32[]{:S(2)}) collective-permute-start(bf16[2,128,1024]{2,1,0:T(8,128)(2,1)S(1)} %collective-permute-done.2.refs_1_), channel_id=1, source_target_pairs={{0,1},{1,0},{2,3},{3,2},{4,5},{5,4},{6,7},{7,6},{8,9},{9,8},{10,11... | collective-permute-start | bytes 1572872 | tf_op jit(solution)/shard_map/weights/ppermute | solution.py:369
  60.7 2.0 %collective-permute-start.7 = (bf16[2,128,1024]{2,1,0:T(8,128)(2,1)S(1)}, bf16[2,128,1024]{2,1,0:T(8,128)(2,1)S(1)}, u32[]{:S(2)}, u32[]{:S(2)}) collective-permute-start(bf16[2,128,1024]{2,1,0:T(8,128)(2,1)S(1)} %collective-permute-done.1.refs_3_), channel_id=1, source_target_pairs={{0,1},{1,0},{2,3},{3,2},{4,5},{5,4},{6,7},{7,6},{8,9},{9,8},{10,11... | collective-permute-start | bytes 1572872 | tf_op jit(solution)/shard_map/weights/ppermute | solution.py:369
  62.7 0.0 collective-permute-done.4.refs_4_
  62.7 0.0 copy-start.10
  62.8 0.0 collective-permute-done.6.refs_6_
  62.8 0.0 collective-permute-done.5.refs_5_
  62.8 1.7 %collective-permute-done.7.refs_7_ = bf16[2,128,1024]{2,1,0:T(8,128)(2,1)S(1)} collective-permute-done((bf16[2,128,1024]{2,1,0:T(8,128)(2,1)S(1)}, bf16[2,128,1024]{2,1,0:T(8,128)(2,1)S(1)}, u32[]{:S(2)}, u32[]{:S(2)}) %collective-permute-start.7) | collective-permute-done | bytes 524320 | tf_op jit(solution)/shard_map/weights/ppermute | solution.py:369
  64.5 0.0 copy-done.9
  64.5 0.0 copy-done.8
  64.6 0.8 copy-done.13
  65.4 5.9 %row_heads.1 = (bf16[256,1024]{1,0:T(8,128)(2,1)}, bf16[512,512]{1,0:T(8,128)(2,1)}, bf16[512,512]{1,0:T(8,128)(2,1)}) custom-call(bf16[256,1024]{1,0:T(8,128)(2,1)} %bitcast.38, bf16[256,1024]{1,0:T(8,128)(2,1)} %bitcast.40, bf16[4,256,256]{2,1,0:T(8,128)(2,1)} %fusion.6.bias_ref, bf16[2,128,1024]{2,1,0:T(8,128)(2,1)} %copy-done, ...), custom_call_target="tpu_custom_call" | custom-call | flops 1400000000 | bytes 12000000 | tf_op jit(solution)/shard_map/row_heads/pallas_call | solution.py:370
  71.3 2.0 %collective-permute-start.8 = (bf16[512,512]{1,0:T(8,128)(2,1)}, bf16[512,512]{1,0:T(8,128)(2,1)S(1)}, u32[]{:S(2)}, u32[]{:S(2)}) collective-permute-start(bf16[512,512]{1,0:T(8,128)(2,1)} %get-tuple-element.32), channel_id=1, source_target_pairs={{0,1},{1,0},{2,3},{3,2},{4,5},{5,4},{6,7},{7,6},{8,9},{9,8},{10,11... | collective-permute-start | bytes 1572872 | tf_op jit(solution)/shard_map/ppermute | solution.py:386
  73.3 1.2 all-to-all-done
  74.6 6.3 %column_heads.1 = (bf16[512,512]{1,0:T(8,128)(2,1)}, bf16[512,512]{1,0:T(8,128)(2,1)}, bf16[512,512]{1,0:T(8,128)(2,1)}) custom-call(bf16[512,1024]{1,0:T(8,128)(2,1)} %bitcast.11.both_ref, bf16[4,256,256]{2,1,0:T(8,128)(2,1)} %fusion.3.bias_ref, bf16[2,128,1024]{2,1,0:T(8,128)(2,1)} %copy-done, bf16[2,128,1024]{2,1,0:T(8,128)(2,1)} %copy-done.8, ...), custom_call_target="tpu_custom_call" | custom-call | flops 1900000000 | bytes 8000000 | tf_op jit(solution)/shard_map/column_heads/pallas_call | solution.py:388
  80.9 1.9 %collective-permute-start.9 = (bf16[512,512]{1,0:T(8,128)(2,1)}, bf16[512,512]{1,0:T(8,128)(2,1)S(1)}, u32[]{:S(2)}, u32[]{:S(2)}) collective-permute-start(bf16[512,512]{1,0:T(8,128)(2,1)} %get-tuple-element.36), channel_id=1, source_target_pairs={{0,1},{1,0},{2,3},{3,2},{4,5},{5,4},{6,7},{7,6},{8,9},{9,8},{10,11... | collective-permute-start | bytes 1572872 | tf_op jit(solution)/shard_map/ppermute | solution.py:408
  82.8 0.0 copy-start.3
  82.9 13.2 %all-to-all-start.1 = ((bf16[64,8,512]{2,1,0:T(8,128)(2,1)}), bf16[64,8,512]{2,1,0:T(8,128)(2,1)S(1)}, u32[]{:S(2)}, u32[]{:S(2)}) async-start(bf16[64,8,512]{2,1,0:T(8,128)(2,1)} %bitcast.44), calls=%async_computation.1 | async-start | bytes 1048576 | tf_op jit(solution)/shard_map/from_columns/all_to_all | solution.py:410
  96.1 0.0 collective-permute-done.8.row_got
  96.1 0.0 collective-permute-done.9.col_got
  96.1 0.0 copy-done.3
  96.1 0.0 copy-done.5
  96.1 0.3 pick.1
  96.4 3.3 %collective-permute-start.10 = (bf16[128,1024]{1,0:T(8,128)(2,1)S(1)}, bf16[128,1024]{1,0:T(8,128)(2,1)S(1)}, u32[]{:S(2)}, u32[]{:S(2)}) collective-permute-start(bf16[128,1024]{1,0:T(8,128)(2,1)S(1)} %get-tuple-element.38), channel_id=1, source_target_pairs={{0,256},{128,384},{256,0},{384,128},{1,257},{129,385},{257,1},{385... | collective-permute-start | bytes 786440 | tf_op jit(solution)/shard_map/gradient_sums/ppermute | solution.py:425
  99.7 4.0 %collective-permute-start.11 = (bf16[128,1024]{1,0:T(8,128)(2,1)S(1)}, bf16[128,1024]{1,0:T(8,128)(2,1)S(1)}, u32[]{:S(2)}, u32[]{:S(2)}) collective-permute-start(bf16[128,1024]{1,0:T(8,128)(2,1)S(1)} %get-tuple-element.39), channel_id=1, source_target_pairs={{0,128},{128,256},{256,384},{384,0},{1,129},{129,257},{257,385},{3... | collective-permute-start | bytes 786440 | tf_op jit(solution)/shard_map/gradient_sums/ppermute | solution.py:425
  103.8 2.1 %collective-permute-start.12 = (bf16[128,1024]{1,0:T(8,128)(2,1)S(1)}, bf16[128,1024]{1,0:T(8,128)(2,1)S(1)}, u32[]{:S(2)}, u32[]{:S(2)}) collective-permute-start(bf16[128,1024]{1,0:T(8,128)(2,1)S(1)} %get-tuple-element.40), channel_id=1, source_target_pairs={{0,384},{128,0},{256,128},{384,256},{1,385},{129,1},{257,129},{385... | collective-permute-start | bytes 786440 | tf_op jit(solution)/shard_map/gradient_sums/ppermute | solution.py:425
  105.9 2.6 %collective-permute-done.10.refs_1_ = bf16[128,1024]{1,0:T(8,128)(2,1)S(1)} collective-permute-done((bf16[128,1024]{1,0:T(8,128)(2,1)S(1)}, bf16[128,1024]{1,0:T(8,128)(2,1)S(1)}, u32[]{:S(2)}, u32[]{:S(2)}) %collective-permute-start.10) | collective-permute-done | bytes 262176 | tf_op jit(solution)/shard_map/gradient_sums/ppermute | solution.py:425
  108.4 3.2 %collective-permute-done.11.refs_2_ = bf16[128,1024]{1,0:T(8,128)(2,1)S(1)} collective-permute-done((bf16[128,1024]{1,0:T(8,128)(2,1)S(1)}, bf16[128,1024]{1,0:T(8,128)(2,1)S(1)}, u32[]{:S(2)}, u32[]{:S(2)}) %collective-permute-start.11) | collective-permute-done | bytes 262176 | tf_op jit(solution)/shard_map/gradient_sums/ppermute | solution.py:425
  111.6 3.1 %collective-permute-done.12.refs_3_ = bf16[128,1024]{1,0:T(8,128)(2,1)S(1)} collective-permute-done((bf16[128,1024]{1,0:T(8,128)(2,1)S(1)}, bf16[128,1024]{1,0:T(8,128)(2,1)S(1)}, u32[]{:S(2)}, u32[]{:S(2)}) %collective-permute-start.12) | collective-permute-done | bytes 262176 | tf_op jit(solution)/shard_map/gradient_sums/ppermute | solution.py:425
  114.7 0.2 spread.1
  114.9 2.9 %collective-permute-start.13 = (bf16[64,1024]{1,0:T(8,128)(2,1)S(1)}, bf16[64,1024]{1,0:T(8,128)(2,1)S(1)}, u32[]{:S(2)}, u32[]{:S(2)}) collective-permute-start(bf16[64,1024]{1,0:T(8,128)(2,1)S(1)} %get-tuple-element.42), channel_id=1, source_target_pairs={{0,66},{2,64},{64,2},{66,0},{1,67},{3,65},{65,3},{67,1},{4,70},{6,... | collective-permute-start | bytes 393224 | tf_op jit(solution)/shard_map/gradient_sums/ppermute | solution.py:438
  117.8 5.2 %collective-permute-done.13.got_ref = bf16[64,1024]{1,0:T(8,128)(2,1)S(1)} collective-permute-done((bf16[64,1024]{1,0:T(8,128)(2,1)S(1)}, bf16[64,1024]{1,0:T(8,128)(2,1)S(1)}, u32[]{:S(2)}, u32[]{:S(2)}) %collective-permute-start.13) | collective-permute-done | bytes 131104 | tf_op jit(solution)/shard_map/gradient_sums/ppermute | solution.py:438
  123.0 0.9 line.1
  123.9 0.0 all-to-all-done.1
  123.9 12.2 %all-to-all-start.2 = ((bf16[32,8,256]{2,1,0:T(8,128)(2,1)}), bf16[32,8,256]{2,1,0:T(8,128)(2,1)S(1)}, u32[]{:S(2)}, u32[]{:S(2)}) async-start(bf16[32,8,256]{2,1,0:T(8,128)(2,1)} %bitcast.16), calls=%async_computation.2 | async-start | bytes 262144 | tf_op jit(solution)/shard_map/gradient_sums/all_to_all | solution.py:449
  136.2 0.0 copy-done.6
  136.2 5.6 %output_products.1 = (bf16[256,1024]{1,0:T(8,128)(2,1)}, bf16[256,1024]{1,0:T(8,128)(2,1)}) custom-call(bf16[256,1024]{1,0:T(8,128)(2,1)} %get-tuple-element.29.row_ref, bf16[512,512]{1,0:T(8,128)(2,1)} %bitcast.43, bf16[2,128,1024]{2,1,0:T(8,128)(2,1)} %copy-done, bf16[2,128,1024]{2,1,0:T(8,128)(2,1)} %copy-done.8, bf16[2,128,1024]{2,1,0:T(8,128)(2,1)} %copy-done.7, ...), custom_call_target="tpu_custom_call" | custom-call | flops 1200000000 | bytes 8000000 | tf_op jit(solution)/shard_map/output_products/pallas_call | solution.py:462
  141.8 0.3 all-to-all-done.2
  142.1 0.6 last.1
  (20 shorter events, 0.1 us)
Async XLA Ops:
  0.6 6.7 %copy-start.2 = (bf16[1,1,256,1024]{3,2,1,0:T(8,128)(2,1)S(1)}, bf16[1,1,256,1024]{3,2,1,0:T(8,128)(2,1)}, u32[]{:S(2)}) copy-start(bf16[1,1,256,1024]{3,2,1,0:T(8,128)(2,1)} %param.9) | copy-start | bytes 1572868
  0.6 6.7 %copy-start.1 = (bf16[1,1,256,1024]{3,2,1,0:T(8,128)(2,1)S(1)}, bf16[1,1,256,1024]{3,2,1,0:T(8,128)(2,1)}, u32[]{:S(2)}) copy-start(bf16[1,1,256,1024]{3,2,1,0:T(8,128)(2,1)} %param.8) | copy-start | bytes 1572868
  2.4 25.2 %collective-permute-start = (bf16[128,1024]{1,0:T(8,128)(2,1)}, bf16[128,1024]{1,0:T(8,128)(2,1)S(1)}, u32[]{:S(2)}, u32[]{:S(2)}) collective-permute-start(bf16[128,1024]{1,0:T(8,128)(2,1)} %pack.1.packed_ref), channel_id=1, source_target_pairs={{0,66},{2,64},{64,2},{66,0},{1,67},{3,65},{65,3},{67,1},{4,70},{6,... | collective-permute-start | bytes 786440 | tf_op jit(solution)/shard_map/weights/ppermute | solution.py:355
  8.8 18.8 %copy-start.4 = (bf16[128,1024]{1,0:T(8,128)(2,1)S(1)}, bf16[128,1024]{1,0:T(8,128)(2,1)}, u32[]{:S(2)}) copy-start(bf16[128,1024]{1,0:T(8,128)(2,1)} %pack.1.packed_ref) | copy-start | bytes 786436
  8.8 65.7 %all-to-all-start = ((bf16[64,8,1024]{2,1,0:T(8,128)(2,1)}), bf16[64,8,1024]{2,1,0:T(8,128)(2,1)}, u32[]{:S(2)}, u32[]{:S(2)}) async-start(bf16[64,8,1024]{2,1,0:T(8,128)(2,1)} %bitcast.10), calls=%async_computation | async-start | bytes 2097152 | tf_op jit(solution)/shard_map/to_columns/all_to_all | solution.py:349
  27.0 0.7 copy-start.14
  27.7 12.2 %copy-start = (bf16[2,128,1024]{2,1,0:T(8,128)(2,1)}, bf16[2,128,1024]{2,1,0:T(8,128)(2,1)S(1)}, u32[]{:S(2)}) copy-start(bf16[2,128,1024]{2,1,0:T(8,128)(2,1)S(1)} %pair.1.refs_0_) | copy-start | bytes 1572868
  27.7 28.6 %collective-permute-start.3 = (bf16[2,128,1024]{2,1,0:T(8,128)(2,1)S(1)}, bf16[2,128,1024]{2,1,0:T(8,128)(2,1)S(1)}, u32[]{:S(2)}, u32[]{:S(2)}) collective-permute-start(bf16[2,128,1024]{2,1,0:T(8,128)(2,1)S(1)} %pair.1.refs_0_), channel_id=1, source_target_pairs={{0,256},{128,384},{256,0},{384,128},{1,257},{129,385},{257,1},{385... | collective-permute-start | bytes 1572872 | tf_op jit(solution)/shard_map/weights/ppermute | solution.py:366
  31.0 27.3 %collective-permute-start.2 = (bf16[2,128,1024]{2,1,0:T(8,128)(2,1)S(1)}, bf16[2,128,1024]{2,1,0:T(8,128)(2,1)S(1)}, u32[]{:S(2)}, u32[]{:S(2)}) collective-permute-start(bf16[2,128,1024]{2,1,0:T(8,128)(2,1)S(1)} %pair.1.refs_0_), channel_id=1, source_target_pairs={{0,128},{128,256},{256,384},{384,0},{1,129},{129,257},{257,385},{3... | collective-permute-start | bytes 1572872 | tf_op jit(solution)/shard_map/weights/ppermute | solution.py:366
  35.1 21.3 %collective-permute-start.1 = (bf16[2,128,1024]{2,1,0:T(8,128)(2,1)S(1)}, bf16[2,128,1024]{2,1,0:T(8,128)(2,1)S(1)}, u32[]{:S(2)}, u32[]{:S(2)}) collective-permute-start(bf16[2,128,1024]{2,1,0:T(8,128)(2,1)S(1)} %pair.1.refs_0_), channel_id=1, source_target_pairs={{0,384},{128,0},{256,128},{384,256},{1,385},{129,1},{257,129},{385... | collective-permute-start | bytes 1572872 | tf_op jit(solution)/shard_map/weights/ppermute | solution.py:366
  37.1 1.4 copy-start.15
  39.9 22.8 %collective-permute-start.4 = (bf16[2,128,1024]{2,1,0:T(8,128)(2,1)S(1)}, bf16[2,128,1024]{2,1,0:T(8,128)(2,1)S(1)}, u32[]{:S(2)}, u32[]{:S(2)}) collective-permute-start(bf16[2,128,1024]{2,1,0:T(8,128)(2,1)S(1)} %pair.1.refs_0_), channel_id=1, source_target_pairs={{0,1},{1,0},{2,3},{3,2},{4,5},{5,4},{6,7},{7,6},{8,9},{9,8},{10,11... | collective-permute-start | bytes 1572872 | tf_op jit(solution)/shard_map/weights/ppermute | solution.py:369
  56.3 8.2 %copy-start.9 = (bf16[2,128,1024]{2,1,0:T(8,128)(2,1)}, bf16[2,128,1024]{2,1,0:T(8,128)(2,1)S(1)}, u32[]{:S(2)}) copy-start(bf16[2,128,1024]{2,1,0:T(8,128)(2,1)S(1)} %collective-permute-done.1.refs_3_) | copy-start | bytes 1572868
  56.3 8.2 %copy-start.7 = (bf16[2,128,1024]{2,1,0:T(8,128)(2,1)}, bf16[2,128,1024]{2,1,0:T(8,128)(2,1)S(1)}, u32[]{:S(2)}) copy-start(bf16[2,128,1024]{2,1,0:T(8,128)(2,1)S(1)} %collective-permute-done.3.refs_2_) | copy-start | bytes 1572868
  56.3 6.4 %collective-permute-start.6 = (bf16[2,128,1024]{2,1,0:T(8,128)(2,1)S(1)}, bf16[2,128,1024]{2,1,0:T(8,128)(2,1)S(1)}, u32[]{:S(2)}, u32[]{:S(2)}) collective-permute-start(bf16[2,128,1024]{2,1,0:T(8,128)(2,1)S(1)} %collective-permute-done.3.refs_2_), channel_id=1, source_target_pairs={{0,1},{1,0},{2,3},{3,2},{4,5},{5,4},{6,7},{7,6},{8,9},{9,8},{10,11... | collective-permute-start | bytes 1572872 | tf_op jit(solution)/shard_map/weights/ppermute | solution.py:369
  58.4 6.1 %copy-start.8 = (bf16[2,128,1024]{2,1,0:T(8,128)(2,1)}, bf16[2,128,1024]{2,1,0:T(8,128)(2,1)S(1)}, u32[]{:S(2)}) copy-start(bf16[2,128,1024]{2,1,0:T(8,128)(2,1)S(1)} %collective-permute-done.2.refs_1_) | copy-start | bytes 1572868
  58.4 4.4 %collective-permute-start.5 = (bf16[2,128,1024]{2,1,0:T(8,128)(2,1)S(1)}, bf16[2,128,1024]{2,1,0:T(8,128)(2,1)S(1)}, u32[]{:S(2)}, u32[]{:S(2)}) collective-permute-start(bf16[2,128,1024]{2,1,0:T(8,128)(2,1)S(1)} %collective-permute-done.2.refs_1_), channel_id=1, source_target_pairs={{0,1},{1,0},{2,3},{3,2},{4,5},{5,4},{6,7},{7,6},{8,9},{9,8},{10,11... | collective-permute-start | bytes 1572872 | tf_op jit(solution)/shard_map/weights/ppermute | solution.py:369
  60.7 3.8 %collective-permute-start.7 = (bf16[2,128,1024]{2,1,0:T(8,128)(2,1)S(1)}, bf16[2,128,1024]{2,1,0:T(8,128)(2,1)S(1)}, u32[]{:S(2)}, u32[]{:S(2)}) collective-permute-start(bf16[2,128,1024]{2,1,0:T(8,128)(2,1)S(1)} %collective-permute-done.1.refs_3_), channel_id=1, source_target_pairs={{0,1},{1,0},{2,3},{3,2},{4,5},{5,4},{6,7},{7,6},{8,9},{9,8},{10,11... | collective-permute-start | bytes 1572872 | tf_op jit(solution)/shard_map/weights/ppermute | solution.py:369
  62.7 1.8 %copy-start.10 = (bf16[2,128,1024]{2,1,0:T(8,128)(2,1)}, bf16[2,128,1024]{2,1,0:T(8,128)(2,1)S(1)}, u32[]{:S(2)}) copy-start(bf16[2,128,1024]{2,1,0:T(8,128)(2,1)S(1)} %collective-permute-done.4.refs_4_) | copy-start | bytes 1572868
  62.8 1.8 %copy-start.11 = (bf16[2,128,1024]{2,1,0:T(8,128)(2,1)}, bf16[2,128,1024]{2,1,0:T(8,128)(2,1)S(1)}, u32[]{:S(2)}) copy-start(bf16[2,128,1024]{2,1,0:T(8,128)(2,1)S(1)} %collective-permute-done.6.refs_6_) | copy-start | bytes 1572868
  62.8 1.7 %copy-start.12 = (bf16[2,128,1024]{2,1,0:T(8,128)(2,1)}, bf16[2,128,1024]{2,1,0:T(8,128)(2,1)S(1)}, u32[]{:S(2)}) copy-start(bf16[2,128,1024]{2,1,0:T(8,128)(2,1)S(1)} %collective-permute-done.5.refs_5_) | copy-start | bytes 1572868
  64.5 0.8 copy-start.13
  71.3 24.8 %collective-permute-start.8 = (bf16[512,512]{1,0:T(8,128)(2,1)}, bf16[512,512]{1,0:T(8,128)(2,1)S(1)}, u32[]{:S(2)}, u32[]{:S(2)}) collective-permute-start(bf16[512,512]{1,0:T(8,128)(2,1)} %get-tuple-element.32), channel_id=1, source_target_pairs={{0,1},{1,0},{2,3},{3,2},{4,5},{5,4},{6,7},{7,6},{8,9},{9,8},{10,11... | collective-permute-start | bytes 1572872 | tf_op jit(solution)/shard_map/ppermute | solution.py:386
  80.9 15.2 %collective-permute-start.9 = (bf16[512,512]{1,0:T(8,128)(2,1)}, bf16[512,512]{1,0:T(8,128)(2,1)S(1)}, u32[]{:S(2)}, u32[]{:S(2)}) collective-permute-start(bf16[512,512]{1,0:T(8,128)(2,1)} %get-tuple-element.36), channel_id=1, source_target_pairs={{0,1},{1,0},{2,3},{3,2},{4,5},{5,4},{6,7},{7,6},{8,9},{9,8},{10,11... | collective-permute-start | bytes 1572872 | tf_op jit(solution)/shard_map/ppermute | solution.py:408
  82.8 13.3 %copy-start.3 = (bf16[512,512]{1,0:T(8,128)(2,1)S(1)}, bf16[512,512]{1,0:T(8,128)(2,1)}, u32[]{:S(2)}) copy-start(bf16[512,512]{1,0:T(8,128)(2,1)} %get-tuple-element.31.row_keep) | copy-start | bytes 1572868
  82.9 13.3 %copy-start.5 = (bf16[512,512]{1,0:T(8,128)(2,1)S(1)}, bf16[512,512]{1,0:T(8,128)(2,1)}, u32[]{:S(2)}) copy-start(bf16[512,512]{1,0:T(8,128)(2,1)} %get-tuple-element.35.col_keep) | copy-start | bytes 1572868
  82.9 41.1 %all-to-all-start.1 = ((bf16[64,8,512]{2,1,0:T(8,128)(2,1)}), bf16[64,8,512]{2,1,0:T(8,128)(2,1)S(1)}, u32[]{:S(2)}, u32[]{:S(2)}) async-start(bf16[64,8,512]{2,1,0:T(8,128)(2,1)} %bitcast.44), calls=%async_computation.1 | async-start | bytes 1048576 | tf_op jit(solution)/shard_map/from_columns/all_to_all | solution.py:410
  96.4 12.0 %collective-permute-start.10 = (bf16[128,1024]{1,0:T(8,128)(2,1)S(1)}, bf16[128,1024]{1,0:T(8,128)(2,1)S(1)}, u32[]{:S(2)}, u32[]{:S(2)}) collective-permute-start(bf16[128,1024]{1,0:T(8,128)(2,1)S(1)} %get-tuple-element.38), channel_id=1, source_target_pairs={{0,256},{128,384},{256,0},{384,128},{1,257},{129,385},{257,1},{385... | collective-permute-start | bytes 786440 | tf_op jit(solution)/shard_map/gradient_sums/ppermute | solution.py:425
  99.7 11.9 %collective-permute-start.11 = (bf16[128,1024]{1,0:T(8,128)(2,1)S(1)}, bf16[128,1024]{1,0:T(8,128)(2,1)S(1)}, u32[]{:S(2)}, u32[]{:S(2)}) collective-permute-start(bf16[128,1024]{1,0:T(8,128)(2,1)S(1)} %get-tuple-element.39), channel_id=1, source_target_pairs={{0,128},{128,256},{256,384},{384,0},{1,129},{129,257},{257,385},{3... | collective-permute-start | bytes 786440 | tf_op jit(solution)/shard_map/gradient_sums/ppermute | solution.py:425
  103.8 10.9 %collective-permute-start.12 = (bf16[128,1024]{1,0:T(8,128)(2,1)S(1)}, bf16[128,1024]{1,0:T(8,128)(2,1)S(1)}, u32[]{:S(2)}, u32[]{:S(2)}) collective-permute-start(bf16[128,1024]{1,0:T(8,128)(2,1)S(1)} %get-tuple-element.40), channel_id=1, source_target_pairs={{0,384},{128,0},{256,128},{384,256},{1,385},{129,1},{257,129},{385... | collective-permute-start | bytes 786440 | tf_op jit(solution)/shard_map/gradient_sums/ppermute | solution.py:425
  114.9 8.1 %collective-permute-start.13 = (bf16[64,1024]{1,0:T(8,128)(2,1)S(1)}, bf16[64,1024]{1,0:T(8,128)(2,1)S(1)}, u32[]{:S(2)}, u32[]{:S(2)}) collective-permute-start(bf16[64,1024]{1,0:T(8,128)(2,1)S(1)} %get-tuple-element.42), channel_id=1, source_target_pairs={{0,66},{2,64},{64,2},{66,0},{1,67},{3,65},{65,3},{67,1},{4,70},{6,... | collective-permute-start | bytes 393224 | tf_op jit(solution)/shard_map/gradient_sums/ppermute | solution.py:438
  123.9 12.2 %copy-start.6 = (bf16[64,8,512]{2,1,0:T(8,128)(2,1)}, bf16[64,8,512]{2,1,0:T(8,128)(2,1)S(1)}, u32[]{:S(2)}) copy-start(bf16[64,8,512]{2,1,0:T(8,128)(2,1)S(1)} %all-to-all-done.1) | copy-start | bytes 1572868
  123.9 18.2 %all-to-all-start.2 = ((bf16[32,8,256]{2,1,0:T(8,128)(2,1)}), bf16[32,8,256]{2,1,0:T(8,128)(2,1)S(1)}, u32[]{:S(2)}, u32[]{:S(2)}) async-start(bf16[32,8,256]{2,1,0:T(8,128)(2,1)} %bitcast.16), calls=%async_computation.2 | async-start | bytes 262144 | tf_op jit(solution)/shard_map/gradient_sums/all_to_all | solution.py:449
